TPU v7x, 32 devices: a whole 2x2x4 slice. The times are simulated.
32 devices in a mesh: blk: 16 (over z, y, core), head: 2 (over x).
Axes of the slice: x: 2, y: 2, z: 4, core: 2. Of those that a mesh axis runs over, the one named last changes fastest.
Arguments:
- tokens: bfloat16 [4096, 2048], P(('blk', 'head')), may hold values from -6 to 6
- attn_gain: bfloat16 [2048], P('blk'), may hold values from 0.25 to 1.75
- w_query: bfloat16 [2048, 2048], P('blk', 'head'), may hold values from -0.125 to 0.125
- w_key: bfloat16 [2048, 1024], P('blk', 'head'), may hold values from -0.125 to 0.125
- w_value: bfloat16 [2048, 1024], P('blk', 'head'), may hold values from -0.125 to 0.125
- w_out: bfloat16 [2048, 2048], P(('head', 'blk')), may hold values from -3.5 to 3.5
- mlp_gain: bfloat16 [2048], P('blk'), may hold values from 0.25 to 1.75
- w_gate: bfloat16 [2048, 8192], P('blk', 'head'), may hold values from -0.125 to 0.125
- w_up: bfloat16 [2048, 8192], P('blk', 'head'), may hold values from -0.125 to 0.125
- w_down: bfloat16 [8192, 2048], P(('head', 'blk')), may hold values from -0.0625 to 0.0625
- block_ids: int32 [4096], P('blk'), may hold values from 0 to 31, never falling along the last dimension, each value on 1 to 256 neighbouring positions
- positions: int32 [4096], P('blk'), may hold values from 0 to 6142, as said below
- cotangent: bfloat16 [4096, 2048], P(('blk', 'head')), may hold values from -6 to 6
Outputs:
- output: bfloat16 [4096, 2048], P(('blk', 'head'))
- tokens_grad: bfloat16 [4096, 2048], P(('blk', 'head'))
- attn_gain_grad: float32 [2048], P('blk')
- w_query_grad: float32 [2048, 2048], P('blk', 'head')
- w_key_grad: float32 [2048, 1024], P('blk', 'head')
- w_value_grad: float32 [2048, 1024], P('blk', 'head')
- w_out_grad: float32 [2048, 2048], P(('head', 'blk'))
- mlp_gain_grad: float32 [2048], P('blk')
- w_gate_grad: float32 [2048, 8192], P('blk', 'head')
- w_up_grad: float32 [2048, 8192], P('blk', 'head')
- w_down_grad: float32 [8192, 2048], P(('head', 'blk'))
Inputs may be any that keep to these rules, and one draw needn't show every extreme that they name: `block_ids`: block numbers never fall along the sequence; each block holds 1 to 256 tokens and some block exactly 256. `positions`: the first token has position 0 and each following one a position 1 or 2 higher; the last token has position 6142.
All inputs are finite; a program needn't handle non-finite values.
Results may differ from a plain program's by a relative error of at most 0.018.
Values may be sent and summed in bfloat16 or wider, within the bound.
A program may use at most 256 MiB of HBM per device.

v0:
```python
import jax
import jax.numpy as jnp
from jax import lax
from jax.sharding import PartitionSpec as P

HD = 256


eps_norm = 1e-06
rope_base = 1000042.0


def rms_scale(rows):
    return lax.rsqrt(jnp.mean(rows * rows, axis=-1, keepdims=True) + eps_norm)


def rope_tables(positions):
    inv_freqs = rope_base ** (-2.0 * jnp.arange(HD // 2, dtype=jnp.float32) / HD)
    angles = positions.astype(jnp.float32)[:, None] * inv_freqs[None, :]
    return (jnp.cos(angles)[:, None, :], jnp.sin(angles)[:, None, :])


def rotate(heads, cos_table, sine_table):
    half_size = heads.shape[-1] // 2
    lower_half = heads[..., :half_size]
    upper_half = heads[..., half_size:]
    return jnp.concatenate(
        [
            lower_half * cos_table - upper_half * sine_table,
            upper_half * cos_table + lower_half * sine_table,
        ],
        axis=-1,
    )


def product(left, right):
    return jnp.dot(left, right, preferred_element_type=jnp.float32)


def times_transposed(left, right):
    return lax.dot_general(
        left, right, (((1,), (1,)), ((), ())), preferred_element_type=jnp.float32
    )


def transposed_times(left, right):
    return lax.dot_general(
        left, right, (((0,), (0,)), ((), ())), preferred_element_type=jnp.float32
    )


def norm_backward(grad_normed, inputs, inv_scale, gain_rows):
    unit_rows = inputs * inv_scale
    grad_unit = grad_normed * gain_rows
    gain_term = jnp.sum(grad_normed * unit_rows, axis=0)
    grad_inputs = inv_scale * (
        grad_unit - unit_rows * jnp.mean(grad_unit * unit_rows, axis=-1, keepdims=True)
    )
    return (grad_inputs, gain_term)


def body(
    tokens,
    attn_gain,
    w_query,
    w_key,
    w_value,
    w_out,
    mlp_gain,
    w_gate,
    w_up,
    w_down,
    block_ids,
    positions,
    cotangent,
):
    rows_own = tokens.shape[0]
    head_rank = lax.axis_index("head")
    tokens_all, cot_all = (
        lax.all_gather(tokens, "head", axis=0, tiled=True),
        lax.all_gather(cotangent, "head", axis=0, tiled=True),
    )
    rows_all = tokens_all.shape[0]
    gain_attn, query_w, key_w, value_w, out_w = (
        lax.all_gather(attn_gain, "blk", axis=0, tiled=True),
        lax.all_gather(w_query, "blk", axis=0, tiled=True),
        lax.all_gather(w_key, "blk", axis=0, tiled=True),
        lax.all_gather(w_value, "blk", axis=0, tiled=True),
        lax.all_gather(w_out, "blk", axis=0, tiled=True),
    )
    gain_mlp, gate_w, up_w, down_w = (
        lax.all_gather(mlp_gain, "blk", axis=0, tiled=True),
        lax.all_gather(w_gate, "blk", axis=0, tiled=True),
        lax.all_gather(w_up, "blk", axis=0, tiled=True),
        lax.all_gather(w_down, "blk", axis=0, tiled=True),
    )
    key_ids = lax.all_gather(block_ids, "blk", axis=0, tiled=True)
    heads_local = query_w.shape[1] // HD
    kv_local = key_w.shape[1] // HD
    kv_width = kv_local * HD
    group_size = heads_local // kv_local
    cos_table, sine_table = rope_tables(positions)
    score_scale = HD ** (-0.5)
    seq_len = key_ids.shape[0]
    key_block = min(2048, seq_len)
    block_total = seq_len // key_block
    block_steps = jnp.arange(block_total)
    top_query = jnp.max(block_ids)
    inputs = tokens_all.astype(jnp.float32)
    inv_attn = rms_scale(inputs)
    normed = (inputs * inv_attn * gain_attn.astype(jnp.float32)).astype(jnp.bfloat16)
    queries = rotate(
        product(normed, query_w).reshape(rows_all, heads_local, HD), cos_table, sine_table
    ).astype(jnp.bfloat16)
    keys_own = rotate(product(normed, key_w).reshape(rows_all, kv_local, HD), cos_table, sine_table)
    keys_own = keys_own.astype(jnp.bfloat16).reshape(rows_all, kv_width)
    values_own = product(normed, value_w).astype(jnp.bfloat16)
    keys_all, values_all = (
        lax.all_gather(keys_own, "blk", axis=0, tiled=True),
        lax.all_gather(values_own, "blk", axis=0, tiled=True),
    )
    grouped = queries.reshape(rows_all, kv_local, group_size, HD)

    def slice_keys(key_start, count):
        key_rows = lax.dynamic_slice_in_dim(keys_all, key_start, count, 0).reshape(
            count, kv_local, HD
        )
        value_rows = lax.dynamic_slice_in_dim(values_all, key_start, count, 0).reshape(
            count, kv_local, HD
        )
        block_keys = lax.dynamic_slice_in_dim(key_ids, key_start, count, 0)
        return (key_rows, value_rows, block_keys)

    def scores_for(key_rows, block_keys):
        scores = (
            jnp.einsum("qkgd,ckd->kgqc", grouped, key_rows, preferred_element_type=jnp.float32)
            * score_scale
        )
        visible = (block_keys[None, :] <= block_ids[:, None])[None, None]
        return (scores, visible)

    def max_sum(state_pair, step_index):
        key_start = step_index * key_block

        def max_live(pair):
            run_max, run_sum = pair
            key_rows, value_rows, block_keys = slice_keys(key_start, key_block)
            scores, visible = scores_for(key_rows, block_keys)
            scores = jnp.where(visible, scores, -1e30)
            new_max = jnp.maximum(run_max, jnp.max(scores, axis=-1))
            kept_terms = jnp.where(visible, jnp.exp(scores - new_max[..., None]), 0.0)
            return (new_max, run_sum * jnp.exp(run_max - new_max) + jnp.sum(kept_terms, axis=-1))

        def max_skipped(pair):
            return pair

        return (lax.cond(key_ids[key_start] <= top_query, max_live, max_skipped, state_pair), None)

    start_max = jnp.full((kv_local, group_size, rows_all), -1e30, jnp.float32)
    start_sum = jnp.zeros((kv_local, group_size, rows_all), jnp.float32)
    (run_max, run_sum), unused_max = lax.scan(max_sum, (start_max, start_sum), block_steps)
    log_total = run_max + jnp.log(run_sum)

    def weighted(accum_rows, step_index):
        key_start = step_index * key_block

        def weighted_live(accum):
            key_rows, value_rows, block_keys = slice_keys(key_start, key_block)
            scores, visible = scores_for(key_rows, block_keys)
            probabilities = jnp.where(visible, jnp.exp(scores - log_total[..., None]), 0.0).astype(
                jnp.bfloat16
            )
            return accum + jnp.einsum(
                "kgqc,ckd->qkgd", probabilities, value_rows, preferred_element_type=jnp.float32
            )

        def weighted_skipped(accum):
            return accum

        return (
            lax.cond(key_ids[key_start] <= top_query, weighted_live, weighted_skipped, accum_rows),
            None,
        )

    attended, unused_rows = lax.scan(
        weighted, jnp.zeros((rows_all, kv_local, group_size, HD), jnp.float32), block_steps
    )
    attended_low = attended.reshape(rows_all, heads_local * HD).astype(jnp.bfloat16)
    branch_sum = lax.psum(product(attended_low, out_w).astype(jnp.bfloat16), "head").astype(
        jnp.float32
    )
    hidden = inputs + branch_sum
    inv_mlp = rms_scale(hidden)
    normed_mlp = (hidden * inv_mlp * gain_mlp.astype(jnp.float32)).astype(jnp.bfloat16)
    gate_pre = product(normed_mlp, gate_w)
    up_pre = product(normed_mlp, up_w)
    sigmoid_gate = jax.nn.sigmoid(gate_pre)
    active = (gate_pre * sigmoid_gate * up_pre).astype(jnp.bfloat16)
    mlp_own = lax.psum_scatter(
        product(active, down_w).astype(jnp.bfloat16), "head", scatter_dimension=0, tiled=True
    ).astype(jnp.float32)
    hidden_own = lax.dynamic_slice_in_dim(hidden, head_rank * rows_own, rows_own, 0)
    output = (hidden_own + mlp_own).astype(jnp.bfloat16)
    gain_attn, query_w, key_w, value_w, out_w = (
        lax.all_gather(attn_gain, "blk", axis=0, tiled=True),
        lax.all_gather(w_query, "blk", axis=0, tiled=True),
        lax.all_gather(w_key, "blk", axis=0, tiled=True),
        lax.all_gather(w_value, "blk", axis=0, tiled=True),
        lax.all_gather(w_out, "blk", axis=0, tiled=True),
    )
    gain_mlp, gate_w, up_w, down_w = (
        lax.all_gather(mlp_gain, "blk", axis=0, tiled=True),
        lax.all_gather(w_gate, "blk", axis=0, tiled=True),
        lax.all_gather(w_up, "blk", axis=0, tiled=True),
        lax.all_gather(w_down, "blk", axis=0, tiled=True),
    )
    grad_active = times_transposed(cot_all, down_w)
    grad_gate = (
        grad_active * up_pre * sigmoid_gate * (1.0 + gate_pre * (1.0 - sigmoid_gate))
    ).astype(jnp.bfloat16)
    grad_up = (grad_active * gate_pre * sigmoid_gate).astype(jnp.bfloat16)
    grad_gate_w = transposed_times(normed_mlp, grad_gate)
    grad_up_w = transposed_times(normed_mlp, grad_up)
    grad_down_w = transposed_times(active, cot_all)
    grad_normed_part = times_transposed(grad_gate, gate_w) + times_transposed(grad_up, up_w)
    grad_normed_mlp = lax.psum(grad_normed_part.astype(jnp.bfloat16), "head").astype(jnp.float32)
    grad_hidden_norm, gain_mlp_term = norm_backward(
        grad_normed_mlp, hidden, inv_mlp, gain_mlp.astype(jnp.float32)
    )
    grad_hidden = cot_all.astype(jnp.float32) + grad_hidden_norm
    mlp_results = (
        lax.psum_scatter(gain_mlp_term, "blk", scatter_dimension=0, tiled=True),
        lax.psum_scatter(grad_gate_w, "blk", scatter_dimension=0, tiled=True),
        lax.psum_scatter(grad_up_w, "blk", scatter_dimension=0, tiled=True),
        lax.psum_scatter(grad_down_w, "blk", scatter_dimension=0, tiled=True),
    )
    grad_branch = grad_hidden.astype(jnp.bfloat16)
    grad_out_w = transposed_times(attended_low, grad_branch)
    grad_attended = times_transposed(grad_branch, out_w).astype(jnp.bfloat16)
    grad_grouped = grad_attended.reshape(rows_all, kv_local, group_size, HD)
    delta_rows = jnp.transpose(
        jnp.sum(grad_grouped.astype(jnp.float32) * attended, axis=-1), (1, 2, 0)
    )

    def pair_backward(key_rows, value_rows, block_keys):
        count = key_rows.shape[0]
        scores, visible = scores_for(key_rows, block_keys)
        probabilities = jnp.where(visible, jnp.exp(scores - log_total[..., None]), 0.0)
        grad_probs = jnp.einsum(
            "qkgd,ckd->kgqc", grad_grouped, value_rows, preferred_element_type=jnp.float32
        )
        grad_scores = (probabilities * (grad_probs - delta_rows[..., None])).astype(jnp.bfloat16)
        query_terms = jnp.einsum(
            "kgqc,ckd->qkgd", grad_scores, key_rows, preferred_element_type=jnp.float32
        )
        key_terms = (
            jnp.einsum("kgqc,qkgd->ckd", grad_scores, grouped, preferred_element_type=jnp.float32)
            * score_scale
        )
        value_terms = jnp.einsum(
            "kgqc,qkgd->ckd",
            probabilities.astype(jnp.bfloat16),
            grad_grouped,
            preferred_element_type=jnp.float32,
        )
        return (
            query_terms,
            key_terms.reshape(count, kv_width),
            value_terms.reshape(count, kv_width),
        )

    query_zeros = jnp.zeros((rows_all, kv_local, group_size, HD), jnp.float32)

    def backward_block(accum_rows, step_index):
        key_start = step_index * key_block

        def backward_live(unused_arg):
            key_rows, value_rows, block_keys = slice_keys(key_start, key_block)
            return pair_backward(key_rows, value_rows, block_keys)

        def backward_skipped(unused_arg):
            empty_terms = jnp.zeros((key_block, kv_width), jnp.float32)
            return (query_zeros, empty_terms, empty_terms)

        query_terms, key_terms, value_terms = lax.cond(
            key_ids[key_start] <= top_query, backward_live, backward_skipped, 0
        )
        return (accum_rows + query_terms, (key_terms, value_terms))

    grad_query_rot, (key_terms, value_terms) = lax.scan(backward_block, query_zeros, block_steps)
    key_terms = key_terms.reshape(seq_len, kv_width)
    value_terms = value_terms.reshape(seq_len, kv_width)
    key_grad_own, value_grad_own = (
        lax.psum_scatter(key_terms, "blk", scatter_dimension=0, tiled=True),
        lax.psum_scatter(value_terms, "blk", scatter_dimension=0, tiled=True),
    )
    grad_query_rot = grad_query_rot * score_scale
    grad_key = rotate(key_grad_own.reshape(rows_all, kv_local, HD), cos_table, -sine_table)
    grad_key = grad_key.reshape(rows_all, kv_width).astype(jnp.bfloat16)
    grad_value = value_grad_own.astype(jnp.bfloat16)
    grad_query = rotate(grad_query_rot.reshape(rows_all, heads_local, HD), cos_table, -sine_table)
    grad_query = grad_query.reshape(rows_all, heads_local * HD).astype(jnp.bfloat16)
    grad_query_w = transposed_times(normed, grad_query)
    grad_key_w = transposed_times(normed, grad_key)
    grad_value_w = transposed_times(normed, grad_value)
    grad_normed_part = (
        times_transposed(grad_query, query_w)
        + times_transposed(grad_key, key_w)
        + times_transposed(grad_value, value_w)
    )
    grad_normed = lax.psum(grad_normed_part.astype(jnp.bfloat16), "head").astype(jnp.float32)
    grad_inputs_norm, gain_attn_term = norm_backward(
        grad_normed, inputs, inv_attn, gain_attn.astype(jnp.float32)
    )
    grad_inputs = grad_hidden + grad_inputs_norm
    grad_own = lax.dynamic_slice_in_dim(grad_inputs, head_rank * rows_own, rows_own, 0).astype(
        jnp.bfloat16
    )
    attn_results = (
        lax.psum_scatter(gain_attn_term, "blk", scatter_dimension=0, tiled=True),
        lax.psum_scatter(grad_query_w, "blk", scatter_dimension=0, tiled=True),
        lax.psum_scatter(grad_key_w, "blk", scatter_dimension=0, tiled=True),
        lax.psum_scatter(grad_value_w, "blk", scatter_dimension=0, tiled=True),
        lax.psum_scatter(grad_out_w, "blk", scatter_dimension=0, tiled=True),
    )
    return (
        output,
        grad_own,
        attn_results[0],
        attn_results[1],
        attn_results[2],
        attn_results[3],
        attn_results[4],
        mlp_results[0],
        mlp_results[1],
        mlp_results[2],
        mlp_results[3],
    )


def solution(mesh):
    placed = (
        P(("blk", "head"), None),
        P("blk"),
        P("blk", "head"),
        P("blk", "head"),
        P("blk", "head"),
        P(("head", "blk"), None),
        P("blk"),
        P("blk", "head"),
        P("blk", "head"),
        P(("head", "blk"), None),
        P("blk"),
        P("blk"),
        P(("blk", "head"), None),
    )
    return jax.shard_map(
        body,
        mesh=mesh,
        in_specs=placed,
        out_specs=(
            P(("blk", "head"), None),
            P(("blk", "head"), None),
            P("blk"),
            P("blk", "head"),
            P("blk", "head"),
            P("blk", "head"),
            P(("head", "blk"), None),
            P("blk"),
            P("blk", "head"),
            P("blk", "head"),
            P(("head", "blk"), None),
        ),
        check_vma=False,
    )
```

profile of v0, /device:TPU:8, one launch (start us, length us, event | category | flops | bytes accessed | tf_op | source)
XLA Modules:
  0.0 2612.0 jit_solution(17004117651422990038)
XLA Ops:
  10.0 18.9 all-gather.1
  33.6 41.1 %all-gather.17.cloned.1.call-done = bf16[2048,512]{1,0:T(8,128)(2,1)} async-done(((bf16[128,512]{1,0:T(8,128)(2,1)}), bf16[2048,512]{1,0:T(8,128)(2,1)}) %all-gather.17.cloned.1.call-update) | async-done | bytes 2097168 | tf_op jit(solution)/shard_map/all_gather | solution.py:88
  79.5 37.6 %all-gather.21.cloned.1.call-done = bf16[2048,512]{1,0:T(8,128)(2,1)} async-done(((bf16[128,512]{1,0:T(8,128)(2,1)}), bf16[2048,512]{1,0:T(8,128)(2,1)}) %all-gather.21.cloned.1.call-update) | async-done | bytes 2097168 | tf_op jit(solution)/shard_map/all_gather | solution.py:87
  122.7 17.4 all-gather
  140.1 29.4 %all-gather.25.cloned.1.call-done = bf16[2048,1024]{1,0:T(8,128)(2,1)} async-done(((bf16[128,1024]{1,0:T(8,128)(2,1)}), bf16[2048,1024]{1,0:T(8,128)(2,1)}) %all-gather.25.cloned.1.call-update) | async-done | bytes 4194320 | tf_op jit(solution)/shard_map/all_gather | solution.py:86
  176.6 44.6 %all-gather.19.cloned.1.call-done = bf16[4096,512]{1,0:T(8,128)(2,1)} async-done(((bf16[256,512]{1,0:T(8,128)(2,1)}), bf16[4096,512]{1,0:T(8,128)(2,1)}) %all-gather.19.cloned.1.call-update) | async-done | bytes 4194320 | tf_op jit(solution)/shard_map/all_gather | solution.py:120
  221.2 6.5 copy.98
  227.8 45.9 %all-gather.23.cloned.1.call-done = bf16[4096,512]{0,1:T(8,128)(2,1)} async-done(((bf16[256,512]{0,1:T(8,128)(2,1)}), bf16[4096,512]{0,1:T(8,128)(2,1)}) %all-gather.23.cloned.1.call-update) | async-done | bytes 4194320 | tf_op jit(solution)/shard_map/all_gather | solution.py:119
  273.7 14.3 while.40
  276.8 8.0 conditional.7
  288.9 18.7 while.41
  292.0 12.4 conditional.8
  292.1 6.4 constant_dynamic-slice_fusion.1
  299.0 5.5 fusion.6
  307.7 18.8 all-gather.27.cloned.1.call-done
  333.9 20.0 all-gather.2
  353.9 19.7 all-reduce.7.cloned.1.call-done
  375.8 125.2 %all-gather.29.cloned.1.call-done = bf16[2048,4096]{1,0:T(8,128)(2,1)} async-done(((bf16[128,4096]{1,0:T(8,128)(2,1)}), bf16[2048,4096]{1,0:T(8,128)(2,1)}) %all-gather.29.cloned.1.call-update) | async-done | bytes 16777232 | tf_op jit(solution)/shard_map/all_gather | solution.py:93
  501.0 10.1 fusion.47
  511.2 117.2 %all-gather.31.cloned.1.call-done = bf16[2048,4096]{1,0:T(8,128)(2,1)} async-done(((bf16[128,4096]{1,0:T(8,128)(2,1)}), bf16[2048,4096]{1,0:T(8,128)(2,1)}) %all-gather.31.cloned.1.call-update) | async-done | bytes 16777232 | tf_op jit(solution)/shard_map/all_gather | solution.py:94
  628.4 10.1 fusion.48
  638.5 12.9 all-gather.35.cloned.1.call-done
  651.4 127.3 %all-gather.33.cloned.1.call-done = bf16[4096,2048]{1,0:T(8,128)(2,1)} async-done(((bf16[256,2048]{1,0:T(8,128)(2,1)}), bf16[4096,2048]{1,0:T(8,128)(2,1)}) %all-gather.33.cloned.1.call-update) | async-done | bytes 16777232 | tf_op jit(solution)/shard_map/all_gather | solution.py:95
  778.7 13.8 multiply_convert_fusion
  792.5 12.3 fusion.49
  804.8 12.5 fusion.22
  817.3 40.1 %all-reduce.9.cloned.1.call-done = bf16[256,2048]{1,0:T(8,128)(2,1)} async-done(((bf16[256,2048]{1,0:T(8,128)(2,1)}), bf16[256,2048]{1,0:T(8,128)(2,1)}) %all-reduce.9.cloned.1.call-update) | async-done | bytes 1048592 | tf_op jit(solution)/shard_map/psum | solution.py:226
  867.9 66.9 %while.42 = (s32[]{:T(128)}, f32[256,2,2,256]{0,3,2,1:T(8,128)S(1)}, f32[2,2048,512]{2,1,0:T(8,128)}, f32[2,2048,512]{2,1,0:T(8,128)}, s32[2]{0:T(128)S(1)}, /*i...) while((s32[]{:T(128)}, ...), condition=%wide.region_21.22_spmd.clone, body=%wide.region_18.0_spmd.clone.sunk | while | flops 5391777792 | bytes 102274456 | solution.py:290
  871.2 17.9 conditional.9
  900.1 7.7 constant_dynamic-update-slice_fusion.3
  921.7 5.4 copy.148
  927.0 7.7 constant_dynamic-update-slice_fusion.3
  935.6 11.9 convolution_convert_fusion
  955.0 97.5 %reduce-scatter.13.cloned.1.call-done = f32[256,512]{1,0:T(8,128)} async-done(((f32[4096,512]{1,0:T(8,128)}), f32[256,512]{1,0:T(8,128)}) %reduce-scatter.13.cloned.1.call-update) | async-done | bytes 524304 | tf_op jit(solution)/shard_map/reduce_scatter | solution.py:294
  1057.8 102.9 %reduce-scatter.15.cloned.1.call-done = f32[256,512]{1,0:T(8,128)} async-done(((f32[4096,512]{1,0:T(8,128)}), f32[256,512]{1,0:T(8,128)}) %reduce-scatter.15.cloned.1.call-update) | async-done | bytes 524304 | tf_op jit(solution)/shard_map/reduce_scatter | solution.py:295
  1164.4 5.7 fusion.42
  1171.7 5.6 fusion.34
  1184.6 17.7 fusion.51
  1202.3 18.1 fusion.52
  1220.7 18.7 fusion.53
  1248.1 54.6 %all-reduce.2 = (f32[2048]{0:T(1024)S(1)}, f32[2048]{0:T(1024)S(1)}) all-reduce(f32[2048]{0:T(1024)S(1)} %get-tuple-element.460, f32[2048]{0:T(1024)S(1)} %copy-done.23), channel_id=5, replica_groups=mesh['blk'=16,'head'=2] {'blk'}, use_global_device_ids=true, to_apply=%region_27.28.clone | all-reduce | flops 4096 | bytes 32768
  1306.5 28.5 %reduce-scatter.17.cloned.1.call-done = f32[128,1024]{1,0:T(8,128)} async-done(((f32[2048,1024]{1,0:T(8,128)}), f32[128,1024]{1,0:T(8,128)}) %reduce-scatter.17.cloned.1.call-update) | async-done | bytes 524304 | tf_op jit(solution)/shard_map/reduce_scatter | solution.py:321
  1335.0 109.1 %reduce-scatter.23.cloned.1.call-done = f32[64,2048]{1,0:T(8,128)} async-done(((f32[1024,2048]{1,0:T(8,128)}), f32[64,2048]{1,0:T(8,128)}) %reduce-scatter.23.cloned.1.call-update) | async-done | bytes 524304 | tf_op jit(solution)/shard_map/reduce_scatter | solution.py:324
  1444.1 75.6 %reduce-scatter.19.cloned.1.call-done = f32[128,512]{1,0:T(8,128)} async-done(((f32[2048,512]{1,0:T(8,128)}), f32[128,512]{1,0:T(8,128)}) %reduce-scatter.19.cloned.1.call-update) | async-done | bytes 262160 | tf_op jit(solution)/shard_map/reduce_scatter | solution.py:322
  1519.7 76.4 %reduce-scatter.21.cloned.1.call-done = f32[128,512]{1,0:T(8,128)} async-done(((f32[2048,512]{1,0:T(8,128)}), f32[128,512]{1,0:T(8,128)}) %reduce-scatter.21.cloned.1.call-update) | async-done | bytes 262160 | tf_op jit(solution)/shard_map/reduce_scatter | solution.py:323
  1596.1 335.7 %reduce-scatter.25.cloned.1.call-done = f32[128,4096]{1,0:T(8,128)} async-done(((f32[2048,4096]{1,0:T(8,128)}), f32[128,4096]{1,0:T(8,128)}) %reduce-scatter.25.cloned.1.call-update) | async-done | bytes 2097168 | tf_op jit(solution)/shard_map/reduce_scatter | solution.py:233
  1931.9 336.6 %reduce-scatter.27.cloned.1.call-done = f32[128,4096]{1,0:T(8,128)} async-done(((f32[2048,4096]{1,0:T(8,128)}), f32[128,4096]{1,0:T(8,128)}) %reduce-scatter.27.cloned.1.call-update) | async-done | bytes 2097168 | tf_op jit(solution)/shard_map/reduce_scatter | solution.py:234
  2268.5 336.5 %reduce-scatter.29.cloned.1.call-done = f32[256,2048]{1,0:T(8,128)} async-done(((f32[4096,2048]{1,0:T(8,128)}), f32[256,2048]{1,0:T(8,128)}) %reduce-scatter.29.cloned.1.call-update) | async-done | bytes 2097168 | tf_op jit(solution)/shard_map/reduce_scatter | solution.py:235
  (215 shorter events, 143.9 us)
Async XLA Ops:
  7.2 24.9 all-gather.15.cloned.1.call-start
  7.9 66.8 %all-gather.17.cloned.1.call-start = ((), (), s32[]{:S(2)}) async-start(), calls=%async_computation.11 | async-start | bytes 2228224 | tf_op jit(solution)/shard_map/all_gather | solution.py:88
  8.7 108.4 %all-gather.21.cloned.1.call-start = ((), (), s32[]{:S(2)}) async-start(), calls=%async_computation.13 | async-start | bytes 2228224 | tf_op jit(solution)/shard_map/all_gather | solution.py:87
  9.4 160.2 %all-gather.25.cloned.1.call-start = ((), (), s32[]{:S(2)}) async-start(), calls=%async_computation.15 | async-start | bytes 4456448 | tf_op jit(solution)/shard_map/all_gather | solution.py:86
  10.0 211.3 %all-gather.19.cloned.1.call-start = ((), (), s32[]{:S(2)}) async-start(), calls=%async_computation.12 | async-start | bytes 4456448 | tf_op jit(solution)/shard_map/all_gather | solution.py:120
  28.9 140.6 %copy-start.17 = (f32[16,1,128]{2,1,0:T(1,128)}, f32[16,1,128]{2,1,0:T(1,128)S(1)}, u32[]{:S(2)}) copy-start(f32[16,1,128]{2,1,0:T(1,128)S(1)} %convert_element_type.146) | copy-start | bytes 24580
  33.6 136.0 %copy-start.21 = (f32[256]{0:T(256)}, f32[256]{0:T(256)S(1)}, u32[]{:S(2)}) copy-start(f32[256]{0:T(256)S(1)} %add_rsqrt_fusion.1) | copy-start | bytes 3076
  74.7 3.5 copy-start.24
  74.7 42.4 %copy-start = (bf16[256,2048]{1,0:T(8,128)(2,1)S(1)}, bf16[256,2048]{1,0:T(8,128)(2,1)}, u32[]{:S(2)}) copy-start(bf16[256,2048]{1,0:T(8,128)(2,1)} %all-gather.15.cloned.1.call-done) | copy-start | bytes 3145732
  78.2 195.5 %all-gather.23.cloned.1.call-start = ((), (), s32[]{:S(2)}) async-start(), calls=%async_computation.14 | async-start | bytes 4456448 | tf_op jit(solution)/shard_map/all_gather | solution.py:119
  79.5 96.3 %copy-start.11 = (f32[256,128]{1,0:T(8,128)}, f32[256,128]{1,0:T(8,128)S(1)}, u32[]{:S(2)}) copy-start(f32[256,128]{1,0:T(8,128)S(1)} %get-tuple-element.557) | copy-start | bytes 393220
  119.4 2.6 copy-start.20
  121.2 205.3 %all-gather.27.cloned.1.call-start = ((), (), s32[]{:S(2)}) async-start(), calls=%async_computation.16 | async-start | bytes 4456448 | tf_op jit(solution)/shard_map/all_gather | solution.py:89
  122.0 251.6 %all-reduce.7.cloned.1.call-start = ((), (), s32[]{:S(2)}) async-start(), calls=%async_computation.17 | async-start | bytes 2097152 | tf_op jit(solution)/shard_map/psum | solution.py:189
  307.6 23.3 copy-start.7
  307.7 23.2 copy-start.13
  330.9 2.9 copy-start.25
  331.0 170.1 %all-gather.29.cloned.1.call-start = ((), (), s32[]{:S(2)}) async-start(), calls=%async_computation.18 | async-start | bytes 17825792 | tf_op jit(solution)/shard_map/all_gather | solution.py:93
  331.7 296.7 %all-gather.31.cloned.1.call-start = ((), (), s32[]{:S(2)}) async-start(), calls=%async_computation.19 | async-start | bytes 17825792 | tf_op jit(solution)/shard_map/all_gather | solution.py:94
  332.3 319.1 %all-gather.35.cloned.1.call-start = ((), (), s32[]{:S(2)}) async-start(), calls=%async_computation.22 | async-start | bytes 1572864 | tf_op jit(solution)/shard_map/all_gather | solution.py:81
  333.0 445.7 %all-gather.33.cloned.1.call-start = ((), (), s32[]{:S(2)}) async-start(), calls=%async_computation.20 | async-start | bytes 17825792 | tf_op jit(solution)/shard_map/all_gather | solution.py:95
  333.6 523.9 %all-reduce.9.cloned.1.call-start = ((), (), s32[]{:S(2)}) async-start(), calls=%async_computation.23 | async-start | bytes 2097152 | tf_op jit(solution)/shard_map/psum | solution.py:226
  373.6 1.7 copy-start.2
  375.8 252.6 %copy-start.6 = (bf16[256,2048]{1,0:T(8,128)(2,1)}, bf16[256,2048]{1,0:T(8,128)(2,1)S(1)}, u32[]{:S(2)}) copy-start(bf16[256,2048]{1,0:T(8,128)(2,1)S(1)} %multiply_convert_fusion.3) | copy-start | bytes 3145732
  817.3 235.2 %reduce-scatter.13.cloned.1.call-start = ((), (), s32[]{:S(2)}) async-start(), calls=%async_computation.24 | async-start | bytes 8912896 | tf_op jit(solution)/shard_map/reduce_scatter | solution.py:294
  857.5 3.2 copy-start.3
  857.5 3.2 copy-start.9
  857.5 3.2 copy-start.10
  860.7 3.7 copy-start.26
  863.0 1.3 copy-start.4
  864.4 3.3 copy-start.8
  934.8 226.0 %reduce-scatter.15.cloned.1.call-start = ((), (), s32[]{:S(2)}) async-start(), calls=%async_computation.25 | async-start | bytes 8912896 | tf_op jit(solution)/shard_map/reduce_scatter | solution.py:295
  935.4 306.0 %reduce-scatter.11.cloned.1.call-start = ((), (), s32[]{:S(2)}) async-start(), calls=%async_computation.21 | async-start | bytes 1572864 | tf_op jit(solution)/shard_map/reduce_scatter | solution.py:199
  947.5 296.3 %all-reduce.11.cloned.1.call-start = ((), (), s32[]{:S(2)}) async-start(), calls=%async_computation.26 | async-start | bytes 2097152 | tf_op jit(solution)/shard_map/psum | solution.py:311
  947.7 1.0 copy-start.16
  1053.9 1.6 copy-start.14
  1057.8 106.5 %copy-start.1 = (bf16[256,2048]{1,0:T(8,128)(2,1)S(1)}, bf16[256,2048]{1,0:T(8,128)(2,1)}, u32[]{:S(2)}) copy-start(bf16[256,2048]{1,0:T(8,128)(2,1)} %all-gather.15.cloned.1.call-done) | copy-start | bytes 3145732
  1057.8 106.5 %copy-start.18 = (f32[16,1,128]{2,1,0:T(1,128)S(1)}, f32[16,1,128]{2,1,0:T(1,128)}, u32[]{:S(2)}) copy-start(f32[16,1,128]{2,1,0:T(1,128)} %copy-done.17) | copy-start | bytes 24580
  1057.8 106.5 %copy-start.22 = (f32[256]{0:T(256)S(1)}, f32[256]{0:T(256)}, u32[]{:S(2)}) copy-start(f32[256]{0:T(256)} %copy-done.21) | copy-start | bytes 3076
  1164.3 170.7 %reduce-scatter.17.cloned.1.call-start = ((), (), s32[]{:S(2)}) async-start(), calls=%async_computation.27 | async-start | bytes 8912896 | tf_op jit(solution)/shard_map/reduce_scatter | solution.py:321
  1170.1 1.6 copy-start.5
  1170.1 274.0 %reduce-scatter.23.cloned.1.call-start = ((), (), s32[]{:S(2)}) async-start(), calls=%async_computation.30 | async-start | bytes 8912896 | tf_op jit(solution)/shard_map/reduce_scatter | solution.py:324
  1177.2 342.5 %reduce-scatter.19.cloned.1.call-start = ((), (), s32[]{:S(2)}) async-start(), calls=%async_computation.28 | async-start | bytes 4456448 | tf_op jit(solution)/shard_map/reduce_scatter | solution.py:322
  1180.1 416.0 %reduce-scatter.21.cloned.1.call-start = ((), (), s32[]{:S(2)}) async-start(), calls=%async_computation.29 | async-start | bytes 4456448 | tf_op jit(solution)/shard_map/reduce_scatter | solution.py:323
  1184.5 747.3 %reduce-scatter.25.cloned.1.call-start = ((), (), s32[]{:S(2)}) async-start(), calls=%async_computation.31 | async-start | bytes 35651584 | tf_op jit(solution)/shard_map/reduce_scatter | solution.py:233
  1202.3 1066.2 %reduce-scatter.27.cloned.1.call-start = ((), (), s32[]{:S(2)}) async-start(), calls=%async_computation.32 | async-start | bytes 35651584 | tf_op jit(solution)/shard_map/reduce_scatter | solution.py:234
  1220.5 1384.5 %reduce-scatter.29.cloned.1.call-start = ((), (), s32[]{:S(2)}) async-start(), calls=%async_computation.33 | async-start | bytes 35651584 | tf_op jit(solution)/shard_map/reduce_scatter | solution.py:235
  1243.8 4.2 copy-start.23
  (4 other events, 3.2 us)
Sparse Core Ops, SparseCore 0:
  9.6 22.4 all-gather.14
  34.2 40.4 all-gather.16
  76.9 40.1 all-gather.20
  119.1 50.4 all-gather.24
  172.2 49.0 all-gather.18
  223.8 49.8 all-gather.22
  275.9 50.5 all-gather.26
  331.1 42.4 all-reduce.6
  376.0 125.0 all-gather.28
  503.3 125.0 all-gather.30
  630.0 21.3 all-gather.34
  653.6 125.0 all-gather.32
  817.4 40.0 all-reduce.8
  934.9 117.5 reduce-scatter.12
  1056.4 104.3 reduce-scatter.14
  1162.9 19.8 reduce-scatter.10
  1185.0 40.0 all-reduce.10
  1229.6 105.3 reduce-scatter.16
  1339.6 104.4 reduce-scatter.22
  1448.4 71.3 reduce-scatter.18
  1524.7 71.4 reduce-scatter.20
  1601.0 330.8 reduce-scatter.24
  1936.7 331.7 reduce-scatter.26
  2273.2 331.7 reduce-scatter.28
where the time goes:
time: 2620 us; the launch traced here: 2610 us
  waiting for transfers between devices  2170 us (83%)
  matrix products  191 us (7%)
  blocking collectives  111 us (4%)
  local copies, waits for them, and re-layouts  84.6 us (3%)
  other arithmetic  26.7 us (1%)
    reduce_scatter x1, waiting for transfers between devices, body(): lax.psum_scatter(grad_up_w, 'blk', scatter_dimension=0, tiled=True)  337 us
    reduce_scatter x1, waiting for transfers between devices, body(): lax.psum_scatter(grad_down_w, 'blk', scatter_dimension=0, tiled=True)  336 us
    reduce_scatter x1, waiting for transfers between devices, body(): lax.psum_scatter(grad_gate_w, 'blk', scatter_dimension=0, tiled=True)  336 us
    all_gather x1, waiting for transfers between devices, body(): lax.all_gather(w_down, 'blk', axis=0, tiled=True)  127 us
    all_gather x1, waiting for transfers between devices, body(): lax.all_gather(w_gate, 'blk', axis=0, tiled=True)  125 us
    all_gather x1, waiting for transfers between devices, body(): lax.all_gather(w_up, 'blk', axis=0, tiled=True)  117 us
    reduce_scatter x1, waiting for transfers between devices, body(): lax.psum_scatter(grad_out_w, 'blk', scatter_dimension=0, tiled=True)  109 us
    reduce_scatter x1, waiting for transfers between devices, body(): lax.psum_scatter(value_terms, 'blk', scatter_dimension=0, tiled=True)  103 us
  transfers between devices with their start and end apart: 24, of which 22 were waited for; matrix products, arithmetic and copies ran while one was open for 7% of the time, Pallas kernels for 0%

commit v1 on v0

--- a/solution.py
+++ b/solution.py
@@ -1,6 +1,8 @@
 import jax
 import jax.numpy as jnp
 from jax import lax
+from jax.experimental import pallas as pl
+from jax.experimental.pallas import tpu as pltpu
 from jax.sharding import PartitionSpec as P
 
 HD = 256
@@ -338,6 +340,1306 @@
     )
 
 
+MESH = pl.DeviceIdType.MESH
+LINE = 4
+VMEM_BYTES = 60 * 2**20
+
+
+def place():
+    blk, head = lax.axis_index("blk"), lax.axis_index("head")
+    return blk // 4, (blk // 2) % 2, blk % 2, head
+
+
+def device(z, y, c, h):
+    return (z * 4 + y * 2 + c, h)
+
+
+def remote(src, dst, send_sem, recv_sem, target):
+    return pltpu.make_async_remote_copy(
+        src_ref=src,
+        dst_ref=dst,
+        send_sem=send_sem,
+        recv_sem=recv_sem,
+        device_id=target,
+        device_id_type=MESH,
+    )
+
+
+def greet(target):
+    pl.semaphore_signal(
+        pltpu.get_barrier_semaphore(), inc=1, device_id=target, device_id_type=MESH
+    )
+
+
+def greet_all(blk_total, head_total):
+    blk, head = lax.axis_index("blk"), lax.axis_index("head")
+    for other in range(blk_total):
+        for half in range(head_total):
+
+            @pl.when(jnp.logical_or(blk != other, head != half))
+            def _():
+                greet((jnp.int32(other), jnp.int32(half)))
+
+    pl.semaphore_wait(pltpu.get_barrier_semaphore(), blk_total * head_total - 1)
+
+
+def greet_plane():
+    z, y, c, h = place()
+
+    @pl.when(z > 0)
+    def _():
+        greet(device(z - 1, y, c, h))
+
+    @pl.when(z < LINE - 1)
+    def _():
+        greet(device(z + 1, y, c, h))
+
+    greet(device(z, 1 - y, c, h))
+    pl.semaphore_wait(
+        pltpu.get_barrier_semaphore(),
+        1 + (z + LINE - 1) // LINE + (LINE - 1 - z + LINE - 1) // LINE,
+    )
+
+
+class Gather:
+    CUTS = ((0, 64), (64, 48), (112, 16), (112, 16))
+    SEMS = [(3, 4)] * 4 + [(4, 2)] * 2 + [(2,)]
+
+    @staticmethod
+    def scratch():
+        return [pltpu.SemaphoreType.DMA(shape) for shape in Gather.SEMS] + [
+            pltpu.SemaphoreType.DMA
+        ]
+
+    def __init__(self, src, out, sems):
+        self.src, self.out = src, out
+        (self.up_s, self.up_r, self.dn_s, self.dn_r, self.y_s, self.y_r, self.b_sr, self.own_sem) = sems
+        self.z, self.y, self.c, self.h = place()
+
+    def piece(self, line, elem):
+        y = 1 - self.y if elem == 3 else self.y
+        start, size = self.CUTS[elem]
+        return self.out.at[line * 2 + y, pl.ds(start, size)]
+
+    def first(self, elem):
+        if elem == 3:
+            return self.piece(self.z, 3)
+        start, size = self.CUTS[elem]
+        return self.src.at[pl.ds(start, size)]
+
+    def up(self, step, elem):
+        src = self.first(elem) if step == 0 else self.piece(self.z - step, elem)
+        return remote(
+            src, self.piece(self.z - step, elem), self.up_s.at[step, elem], self.up_r.at[step, elem],
+            device(self.z + 1, self.y, self.c, self.h),
+        )
+
+    def down(self, step, elem):
+        src = self.first(elem) if step == 0 else self.piece(self.z + step, elem)
+        return remote(
+            src, self.piece(self.z + step, elem), self.dn_s.at[step, elem], self.dn_r.at[step, elem],
+            device(self.z - 1, self.y, self.c, self.h),
+        )
+
+    def up_in(self, step, elem):
+        ref = self.piece(self.z - 1 - step, elem)
+        return remote(ref, ref, self.up_s.at[step, elem], self.up_r.at[step, elem], device(self.z, self.y, self.c, self.h))
+
+    def down_in(self, step, elem):
+        ref = self.piece(self.z + 1 + step, elem)
+        return remote(ref, ref, self.dn_s.at[step, elem], self.dn_r.at[step, elem], device(self.z, self.y, self.c, self.h))
+
+    def across(self, line, elem, own=False):
+        src = self.first(elem) if own else self.piece(line, elem)
+        return remote(
+            src, self.piece(line, elem), self.y_s.at[line, elem], self.y_r.at[line, elem],
+            device(self.z, 1 - self.y, self.c, self.h),
+        )
+
+    def across_in(self, line, elem):
+        start, size = self.CUTS[elem]
+        ref = self.out.at[line * 2 + 1 - self.y, pl.ds(start, size)]
+        return remote(ref, ref, self.y_s.at[line, elem], self.y_r.at[line, elem], device(self.z, self.y, self.c, self.h))
+
+    def across_b(self):
+        return remote(
+            self.first(2), self.piece(self.z, 2), self.b_sr.at[0], self.b_sr.at[1],
+            device(self.z, 1 - self.y, self.c, self.h),
+        )
+
+    def across_b_in(self):
+        ref = self.piece(self.z, 3)
+        return remote(ref, ref, self.b_sr.at[0], self.b_sr.at[1], device(self.z, self.y, self.c, self.h))
+
+    def own_copy(self):
+        return pltpu.make_async_copy(self.src, self.out.at[self.z * 2 + self.y], self.own_sem)
+
+    def start(self):
+        self.own_copy().start()
+        self.across_b().start()
+        for elem in (0, 1, 2):
+
+            @pl.when(self.z < LINE - 1)
+            def _():
+                self.up(0, elem).start()
+
+            @pl.when(self.z > 0)
+            def _():
+                self.down(0, elem).start()
+
+            if elem < 2:
+                self.across(self.z, elem, own=True).start()
+
+    def relay_b(self):
+        self.across_b_in().wait_recv()
+
+        @pl.when(self.z < LINE - 1)
+        def _():
+            self.up(0, 3).start()
+
+        @pl.when(self.z > 0)
+        def _():
+            self.down(0, 3).start()
+
+    def relay(self, step, elem):
+        @pl.when(self.z - 1 - step >= 0)
+        def _():
+            self.up_in(step, elem).wait_recv()
+            if step < LINE - 2:
+
+                @pl.when(self.z < LINE - 1)
+                def _():
+                    self.up(step + 1, elem).start()
+
+            if elem < 2:
+                self.across(self.z - 1 - step, elem).start()
+
+        @pl.when(self.z + 1 + step <= LINE - 1)
+        def _():
+            self.down_in(step, elem).wait_recv()
+            if step < LINE - 2:
+
+                @pl.when(self.z > 0)
+                def _():
+                    self.down(step + 1, elem).start()
+
+            if elem < 2:
+                self.across(self.z + 1 + step, elem).start()
+
+    def relays(self):
+        self.relay_b()
+        for step in range(LINE - 1):
+            for elem in (0, 1, 2, 3):
+                self.relay(step, elem)
+
+    def finish(self):
+        for line in range(LINE):
+            for elem in (0, 1):
+                self.across_in(line, elem).wait_recv()
+        for line in range(LINE):
+            for elem in (0, 1):
+                self.across(line, elem).wait_send()
+        self.across_b().wait_send()
+        for step in range(LINE - 1):
+            for elem in range(4):
+
+                @pl.when(jnp.logical_and(self.z < LINE - 1, self.z - step >= 0))
+                def _():
+                    self.up(step, elem).wait_send()
+
+                @pl.when(jnp.logical_and(self.z > 0, self.z + step <= LINE - 1))
+                def _():
+                    self.down(step, elem).wait_send()
+
+        self.own_copy().wait()
+
+
+def gather_kernel(src, out, *sems):
+    greet_plane()
+    gather = Gather(src, out, sems)
+    gather.start()
+    gather.relays()
+    gather.finish()
+
+
+ANY = pl.BlockSpec(memory_space=pl.ANY)
+INSIDE = pl.BlockSpec(memory_space=pltpu.VMEM)
+
+
+def kernel_params(collective_id):
+    return pltpu.CompilerParams(
+        collective_id=collective_id, has_side_effects=True, vmem_limit_bytes=VMEM_BYTES
+    )
+
+
+def gather_plane(rows):
+    return pl.pallas_call(
+        gather_kernel,
+        out_shape=jax.ShapeDtypeStruct((2 * LINE,) + rows.shape, rows.dtype),
+        in_specs=[ANY],
+        out_specs=ANY,
+        scratch_shapes=Gather.scratch(),
+        compiler_params=kernel_params(1),
+        name="gather_plane",
+    )(rows)
+
+
+class Reduce:
+    CUTS = ((0, 64), (64, 64))
+
+    @staticmethod
+    def scratch(width):
+        inbox = pltpu.VMEM((LINE, 128, width), jnp.bfloat16)
+        return [inbox] * 3 + [pltpu.SemaphoreType.DMA((LINE, 2))] * 6
+
+    def __init__(self, parts, refs):
+        self.parts = parts
+        self.y_in, self.up_in, self.dn_in = refs[:3]
+        self.y_s, self.y_r, self.up_s, self.up_r, self.dn_s, self.dn_r = refs[3:]
+        self.z, self.y, self.c, self.h = place()
+        z = self.z
+        self.order = (3 - 3 * (z // 2), (2 + 3 * z) % 5, 1 + z % 2, z)
+
+    def rows(self, cut):
+        return pl.ds(*self.CUTS[cut])
+
+    def across(self, line, cut):
+        return remote(
+            self.parts.at[line * 2 + 1 - self.y, self.rows(cut)], self.y_in.at[line, self.rows(cut)],
+            self.y_s.at[line, cut], self.y_r.at[line, cut], device(self.z, 1 - self.y, self.c, self.h),
+        )
+
+    def up(self, line, cut):
+        return remote(
+            self.parts.at[line * 2 + self.y, self.rows(cut)], self.up_in.at[line, self.rows(cut)],
+            self.up_s.at[line, cut], self.up_r.at[line, cut], device(self.z + 1, self.y, self.c, self.h),
+        )
+
+    def down(self, line, cut):
+        return remote(
+            self.parts.at[line * 2 + self.y, self.rows(cut)], self.dn_in.at[line, self.rows(cut)],
+            self.dn_s.at[line, cut], self.dn_r.at[line, cut], device(self.z - 1, self.y, self.c, self.h),
+        )
+
+    def start(self, place_at):
+        for cut in range(2):
+            self.across(self.order[place_at], cut).start()
+
+    def own(self, line, cut):
+        return self.parts.at[line * 2 + self.y, self.rows(cut)]
+
+    def relay(self, place_at):
+        line = self.order[place_at]
+        for cut in range(2):
+            rows = self.rows(cut)
+            self.across(line, cut).wait_recv()
+            target = self.parts.at[line * 2 + self.y]
+
+            @pl.when(line > self.z)
+            def _():
+                @pl.when(self.z > 0)
+                def _():
+                    self.up(line, cut).wait_recv()
+                    total = (
+                        target[rows].astype(jnp.float32)
+                        + self.y_in[line, rows].astype(jnp.float32)
+                        + self.up_in[line, rows].astype(jnp.float32)
+                    )
+                    target[rows] = total.astype(jnp.bfloat16)
+
+                @pl.when(self.z == 0)
+                def _():
+                    total = target[rows].astype(jnp.float32) + self.y_in[line, rows].astype(jnp.float32)
+                    target[rows] = total.astype(jnp.bfloat16)
+
+                self.up(line, cut).start()
+
+            @pl.when(line < self.z)
+            def _():
+                @pl.when(self.z < LINE - 1)
+                def _():
+                    self.down(line, cut).wait_recv()
+                    total = (
+                        target[rows].astype(jnp.float32)
+                        + self.y_in[line, rows].astype(jnp.float32)
+                        + self.dn_in[line, rows].astype(jnp.float32)
+                    )
+                    target[rows] = total.astype(jnp.bfloat16)
+
+                @pl.when(self.z == LINE - 1)
+                def _():
+                    total = target[rows].astype(jnp.float32) + self.y_in[line, rows].astype(jnp.float32)
+                    target[rows] = total.astype(jnp.bfloat16)
+
+                self.down(line, cut).start()
+
+    def total(self, out):
+        line = self.z
+        for cut in range(2):
+            rows = self.rows(cut)
+            self.across(line, cut).wait_recv()
+            out[rows] = self.parts[line * 2 + self.y, rows].astype(jnp.float32) + self.y_in[line, rows].astype(jnp.float32)
+        for cut in range(2):
+            rows = self.rows(cut)
+
+            @pl.when(self.z > 0)
+            def _():
+                self.up(line, cut).wait_recv()
+                out[rows] += self.up_in[line, rows].astype(jnp.float32)
+
+            @pl.when(self.z < LINE - 1)
+            def _():
+                self.down(line, cut).wait_recv()
+                out[rows] += self.dn_in[line, rows].astype(jnp.float32)
+
+    def finish(self):
+        for line in range(LINE):
+            for cut in range(2):
+                self.across(line, cut).wait_send()
+
+                @pl.when(self.z < line)
+                def _():
+                    self.up(line, cut).wait_send()
+
+                @pl.when(self.z > line)
+                def _():
+                    self.down(line, cut).wait_send()
+
+
+def reduce_kernel(parts_in, out, parts, in_sem, *refs):
+    load = pltpu.make_async_copy(parts_in, parts, in_sem)
+    load.start()
+    greet_plane()
+    reduce = Reduce(parts, refs)
+    load.wait()
+    for place_at in range(4):
+        reduce.start(place_at)
+    for place_at in range(3):
+        reduce.relay(place_at)
+    reduce.total(out)
+    reduce.finish()
+
+
+def reduce_plane(parts):
+    shape = parts.shape
+    return pl.pallas_call(
+        reduce_kernel,
+        out_shape=jax.ShapeDtypeStruct(shape[1:], jnp.float32),
+        in_specs=[ANY],
+        out_specs=INSIDE,
+        scratch_shapes=[pltpu.VMEM(shape, jnp.bfloat16), pltpu.SemaphoreType.DMA] + Reduce.scratch(shape[2]),
+        compiler_params=kernel_params(2),
+        name="reduce_plane",
+    )(parts)
+
+
+def dma(*shape):
+    return pltpu.SemaphoreType.DMA(shape) if shape else pltpu.SemaphoreType.DMA
+
+
+def local(src, dst, sem):
+    return pltpu.make_async_copy(src, dst, sem)
+
+
+class AttnSpread:
+    @staticmethod
+    def scratch():
+        return [dma(3, 4, 2), dma(3, 8), dma(3), dma(2), dma(2), dma(2), dma(1), dma(2)]
+
+    def __init__(self, weights, outs, sems):
+        self.weights, (self.qkv, self.out_w) = weights, outs
+        (self.s, self.r, self.own, self.sib, self.o_s, self.o_r, self.o_own, self.o_sib) = sems
+        self.z, self.y, self.c, self.h = place()
+
+    def source(self, kind, line):
+        start = line * HD if kind == 0 else (line // 2) * HD
+        return self.weights[kind].at[:, pl.ds(start, HD)]
+
+    def slot(self, kind, chip):
+        return self.qkv.at[chip, self.c, :, pl.ds(kind * HD, HD)]
+
+    def is_self(self, line, half):
+        return (self.z == line) & (self.y == self.h) & (self.h == half)
+
+    def push(self, kind, line, half):
+        chip = self.z * 2 + self.y
+        return remote(
+            self.source(kind, line), self.slot(kind, chip), self.s.at[kind, line, half], self.r.at[kind, chip],
+            device(line, self.h, self.c, half),
+        )
+
+    def keep(self, kind, line):
+        return local(self.source(kind, line), self.slot(kind, self.z * 2 + self.y), self.own.at[kind])
+
+    def pull(self, kind, chip):
+        ref = self.slot(kind, chip)
+        return remote(ref, ref, self.s.at[kind, 0, 0], self.r.at[kind, chip], device(self.z, self.y, self.c, self.h))
+
+    def from_self(self, chip):
+        return (self.z * 2 + self.y == chip) & (self.h == self.y)
+
+    def share(self):
+        ref = self.qkv.at[:, self.c]
+        return remote(ref, ref, self.sib.at[0], self.sib.at[1], device(self.z, self.y, 1 - self.c, self.h))
+
+    def share_in(self):
+        ref = self.qkv.at[:, 1 - self.c]
+        return remote(ref, ref, self.sib.at[0], self.sib.at[1], device(self.z, self.y, self.c, self.h))
+
+    def out_push(self, half):
+        return remote(
+            self.weights[3], self.out_w.at[self.y, self.c], self.o_s.at[half], self.o_r.at[self.y],
+            device(self.z, self.h, self.c, half),
+        )
+
+    def out_keep(self):
+        return local(self.weights[3], self.out_w.at[self.y, self.c], self.o_own.at[0])
+
+    def out_pull(self, pair):
+        ref = self.out_w.at[pair, self.c]
+        return remote(ref, ref, self.o_s.at[0], self.o_r.at[pair], device(self.z, self.y, self.c, self.h))
+
+    def out_share(self):
+        ref = self.out_w.at[:, self.c]
+        return remote(ref, ref, self.o_sib.at[0], self.o_sib.at[1], device(self.z, self.y, 1 - self.c, self.h))
+
+    def out_share_in(self):
+        ref = self.out_w.at[:, 1 - self.c]
+        return remote(ref, ref, self.o_sib.at[0], self.o_sib.at[1], device(self.z, self.y, self.c, self.h))
+
+    def each_push(self, act_remote, act_local):
+        for line in range(LINE):
+            for half in range(2):
+                mine = self.is_self(line, half)
+
+                @pl.when(jnp.logical_not(mine))
+                def _():
+                    for kind in range(3):
+                        act_remote(self.push(kind, line, half))
+
+                @pl.when(mine)
+                def _():
+                    for kind in range(3):
+                        act_local(self.keep(kind, line))
+
+    def each_out_push(self, act_remote, act_local):
+        for half in range(2):
+            mine = (self.y == self.h) & (self.h == half)
+
+            @pl.when(jnp.logical_not(mine))
+            def _():
+                act_remote(self.out_push(half))
+
+            @pl.when(mine)
+            def _():
+                act_local(self.out_keep())
+
+    def start(self):
+        self.each_push(lambda copy: copy.start(), lambda copy: copy.start())
+        self.each_out_push(lambda copy: copy.start(), lambda copy: copy.start())
+
+    def relay(self):
+        self.each_push(lambda copy: None, lambda copy: copy.wait())
+        for chip in range(8):
+
+            @pl.when(jnp.logical_not(self.from_self(chip)))
+            def _():
+                for kind in range(3):
+                    self.pull(kind, chip).wait_recv()
+
+        self.share().start()
+        self.each_out_push(lambda copy: None, lambda copy: copy.wait())
+        for pair in range(2):
+
+            @pl.when(jnp.logical_not((self.y == pair) & (self.h == self.y)))
+            def _():
+                self.out_pull(pair).wait_recv()
+
+        self.out_share().start()
+
+    def finish(self):
+        self.share_in().wait_recv()
+        self.out_share_in().wait_recv()
+        self.share().wait_send()
+        self.out_share().wait_send()
+        self.each_push(lambda copy: copy.wait_send(), lambda copy: None)
+        self.each_out_push(lambda copy: copy.wait_send(), lambda copy: None)
+
+
+class MlpSpread:
+    @staticmethod
+    def scratch():
+        return [dma(2, 8), dma(2, 8), dma(2, 8), dma(2, 8), dma(2), dma(2, 2), dma(1), dma(2), dma(2)]
+
+    def __init__(self, weights, outs, sems):
+        self.weights, self.outs = weights, outs
+        (self.s, self.r, self.x_s, self.x_r, self.own, self.sib, self.d_own, self.d_x, self.d_sib) = sems
+        self.z, self.y, self.c, self.h = place()
+        self.chip = self.z * 2 + self.y
+        self.part = weights[0].shape[1] // 8
+
+    def columns(self, index):
+        return pl.ds(pl.multiple_of(index * self.part, self.part), self.part)
+
+    def slot(self, kind, chip):
+        return self.outs[kind].at[chip, self.c, :, self.columns(self.h)]
+
+    def other(self, step):
+        return (self.chip + step) % 8
+
+    def source_of(self, step):
+        return (self.chip + 8 - step) % 8
+
+    def push(self, kind, step):
+        chip = self.other(step)
+        return remote(
+            self.weights[kind].at[:, self.columns(chip)], self.slot(kind, self.chip), self.s.at[kind, step],
+            self.r.at[kind, step], device(chip // 2, chip % 2, self.c, self.h),
+        )
+
+    def pull(self, kind, step):
+        ref = self.slot(kind, self.source_of(step))
+        return remote(ref, ref, self.s.at[kind, step], self.r.at[kind, step], device(self.z, self.y, self.c, self.h))
+
+    def keep(self, kind):
+        return local(self.weights[kind].at[:, self.columns(self.chip)], self.slot(kind, self.chip), self.own.at[kind])
+
+    def over(self, kind, step):
+        ref = self.slot(kind, self.source_of(step))
+        return remote(
+            ref, ref, self.x_s.at[kind, step], self.x_r.at[kind, step], device(self.z, self.y, self.c, 1 - self.h)
+        )
+
+    def over_in(self, kind, step):
+        ref = self.outs[kind].at[self.source_of(step), self.c, :, self.columns(1 - self.h)]
+        return remote(
+            ref, ref, self.x_s.at[kind, step], self.x_r.at[kind, step], device(self.z, self.y, self.c, self.h)
+        )
+
+    def share(self, kind):
+        ref = self.outs[kind].at[:, self.c]
+        return remote(
+            ref, ref, self.sib.at[kind, 0], self.sib.at[kind, 1], device(self.z, self.y, 1 - self.c, self.h)
+        )
+
+    def share_in(self, kind):
+        ref = self.outs[kind].at[:, 1 - self.c]
+        return remote(ref, ref, self.sib.at[kind, 0], self.sib.at[kind, 1], device(self.z, self.y, self.c, self.h))
+
+    def down_keep(self):
+        return local(self.weights[2], self.outs[2].at[self.h, self.c], self.d_own.at[0])
+
+    def down_over(self):
+        return remote(
+            self.weights[2], self.outs[2].at[self.h, self.c], self.d_x.at[0], self.d_x.at[1],
+            device(self.z, self.y, self.c, 1 - self.h),
+        )
+
+    def down_over_in(self):
+        ref = self.outs[2].at[1 - self.h, self.c]
+        return remote(ref, ref, self.d_x.at[0], self.d_x.at[1], device(self.z, self.y, self.c, self.h))
+
+    def down_share(self):
+        ref = self.outs[2].at[:, self.c]
+        return remote(ref, ref, self.d_sib.at[0], self.d_sib.at[1], device(self.z, self.y, 1 - self.c, self.h))
+
+    def down_share_in(self):
+        ref = self.outs[2].at[:, 1 - self.c]
+        return remote(ref, ref, self.d_sib.at[0], self.d_sib.at[1], device(self.z, self.y, self.c, self.h))
+
+    def start(self, kinds=(0, 1)):
+        for kind in kinds:
+            self.keep(kind).start()
+            for step in range(1, 8):
+                self.push(kind, step).start()
+
+    def start_down(self):
+        self.down_keep().start()
+        self.down_over().start()
+
+    def relay(self, kind):
+        self.keep(kind).wait()
+        self.over(kind, 0).start()
+        for step in range(1, 8):
+            self.pull(kind, step).wait_recv()
+            self.over(kind, step).start()
+
+    def relay_share(self, kind):
+        for step in range(8):
+            self.over_in(kind, step).wait_recv()
+        self.share(kind).start()
+
+    def relay_down(self):
+        self.down_keep().wait()
+        self.down_over_in().wait_recv()
+        self.down_share().start()
+
+    def finish(self):
+        for kind in range(2):
+            self.share_in(kind).wait_recv()
+            self.share(kind).wait_send()
+            for step in range(8):
+                self.over(kind, step).wait_send()
+                if step:
+                    self.push(kind, step).wait_send()
+        self.down_share_in().wait_recv()
+        self.down_share().wait_send()
+        self.down_over().wait_send()
+
+
+class NoteSpread:
+    @staticmethod
+    def scratch():
+        return [dma(16), dma(16), dma(1)]
+
+    def __init__(self, note, out, sems):
+        self.note, self.out = note, out
+        self.s, self.r, self.own = sems
+        self.blk, self.h = lax.axis_index("blk"), lax.axis_index("head")
+
+    def push(self, step):
+        other = (self.blk + step) % 16
+        return remote(self.note, self.out.at[self.blk], self.s.at[step], self.r.at[step], (other, self.h))
+
+    def pull(self, step):
+        ref = self.out.at[(self.blk + 16 - step) % 16]
+        return remote(ref, ref, self.s.at[step], self.r.at[step], (self.blk, self.h))
+
+    def keep(self):
+        return local(self.note, self.out.at[self.blk], self.own.at[0])
+
+    def start(self):
+        self.keep().start()
+        for step in range(1, 16):
+            self.push(step).start()
+
+    def finish(self):
+        self.keep().wait()
+        for step in range(1, 16):
+            self.pull(step).wait_recv()
+            self.push(step).wait_send()
+
+
+def split_refs(refs, counts):
+    groups, at = [], 0
+    for count in counts:
+        groups.append(refs[at : at + count])
+        at += count
+    return groups
+
+
+def spread_kernel(tokens, cot, note, wq, wk, wv, wo, wg, wu, wd, tok_out, cot_out, note_out, qkv, out_w, gate, up, down, *sems):
+    tok_sems, cot_sems, note_sems, attn_sems, mlp_sems = split_refs(sems, (8, 8, 3, 8, 9))
+    greet_all(16, 2)
+    tok = Gather(tokens, tok_out, tok_sems)
+    notes = NoteSpread(note, note_out, note_sems)
+    attn = AttnSpread((wq, wk, wv, wo), (qkv, out_w), attn_sems)
+    mlp = MlpSpread((wg, wu, wd), (gate, up, down), mlp_sems)
+    tok.start()
+    notes.start()
+    attn.start()
+    mlp.start_down()
+    tok.relays()
+    attn.relay()
+    mlp.start()
+    cots = Gather(cot, cot_out, cot_sems)
+    cots.start()
+    mlp.relay(0)
+    cots.relays()
+    mlp.relay(1)
+    mlp.relay_share(0)
+    mlp.relay_share(1)
+    mlp.relay_down()
+    tok.finish()
+    cots.finish()
+    notes.finish()
+    attn.finish()
+    mlp.finish()
+
+
+def spread(tokens, cot, note, wq, wk, wv, wo, wg, wu, wd):
+    def shape(*dims):
+        return jax.ShapeDtypeStruct(dims, jnp.bfloat16)
+
+    rows, width = tokens.shape
+    depth = wq.shape[0]
+    part = wg.shape[1] // 8
+    return pl.pallas_call(
+        spread_kernel,
+        out_shape=(
+            shape(8, rows, width),
+            shape(8, rows, width),
+            jax.ShapeDtypeStruct((16,) + note.shape, jnp.float32),
+            shape(8, 2, depth, 3 * HD),
+            shape(2, 2, wo.shape[0], width),
+            shape(8, 2, depth, 2 * part),
+            shape(8, 2, depth, 2 * part),
+            shape(2, 2, wd.shape[0], width),
+        ),
+        in_specs=[ANY] * 10,
+        out_specs=(ANY,) * 8,
+        scratch_shapes=Gather.scratch() + Gather.scratch() + NoteSpread.scratch() + AttnSpread.scratch() + MlpSpread.scratch(),
+        compiler_params=kernel_params(3),
+        name="spread",
+    )(tokens, cot, note, wq, wk, wv, wo, wg, wu, wd)
+
+
+def greet_square(z, y, c, h):
+    greet(device(z, y, 1 - c, h))
+    greet(device(z, y, c, 1 - h))
+    pl.semaphore_wait(pltpu.get_barrier_semaphore(), 2)
+
+
+def keys_kernel(kv, out, own, x_s, x_r, c_s, c_r):
+    z, y, c, h = place()
+    greet_square(z, y, c, h)
+
+    def keep(cut):
+        rows = pl.ds(cut * 2, 2)
+        return local(kv.at[rows], out.at[rows, c, h], own.at[cut])
+
+    def over(cut, half):
+        rows = pl.ds(cut * 2, 2)
+        return remote(kv.at[rows], out.at[rows, c, half], x_s.at[cut], x_r.at[cut], device(z, y, c, 1 - h))
+
+    def share(cut, core):
+        ref = out.at[pl.ds(cut * 2, 2), core]
+        return remote(ref, ref, c_s.at[cut], c_r.at[cut], device(z, y, 1 - c, h))
+
+    for cut in range(4):
+        over(cut, h).start()
+        keep(cut).start()
+    for cut in range(4):
+        keep(cut).wait()
+        over(cut, 1 - h).wait_recv()
+        share(cut, c).start()
+    for cut in range(4):
+        share(cut, 1 - c).wait_recv()
+        share(cut, c).wait_send()
+        over(cut, h).wait_send()
+
+
+def gather_keys(kv):
+    eight, rows, width = kv.shape
+    return pl.pallas_call(
+        keys_kernel,
+        out_shape=jax.ShapeDtypeStruct((eight, 2, 2, rows, width), kv.dtype),
+        in_specs=[ANY],
+        out_specs=ANY,
+        scratch_shapes=[dma(4)] * 5,
+        compiler_params=kernel_params(4),
+        name="gather_keys",
+    )(kv)
+
+
+def add_into(target, *others):
+    total = target[...].astype(jnp.float32)
+    for other in others:
+        total += other[...].astype(jnp.float32)
+    target[...] = total.astype(target.dtype)
+
+
+def key_grads_kernel(parts_in, out, parts, sib_in, x_in, z_in, load_sem, c_s, c_r, x_s, x_r, z_s, z_r):
+    z, y, c, h = place()
+    pair = z + 1 - 2 * (z % 2)
+    load = local(parts_in, parts, load_sem)
+    load.start()
+    greet(device(z, y, 1 - c, h))
+    greet(device(z, y, c, 1 - h))
+    greet(device(pair, y, c, h))
+    pl.semaphore_wait(pltpu.get_barrier_semaphore(), 3)
+    load.wait()
+
+    def share(cut):
+        rows = pl.ds(cut * 2, 2)
+        return remote(
+            parts.at[rows, 1 - c], sib_in.at[rows], c_s.at[cut], c_r.at[cut], device(z, y, 1 - c, h)
+        )
+
+    def over(cut):
+        rows = pl.ds(cut * 2, 2)
+        return remote(
+            parts.at[rows, c, 1 - h], x_in.at[rows], x_s.at[cut], x_r.at[cut], device(z, y, c, 1 - h)
+        )
+
+    def across(cut, column):
+        rows = pl.ds(cut * 2, 2)
+        columns = pl.ds(pl.multiple_of(column * HD, HD), HD)
+        return remote(
+            parts.at[rows, c, h, :, columns], z_in.at[rows], z_s.at[cut], z_r.at[cut], device(pair, y, c, h)
+        )
+
+    for cut in range(4):
+        share(cut).start()
+    for cut in range(4):
+        rows = pl.ds(cut * 2, 2)
+        share(cut).wait_recv()
+        add_into(parts.at[rows, c, 1 - h], sib_in.at[rows, 1 - h])
+        over(cut).start()
+    for cut in range(4):
+        rows = pl.ds(cut * 2, 2)
+        over(cut).wait_recv()
+        add_into(parts.at[rows, c, h], sib_in.at[rows, h], x_in.at[rows])
+        across(cut, 1 - z % 2).start()
+    for cut in range(4):
+        rows = pl.ds(cut * 2, 2)
+        columns = pl.ds(pl.multiple_of((z % 2) * HD, HD), HD)
+        across(cut, 0).wait_recv()
+        out[rows] = parts[rows, c, h, :, columns].astype(jnp.float32) + z_in[rows].astype(jnp.float32)
+    for cut in range(4):
+        share(cut).wait_send()
+        over(cut).wait_send()
+        across(cut, 0).wait_send()
+
+
+def reduce_keys(parts):
+    eight, cores, halves, rows, width = parts.shape
+
+    def room(*dims):
+        return pltpu.VMEM(dims, jnp.bfloat16)
+
+    return pl.pallas_call(
+        key_grads_kernel,
+        out_shape=jax.ShapeDtypeStruct((eight, rows, HD), jnp.float32),
+        in_specs=[ANY],
+        out_specs=INSIDE,
+        scratch_shapes=[
+            room(*parts.shape), room(eight, 2, rows, width), room(eight, rows, width), room(eight, rows, HD), dma(),
+        ] + [dma(4)] * 6,
+        compiler_params=kernel_params(5),
+        name="reduce_keys",
+    )(parts)
+
+
+def weight_grads_kernel(
+    gate_in, up_in, down_in, query_in, side_in, out_in, gains_in,
+    gate_out, up_out, down_out, query_out, key_out, value_out, out_out, gains_out,
+    gate, up, down, query, side, outw,
+    gate_sib, up_sib, down_sib, query_sib, side_sib, outw_sib,
+    gate_x, up_x, down_x, query_x, side_x, outw_x,
+    gains_box,
+    load_sems, sib_s, sib_r, x_s, x_r, a2a_s, a2a_r, small_s, small_r, y_sr, gain_s, gain_r, keep_sems,
+):
+    z, y, c, h = place()
+    chip = z * 2 + y
+    blk = lax.axis_index("blk")
+    me = device(z, y, c, h)
+    loads = [
+        local(src, dst, load_sems.at[i])
+        for i, (src, dst) in enumerate(
+            ((gate_in, gate), (up_in, up), (down_in, down), (query_in, query), (side_in, side), (out_in, outw))
+        )
+    ]
+    for load in loads:
+        load.start()
+    greet_all(16, 2)
+
+    def gain_push(step):
+        other = (blk + (step // 2)) % 16
+        half = (h + step % 2) % 2
+        return remote(
+            gains_in.at[other], gains_box.at[step], gain_s.at[step], gain_r.at[step], (other, half)
+        )
+
+    for step in range(1, 32):
+        gain_push(step).start()
+    keep_gain = local(gains_in.at[blk], gains_box.at[0], keep_sems.at[0])
+    keep_gain.start()
+
+    stores = ((gate, gate_sib), (up, up_sib), (down, down_sib), (query, query_sib), (side, side_sib), (outw, outw_sib))
+
+    def share(i):
+        store, box = stores[i]
+        return remote(store.at[:, 1 - c], box, sib_s.at[i], sib_r.at[i], device(z, y, 1 - c, h))
+
+    order = (0, 1, 2, 3, 4, 5)
+    for i in order:
+        loads[i].wait()
+        share(i).start()
+
+    half_width = gate.shape[3] // 2
+
+    def columns(index):
+        return pl.ds(pl.multiple_of(index * half_width, half_width), half_width)
+
+    def over(i):
+        if i < 2:
+            store, box = ((gate, gate_x), (up, up_x))[i]
+            src = store.at[:, c, :, columns(1 - h)]
+        elif i == 2:
+            src, box = down.at[1 - h, c], down_x
+        else:
+            store, box = {3: (query, query_x), 4: (side, side_x), 5: (outw, outw_x)}[i]
+            src = store.at[:, c]
+        return remote(src, box, x_s.at[i], x_r.at[i], device(z, y, c, 1 - h))
+
+    outs = (gate_out, up_out)
+
+    def scatter(i, step):
+        store = (gate, up)[i]
+        target = (chip + step) % 8
+        return remote(
+            store.at[target, c, :, columns(h)], outs[i].at[:, columns(chip)], a2a_s.at[i, step], a2a_r.at[i, step],
+            device(target // 2, target % 2, c, h),
+        )
+
+    def scatter_in(i, step):
+        source = (chip + 8 - step) % 8
+        ref = outs[i].at[:, columns(source)]
+        return remote(ref, ref, a2a_s.at[i, step], a2a_r.at[i, step], me)
+
+    def scatter_keep(i):
+        store = (gate, up)[i]
+        return local(store.at[chip, c, :, columns(h)], outs[i].at[:, columns(chip)], keep_sems.at[1 + i])
+
+    for i in (0, 1):
+        store, box = stores[i]
+        share(i).wait_recv()
+
+        @pl.loop(0, 8)
+        def _(p):
+            add_into(store.at[p, c], box.at[p])
+
+        over(i).start()
+    share(2).wait_recv()
+    for half in range(2):
+        add_into(down.at[half, c], down_sib.at[half])
+    over(2).start()
+    for i in (3, 4, 5):
+        store, box = stores[i]
+        share(i).wait_recv()
+        for p in range(box.shape[0]):
+            add_into(store.at[p, c], box.at[p])
+
+        @pl.when(h != y)
+        def _():
+            over(i).start()
+
+    def small_out(kind, target):
+        if kind == 0:
+            return query_out.at[:, pl.ds(pl.multiple_of(z * HD, HD), HD)]
+        return (key_out, value_out)[kind - 1].at[:, pl.ds(pl.multiple_of((z // 2) * HD, HD), HD)]
+
+    def small(kind, step):
+        store = query if kind == 0 else side
+        target = (chip + step) % 8
+        return remote(
+            store.at[target, c], small_out(kind, target), small_s.at[kind, step], small_r.at[kind, z, step],
+            device(target // 2, target % 2, c, h),
+        )
+
+    def small_keep(kind):
+        store = query if kind == 0 else side
+        return local(store.at[chip, c], small_out(kind, chip), keep_sems.at[3 + kind])
+
+    def out_move():
+        return remote(outw.at[1 - y, c], out_out, y_sr.at[0], y_sr.at[1], device(z, 1 - y, c, h))
+
+    def out_keep():
+        return local(outw.at[y, c], out_out, keep_sems.at[6])
+
+    for i, box in ((0, gate_x), (1, up_x)):
+        store = (gate, up)[i]
+        over(i).wait_recv()
+
+        @pl.loop(0, 8)
+        def _(p):
+            add_into(store.at[p, c, :, columns(h)], box.at[p])
+
+        scatter_keep(i).start()
+        for step in range(1, 8):
+            scatter(i, step).start()
+
+    @pl.when(h == y)
+    def _():
+        for i in (3, 4, 5):
+            store, box = {3: (query, query_x), 4: (side, side_x), 5: (outw, outw_x)}[i]
+            over(i).wait_recv()
+            for p in range(box.shape[0]):
+                add_into(store.at[p, c], box.at[p])
+        small_keep(0).start()
+        for step in range(1, 8):
+            small(0, step).start()
+
+        @pl.when(z % 2 == 0)
+        def _():
+            small_keep(1).start()
+            for step in range(1, 8):
+                small(1, step).start()
+
+        @pl.when(z % 2 == 1)
+        def _():
+            small_keep(2).start()
+            for step in range(1, 8):
+                small(2, step).start()
+
+        out_move().start()
+        out_keep().start()
+
+    over(2).wait_recv()
+    down_out[...] = (
+        down[h, c].astype(jnp.float32) + down_x[...].astype(jnp.float32)
+    )
+
+    keep_gain.wait()
+    for step in range(1, 32):
+        gain_push(step).wait_recv()
+    total = gains_box[0]
+    for step in range(1, 32):
+        total += gains_box[step]
+    gains_out[...] = total
+
+    for i in (0, 1):
+        for step in range(1, 8):
+            scatter_in(i, step).wait_recv()
+        scatter_keep(i).wait()
+
+    def small_in(kind, line, step):
+        if kind == 0:
+            ref = query_out.at[:, pl.ds(line * HD, HD)]
+        else:
+            ref = (key_out, value_out)[kind - 1].at[:, pl.ds((line // 2) * HD, HD)]
+        return remote(ref, ref, small_s.at[kind, step], small_r.at[kind, line, step], me)
+
+    for kind in range(3):
+        for line in range(LINE):
+            if kind and line % 2 != kind - 1:
+                continue
+            source = line * 2 + h
+            step = (chip + 8 - source) % 8
+
+            @pl.when(step != 0)
+            def _():
+                small_in(kind, line, step).wait_recv()
+
+            @pl.when(step == 0)
+            def _():
+                small_keep(kind).wait()
+
+    @pl.when(h != y)
+    def _():
+        remote(out_out, out_out, y_sr.at[0], y_sr.at[1], me).wait_recv()
+        for i in (3, 4, 5):
+            over(i).wait_send()
+
+    @pl.when(h == y)
+    def _():
+        out_keep().wait()
+        out_move().wait_send()
+        for step in range(1, 8):
+            small(0, step).wait_send()
+
+        @pl.when(z % 2 == 0)
+        def _():
+            for step in range(1, 8):
+                small(1, step).wait_send()
+
+        @pl.when(z % 2 == 1)
+        def _():
+            for step in range(1, 8):
+                small(2, step).wait_send()
+
+    for i in range(6):
+        share(i).wait_send()
+    for i in range(3):
+        over(i).wait_send()
+    for i in (0, 1):
+        for step in range(1, 8):
+            scatter(i, step).wait_send()
+    for step in range(1, 32):
+        gain_push(step).wait_send()
+
+
+def reduce_weights(gate, up, down, query, side, outw, gains):
+    parts = (gate, up, down, query, side, outw)
+
+    def room(*dims):
+        return pltpu.VMEM(dims, jnp.bfloat16)
+
+    def shape(*dims, dtype=jnp.bfloat16):
+        return jax.ShapeDtypeStruct(dims, dtype)
+
+    depth, wide = gate.shape[2], gate.shape[3]
+    sib = [room(part.shape[0], *part.shape[2:]) for part in parts]
+    over = [
+        room(8, depth, wide // 2), room(8, depth, wide // 2), room(*down.shape[2:]),
+        room(8, depth, HD), room(8, depth, HD), room(2, *outw.shape[2:]),
+    ]
+    return pl.pallas_call(
+        weight_grads_kernel,
+        out_shape=(
+            shape(depth, 4 * wide), shape(depth, 4 * wide), shape(*down.shape[2:], dtype=jnp.float32),
+            shape(depth, 4 * HD), shape(depth, 2 * HD), shape(depth, 2 * HD), shape(*outw.shape[2:]),
+            shape(*gains.shape[1:], dtype=jnp.float32),
+        ),
+        in_specs=[ANY] * 7,
+        out_specs=(ANY, ANY, INSIDE, ANY, ANY, ANY, ANY, INSIDE),
+        scratch_shapes=[room(*part.shape) for part in parts] + sib + over + [
+            pltpu.VMEM((32,) + gains.shape[1:], jnp.float32),
+            dma(6), dma(6), dma(6), dma(6), dma(6), dma(2, 8), dma(2, 8), dma(3, 8), dma(3, 4, 8), dma(2),
+            dma(32), dma(32), dma(8),
+        ],
+        compiler_params=kernel_params(6),
+        name="reduce_weights",
+    )(gate, up, down, query, side, outw, gains)
+
+
+def fast_body(
+    tokens,
+    attn_gain,
+    w_query,
+    w_key,
+    w_value,
+    w_out,
+    mlp_gain,
+    w_gate,
+    w_up,
+    w_down,
+    block_ids,
+    positions,
+    cotangent,
+):
+    z, y, core, half = place()
+    rows, width = tokens.shape
+    token_rows = 8 * rows
+    f32, bf16 = jnp.float32, jnp.bfloat16
+
+    def own_half(values):
+        return lax.dynamic_index_in_dim(values, half, 0, False)
+
+    note = jnp.concatenate(
+        [
+            positions.astype(f32).reshape(2, rows),
+            block_ids.astype(f32).reshape(2, rows),
+            attn_gain.astype(f32)[None],
+            mlp_gain.astype(f32)[None],
+            jnp.zeros((2, rows), f32),
+        ]
+    )
+    tokens_all, cot_all, notes, qkv_w, out_w, gate_w, up_w, down_w = spread(
+        tokens, cotangent, note, w_query, w_key, w_value, w_out, w_gate, w_up, w_down
+    )
+    tokens_all = tokens_all.reshape(token_rows, width)
+    cot_all = cot_all.reshape(token_rows, width)
+    qkv_w = qkv_w.reshape(width, 3 * HD)
+    out_w = out_w.reshape(HD, width)
+    hidden_part = gate_w.shape[3]
+    gate_w = gate_w.reshape(width, hidden_part)
+    up_w = up_w.reshape(width, hidden_part)
+    down_w = down_w.reshape(hidden_part, width)
+    gain_attn = notes[:, 4].reshape(1, width)
+    gain_mlp = notes[:, 5].reshape(1, width)
+    mine = lax.dynamic_index_in_dim(notes.reshape(8, 2, 8, rows), core, 1, False)
+    positions_mine = lax.dynamic_index_in_dim(mine[:, 0:2], half, 1, False).reshape(token_rows)
+    ids_mine = lax.dynamic_index_in_dim(mine[:, 2:4], half, 1, False).reshape(token_rows)
+    key_ids = notes[:, 2:4].reshape(32 * rows)
+
+    inputs_all = tokens_all.astype(f32)
+    normed = (inputs_all * rms_scale(inputs_all) * gain_attn).astype(bf16)
+    cos_table, sine_table = rope_tables(positions_mine)
+    cos_table, sine_table = cos_table[:, 0], sine_table[:, 0]
+    projected = product(normed, qkv_w)
+    query = rotate(projected[:, :HD], cos_table, sine_table).astype(bf16)
+    key = rotate(projected[:, HD : 2 * HD], cos_table, sine_table).astype(bf16)
+    value = projected[:, 2 * HD :].astype(bf16)
+    keys_values = gather_keys(jnp.concatenate([key, value], axis=1).reshape(8, rows, 2 * HD))
+    keys_values = keys_values.reshape(32 * rows, 2 * HD)
+    keys, values = keys_values[:, :HD], keys_values[:, HD:]
+    score_scale = HD ** (-0.5)
+    visible = key_ids[None, :] <= ids_mine[:, None]
+    scores = jnp.where(visible, times_transposed(query, keys) * score_scale, -1e30)
+    row_max = jnp.max(scores, axis=-1, keepdims=True)
+    weights = jnp.exp(scores - row_max)
+    log_total = row_max + jnp.log(jnp.sum(weights, axis=-1, keepdims=True))
+    probabilities = jnp.exp(scores - log_total)
+    attended = product(probabilities.astype(bf16), values)
+    attended_low = attended.astype(bf16)
+    branch = reduce_plane(product(attended_low, out_w).astype(bf16).reshape(8, rows, width))
+
+    inputs = tokens.astype(f32)
+    inv_attn = rms_scale(inputs)
+    hidden = inputs + branch
+    inv_mlp = rms_scale(hidden)
+    normed_mlp = gather_plane((hidden * inv_mlp * gain_mlp).astype(bf16)).reshape(token_rows, width)
+    gate_pre = product(normed_mlp, gate_w)
+    up_pre = product(normed_mlp, up_w)
+    sigmoid_gate = jax.nn.sigmoid(gate_pre)
+    active = (gate_pre * sigmoid_gate * up_pre).astype(bf16)
+    mlp_own = reduce_plane(product(active, down_w).astype(bf16).reshape(8, rows, width))
+    output = (hidden + mlp_own).astype(bf16)
+    grad_active = times_transposed(cot_all, down_w)
+    grad_gate = (
+        grad_active * up_pre * sigmoid_gate * (1.0 + gate_pre * (1.0 - sigmoid_gate))
+    ).astype(bf16)
+    grad_up = (grad_active * gate_pre * sigmoid_gate).astype(bf16)
+    grad_normed_part = times_transposed(grad_gate, gate_w) + times_transposed(grad_up, up_w)
+    grad_normed_mlp = reduce_plane(grad_normed_part.astype(bf16).reshape(8, rows, width))
+    grad_gate_w = transposed_times(normed_mlp, grad_gate)
+    grad_up_w = transposed_times(normed_mlp, grad_up)
+    grad_down_w = transposed_times(active, cot_all)
+    grad_hidden_norm, gain_mlp_term = norm_backward(grad_normed_mlp, hidden, inv_mlp, gain_mlp)
+    grad_hidden = cotangent.astype(f32) + grad_hidden_norm
+
+    grad_branch = gather_plane(grad_hidden.astype(bf16)).reshape(token_rows, width)
+    grad_out_w = transposed_times(attended_low, grad_branch)
+    grad_attended = times_transposed(grad_branch, out_w).astype(bf16)
+    delta = jnp.sum(grad_attended.astype(f32) * attended, axis=-1, keepdims=True)
+    grad_probs = times_transposed(grad_attended, values)
+    grad_scores = (probabilities * (grad_probs - delta)).astype(bf16)
+    grad_query_rot = product(grad_scores, keys) * score_scale
+    grad_key_rot = transposed_times(grad_scores, query) * score_scale
+    grad_value_part = transposed_times(probabilities.astype(bf16), grad_attended)
+    side = reduce_keys(
+        jnp.concatenate([grad_key_rot, grad_value_part], axis=1)
+        .astype(bf16)
+        .reshape(8, 2, 2, rows, 2 * HD)
+    ).reshape(token_rows, HD)
+    is_key = z % 2 == 0
+    side_grad = jnp.where(is_key, rotate(side, cos_table, -sine_table), side).astype(bf16)
+    grad_query = rotate(grad_query_rot, cos_table, -sine_table).astype(bf16)
+    side_w = jnp.where(is_key, qkv_w[:, HD : 2 * HD], qkv_w[:, 2 * HD :])
+    grad_normed_part = times_transposed(grad_query, qkv_w[:, :HD]) + times_transposed(
+        side_grad, side_w
+    )
+    grad_normed = reduce_plane(grad_normed_part.astype(bf16).reshape(8, rows, width))
+    grad_query_w = transposed_times(normed, grad_query)
+    grad_side_w = transposed_times(normed, side_grad)
+    grad_inputs_norm, gain_attn_term = norm_backward(grad_normed, inputs, inv_attn, gain_attn)
+    tokens_grad = (grad_hidden + grad_inputs_norm).astype(bf16)
+
+    gains = jnp.concatenate(
+        [
+            gain_attn_term.reshape(16, 1, rows),
+            gain_mlp_term.reshape(16, 1, rows),
+            jnp.zeros((16, 6, rows), f32),
+        ],
+        axis=1,
+    )
+    depth = w_query.shape[0]
+    gate_grad, up_grad, down_grad, query_grad, key_grad, value_grad, out_grad, gain_grads = reduce_weights(
+        grad_gate_w.astype(bf16).reshape(8, 2, depth, hidden_part),
+        grad_up_w.astype(bf16).reshape(8, 2, depth, hidden_part),
+        grad_down_w.astype(bf16).reshape(2, 2, w_down.shape[0], width),
+        grad_query_w.astype(bf16).reshape(8, 2, depth, HD),
+        grad_side_w.astype(bf16).reshape(8, 2, depth, HD),
+        grad_out_w.astype(bf16).reshape(2, 2, w_out.shape[0], width),
+        gains,
+    )
+    return (
+        output,
+        tokens_grad,
+        gain_grads[0],
+        query_grad.astype(f32),
+        key_grad.astype(f32),
+        value_grad.astype(f32),
+        out_grad.astype(f32),
+        gain_grads[1],
+        gate_grad.astype(f32),
+        up_grad.astype(f32),
+        down_grad,
+    )
+
+
 def solution(mesh):
     placed = (
         P(("blk", "head"), None),
@@ -354,8 +1656,9 @@
         P("blk"),
         P(("blk", "head"), None),
     )
+    fits = mesh.shape["blk"] == 16 and mesh.shape["head"] == 2
     return jax.shard_map(
-        body,
+        fast_body if fits else body,
         mesh=mesh,
         in_specs=placed,
         out_specs=(

time: 2620 us -> 877 us (0.33)
  waiting for transfers between devices: 2170 us -> 0 us
  Pallas kernels: 0 us -> 675 us
  blocking collectives: 111 us -> 0 us
  local copies, waits for them, and re-layouts: 84.6 us -> 12.4 us
  matrix products: 191 us -> 122 us
  other arithmetic: 26.7 us -> 57.7 us
    reduce_scatter x10 -> x0, waiting for transfers between devices: 1500 us -> none  [the longest x1 337 us: body(): lax.psum_scatter(grad_up_w, 'blk', scatter_dimension=0, tiled=True)]
    pallas_call x0 -> x10, Pallas kernels: none -> 675 us  [the longest x4 210 us: reduce_plane(): pl.pallas_call(reduce_kernel, out_shape=jax.ShapeDtypeStruct(shape[1:], j...]
    all_gather x11 -> x0, waiting for transfers between devices: 603 us -> none  [the longest x1 127 us: body(): lax.all_gather(w_down, 'blk', axis=0, tiled=True)]
    psum x3 -> x0, waiting for transfers between devices: 59.8 us -> none  [the longest x2 40.1 us: body(): lax.psum(grad_normed_part.astype(jnp.bfloat16), 'head').astype(jnp.float32)]
    all_gather x3 -> x0, blocking collectives: 56.3 us -> none  [the longest x1 20 us: body(): lax.all_gather(mlp_gain, 'blk', axis=0, tiled=True)]
    unnamed x1 -> x0, blocking collectives: 54.6 us -> none
    dynamic_update_slice x6 -> x0, local copies, waits for them, and re-layouts: 36.8 us -> none  [body(): lax.scan(backward_block, query_zeros, block_steps)]
    dot_general x7 -> x8, matrix products: 72.5 us -> 42.3 us  [transposed_times(): lax.dot_general(left, right, (((0,), (0,)), ((), ())), preferred_element_...]
  transfers between devices with their start and end apart: 24 -> 0, of which waited for: 22 -> 0; matrix products, arithmetic and copies ran while one was open for 7% -> 0% of each run, Pallas kernels for 0% -> 0%
where the time goes in v1:
time: 877 us; the launch traced here: 869 us
  Pallas kernels  675 us (77%)
  matrix products  122 us (14%)
  other arithmetic  57.7 us (7%)
  local copies, waits for them, and re-layouts  12.4 us (1%)
    pallas_call x4, Pallas kernels, reduce_plane(): pl.pallas_call(reduce_kernel, out_shape=jax.ShapeDtypeStruct(shape[1:], j...  210 us
    pallas_call x1, Pallas kernels, spread(): pl.pallas_call(spread_kernel, out_shape=(shape(8, rows, width), shape(8,...  173 us
    pallas_call x1, Pallas kernels, reduce_weights(): pl.pallas_call(weight_grads_kernel, out_shape=(shape(depth, 4 * wide), sh...  138 us
    pallas_call x2, Pallas kernels, gather_plane(): pl.pallas_call(gather_kernel, out_shape=jax.ShapeDtypeStruct((2 * LINE,)...  84.2 us
    dot_general x8, matrix products, times_transposed(): lax.dot_general(left, right, (((1,), (1,)), ((), ())), preferred_element_...  47.8 us
    dot_general x8, matrix products, transposed_times(): lax.dot_general(left, right, (((0,), (0,)), ((), ())), preferred_element_...  42.3 us
    pallas_call x1, Pallas kernels, gather_keys(): pl.pallas_call(keys_kernel, out_shape=jax.ShapeDtypeStruct((eight, 2, 2,...  36.3 us
    pallas_call x1, Pallas kernels, reduce_keys(): pl.pallas_call(key_grads_kernel, out_shape=jax.ShapeDtypeStruct((eight, r...  33.5 us

profile of v1, /device:TPU:8, one launch (start us, length us, event | category | flops | bytes accessed | tf_op | source)
XLA Modules:
  0.0 868.9 jit_solution(11658682988588732173)
XLA Ops:
  3.3 172.9 %spread.1 = (bf16[8,128,2048]{2,1,0:T(8,128)(2,1)}, bf16[8,128,2048]{2,1,0:T(8,128)(2,1)}, f32[16,8,128]{2,1,0:T(8,128)}, bf16[8,2,128,768]{3,2,1,0:T(8,128)(2,1...) custom-call(bf16[128,2048]{1,0:T(8,128)(2,1)} %tokens.1, ...), custom_call_target="tpu_custom_call" | custom-call | tf_op jit(solution)/shard_map/spread/pallas_call | solution.py:1067
  176.2 3.2 multiply_reduce_fusion
  181.5 3.0 fusion.2
  185.6 3.6 fusion.78
  189.3 2.7 fusion.54
  193.4 36.3 %gather_keys.1 = bf16[8,2,2,128,512]{4,3,2,1,0:T(8,128)(2,1)} custom-call(bf16[8,128,512]{2,1,0:T(8,128)(2,1)} %bitcast.103), custom_call_target="tpu_custom_call" | custom-call | tf_op jit(solution)/shard_map/gather_keys/pallas_call | solution.py:1124
  229.7 9.9 %fusion.77 = (f32[1024]{0:T(1024)S(1)}, f32[1024,4096]{1,0:T(8,128)}) fusion(bf16[4096,512]{1,0:T(8,128)(2,1)} %bitcast.96, bf16[1024,128]{0,1:T(8,128)(2,1)S(1)} %get-tuple-element.55, bf16[1024,128]{0,1:T(8,128)(2,1)S(1)} %get-tuple-element.52, f32[1024]{0:T(1024)S(1)} %bitcast.141, f32[4096]{0:T(1024)S(1)} %bitcast.140), kind=kOutput, calls=%fused_computation.134 | convolution fusion | flops 2165308416 | bytes 19423232 | tf_op jit(solution)/shard_map/dot_general | solution.py:43
  239.7 8.1 exponential_reduce_fusion
  247.8 7.4 fusion
  255.2 2.4 fusion.6
  258.5 3.3 convolution_convert_fusion.1
  261.8 63.5 %reduce_plane.4 = f32[128,2048]{1,0:T(8,128)} custom-call(bf16[8,128,2048]{2,1,0:T(8,128)(2,1)} %bitcast.94), custom_call_target="tpu_custom_call" | custom-call | tf_op jit(solution)/shard_map/reduce_plane/pallas_call | solution.py:725
  327.8 43.4 %gather_plane.2 = bf16[8,128,2048]{2,1,0:T(8,128)(2,1)} custom-call(bf16[128,2048]{1,0:T(8,128)(2,1)} %multiply_convert_fusion.5.src), custom_call_target="tpu_custom_call" | custom-call | tf_op jit(solution)/shard_map/gather_plane/pallas_call | solution.py:576
  371.3 7.9 fusion.80
  379.2 6.1 fusion.79
  385.3 9.4 %multiply_convert_fusion.2 = (bf16[1024,1024]{1,0:T(8,128)(2,1)}, bf16[1024,1024]{1,0:T(8,128)(2,1)}, bf16[1024,1024]{1,0:T(8,128)(2,1)S(1)}) fusion(f32[1024,1024]{1,0:T(8,128)} %fusion.79, f32[1024,1024]{1,0:T(8,128)S(1)} %fusion.80, bf16[1024,2048]{1,0:T(8,128)(2,1)S(1)} %bitcast.148, bf16[1024,2048]{1,0:T(8,128)(2,1)S(1)} %bitcast.146), kind=kOutput, calls=%fused_computation.16 | convolution fusion | flops 4311744512 | bytes 23068672 | tf_op jit(solution)/shard_map/dot_general | solution.py:43
  394.7 6.2 convolution_convert_fusion.2
  400.9 6.1 convolution_convert_fusion.5
  407.0 47.6 %reduce_plane.5 = f32[128,2048]{1,0:T(8,128)} custom-call(bf16[8,128,2048]{2,1,0:T(8,128)(2,1)} %bitcast.101), custom_call_target="tpu_custom_call" | custom-call | tf_op jit(solution)/shard_map/reduce_plane/pallas_call | solution.py:725
  454.7 9.5 %convolution_convert_fusion.3 = bf16[2048,1024]{1,0:T(8,128)(2,1)} fusion(bf16[1024,2048]{1,0:T(8,128)(2,1)} %bitcast.105, bf16[1024,1024]{1,0:T(8,128)(2,1)} %get-tuple-element.49), kind=kOutput, calls=%fused_computation.22 | convolution fusion | flops 4297064448 | bytes 10485760 | tf_op jit(solution)/shard_map/dot_general | solution.py:49
  464.2 6.8 convolution_convert_fusion.4
  471.0 4.5 fusion.81
  475.6 6.2 add_convert_fusion.1
  481.8 48.7 %reduce_plane.6 = f32[128,2048]{1,0:T(8,128)} custom-call(bf16[8,128,2048]{2,1,0:T(8,128)(2,1)} %bitcast.100), custom_call_target="tpu_custom_call" | custom-call | tf_op jit(solution)/shard_map/reduce_plane/pallas_call | solution.py:725
  532.1 2.3 fusion.74.src
  534.4 40.7 %gather_plane.3 = bf16[8,128,2048]{2,1,0:T(8,128)(2,1)} custom-call(bf16[128,2048]{1,0:T(8,128)(2,1)} %fusion.74.src), custom_call_target="tpu_custom_call" | custom-call | tf_op jit(solution)/shard_map/gather_plane/pallas_call | solution.py:576
  575.1 3.9 multiply_reduce_fusion.2
  579.1 2.3 convolution_convert_fusion.6
  581.4 7.4 convolution_convert_fusion
  588.7 9.0 %multiply_convert_fusion = bf16[1024,4096]{1,0:T(8,128)(2,1)S(1)} fusion(f32[1024,4096]{1,0:T(8,128)} %get-tuple-element.72, bf16[1024,256]{0,1:T(8,128)(2,1)} %copy-done.17, f32[1024]{0:T(1024)S(1)} %get-tuple-element.73, f32[1024]{0:T(1024)S(1)} %log_add_fusion, bf16[4096,512]{1,0:T(8,128)(2,1)S(1)} %bitcast.98), kind=kOutput, calls=%fused_computation | convolution fusion | flops 2164260864 | bytes 27795456 | tf_op jit(solution)/shard_map/dot_general | solution.py:43
  597.8 2.4 fusion.14
  600.2 2.7 fusion.3
  603.0 2.3 fusion.48
  605.3 2.4 convolution_convert_fusion.7
  607.7 2.3 pad_maximum_fusion.parts_in
  610.0 33.5 %reduce_keys.1 = f32[8,128,256]{2,1,0:T(8,128)} custom-call(bf16[8,2,2,128,512]{4,3,2,1,0:T(8,128)(2,1)} %pad_maximum_fusion.parts_in), custom_call_target="tpu_custom_call" | custom-call | tf_op jit(solution)/shard_map/reduce_keys/pallas_call | solution.py:1201
  645.1 3.2 fusion.51
  649.2 1.8 copy.29
  651.0 5.1 fusion.4
  657.4 3.5 add_convert_fusion
  660.9 50.2 %reduce_plane.7 = f32[128,2048]{1,0:T(8,128)} custom-call(bf16[8,128,2048]{2,1,0:T(8,128)(2,1)} %bitcast.95), custom_call_target="tpu_custom_call" | custom-call | tf_op jit(solution)/shard_map/reduce_plane/pallas_call | solution.py:725
  712.7 3.0 fusion.21
  716.4 138.2 %reduce_weights.1 = (bf16[128,4096]{1,0:T(8,128)(2,1)}, bf16[128,4096]{1,0:T(8,128)(2,1)}, f32[256,2048]{1,0:T(8,128)}, bf16[128,1024]{1,0:T(8,128)(2,1)}, bf16[...) custom-call(bf16[8,2,128,1024]{3,2,1,0:T(8,128)(2,1)} %bitcast.113, ...), custom_call_target="tpu_custom_call" | custom-call | tf_op jit(solution)/shard_map/reduce_weights/pallas_call | solution.py:1468
  855.9 1.6 convert_element_type.166
  857.5 1.8 convert_element_type.167
  859.3 1.8 convert_element_type.165
  861.1 1.8 convert_element_type.168
  862.9 2.8 convert_element_type.169
  (116 shorter events, 22.3 us)
Async XLA Ops:
  0.7 188.6 %copy-start.31 = (f32[128]{0:T(128)}, f32[128]{0:T(128)S(1)}, u32[]{:S(2)}) copy-start(f32[128]{0:T(128)S(1)} %multiply_power_fusion) | copy-start | bytes 1540
  176.2 4.1 copy-start.30
  176.2 4.2 copy-start
  180.3 1.1 copy-start.26
  180.4 9.0 %copy-start.28 = (f32[8,1,128]{2,1,0:T(1,128)}, f32[8,1,128]{2,1,0:T(1,128)S(1)}, u32[]{:S(2)}) copy-start(f32[8,1,128]{2,1,0:T(1,128)S(1)} %constant_dynamic-slice_fusion) | copy-start | bytes 12292
  181.4 3.8 copy-start.10
  181.4 4.1 copy-start.15
  192.0 37.7 %copy-start.24 = (bf16[1024,128]{0,1:T(8,128)(2,1)}, bf16[1024,128]{0,1:T(8,128)(2,1)S(1)}, u32[]{:S(2)}) copy-start(bf16[1024,128]{0,1:T(8,128)(2,1)S(1)} %get-tuple-element.55) | copy-start | bytes 786436
  247.8 7.4 copy-start.2
  255.2 3.3 copy-start.4
  255.2 3.3 copy-start.18
  261.8 63.5 %copy-start.5 = (bf16[128,2048]{1,0:T(8,128)(2,1)S(1)}, bf16[128,2048]{1,0:T(8,128)(2,1)}, u32[]{:S(2)}) copy-start(bf16[128,2048]{1,0:T(8,128)(2,1)} %tokens.1) | copy-start | bytes 1572868
  371.2 7.9 copy-start.7
  371.3 7.9 copy-start.35
  379.2 6.1 copy-start.37
  379.2 6.1 copy-start.38
  454.6 9.6 %copy-start.8 = (bf16[8,128,2048]{2,1,0:T(8,128)(2,1)S(1)}, bf16[8,128,2048]{2,1,0:T(8,128)(2,1)}, u32[]{:S(2)}) copy-start(bf16[8,128,2048]{2,1,0:T(8,128)(2,1)} %gather_plane.2) | copy-start | bytes 12582916
  454.6 9.6 %copy-start.39 = (bf16[1024,1024]{1,0:T(8,128)(2,1)S(1)}, bf16[1024,1024]{1,0:T(8,128)(2,1)}, u32[]{:S(2)}) copy-start(bf16[1024,1024]{1,0:T(8,128)(2,1)} %get-tuple-element.50) | copy-start | bytes 6291460
  464.2 6.8 copy-start.36
  471.0 4.6 copy-start.34
  471.0 4.6 copy-start.40
  481.7 50.3 %copy-start.6 = (bf16[128,2048]{1,0:T(8,128)(2,1)S(1)}, bf16[128,2048]{1,0:T(8,128)(2,1)}, u32[]{:S(2)}) copy-start(bf16[128,2048]{1,0:T(8,128)(2,1)} %cot.1) | copy-start | bytes 1572868
  575.1 3.9 copy-start.9
  579.1 9.6 %copy-start.17 = (bf16[1024,256]{0,1:T(8,128)(2,1)}, bf16[1024,256]{0,1:T(8,128)(2,1)S(1)}, u32[]{:S(2)}) copy-start(bf16[1024,256]{0,1:T(8,128)(2,1)S(1)} %get-tuple-element.74) | copy-start | bytes 1572868
  581.4 7.4 copy-start.3
  597.8 2.4 copy-start.25
  600.2 2.7 copy-start.29
  600.2 2.7 copy-start.32
  600.2 5.1 copy-start.11
  602.9 4.7 copy-start.14
  605.3 2.4 copy-start.20
  605.3 2.4 copy-start.22
  651.0 5.1 copy-start.16
  651.0 5.1 copy-start.21
  651.0 5.1 copy-start.23
  656.1 1.3 copy-start.12
  660.9 50.2 %copy-start.27 = (f32[16,1,128]{2,1,0:T(1,128)S(1)}, f32[16,1,128]{2,1,0:T(1,128)}, u32[]{:S(2)}) copy-start(f32[16,1,128]{2,1,0:T(1,128)} %copy-done.26) | copy-start | bytes 24580
  660.9 51.8 %copy-start.1 = (f32[128,2048]{1,0:T(8,128)S(1)}, f32[128,2048]{1,0:T(8,128)}, u32[]{:S(2)}) copy-start(f32[128,2048]{1,0:T(8,128)} %reduce_plane.6) | copy-start | bytes 3145732
  711.1 4.6 copy-start.33
  854.6 11.0 %copy-start.19 = (bf16[128,4096]{1,0:T(8,128)(2,1)S(1)}, bf16[128,4096]{1,0:T(8,128)(2,1)}, u32[]{:S(2)}) copy-start(bf16[128,4096]{1,0:T(8,128)(2,1)} %get-tuple-element.41) | copy-start | bytes 3145732
  857.5 9.6 %copy-start.13 = (f32[256,2048]{1,0:T(8,128)S(1)}, f32[256,2048]{1,0:T(8,128)}, u32[]{:S(2)}) copy-start(f32[256,2048]{1,0:T(8,128)} %get-tuple-element.100) | copy-start | bytes 6291460

commit v2 on v1

--- a/solution.py
+++ b/solution.py
@@ -383,7 +383,7 @@
     pl.semaphore_wait(pltpu.get_barrier_semaphore(), blk_total * head_total - 1)
 
 
-def greet_plane():
+def greet_plane(more=0):
     z, y, c, h = place()
 
     @pl.when(z > 0)
@@ -397,7 +397,7 @@
     greet(device(z, 1 - y, c, h))
     pl.semaphore_wait(
         pltpu.get_barrier_semaphore(),
-        1 + (z + LINE - 1) // LINE + (LINE - 1 - z + LINE - 1) // LINE,
+        1 + more + (z + LINE - 1) // LINE + (LINE - 1 - z + LINE - 1) // LINE,
     )
 
 
@@ -576,7 +576,7 @@
     return pl.pallas_call(
         gather_kernel,
         out_shape=jax.ShapeDtypeStruct((2 * LINE,) + rows.shape, rows.dtype),
-        in_specs=[ANY],
+        in_specs=[INSIDE],
         out_specs=ANY,
         scratch_shapes=Gather.scratch(),
         compiler_params=kernel_params(1),
@@ -744,136 +744,172 @@
 class AttnSpread:
     @staticmethod
     def scratch():
-        return [dma(3, 4, 2), dma(3, 8), dma(3), dma(2), dma(2), dma(2), dma(1), dma(2)]
+        return [dma(3, 4), dma(3, 4), dma(3, 8), dma(3), dma(4), dma(4), dma(4), dma(4), dma(4), dma(4)]
 
     def __init__(self, weights, outs, sems):
         self.weights, (self.qkv, self.out_w) = weights, outs
-        (self.s, self.r, self.own, self.sib, self.o_s, self.o_r, self.o_own, self.o_sib) = sems
+        (self.s, self.f_s, self.r, self.own, self.x_s, self.x_r, self.c_s, self.c_r, self.o_s, self.o_r) = sems
         self.z, self.y, self.c, self.h = place()
+        self.chip = self.z * 2 + self.y
+        self.me = device(self.z, self.y, self.c, self.h)
+        self.owner = self.h == self.y
 
     def source(self, kind, line):
         start = line * HD if kind == 0 else (line // 2) * HD
-        return self.weights[kind].at[:, pl.ds(start, HD)]
+        return self.weights[kind].at[:, pl.ds(pl.multiple_of(start, HD), HD)]
 
     def slot(self, kind, chip):
         return self.qkv.at[chip, self.c, :, pl.ds(kind * HD, HD)]
 
-    def is_self(self, line, half):
-        return (self.z == line) & (self.y == self.h) & (self.h == half)
-
-    def push(self, kind, line, half):
-        chip = self.z * 2 + self.y
-        return remote(
-            self.source(kind, line), self.slot(kind, chip), self.s.at[kind, line, half], self.r.at[kind, chip],
-            device(line, self.h, self.c, half),
-        )
-
-    def keep(self, kind, line):
-        return local(self.source(kind, line), self.slot(kind, self.z * 2 + self.y), self.own.at[kind])
+    def push(self, kind, step):
+        line = (self.z + step) % LINE
+        return remote(
+            self.source(kind, line), self.slot(kind, self.chip), self.s.at[kind, step], self.r.at[kind, self.chip],
+            device(line, self.h, self.c, self.h),
+        )
+
+    def push_far(self, kind, step):
+        line = (self.z + step) % LINE
+        return remote(
+            self.source(kind, line), self.slot(kind, self.chip), self.f_s.at[kind, step], self.r.at[kind, self.chip],
+            device(line, self.h, self.c, 1 - self.h),
+        )
+
+    def keep(self, kind):
+        return local(self.source(kind, self.z), self.slot(kind, self.chip), self.own.at[kind])
 
     def pull(self, kind, chip):
         ref = self.slot(kind, chip)
-        return remote(ref, ref, self.s.at[kind, 0, 0], self.r.at[kind, chip], device(self.z, self.y, self.c, self.h))
-
-    def from_self(self, chip):
-        return (self.z * 2 + self.y == chip) & (self.h == self.y)
-
-    def share(self):
-        ref = self.qkv.at[:, self.c]
-        return remote(ref, ref, self.sib.at[0], self.sib.at[1], device(self.z, self.y, 1 - self.c, self.h))
-
-    def share_in(self):
-        ref = self.qkv.at[:, 1 - self.c]
-        return remote(ref, ref, self.sib.at[0], self.sib.at[1], device(self.z, self.y, self.c, self.h))
-
-    def out_push(self, half):
-        return remote(
-            self.weights[3], self.out_w.at[self.y, self.c], self.o_s.at[half], self.o_r.at[self.y],
-            device(self.z, self.h, self.c, half),
+        return remote(ref, ref, self.s.at[kind, 0], self.r.at[kind, chip], self.me)
+
+    def near(self, step):
+        return ((self.z + LINE - step) % LINE) * 2 + self.y
+
+    def far(self, step):
+        return ((self.z + LINE - step) % LINE) * 2 + 1 - self.y
+
+    def over(self, step):
+        ref = self.qkv.at[self.near(step), self.c]
+        return remote(ref, ref, self.x_s.at[step], self.x_r.at[step], device(self.z, self.y, self.c, 1 - self.h))
+
+    def share(self, line, core):
+        ref = self.qkv.at[pl.ds(line * 2, 2), core]
+        return remote(ref, ref, self.c_s.at[line], self.c_r.at[line], device(self.z, self.y, 1 - self.c, self.h))
+
+    def out_push(self):
+        return remote(
+            self.weights[3], self.out_w.at[self.y, self.c], self.o_s.at[0], self.o_r.at[0],
+            device(self.z, 1 - self.y, self.c, self.h),
         )
 
     def out_keep(self):
-        return local(self.weights[3], self.out_w.at[self.y, self.c], self.o_own.at[0])
-
-    def out_pull(self, pair):
-        ref = self.out_w.at[pair, self.c]
-        return remote(ref, ref, self.o_s.at[0], self.o_r.at[pair], device(self.z, self.y, self.c, self.h))
-
-    def out_share(self):
+        return local(self.weights[3], self.out_w.at[self.y, self.c], self.o_s.at[1])
+
+    def out_pull(self):
+        ref = self.out_w.at[1 - self.y, self.c]
+        return remote(ref, ref, self.o_s.at[0], self.o_r.at[0], self.me)
+
+    def out_over(self):
         ref = self.out_w.at[:, self.c]
-        return remote(ref, ref, self.o_sib.at[0], self.o_sib.at[1], device(self.z, self.y, 1 - self.c, self.h))
-
-    def out_share_in(self):
-        ref = self.out_w.at[:, 1 - self.c]
-        return remote(ref, ref, self.o_sib.at[0], self.o_sib.at[1], device(self.z, self.y, self.c, self.h))
-
-    def each_push(self, act_remote, act_local):
-        for line in range(LINE):
-            for half in range(2):
-                mine = self.is_self(line, half)
-
-                @pl.when(jnp.logical_not(mine))
-                def _():
-                    for kind in range(3):
-                        act_remote(self.push(kind, line, half))
-
-                @pl.when(mine)
-                def _():
-                    for kind in range(3):
-                        act_local(self.keep(kind, line))
-
-    def each_out_push(self, act_remote, act_local):
-        for half in range(2):
-            mine = (self.y == self.h) & (self.h == half)
-
-            @pl.when(jnp.logical_not(mine))
+        return remote(ref, ref, self.o_s.at[2], self.o_r.at[2], device(self.z, self.y, self.c, 1 - self.h))
+
+    def out_share(self, core):
+        ref = self.out_w.at[:, core]
+        return remote(ref, ref, self.o_s.at[3], self.o_r.at[3], device(self.z, self.y, 1 - self.c, self.h))
+
+    def start(self):
+        for kind in range(3):
+
+            @pl.when(self.owner)
             def _():
-                act_remote(self.out_push(half))
-
-            @pl.when(mine)
+                self.keep(kind).start()
+
+            @pl.when(jnp.logical_not(self.owner))
             def _():
-                act_local(self.out_keep())
-
-    def start(self):
-        self.each_push(lambda copy: copy.start(), lambda copy: copy.start())
-        self.each_out_push(lambda copy: copy.start(), lambda copy: copy.start())
-
-    def relay(self):
-        self.each_push(lambda copy: None, lambda copy: copy.wait())
-        for chip in range(8):
-
-            @pl.when(jnp.logical_not(self.from_self(chip)))
+                self.push(kind, 0).start()
+                self.push_far(kind, 0).start()
+
+        for step in range(1, LINE):
+            for kind in range(3):
+                self.push(kind, step).start()
+
+            @pl.when(jnp.logical_not(self.owner))
             def _():
                 for kind in range(3):
-                    self.pull(kind, chip).wait_recv()
-
-        self.share().start()
-        self.each_out_push(lambda copy: None, lambda copy: copy.wait())
-        for pair in range(2):
-
-            @pl.when(jnp.logical_not((self.y == pair) & (self.h == self.y)))
+                    self.push_far(kind, step).start()
+
+        @pl.when(self.owner)
+        def _():
+            self.out_keep().start()
+
+        @pl.when(jnp.logical_not(self.owner))
+        def _():
+            self.out_push().start()
+
+    def relay(self):
+        @pl.when(self.owner)
+        def _():
+            for step in range(LINE):
+                for kind in range(3):
+                    if step:
+                        self.pull(kind, self.near(step)).wait_recv()
+                    else:
+                        self.keep(kind).wait()
+                self.over(step).start()
+            self.out_keep().wait()
+            self.out_pull().wait_recv()
+            self.out_over().start()
+
+    def relay_share(self):
+        for step in range(LINE):
+
+            @pl.when(jnp.logical_not(self.owner))
             def _():
-                self.out_pull(pair).wait_recv()
-
-        self.out_share().start()
+                self.over(step).wait_recv()
+
+            for kind in range(3):
+                self.pull(kind, self.far(step)).wait_recv()
+            self.share((self.z + LINE - step) % LINE, self.c).start()
+
+        @pl.when(jnp.logical_not(self.owner))
+        def _():
+            self.out_over().wait_recv()
+
+        self.out_share(self.c).start()
 
     def finish(self):
-        self.share_in().wait_recv()
-        self.out_share_in().wait_recv()
-        self.share().wait_send()
-        self.out_share().wait_send()
-        self.each_push(lambda copy: copy.wait_send(), lambda copy: None)
-        self.each_out_push(lambda copy: copy.wait_send(), lambda copy: None)
+        for line in range(LINE):
+            self.share(line, 1 - self.c).wait_recv()
+            self.share(line, self.c).wait_send()
+        self.out_share(1 - self.c).wait_recv()
+        self.out_share(self.c).wait_send()
+        for kind in range(3):
+            for step in range(1, LINE):
+                self.push(kind, step).wait_send()
+
+        @pl.when(self.owner)
+        def _():
+            for step in range(LINE):
+                self.over(step).wait_send()
+            self.out_over().wait_send()
+
+        @pl.when(jnp.logical_not(self.owner))
+        def _():
+            for kind in range(3):
+                self.push(kind, 0).wait_send()
+                for step in range(LINE):
+                    self.push_far(kind, step).wait_send()
+            self.out_push().wait_send()
 
 
 class MlpSpread:
     @staticmethod
     def scratch():
-        return [dma(2, 8), dma(2, 8), dma(2, 8), dma(2, 8), dma(2), dma(2, 2), dma(1), dma(2), dma(2)]
+        return [dma(2, 8), dma(2, 8), dma(2)]
 
     def __init__(self, weights, outs, sems):
         self.weights, self.outs = weights, outs
-        (self.s, self.r, self.x_s, self.x_r, self.own, self.sib, self.d_own, self.d_x, self.d_sib) = sems
+        self.s, self.r, self.own = sems
         self.z, self.y, self.c, self.h = place()
         self.chip = self.z * 2 + self.y
         self.part = weights[0].shape[1] // 8
@@ -881,110 +917,130 @@
     def columns(self, index):
         return pl.ds(pl.multiple_of(index * self.part, self.part), self.part)
 
-    def slot(self, kind, chip):
-        return self.outs[kind].at[chip, self.c, :, self.columns(self.h)]
-
-    def other(self, step):
-        return (self.chip + step) % 8
-
-    def source_of(self, step):
-        return (self.chip + 8 - step) % 8
-
     def push(self, kind, step):
-        chip = self.other(step)
-        return remote(
-            self.weights[kind].at[:, self.columns(chip)], self.slot(kind, self.chip), self.s.at[kind, step],
+        chip = (self.chip + step) % 8
+        return remote(
+            self.weights[kind].at[:, self.columns(chip)], self.outs[kind].at[self.chip], self.s.at[kind, step],
             self.r.at[kind, step], device(chip // 2, chip % 2, self.c, self.h),
         )
 
     def pull(self, kind, step):
-        ref = self.slot(kind, self.source_of(step))
+        ref = self.outs[kind].at[(self.chip + 8 - step) % 8]
         return remote(ref, ref, self.s.at[kind, step], self.r.at[kind, step], device(self.z, self.y, self.c, self.h))
 
     def keep(self, kind):
-        return local(self.weights[kind].at[:, self.columns(self.chip)], self.slot(kind, self.chip), self.own.at[kind])
-
-    def over(self, kind, step):
-        ref = self.slot(kind, self.source_of(step))
-        return remote(
-            ref, ref, self.x_s.at[kind, step], self.x_r.at[kind, step], device(self.z, self.y, self.c, 1 - self.h)
-        )
-
-    def over_in(self, kind, step):
-        ref = self.outs[kind].at[self.source_of(step), self.c, :, self.columns(1 - self.h)]
-        return remote(
-            ref, ref, self.x_s.at[kind, step], self.x_r.at[kind, step], device(self.z, self.y, self.c, self.h)
-        )
-
-    def share(self, kind):
-        ref = self.outs[kind].at[:, self.c]
-        return remote(
-            ref, ref, self.sib.at[kind, 0], self.sib.at[kind, 1], device(self.z, self.y, 1 - self.c, self.h)
-        )
-
-    def share_in(self, kind):
-        ref = self.outs[kind].at[:, 1 - self.c]
-        return remote(ref, ref, self.sib.at[kind, 0], self.sib.at[kind, 1], device(self.z, self.y, self.c, self.h))
-
-    def down_keep(self):
-        return local(self.weights[2], self.outs[2].at[self.h, self.c], self.d_own.at[0])
-
-    def down_over(self):
-        return remote(
-            self.weights[2], self.outs[2].at[self.h, self.c], self.d_x.at[0], self.d_x.at[1],
-            device(self.z, self.y, self.c, 1 - self.h),
-        )
-
-    def down_over_in(self):
-        ref = self.outs[2].at[1 - self.h, self.c]
-        return remote(ref, ref, self.d_x.at[0], self.d_x.at[1], device(self.z, self.y, self.c, self.h))
-
-    def down_share(self):
-        ref = self.outs[2].at[:, self.c]
-        return remote(ref, ref, self.d_sib.at[0], self.d_sib.at[1], device(self.z, self.y, 1 - self.c, self.h))
-
-    def down_share_in(self):
-        ref = self.outs[2].at[:, 1 - self.c]
-        return remote(ref, ref, self.d_sib.at[0], self.d_sib.at[1], device(self.z, self.y, self.c, self.h))
-
-    def start(self, kinds=(0, 1)):
-        for kind in kinds:
+        return local(self.weights[kind].at[:, self.columns(self.chip)], self.outs[kind].at[self.chip], self.own.at[kind])
+
+    def start(self):
+        for kind in range(2):
             self.keep(kind).start()
             for step in range(1, 8):
                 self.push(kind, step).start()
 
-    def start_down(self):
-        self.down_keep().start()
-        self.down_over().start()
-
-    def relay(self, kind):
-        self.keep(kind).wait()
-        self.over(kind, 0).start()
-        for step in range(1, 8):
-            self.pull(kind, step).wait_recv()
-            self.over(kind, step).start()
-
-    def relay_share(self, kind):
-        for step in range(8):
-            self.over_in(kind, step).wait_recv()
-        self.share(kind).start()
-
-    def relay_down(self):
-        self.down_keep().wait()
-        self.down_over_in().wait_recv()
-        self.down_share().start()
-
     def finish(self):
         for kind in range(2):
-            self.share_in(kind).wait_recv()
-            self.share(kind).wait_send()
-            for step in range(8):
-                self.over(kind, step).wait_send()
-                if step:
-                    self.push(kind, step).wait_send()
-        self.down_share_in().wait_recv()
-        self.down_share().wait_send()
-        self.down_over().wait_send()
+            self.keep(kind).wait()
+            for step in range(1, 8):
+                self.pull(kind, step).wait_recv()
+                self.push(kind, step).wait_send()
+
+
+class MlpShare:
+    @staticmethod
+    def scratch():
+        return [dma(2), dma(2, 2), dma(2, 2), dma(2, 2), dma(2, 2)]
+
+    def __init__(self, quarters, outs, sems):
+        self.quarters, self.outs = quarters, outs
+        self.own, self.x_s, self.x_r, self.c_s, self.c_r = sems
+        self.z, self.y, self.c, self.h = place()
+        self.part = quarters[0].shape[2]
+
+    def slot(self, kind, cut, half):
+        columns = pl.ds(pl.multiple_of(half * self.part, self.part), self.part)
+        return self.outs[kind].at[pl.ds(cut * 4, 4), self.c, :, columns]
+
+    def keep(self, kind):
+        columns = pl.ds(pl.multiple_of(self.h * self.part, self.part), self.part)
+        return local(self.quarters[kind], self.outs[kind].at[:, self.c, :, columns], self.own.at[kind])
+
+    def over(self, kind, cut, half):
+        return remote(
+            self.quarters[kind].at[pl.ds(cut * 4, 4)], self.slot(kind, cut, half), self.x_s.at[kind, cut],
+            self.x_r.at[kind, cut], device(self.z, self.y, self.c, 1 - self.h),
+        )
+
+    def share(self, kind, cut, core):
+        ref = self.outs[kind].at[pl.ds(cut * 4, 4), core]
+        return remote(
+            ref, ref, self.c_s.at[kind, cut], self.c_r.at[kind, cut], device(self.z, self.y, 1 - self.c, self.h)
+        )
+
+    def start(self):
+        for kind in range(2):
+            for cut in range(2):
+                self.over(kind, cut, self.h).start()
+            self.keep(kind).start()
+
+    def relay(self):
+        for kind in range(2):
+            self.keep(kind).wait()
+            for cut in range(2):
+                self.over(kind, cut, 1 - self.h).wait_recv()
+                self.share(kind, cut, self.c).start()
+
+    def finish(self):
+        for kind in range(2):
+            for cut in range(2):
+                self.share(kind, cut, 1 - self.c).wait_recv()
+                self.share(kind, cut, self.c).wait_send()
+                self.over(kind, cut, self.h).wait_send()
+
+
+class DownSpread:
+    @staticmethod
+    def scratch():
+        return [dma(1), dma(2), dma(2)]
+
+    def __init__(self, weight, out, sems):
+        self.weight, self.out = weight, out
+        self.d_own, self.d_x, self.d_sib = sems
+        self.z, self.y, self.c, self.h = place()
+
+    def keep(self):
+        return local(self.weight, self.out.at[self.h, self.c], self.d_own.at[0])
+
+    def over(self):
+        return remote(
+            self.weight, self.out.at[self.h, self.c], self.d_x.at[0], self.d_x.at[1],
+            device(self.z, self.y, self.c, 1 - self.h),
+        )
+
+    def over_in(self):
+        ref = self.out.at[1 - self.h, self.c]
+        return remote(ref, ref, self.d_x.at[0], self.d_x.at[1], device(self.z, self.y, self.c, self.h))
+
+    def share(self):
+        ref = self.out.at[:, self.c]
+        return remote(ref, ref, self.d_sib.at[0], self.d_sib.at[1], device(self.z, self.y, 1 - self.c, self.h))
+
+    def share_in(self):
+        ref = self.out.at[:, 1 - self.c]
+        return remote(ref, ref, self.d_sib.at[0], self.d_sib.at[1], device(self.z, self.y, self.c, self.h))
+
+    def start(self):
+        self.keep().start()
+        self.over().start()
+
+    def relay(self):
+        self.keep().wait()
+        self.over_in().wait_recv()
+        self.share().start()
+
+    def finish(self):
+        self.share_in().wait_recv()
+        self.share().wait_send()
+        self.over().wait_send()
 
 
 class NoteSpread:
@@ -1028,108 +1084,246 @@
     return groups
 
 
-def spread_kernel(tokens, cot, note, wq, wk, wv, wo, wg, wu, wd, tok_out, cot_out, note_out, qkv, out_w, gate, up, down, *sems):
-    tok_sems, cot_sems, note_sems, attn_sems, mlp_sems = split_refs(sems, (8, 8, 3, 8, 9))
+def spread_kernel(tokens, note, wq, wk, wv, wo, tok_out, note_out, qkv, out_w, *sems):
+    tok_sems, note_sems, attn_sems = split_refs(sems, (8, 3, 10))
     greet_all(16, 2)
     tok = Gather(tokens, tok_out, tok_sems)
     notes = NoteSpread(note, note_out, note_sems)
     attn = AttnSpread((wq, wk, wv, wo), (qkv, out_w), attn_sems)
-    mlp = MlpSpread((wg, wu, wd), (gate, up, down), mlp_sems)
+    attn.start()
     tok.start()
     notes.start()
-    attn.start()
-    mlp.start_down()
-    tok.relays()
+    tok.relay_b()
+    for elem in (2, 0, 1, 3):
+        tok.relay(0, elem)
     attn.relay()
-    mlp.start()
-    cots = Gather(cot, cot_out, cot_sems)
-    cots.start()
-    mlp.relay(0)
-    cots.relays()
-    mlp.relay(1)
-    mlp.relay_share(0)
-    mlp.relay_share(1)
-    mlp.relay_down()
-    tok.finish()
-    cots.finish()
+    for elem in (2, 0, 1, 3):
+        tok.relay(1, elem)
+    attn.relay_share()
+    for elem in (2, 0, 1, 3):
+        tok.relay(2, elem)
     notes.finish()
     attn.finish()
-    mlp.finish()
-
-
-def spread(tokens, cot, note, wq, wk, wv, wo, wg, wu, wd):
+    tok.finish()
+
+
+def spread(tokens, note, wq, wk, wv, wo):
     def shape(*dims):
         return jax.ShapeDtypeStruct(dims, jnp.bfloat16)
 
     rows, width = tokens.shape
     depth = wq.shape[0]
-    part = wg.shape[1] // 8
     return pl.pallas_call(
         spread_kernel,
         out_shape=(
             shape(8, rows, width),
-            shape(8, rows, width),
             jax.ShapeDtypeStruct((16,) + note.shape, jnp.float32),
             shape(8, 2, depth, 3 * HD),
             shape(2, 2, wo.shape[0], width),
-            shape(8, 2, depth, 2 * part),
-            shape(8, 2, depth, 2 * part),
-            shape(2, 2, wd.shape[0], width),
         ),
-        in_specs=[ANY] * 10,
-        out_specs=(ANY,) * 8,
-        scratch_shapes=Gather.scratch() + Gather.scratch() + NoteSpread.scratch() + AttnSpread.scratch() + MlpSpread.scratch(),
+        in_specs=[INSIDE] * 6,
+        out_specs=(ANY,) * 4,
+        scratch_shapes=Gather.scratch() + NoteSpread.scratch() + AttnSpread.scratch(),
         compiler_params=kernel_params(3),
         name="spread",
-    )(tokens, cot, note, wq, wk, wv, wo, wg, wu, wd)
-
-
-def greet_square(z, y, c, h):
+    )(tokens, note, wq, wk, wv, wo)
+
+
+def reduce_share_kernel(parts_in, gate_in, up_in, out, gate, up, parts, in_sem, *refs):
+    reduce_refs, share_sems = split_refs(refs, (9, 5))
+    load = pltpu.make_async_copy(parts_in, parts, in_sem)
+    load.start()
+    z, y, c, h = place()
     greet(device(z, y, 1 - c, h))
     greet(device(z, y, c, 1 - h))
-    pl.semaphore_wait(pltpu.get_barrier_semaphore(), 2)
-
-
-def keys_kernel(kv, out, own, x_s, x_r, c_s, c_r):
+    greet_plane(2)
+    reduce = Reduce(parts, reduce_refs)
+    share = MlpShare((gate_in, up_in), (gate, up), share_sems)
+    share.start()
+    load.wait()
+    for place_at in range(4):
+        reduce.start(place_at)
+    for place_at in range(3):
+        reduce.relay(place_at)
+    reduce.total(out)
+    reduce.finish()
+    share.relay()
+    share.finish()
+
+
+def reduce_share(parts, gate, up):
+    shape = parts.shape
+    eight, depth, part = gate.shape
+    full = jax.ShapeDtypeStruct((eight, 2, depth, 2 * part), gate.dtype)
+    return pl.pallas_call(
+        reduce_share_kernel,
+        out_shape=(jax.ShapeDtypeStruct(shape[1:], jnp.float32), full, full),
+        in_specs=[ANY, INSIDE, INSIDE],
+        out_specs=(INSIDE, ANY, ANY),
+        scratch_shapes=[pltpu.VMEM(shape, jnp.bfloat16), dma()] + Reduce.scratch(shape[2]) + MlpShare.scratch(),
+        compiler_params=kernel_params(7),
+        name="reduce_share",
+    )(parts, gate, up)
+
+
+def gather_share_kernel(src, wd, out, down, *sems):
+    gather_sems, down_sems = split_refs(sems, (8, 3))
     z, y, c, h = place()
-    greet_square(z, y, c, h)
+    greet(device(z, y, 1 - c, h))
+    greet(device(z, y, c, 1 - h))
+    greet_plane(2)
+    gather = Gather(src, out, gather_sems)
+    downs = DownSpread(wd, down, down_sems)
+    gather.start()
+    downs.start()
+    gather.relays()
+    downs.relay()
+    gather.finish()
+    downs.finish()
+
+
+def gather_share(rows, wd):
+    return pl.pallas_call(
+        gather_share_kernel,
+        out_shape=(
+            jax.ShapeDtypeStruct((2 * LINE,) + rows.shape, rows.dtype),
+            jax.ShapeDtypeStruct((2, 2) + wd.shape, wd.dtype),
+        ),
+        in_specs=[INSIDE] * 2,
+        out_specs=(ANY,) * 2,
+        scratch_shapes=Gather.scratch() + DownSpread.scratch(),
+        compiler_params=kernel_params(8),
+        name="gather_share",
+    )(rows, wd)
+
+
+def attend_kernel(
+    query, kv, query_ids, key_ids, cot, wg, wu,
+    kv_out, attended_out, attended_low_out, log_out, cot_out, gate, up,
+    keys, scores, total, own, x_s, x_r, c_s, c_r, out_sem, *sems,
+):
+    z, y, c, h = place()
+    cot_sems, mlp_sems = split_refs(sems, (8, 3))
+    greet_all(16, 2)
+    rows, width = key_ids.shape[2], query.shape[1]
+    pair = query.shape[0] // LINE
+    cots = Gather(cot, cot_out, cot_sems)
+    mlp = MlpSpread((wg, wu), (gate, up), mlp_sems)
 
     def keep(cut):
-        rows = pl.ds(cut * 2, 2)
-        return local(kv.at[rows], out.at[rows, c, h], own.at[cut])
+        part = pl.ds(cut * 2, 2)
+        return local(kv.at[part], keys.at[part, c, h], own.at[cut])
 
     def over(cut, half):
-        rows = pl.ds(cut * 2, 2)
-        return remote(kv.at[rows], out.at[rows, c, half], x_s.at[cut], x_r.at[cut], device(z, y, c, 1 - h))
+        part = pl.ds(cut * 2, 2)
+        return remote(kv.at[part], keys.at[part, c, half], x_s.at[cut], x_r.at[cut], device(z, y, c, 1 - h))
 
     def share(cut, core):
-        ref = out.at[pl.ds(cut * 2, 2), core]
+        ref = keys.at[pl.ds(cut * 2, 2), core]
         return remote(ref, ref, c_s.at[cut], c_r.at[cut], device(z, y, 1 - c, h))
 
-    for cut in range(4):
+    for cut in range(LINE):
         over(cut, h).start()
         keep(cut).start()
-    for cut in range(4):
+    mlp.start()
+    cots.start()
+
+    def pass_on(cut):
         keep(cut).wait()
         over(cut, 1 - h).wait_recv()
         share(cut, c).start()
-    for cut in range(4):
-        share(cut, 1 - c).wait_recv()
+
+    def attend(place_at):
+        part = pl.ds(place_at * pair, pair)
+        count = min(2 * place_at + 3, 8)
+        ids = query_ids[part]
+
+        def maxima(block, best):
+            key = keys[block, :, :, :, :width].reshape(rows, width)
+            part_scores = times_transposed(query[part], key)
+            part_scores = jnp.where(key_ids[block] <= ids, part_scores, -1e30)
+            scores[block] = part_scores
+            for lane in range(rows // 128):
+                best = jnp.maximum(best, part_scores[:, lane * 128 : lane * 128 + 128])
+            return best
+
+        best = lax.fori_loop(0, count, maxima, jnp.full((pair, 128), -1e30, jnp.float32))
+        row_max = jnp.max(best, axis=1, keepdims=True)
+        total[...] = jnp.zeros_like(total)
+
+        def mix(block, sums):
+            weights = jnp.exp(scores[block] - row_max)
+            value = keys[block, :, :, :, width:].reshape(rows, width)
+            total[...] += product(weights.astype(jnp.bfloat16), value)
+            for lane in range(rows // 128):
+                sums = sums + weights[:, lane * 128 : lane * 128 + 128]
+            return sums
+
+        sums = lax.fori_loop(0, count, mix, jnp.zeros((pair, 128), jnp.float32))
+        row_sum = jnp.sum(sums, axis=1, keepdims=True)
+        mixed = total[...] / row_sum
+        attended_out[part] = mixed
+        attended_low_out[part] = mixed.astype(jnp.bfloat16)
+        log_out[part] = row_max + jnp.log(row_sum)
+
+    pass_on(0)
+    pass_on(1)
+    share(0, 1 - c).wait_recv()
+    share(1, 1 - c).wait_recv()
+    attend(0)
+    cots.relay_b()
+    for elem in (2, 0, 1, 3):
+        cots.relay(0, elem)
+    pass_on(2)
+    share(2, 1 - c).wait_recv()
+    attend(1)
+    pass_on(3)
+    share(3, 1 - c).wait_recv()
+    store = local(keys, kv_out, out_sem)
+    store.start()
+    attend(2)
+    for elem in (2, 0, 1, 3):
+        cots.relay(1, elem)
+    attend(3)
+    for elem in (2, 0, 1, 3):
+        cots.relay(2, elem)
+    cots.finish()
+    mlp.finish()
+    for cut in range(LINE):
         share(cut, c).wait_send()
         over(cut, h).wait_send()
-
-
-def gather_keys(kv):
+    store.wait()
+
+
+def attend_keys(query, kv, query_ids, key_ids, cot, wg, wu):
     eight, rows, width = kv.shape
+    depth, part = wg.shape[0], wg.shape[1] // 8
+    tokens = query.shape[0]
+
+    def shape(*dims, dtype=jnp.bfloat16):
+        return jax.ShapeDtypeStruct(dims, dtype)
+
     return pl.pallas_call(
-        keys_kernel,
-        out_shape=jax.ShapeDtypeStruct((eight, 2, 2, rows, width), kv.dtype),
-        in_specs=[ANY],
-        out_specs=ANY,
-        scratch_shapes=[dma(4)] * 5,
+        attend_kernel,
+        out_shape=(
+            shape(eight, 2, 2, rows, width),
+            shape(tokens, HD, dtype=jnp.float32),
+            shape(tokens, HD),
+            shape(tokens, 1, dtype=jnp.float32),
+            shape(8, *cot.shape),
+            shape(8, depth, part),
+            shape(8, depth, part),
+        ),
+        in_specs=[INSIDE] * 7,
+        out_specs=(ANY, INSIDE, INSIDE, INSIDE, ANY, ANY, ANY),
+        scratch_shapes=[
+            pltpu.VMEM((eight, 2, 2, rows, width), jnp.bfloat16),
+            pltpu.VMEM((eight, tokens // LINE, 4 * rows), jnp.float32),
+            pltpu.VMEM((tokens // LINE, HD), jnp.float32),
+        ] + [dma(4)] * 5 + [dma()] + Gather.scratch() + MlpSpread.scratch(),
         compiler_params=kernel_params(4),
-        name="gather_keys",
-    )(kv)
+        name="attend_keys",
+    )(query, kv, query_ids, key_ids, cot, wg, wu)
 
 
 def add_into(target, *others):
@@ -1139,349 +1333,601 @@
     target[...] = total.astype(target.dtype)
 
 
-def key_grads_kernel(parts_in, out, parts, sib_in, x_in, z_in, load_sem, c_s, c_r, x_s, x_r, z_s, z_r):
+class QuarterReduce:
+    @staticmethod
+    def scratch(depth, wide):
+        store = pltpu.VMEM((8, 2, depth, wide), jnp.bfloat16)
+        sib = pltpu.VMEM((8, depth, wide), jnp.bfloat16)
+        over = pltpu.VMEM((8, depth, wide // 2), jnp.bfloat16)
+        return [store, store, sib, sib, over, over] + [dma(2)] + [dma(2, 2)] * 4
+
+    def __init__(self, sources, outs, refs):
+        self.sources, self.outs = sources, outs
+        self.store, self.sib, self.box = refs[0:2], refs[2:4], refs[4:6]
+        self.load_s, self.c_s, self.c_r, self.x_s, self.x_r = refs[6:]
+        self.z, self.y, self.c, self.h = place()
+        self.part = self.box[0].shape[2]
+
+    def columns(self, half):
+        return pl.ds(pl.multiple_of(half * self.part, self.part), self.part)
+
+    def load(self, kind):
+        return local(self.sources[kind], self.store[kind], self.load_s.at[kind])
+
+    def share(self, kind, cut):
+        chips = pl.ds(cut * 4, 4)
+        return remote(
+            self.store[kind].at[chips, 1 - self.c], self.sib[kind].at[chips], self.c_s.at[kind, cut],
+            self.c_r.at[kind, cut], device(self.z, self.y, 1 - self.c, self.h),
+        )
+
+    def over(self, kind, cut):
+        chips = pl.ds(cut * 4, 4)
+        return remote(
+            self.store[kind].at[chips, self.c, :, self.columns(1 - self.h)], self.box[kind].at[chips],
+            self.x_s.at[kind, cut], self.x_r.at[kind, cut], device(self.z, self.y, self.c, 1 - self.h),
+        )
+
+    def start_loads(self):
+        for kind in range(2):
+            self.load(kind).start()
+
+    def start(self, kind):
+        self.load(kind).wait()
+        for cut in range(2):
+            self.share(kind, cut).start()
+
+    def relay(self, kind):
+        columns = self.columns(1 - self.h)
+        for cut in range(2):
+            self.share(kind, cut).wait_recv()
+
+            @pl.loop(cut * 4, cut * 4 + 4)
+            def _(chip):
+                add_into(self.store[kind].at[chip, self.c, :, columns], self.sib[kind].at[chip, :, columns])
+
+            self.over(kind, cut).start()
+
+    def finish(self, kind):
+        columns = self.columns(self.h)
+        for cut in range(2):
+            self.over(kind, cut).wait_recv()
+
+            @pl.loop(cut * 4, cut * 4 + 4)
+            def _(chip):
+                total = self.store[kind][chip, self.c, :, columns].astype(jnp.float32)
+                total += self.sib[kind][chip, :, columns].astype(jnp.float32)
+                total += self.box[kind][chip].astype(jnp.float32)
+                self.outs[kind][chip] = total.astype(jnp.bfloat16)
+
+        for cut in range(2):
+            self.share(kind, cut).wait_send()
+            self.over(kind, cut).wait_send()
+
+
+class QuarterScatter:
+    @staticmethod
+    def scratch():
+        return [dma(2, 8), dma(2, 8), dma(2)]
+
+    def __init__(self, quarters, outs, sems):
+        self.quarters, self.outs = quarters, outs
+        self.s, self.r, self.own = sems
+        self.z, self.y, self.c, self.h = place()
+        self.chip = self.z * 2 + self.y
+        self.part = quarters[0].shape[2]
+
+    def columns(self, chip):
+        return pl.ds(pl.multiple_of(chip * self.part, self.part), self.part)
+
+    def push(self, kind, step):
+        target = (self.chip + step) % 8
+        return remote(
+            self.quarters[kind].at[target], self.outs[kind].at[:, self.columns(self.chip)], self.s.at[kind, step],
+            self.r.at[kind, step], device(target // 2, target % 2, self.c, self.h),
+        )
+
+    def pull(self, kind, step):
+        ref = self.outs[kind].at[:, self.columns((self.chip + 8 - step) % 8)]
+        return remote(ref, ref, self.s.at[kind, step], self.r.at[kind, step], device(self.z, self.y, self.c, self.h))
+
+    def keep(self, kind):
+        return local(self.quarters[kind].at[self.chip], self.outs[kind].at[:, self.columns(self.chip)], self.own.at[kind])
+
+    def start(self):
+        for kind in range(2):
+            self.keep(kind).start()
+            for step in range(1, 8):
+                self.push(kind, step).start()
+
+    def finish(self):
+        for kind in range(2):
+            self.keep(kind).wait()
+            for step in range(1, 8):
+                self.pull(kind, step).wait_recv()
+                self.push(kind, step).wait_send()
+
+
+class DownReduce:
+    @staticmethod
+    def scratch(rows, width):
+        return [
+            pltpu.VMEM((2, 2, rows, width), jnp.bfloat16),
+            pltpu.VMEM((2, rows, width), jnp.bfloat16),
+            pltpu.VMEM((rows, width), jnp.bfloat16),
+            dma(1), dma(2), dma(2),
+        ]
+
+    def __init__(self, source, out, refs):
+        self.source, self.out = source, out
+        self.store, self.sib, self.box, self.load_s, self.c_sr, self.x_sr = refs
+        self.z, self.y, self.c, self.h = place()
+
+    def load(self):
+        return local(self.source, self.store, self.load_s.at[0])
+
+    def share(self):
+        return remote(
+            self.store.at[:, 1 - self.c], self.sib, self.c_sr.at[0], self.c_sr.at[1],
+            device(self.z, self.y, 1 - self.c, self.h),
+        )
+
+    def over(self):
+        return remote(
+            self.store.at[1 - self.h, self.c], self.box, self.x_sr.at[0], self.x_sr.at[1],
+            device(self.z, self.y, self.c, 1 - self.h),
+        )
+
+    def start(self):
+        self.load().wait()
+        self.share().start()
+
+    def relay(self):
+        self.share().wait_recv()
+        add_into(self.store.at[1 - self.h, self.c], self.sib.at[1 - self.h])
+        self.over().start()
+
+    def finish(self):
+        self.over().wait_recv()
+        total = self.store[self.h, self.c].astype(jnp.float32) + self.sib[self.h].astype(jnp.float32)
+        self.out[...] = total + self.box[...].astype(jnp.float32)
+        self.share().wait_send()
+        self.over().wait_send()
+
+
+def reduce_grads_kernel(parts_in, gate_in, up_in, out, gate, up, parts, in_sem, *refs):
+    reduce_refs, grad_refs = split_refs(refs, (9, 11))
+    load = pltpu.make_async_copy(parts_in, parts, in_sem)
+    load.start()
     z, y, c, h = place()
-    pair = z + 1 - 2 * (z % 2)
-    load = local(parts_in, parts, load_sem)
-    load.start()
+    grads = QuarterReduce((gate_in, up_in), (gate, up), grad_refs)
+    grads.start_loads()
     greet(device(z, y, 1 - c, h))
     greet(device(z, y, c, 1 - h))
-    greet(device(pair, y, c, h))
-    pl.semaphore_wait(pltpu.get_barrier_semaphore(), 3)
+    greet_plane(2)
+    reduce = Reduce(parts, reduce_refs)
     load.wait()
-
-    def share(cut):
-        rows = pl.ds(cut * 2, 2)
-        return remote(
-            parts.at[rows, 1 - c], sib_in.at[rows], c_s.at[cut], c_r.at[cut], device(z, y, 1 - c, h)
-        )
-
-    def over(cut):
-        rows = pl.ds(cut * 2, 2)
-        return remote(
-            parts.at[rows, c, 1 - h], x_in.at[rows], x_s.at[cut], x_r.at[cut], device(z, y, c, 1 - h)
-        )
-
-    def across(cut, column):
-        rows = pl.ds(cut * 2, 2)
-        columns = pl.ds(pl.multiple_of(column * HD, HD), HD)
-        return remote(
-            parts.at[rows, c, h, :, columns], z_in.at[rows], z_s.at[cut], z_r.at[cut], device(pair, y, c, h)
-        )
-
-    for cut in range(4):
-        share(cut).start()
-    for cut in range(4):
-        rows = pl.ds(cut * 2, 2)
-        share(cut).wait_recv()
-        add_into(parts.at[rows, c, 1 - h], sib_in.at[rows, 1 - h])
-        over(cut).start()
-    for cut in range(4):
-        rows = pl.ds(cut * 2, 2)
-        over(cut).wait_recv()
-        add_into(parts.at[rows, c, h], sib_in.at[rows, h], x_in.at[rows])
-        across(cut, 1 - z % 2).start()
-    for cut in range(4):
-        rows = pl.ds(cut * 2, 2)
-        columns = pl.ds(pl.multiple_of((z % 2) * HD, HD), HD)
-        across(cut, 0).wait_recv()
-        out[rows] = parts[rows, c, h, :, columns].astype(jnp.float32) + z_in[rows].astype(jnp.float32)
-    for cut in range(4):
-        share(cut).wait_send()
-        over(cut).wait_send()
-        across(cut, 0).wait_send()
-
-
-def reduce_keys(parts):
-    eight, cores, halves, rows, width = parts.shape
-
-    def room(*dims):
-        return pltpu.VMEM(dims, jnp.bfloat16)
-
+    for place_at in range(4):
+        reduce.start(place_at)
+    grads.start(0)
+    grads.start(1)
+    grads.relay(0)
+    reduce.relay(0)
+    grads.relay(1)
+    reduce.relay(1)
+    reduce.relay(2)
+    reduce.total(out)
+    grads.finish(0)
+    grads.finish(1)
+    reduce.finish()
+
+
+def reduce_grads(parts, gate, up):
+    shape = parts.shape
+    depth, wide = gate.shape[2:]
+    quarter = jax.ShapeDtypeStruct((8, depth, wide // 2), gate.dtype)
     return pl.pallas_call(
-        key_grads_kernel,
-        out_shape=jax.ShapeDtypeStruct((eight, rows, HD), jnp.float32),
-        in_specs=[ANY],
-        out_specs=INSIDE,
-        scratch_shapes=[
-            room(*parts.shape), room(eight, 2, rows, width), room(eight, rows, width), room(eight, rows, HD), dma(),
-        ] + [dma(4)] * 6,
-        compiler_params=kernel_params(5),
-        name="reduce_keys",
-    )(parts)
-
-
-def weight_grads_kernel(
-    gate_in, up_in, down_in, query_in, side_in, out_in, gains_in,
-    gate_out, up_out, down_out, query_out, key_out, value_out, out_out, gains_out,
-    gate, up, down, query, side, outw,
-    gate_sib, up_sib, down_sib, query_sib, side_sib, outw_sib,
-    gate_x, up_x, down_x, query_x, side_x, outw_x,
-    gains_box,
-    load_sems, sib_s, sib_r, x_s, x_r, a2a_s, a2a_r, small_s, small_r, y_sr, gain_s, gain_r, keep_sems,
+        reduce_grads_kernel,
+        out_shape=(jax.ShapeDtypeStruct(shape[1:], jnp.float32), quarter, quarter),
+        in_specs=[ANY] * 3,
+        out_specs=(INSIDE,) * 3,
+        scratch_shapes=[pltpu.VMEM(shape, jnp.bfloat16), dma()]
+        + Reduce.scratch(shape[2])
+        + QuarterReduce.scratch(depth, wide),
+        compiler_params=kernel_params(9),
+        name="reduce_grads",
+    )(parts, gate, up)
+
+
+def gather_grads_kernel(src, down_in, out, down, *refs):
+    gather_sems, down_refs = split_refs(refs, (8, 6))
+    z, y, c, h = place()
+    downs = DownReduce(down_in, down, down_refs)
+    downs.load().start()
+    greet(device(z, y, 1 - c, h))
+    greet(device(z, y, c, 1 - h))
+    greet_plane(2)
+    gather = Gather(src, out, gather_sems)
+    gather.start()
+    downs.start()
+    gather.relay_b()
+    downs.relay()
+    for step in range(LINE - 1):
+        for elem in (2, 0, 1, 3):
+            gather.relay(step, elem)
+    downs.finish()
+    gather.finish()
+
+
+def gather_grads(rows, down):
+    return pl.pallas_call(
+        gather_grads_kernel,
+        out_shape=(
+            jax.ShapeDtypeStruct((2 * LINE,) + rows.shape, rows.dtype),
+            jax.ShapeDtypeStruct(down.shape[2:], jnp.float32),
+        ),
+        in_specs=[INSIDE, ANY],
+        out_specs=(ANY, INSIDE),
+        scratch_shapes=Gather.scratch() + DownReduce.scratch(*down.shape[2:]),
+        compiler_params=kernel_params(10),
+        name="gather_grads",
+    )(rows, down)
+
+
+def attend_back_kernel(
+    query, grad_out, keys_in, keys_turned, log_row, delta_row, query_row, key_column, gate_in, up_in,
+    side_out, grad_query, gate, up,
+    keys, turned, parts, grad_key, grad_value, sib_in, x_in, z_in,
+    load_s, c_s, c_r, x_s, x_r, z_s, z_r, *sems,
 ):
     z, y, c, h = place()
-    chip = z * 2 + y
-    blk = lax.axis_index("blk")
-    me = device(z, y, c, h)
-    loads = [
-        local(src, dst, load_sems.at[i])
-        for i, (src, dst) in enumerate(
-            ((gate_in, gate), (up_in, up), (down_in, down), (query_in, query), (side_in, side), (out_in, outw))
-        )
-    ]
+    mate = z + 1 - 2 * (z % 2)
+    loads = [local(keys_in, keys, load_s.at[0]), local(keys_turned, turned, load_s.at[1])]
     for load in loads:
         load.start()
     greet_all(16, 2)
-
-    def gain_push(step):
-        other = (blk + (step // 2)) % 16
-        half = (h + step % 2) % 2
-        return remote(
-            gains_in.at[other], gains_box.at[step], gain_s.at[step], gain_r.at[step], (other, half)
-        )
-
-    for step in range(1, 32):
-        gain_push(step).start()
-    keep_gain = local(gains_in.at[blk], gains_box.at[0], keep_sems.at[0])
-    keep_gain.start()
-
-    stores = ((gate, gate_sib), (up, up_sib), (down, down_sib), (query, query_sib), (side, side_sib), (outw, outw_sib))
-
-    def share(i):
-        store, box = stores[i]
-        return remote(store.at[:, 1 - c], box, sib_s.at[i], sib_r.at[i], device(z, y, 1 - c, h))
-
-    order = (0, 1, 2, 3, 4, 5)
-    for i in order:
-        loads[i].wait()
-        share(i).start()
-
-    half_width = gate.shape[3] // 2
-
-    def columns(index):
-        return pl.ds(pl.multiple_of(index * half_width, half_width), half_width)
-
-    def over(i):
-        if i < 2:
-            store, box = ((gate, gate_x), (up, up_x))[i]
-            src = store.at[:, c, :, columns(1 - h)]
-        elif i == 2:
-            src, box = down.at[1 - h, c], down_x
-        else:
-            store, box = {3: (query, query_x), 4: (side, side_x), 5: (outw, outw_x)}[i]
-            src = store.at[:, c]
-        return remote(src, box, x_s.at[i], x_r.at[i], device(z, y, c, 1 - h))
-
-    outs = (gate_out, up_out)
-
-    def scatter(i, step):
-        store = (gate, up)[i]
-        target = (chip + step) % 8
-        return remote(
-            store.at[target, c, :, columns(h)], outs[i].at[:, columns(chip)], a2a_s.at[i, step], a2a_r.at[i, step],
-            device(target // 2, target % 2, c, h),
-        )
-
-    def scatter_in(i, step):
-        source = (chip + 8 - step) % 8
-        ref = outs[i].at[:, columns(source)]
-        return remote(ref, ref, a2a_s.at[i, step], a2a_r.at[i, step], me)
-
-    def scatter_keep(i):
-        store = (gate, up)[i]
-        return local(store.at[chip, c, :, columns(h)], outs[i].at[:, columns(chip)], keep_sems.at[1 + i])
-
-    for i in (0, 1):
-        store, box = stores[i]
-        share(i).wait_recv()
-
-        @pl.loop(0, 8)
-        def _(p):
-            add_into(store.at[p, c], box.at[p])
-
-        over(i).start()
-    share(2).wait_recv()
-    for half in range(2):
-        add_into(down.at[half, c], down_sib.at[half])
-    over(2).start()
-    for i in (3, 4, 5):
-        store, box = stores[i]
-        share(i).wait_recv()
-        for p in range(box.shape[0]):
-            add_into(store.at[p, c], box.at[p])
-
-        @pl.when(h != y)
-        def _():
-            over(i).start()
-
-    def small_out(kind, target):
-        if kind == 0:
-            return query_out.at[:, pl.ds(pl.multiple_of(z * HD, HD), HD)]
-        return (key_out, value_out)[kind - 1].at[:, pl.ds(pl.multiple_of((z // 2) * HD, HD), HD)]
-
-    def small(kind, step):
-        store = query if kind == 0 else side
-        target = (chip + step) % 8
-        return remote(
-            store.at[target, c], small_out(kind, target), small_s.at[kind, step], small_r.at[kind, z, step],
-            device(target // 2, target % 2, c, h),
-        )
-
-    def small_keep(kind):
-        store = query if kind == 0 else side
-        return local(store.at[chip, c], small_out(kind, chip), keep_sems.at[3 + kind])
-
-    def out_move():
-        return remote(outw.at[1 - y, c], out_out, y_sr.at[0], y_sr.at[1], device(z, 1 - y, c, h))
-
-    def out_keep():
-        return local(outw.at[y, c], out_out, keep_sems.at[6])
-
-    for i, box in ((0, gate_x), (1, up_x)):
-        store = (gate, up)[i]
-        over(i).wait_recv()
-
-        @pl.loop(0, 8)
-        def _(p):
-            add_into(store.at[p, c, :, columns(h)], box.at[p])
-
-        scatter_keep(i).start()
-        for step in range(1, 8):
-            scatter(i, step).start()
-
-    @pl.when(h == y)
-    def _():
-        for i in (3, 4, 5):
-            store, box = {3: (query, query_x), 4: (side, side_x), 5: (outw, outw_x)}[i]
-            over(i).wait_recv()
-            for p in range(box.shape[0]):
-                add_into(store.at[p, c], box.at[p])
-        small_keep(0).start()
-        for step in range(1, 8):
-            small(0, step).start()
-
-        @pl.when(z % 2 == 0)
-        def _():
-            small_keep(1).start()
-            for step in range(1, 8):
-                small(1, step).start()
-
-        @pl.when(z % 2 == 1)
-        def _():
-            small_keep(2).start()
-            for step in range(1, 8):
-                small(2, step).start()
-
-        out_move().start()
-        out_keep().start()
-
-    over(2).wait_recv()
-    down_out[...] = (
-        down[h, c].astype(jnp.float32) + down_x[...].astype(jnp.float32)
-    )
-
-    keep_gain.wait()
-    for step in range(1, 32):
-        gain_push(step).wait_recv()
-    total = gains_box[0]
-    for step in range(1, 32):
-        total += gains_box[step]
-    gains_out[...] = total
-
-    for i in (0, 1):
-        for step in range(1, 8):
-            scatter_in(i, step).wait_recv()
-        scatter_keep(i).wait()
-
-    def small_in(kind, line, step):
-        if kind == 0:
-            ref = query_out.at[:, pl.ds(line * HD, HD)]
-        else:
-            ref = (key_out, value_out)[kind - 1].at[:, pl.ds((line // 2) * HD, HD)]
-        return remote(ref, ref, small_s.at[kind, step], small_r.at[kind, line, step], me)
-
-    for kind in range(3):
-        for line in range(LINE):
-            if kind and line % 2 != kind - 1:
-                continue
-            source = line * 2 + h
-            step = (chip + 8 - source) % 8
-
-            @pl.when(step != 0)
-            def _():
-                small_in(kind, line, step).wait_recv()
-
-            @pl.when(step == 0)
-            def _():
-                small_keep(kind).wait()
-
-    @pl.when(h != y)
-    def _():
-        remote(out_out, out_out, y_sr.at[0], y_sr.at[1], me).wait_recv()
-        for i in (3, 4, 5):
-            over(i).wait_send()
-
-    @pl.when(h == y)
-    def _():
-        out_keep().wait()
-        out_move().wait_send()
-        for step in range(1, 8):
-            small(0, step).wait_send()
-
-        @pl.when(z % 2 == 0)
-        def _():
-            for step in range(1, 8):
-                small(1, step).wait_send()
-
-        @pl.when(z % 2 == 1)
-        def _():
-            for step in range(1, 8):
-                small(2, step).wait_send()
-
-    for i in range(6):
-        share(i).wait_send()
-    for i in range(3):
-        over(i).wait_send()
-    for i in (0, 1):
-        for step in range(1, 8):
-            scatter(i, step).wait_send()
-    for step in range(1, 32):
-        gain_push(step).wait_send()
-
-
-def reduce_weights(gate, up, down, query, side, outw, gains):
-    parts = (gate, up, down, query, side, outw)
-
-    def room(*dims):
-        return pltpu.VMEM(dims, jnp.bfloat16)
+    scatter = QuarterScatter((gate_in, up_in), (gate, up), sems)
+    scatter.start()
+    rows, width = key_column.shape[1], query.shape[1]
+    pair = query.shape[0] // LINE
+
+    def share(block):
+        return remote(
+            parts.at[block, 1 - c], sib_in.at[block], c_s.at[block], c_r.at[block], device(z, y, 1 - c, h)
+        )
+
+    def over(block):
+        return remote(
+            parts.at[block, c, 1 - h], x_in.at[block], x_s.at[block], x_r.at[block], device(z, y, c, 1 - h)
+        )
+
+    def columns(kind):
+        return pl.ds(pl.multiple_of(kind * width, width), width)
+
+    def across(block):
+        return remote(
+            parts.at[block, c, h, :, columns(1 - z % 2)], z_in.at[block], z_s.at[block], z_r.at[block],
+            device(mate, y, c, h),
+        )
+
+    def stage_two(block):
+        share(block).wait_recv()
+        add_into(parts.at[block, c, 1 - h], sib_in.at[block, 1 - h])
+        over(block).start()
+
+    def stage_three(block):
+        over(block).wait_recv()
+        add_into(parts.at[block, c, h], sib_in.at[block, h], x_in.at[block])
+        across(block).start()
+
+    def stage_four(block):
+        across(block).wait_recv()
+        side_out[block] = parts[block, c, h, :, columns(z % 2)].astype(jnp.float32) + z_in[block].astype(jnp.float32)
+
+    for load in loads:
+        load.wait()
+    grad_query[...] = jnp.zeros_like(grad_query)
+    for block in range(8):
+        key = keys[block, :, :, :, :width].reshape(rows, width)
+        value = keys[block, :, :, :, width:].reshape(rows, width)
+        grad_key[...] = jnp.zeros_like(grad_key)
+        grad_value[...] = jnp.zeros_like(grad_value)
+
+        @pl.loop(max(0, (block - 1) // 2), LINE)
+        def _(place_at):
+            part = pl.ds(pl.multiple_of(place_at * pair, pair), pair)
+            part_scores = times_transposed(key, query[part])
+            visible = key_column[block] <= query_row[place_at]
+            weights = jnp.where(visible, jnp.exp(part_scores - log_row[place_at]), 0.0)
+            grad_weights = times_transposed(value, grad_out[part])
+            grad_scores = (weights * (grad_weights - delta_row[place_at])).astype(jnp.bfloat16)
+            grad_key[...] += product(grad_scores, query[part])
+            grad_value[...] += product(weights.astype(jnp.bfloat16), grad_out[part])
+            grad_query[place_at] += product(turned[block], grad_scores)
+
+        parts[block, :, :, :, :width] = grad_key[...].astype(jnp.bfloat16).reshape(2, 2, rows // 4, width)
+        parts[block, :, :, :, width:] = grad_value[...].astype(jnp.bfloat16).reshape(2, 2, rows // 4, width)
+        share(block).start()
+        if block >= 1:
+            stage_two(block - 1)
+        if block >= 4:
+            stage_three(block - 4)
+    stage_two(7)
+    for block in range(4, 8):
+        stage_three(block)
+        stage_four(block - 4)
+    for block in range(4, 8):
+        stage_four(block)
+    for block in range(8):
+        share(block).wait_send()
+        over(block).wait_send()
+        across(block).wait_send()
+    scatter.finish()
+
+
+def attend_back(query, grad_out, keys, keys_turned, log_row, delta_row, query_row, key_column, gate, up):
+    eight, _, _, rows, width = keys.shape
+    tokens = query.shape[0]
+    depth, part = gate.shape[1:]
+
+    def room(*dims, dtype=jnp.bfloat16):
+        return pltpu.VMEM(dims, dtype)
 
     def shape(*dims, dtype=jnp.bfloat16):
         return jax.ShapeDtypeStruct(dims, dtype)
 
-    depth, wide = gate.shape[2], gate.shape[3]
-    sib = [room(part.shape[0], *part.shape[2:]) for part in parts]
-    over = [
-        room(8, depth, wide // 2), room(8, depth, wide // 2), room(*down.shape[2:]),
-        room(8, depth, HD), room(8, depth, HD), room(2, *outw.shape[2:]),
-    ]
     return pl.pallas_call(
-        weight_grads_kernel,
+        attend_back_kernel,
         out_shape=(
-            shape(depth, 4 * wide), shape(depth, 4 * wide), shape(*down.shape[2:], dtype=jnp.float32),
-            shape(depth, 4 * HD), shape(depth, 2 * HD), shape(depth, 2 * HD), shape(*outw.shape[2:]),
-            shape(*gains.shape[1:], dtype=jnp.float32),
+            shape(eight, rows, HD, dtype=jnp.float32),
+            shape(LINE, HD, tokens // LINE, dtype=jnp.float32),
+            shape(depth, 8 * part),
+            shape(depth, 8 * part),
         ),
-        in_specs=[ANY] * 7,
-        out_specs=(ANY, ANY, INSIDE, ANY, ANY, ANY, ANY, INSIDE),
-        scratch_shapes=[room(*part.shape) for part in parts] + sib + over + [
-            pltpu.VMEM((32,) + gains.shape[1:], jnp.float32),
-            dma(6), dma(6), dma(6), dma(6), dma(6), dma(2, 8), dma(2, 8), dma(3, 8), dma(3, 4, 8), dma(2),
-            dma(32), dma(32), dma(8),
-        ],
+        in_specs=[INSIDE, INSIDE, ANY, ANY, INSIDE, INSIDE, INSIDE, INSIDE, INSIDE, INSIDE],
+        out_specs=(INSIDE, INSIDE, ANY, ANY),
+        scratch_shapes=[
+            room(*keys.shape), room(*keys_turned.shape), room(*keys.shape),
+            room(4 * rows, HD, dtype=jnp.float32), room(4 * rows, HD, dtype=jnp.float32),
+            room(eight, 2, rows, width), room(eight, rows, width), room(eight, rows, HD),
+            dma(2),
+        ] + [dma(8)] * 6 + QuarterScatter.scratch(),
+        compiler_params=kernel_params(11),
+        name="attend_back",
+    )(query, grad_out, keys, keys_turned, log_row, delta_row, query_row, key_column, gate, up)
+
+
+class HeadGrads:
+    @staticmethod
+    def scratch(depth, out_rows, width):
+        def room(*dims):
+            return pltpu.VMEM(dims, jnp.bfloat16)
+
+        return [
+            room(8, 2, depth, HD), room(8, 2, depth, HD), room(2, 2, out_rows, width),
+            room(8, depth, HD), room(8, depth, HD), room(2, out_rows, width),
+            room(8, depth, HD), room(8, depth, HD), room(2, out_rows, width),
+            dma(3), dma(3), dma(3), dma(3), dma(3), dma(3, 8), dma(3, 4, 8), dma(2), dma(4),
+        ]
+
+    def __init__(self, sources, outs, refs):
+        self.sources, self.outs = sources, outs
+        self.store, self.sib, self.box = refs[0:3], refs[3:6], refs[6:9]
+        (self.load_s, self.c_s, self.c_r, self.x_s, self.x_r, self.s, self.r, self.y_sr, self.own) = refs[9:]
+        self.z, self.y, self.c, self.h = place()
+        self.chip = self.z * 2 + self.y
+        self.me = device(self.z, self.y, self.c, self.h)
+        self.owner = self.h == self.y
+
+    def load(self, i):
+        return local(self.sources[i], self.store[i], self.load_s.at[i])
+
+    def share(self, i):
+        return remote(
+            self.store[i].at[:, 1 - self.c], self.sib[i], self.c_s.at[i], self.c_r.at[i],
+            device(self.z, self.y, 1 - self.c, self.h),
+        )
+
+    def over(self, i):
+        return remote(
+            self.store[i].at[:, self.c], self.box[i], self.x_s.at[i], self.x_r.at[i],
+            device(self.z, self.y, self.c, 1 - self.h),
+        )
+
+    def target(self, kind, line):
+        start = line * HD if kind == 0 else (line // 2) * HD
+        return self.outs[kind].at[:, pl.ds(pl.multiple_of(start, HD), HD)]
+
+    def push(self, kind, step):
+        chip = (self.chip + step) % 8
+        return remote(
+            self.store[min(kind, 1)].at[chip, self.c], self.target(kind, self.z), self.s.at[kind, step],
+            self.r.at[kind, self.z, step], device(chip // 2, chip % 2, self.c, self.h),
+        )
+
+    def keep(self, kind):
+        return local(self.store[min(kind, 1)].at[self.chip, self.c], self.target(kind, self.z), self.own.at[kind])
+
+    def pull(self, kind, line, step):
+        ref = self.target(kind, line)
+        return remote(ref, ref, self.s.at[kind, step], self.r.at[kind, line, step], self.me)
+
+    def out_move(self):
+        return remote(
+            self.store[2].at[1 - self.y, self.c], self.outs[3], self.y_sr.at[0], self.y_sr.at[1],
+            device(self.z, 1 - self.y, self.c, self.h),
+        )
+
+    def out_keep(self):
+        return local(self.store[2].at[self.y, self.c], self.outs[3], self.own.at[3])
+
+    def start_loads(self):
+        for i in range(3):
+            self.load(i).start()
+
+    def start(self):
+        for i in (2, 0, 1):
+            self.load(i).wait()
+            self.share(i).start()
+
+    def relay(self):
+        for i in (2, 0, 1):
+            self.share(i).wait_recv()
+
+            @pl.loop(0, self.sib[i].shape[0])
+            def _(at):
+                add_into(self.store[i].at[at, self.c], self.sib[i].at[at])
+
+            @pl.when(jnp.logical_not(self.owner))
+            def _():
+                self.over(i).start()
+
+    def scatter(self):
+        @pl.when(self.owner)
+        def _():
+            for i in (2, 0, 1):
+                self.over(i).wait_recv()
+
+                @pl.loop(0, self.sib[i].shape[0])
+                def _(at):
+                    add_into(self.store[i].at[at, self.c], self.box[i].at[at])
+
+                if i == 2:
+                    self.out_move().start()
+                    self.out_keep().start()
+                elif i == 0:
+                    self.keep(0).start()
+                    for step in range(1, 8):
+                        self.push(0, step).start()
+                else:
+                    for kind in (1, 2):
+
+                        @pl.when(self.z % 2 == kind - 1)
+                        def _():
+                            self.keep(kind).start()
+                            for step in range(1, 8):
+                                self.push(kind, step).start()
+
+    def finish(self):
+        for kind in range(3):
+            for line in range(LINE):
+                if kind and line % 2 != kind - 1:
+                    continue
+                step = (self.chip + 8 - (line * 2 + self.h)) % 8
+
+                @pl.when(step != 0)
+                def _():
+                    self.pull(kind, line, step).wait_recv()
+
+                @pl.when(step == 0)
+                def _():
+                    self.keep(kind).wait()
+
+        @pl.when(jnp.logical_not(self.owner))
+        def _():
+            remote(self.outs[3], self.outs[3], self.y_sr.at[0], self.y_sr.at[1], self.me).wait_recv()
+            for i in range(3):
+                self.over(i).wait_send()
+
+        @pl.when(self.owner)
+        def _():
+            self.out_keep().wait()
+            self.out_move().wait_send()
+            for step in range(1, 8):
+                self.push(0, step).wait_send()
+            for kind in (1, 2):
+
+                @pl.when(self.z % 2 == kind - 1)
+                def _():
+                    for step in range(1, 8):
+                        self.push(kind, step).wait_send()
+
+        for i in range(3):
+            self.share(i).wait_send()
+
+
+def reduce_heads_kernel(
+    parts_in, query_in, side_in, out_in, out, query, key, value, outw, parts, in_sem, *refs
+):
+    reduce_refs, head_refs = split_refs(refs, (9, 18))
+    load = pltpu.make_async_copy(parts_in, parts, in_sem)
+    load.start()
+    heads = HeadGrads((query_in, side_in, out_in), (query, key, value, outw), head_refs)
+    heads.start_loads()
+    greet_all(16, 2)
+    reduce = Reduce(parts, reduce_refs)
+    load.wait()
+    for place_at in range(4):
+        reduce.start(place_at)
+    heads.start()
+    heads.relay()
+    reduce.relay(0)
+    reduce.relay(1)
+    heads.scatter()
+    reduce.relay(2)
+    reduce.total(out)
+    heads.finish()
+    reduce.finish()
+
+
+def reduce_heads(parts, query, side, outw):
+    shape = parts.shape
+    depth = query.shape[2]
+    out_rows, width = outw.shape[2:]
+
+    def room(*dims):
+        return jax.ShapeDtypeStruct(dims, jnp.bfloat16)
+
+    return pl.pallas_call(
+        reduce_heads_kernel,
+        out_shape=(
+            jax.ShapeDtypeStruct(shape[1:], jnp.float32),
+            room(depth, 4 * HD), room(depth, 2 * HD), room(depth, 2 * HD), room(out_rows, width),
+        ),
+        in_specs=[ANY] * 4,
+        out_specs=(INSIDE, ANY, ANY, ANY, ANY),
+        scratch_shapes=[pltpu.VMEM(shape, jnp.bfloat16), dma()]
+        + Reduce.scratch(shape[2])
+        + HeadGrads.scratch(depth, out_rows, width),
         compiler_params=kernel_params(6),
-        name="reduce_weights",
-    )(gate, up, down, query, side, outw, gains)
+        name="reduce_heads",
+    )(parts, query, side, outw)
+
+
+def gains_kernel(gains, out, box, own, send_sems, recv_sems):
+    blk, h = lax.axis_index("blk"), lax.axis_index("head")
+    greet_all(16, 2)
+
+    def push(step):
+        other = (blk + step // 2) % 16
+        return remote(
+            gains.at[other], box.at[step], send_sems.at[step], recv_sems.at[step], (other, (h + step % 2) % 2)
+        )
+
+    keep = local(gains.at[blk], box.at[0], own.at[0])
+    keep.start()
+    for step in range(1, 32):
+        push(step).start()
+    keep.wait()
+    total = box[0]
+    for step in range(1, 32):
+        push(step).wait_recv()
+        total += box[step]
+    out[...] = total
+    for step in range(1, 32):
+        push(step).wait_send()
+
+
+def reduce_gains(gains):
+    return pl.pallas_call(
+        gains_kernel,
+        out_shape=jax.ShapeDtypeStruct(gains.shape[1:], gains.dtype),
+        in_specs=[INSIDE],
+        out_specs=INSIDE,
+        scratch_shapes=[pltpu.VMEM((32,) + gains.shape[1:], gains.dtype), dma(1), dma(32), dma(32)],
+        compiler_params=kernel_params(12),
+        name="reduce_gains",
+    )(gains)
 
 
 def fast_body(
@@ -1516,17 +1962,10 @@
             jnp.zeros((2, rows), f32),
         ]
     )
-    tokens_all, cot_all, notes, qkv_w, out_w, gate_w, up_w, down_w = spread(
-        tokens, cotangent, note, w_query, w_key, w_value, w_out, w_gate, w_up, w_down
-    )
+    tokens_all, notes, qkv_w, out_w = spread(tokens, note, w_query, w_key, w_value, w_out)
     tokens_all = tokens_all.reshape(token_rows, width)
-    cot_all = cot_all.reshape(token_rows, width)
     qkv_w = qkv_w.reshape(width, 3 * HD)
     out_w = out_w.reshape(HD, width)
-    hidden_part = gate_w.shape[3]
-    gate_w = gate_w.reshape(width, hidden_part)
-    up_w = up_w.reshape(width, hidden_part)
-    down_w = down_w.reshape(hidden_part, width)
     gain_attn = notes[:, 4].reshape(1, width)
     gain_mlp = notes[:, 5].reshape(1, width)
     mine = lax.dynamic_index_in_dim(notes.reshape(8, 2, 8, rows), core, 1, False)
@@ -1534,6 +1973,7 @@
     ids_mine = lax.dynamic_index_in_dim(mine[:, 2:4], half, 1, False).reshape(token_rows)
     key_ids = notes[:, 2:4].reshape(32 * rows)
 
+    score_scale = HD ** (-0.5)
     inputs_all = tokens_all.astype(f32)
     normed = (inputs_all * rms_scale(inputs_all) * gain_attn).astype(bf16)
     cos_table, sine_table = rope_tables(positions_mine)
@@ -1542,25 +1982,31 @@
     query = rotate(projected[:, :HD], cos_table, sine_table).astype(bf16)
     key = rotate(projected[:, HD : 2 * HD], cos_table, sine_table).astype(bf16)
     value = projected[:, 2 * HD :].astype(bf16)
-    keys_values = gather_keys(jnp.concatenate([key, value], axis=1).reshape(8, rows, 2 * HD))
-    keys_values = keys_values.reshape(32 * rows, 2 * HD)
-    keys, values = keys_values[:, :HD], keys_values[:, HD:]
-    score_scale = HD ** (-0.5)
-    visible = key_ids[None, :] <= ids_mine[:, None]
-    scores = jnp.where(visible, times_transposed(query, keys) * score_scale, -1e30)
-    row_max = jnp.max(scores, axis=-1, keepdims=True)
-    weights = jnp.exp(scores - row_max)
-    log_total = row_max + jnp.log(jnp.sum(weights, axis=-1, keepdims=True))
-    probabilities = jnp.exp(scores - log_total)
-    attended = product(probabilities.astype(bf16), values)
-    attended_low = attended.astype(bf16)
-    branch = reduce_plane(product(attended_low, out_w).astype(bf16).reshape(8, rows, width))
+    scaled_query = (query.astype(f32) * score_scale).astype(bf16)
+    keys_values, attended, attended_low, log_total, cot_all, gate_w, up_w = attend_keys(
+        scaled_query,
+        jnp.concatenate([key, value], axis=1).reshape(8, rows, 2 * HD),
+        ids_mine[:, None],
+        key_ids.reshape(8, 1, 4 * rows),
+        cotangent,
+        w_gate,
+        w_up,
+    )
+    cot_all = cot_all.reshape(token_rows, width)
+    branch, gate_w, up_w = reduce_share(
+        product(attended_low, out_w).astype(bf16).reshape(8, rows, width), gate_w, up_w
+    )
+    hidden_part = gate_w.shape[3]
+    gate_w = gate_w.reshape(width, hidden_part)
+    up_w = up_w.reshape(width, hidden_part)
 
     inputs = tokens.astype(f32)
     inv_attn = rms_scale(inputs)
     hidden = inputs + branch
     inv_mlp = rms_scale(hidden)
-    normed_mlp = gather_plane((hidden * inv_mlp * gain_mlp).astype(bf16)).reshape(token_rows, width)
+    normed_mlp, down_w = gather_share((hidden * inv_mlp * gain_mlp).astype(bf16), w_down)
+    normed_mlp = normed_mlp.reshape(token_rows, width)
+    down_w = down_w.reshape(hidden_part, width)
     gate_pre = product(normed_mlp, gate_w)
     up_pre = product(normed_mlp, up_w)
     sigmoid_gate = jax.nn.sigmoid(gate_pre)
@@ -1573,27 +2019,38 @@
     ).astype(bf16)
     grad_up = (grad_active * gate_pre * sigmoid_gate).astype(bf16)
     grad_normed_part = times_transposed(grad_gate, gate_w) + times_transposed(grad_up, up_w)
-    grad_normed_mlp = reduce_plane(grad_normed_part.astype(bf16).reshape(8, rows, width))
-    grad_gate_w = transposed_times(normed_mlp, grad_gate)
-    grad_up_w = transposed_times(normed_mlp, grad_up)
-    grad_down_w = transposed_times(active, cot_all)
+    depth = w_query.shape[0]
+    grad_normed_mlp, gate_quarter, up_quarter = reduce_grads(
+        grad_normed_part.astype(bf16).reshape(8, rows, width),
+        transposed_times(normed_mlp, grad_gate).astype(bf16).reshape(8, 2, depth, hidden_part),
+        transposed_times(normed_mlp, grad_up).astype(bf16).reshape(8, 2, depth, hidden_part),
+    )
+    grad_down_w = transposed_times(active, cot_all).astype(bf16)
     grad_hidden_norm, gain_mlp_term = norm_backward(grad_normed_mlp, hidden, inv_mlp, gain_mlp)
     grad_hidden = cotangent.astype(f32) + grad_hidden_norm
 
-    grad_branch = gather_plane(grad_hidden.astype(bf16)).reshape(token_rows, width)
+    grad_branch, down_grad = gather_grads(
+        grad_hidden.astype(bf16), grad_down_w.reshape(2, 2, w_down.shape[0], width)
+    )
+    grad_branch = grad_branch.reshape(token_rows, width)
     grad_out_w = transposed_times(attended_low, grad_branch)
     grad_attended = times_transposed(grad_branch, out_w).astype(bf16)
-    delta = jnp.sum(grad_attended.astype(f32) * attended, axis=-1, keepdims=True)
-    grad_probs = times_transposed(grad_attended, values)
-    grad_scores = (probabilities * (grad_probs - delta)).astype(bf16)
-    grad_query_rot = product(grad_scores, keys) * score_scale
-    grad_key_rot = transposed_times(grad_scores, query) * score_scale
-    grad_value_part = transposed_times(probabilities.astype(bf16), grad_attended)
-    side = reduce_keys(
-        jnp.concatenate([grad_key_rot, grad_value_part], axis=1)
-        .astype(bf16)
-        .reshape(8, 2, 2, rows, 2 * HD)
-    ).reshape(token_rows, HD)
+    delta = jnp.sum(grad_attended.astype(f32) * attended, axis=-1)
+    keys_turned = jnp.swapaxes(keys_values[..., :HD].reshape(8, 4 * rows, HD), 1, 2)
+    side, grad_query_rot, gate_grad, up_grad = attend_back(
+        scaled_query,
+        grad_attended,
+        keys_values,
+        keys_turned,
+        log_total.reshape(LINE, 1, token_rows // LINE),
+        delta.reshape(LINE, 1, token_rows // LINE),
+        ids_mine.reshape(LINE, 1, token_rows // LINE),
+        key_ids.reshape(8, 4 * rows, 1),
+        gate_quarter,
+        up_quarter,
+    )
+    side = side.reshape(token_rows, HD)
+    grad_query_rot = jnp.swapaxes(grad_query_rot, 1, 2).reshape(token_rows, HD) * score_scale
     is_key = z % 2 == 0
     side_grad = jnp.where(is_key, rotate(side, cos_table, -sine_table), side).astype(bf16)
     grad_query = rotate(grad_query_rot, cos_table, -sine_table).astype(bf16)
@@ -1601,9 +2058,12 @@
     grad_normed_part = times_transposed(grad_query, qkv_w[:, :HD]) + times_transposed(
         side_grad, side_w
     )
-    grad_normed = reduce_plane(grad_normed_part.astype(bf16).reshape(8, rows, width))
-    grad_query_w = transposed_times(normed, grad_query)
-    grad_side_w = transposed_times(normed, side_grad)
+    grad_normed, query_grad, key_grad, value_grad, out_grad = reduce_heads(
+        grad_normed_part.astype(bf16).reshape(8, rows, width),
+        transposed_times(normed, grad_query).astype(bf16).reshape(8, 2, depth, HD),
+        transposed_times(normed, side_grad).astype(bf16).reshape(8, 2, depth, HD),
+        grad_out_w.astype(bf16).reshape(2, 2, w_out.shape[0], width),
+    )
     grad_inputs_norm, gain_attn_term = norm_backward(grad_normed, inputs, inv_attn, gain_attn)
     tokens_grad = (grad_hidden + grad_inputs_norm).astype(bf16)
 
@@ -1615,16 +2075,7 @@
         ],
         axis=1,
     )
-    depth = w_query.shape[0]
-    gate_grad, up_grad, down_grad, query_grad, key_grad, value_grad, out_grad, gain_grads = reduce_weights(
-        grad_gate_w.astype(bf16).reshape(8, 2, depth, hidden_part),
-        grad_up_w.astype(bf16).reshape(8, 2, depth, hidden_part),
-        grad_down_w.astype(bf16).reshape(2, 2, w_down.shape[0], width),
-        grad_query_w.astype(bf16).reshape(8, 2, depth, HD),
-        grad_side_w.astype(bf16).reshape(8, 2, depth, HD),
-        grad_out_w.astype(bf16).reshape(2, 2, w_out.shape[0], width),
-        gains,
-    )
+    gain_grads = reduce_gains(gains)
     return (
         output,
         tokens_grad,

time: 877 us -> 777 us (0.89)
  Pallas kernels: 675 us -> 583 us
  local copies, waits for them, and re-layouts: 12.4 us -> 31 us
  matrix products: 122 us -> 108 us
  other arithmetic: 57.7 us -> 44 us
    pallas_call x4 -> x1, Pallas kernels: 210 us -> 52 us  [reduce_plane(): pl.pallas_call(reduce_kernel, out_shape=jax.ShapeDtypeStruct(shape[1:], j...]
    pallas_call x6 -> x9, Pallas kernels: 465 us -> 531 us  [the longest x1 98.3 us: attend_keys(): pl.pallas_call(attend_kernel, out_shape=(shape(eight, 2, 2, rows, width),...]
    dot_general x8 -> x6, matrix products: 42.3 us -> 27.8 us  [transposed_times(): lax.dot_general(left, right, (((0,), (0,)), ((), ())), preferred_element_...]
    dot_general x7 -> x5, matrix products: 31.8 us -> 33.6 us  [product(): return jnp.dot(left, right, preferred_element_type=jnp.float32)]
    dot_general x8 -> x6, matrix products: 47.8 us -> 46.4 us  [times_transposed(): lax.dot_general(left, right, (((1,), (1,)), ((), ())), preferred_element_...]
where the time goes in v2:
time: 777 us; the launch traced here: 767 us
  Pallas kernels  583 us (75%)
  matrix products  108 us (14%)
  other arithmetic  44 us (6%)
  local copies, waits for them, and re-layouts  31 us (4%)
    pallas_call x1, Pallas kernels, attend_keys(): pl.pallas_call(attend_kernel, out_shape=(shape(eight, 2, 2, rows, width),...  98.3 us
    pallas_call x1, Pallas kernels, spread(): pl.pallas_call(spread_kernel, out_shape=(shape(8, rows, width), jax.Shape...  86.1 us
    pallas_call x1, Pallas kernels, reduce_heads(): pl.pallas_call(reduce_heads_kernel, out_shape=(jax.ShapeDtypeStruct(shape...  69.7 us
    pallas_call x1, Pallas kernels, reduce_share(): pl.pallas_call(reduce_share_kernel, out_shape=(jax.ShapeDtypeStruct(shape...  58.5 us
    pallas_call x1, Pallas kernels, attend_back(): pl.pallas_call(attend_back_kernel, out_shape=(shape(eight, rows, HD, dtyp...  56.2 us
    pallas_call x1, Pallas kernels, reduce_grads(): pl.pallas_call(reduce_grads_kernel, out_shape=(jax.ShapeDtypeStruct(shape...  55.5 us
    pallas_call x1, Pallas kernels, reduce_plane(): pl.pallas_call(reduce_kernel, out_shape=jax.ShapeDtypeStruct(shape[1:], j...  52 us
    pallas_call x1, Pallas kernels, gather_grads(): pl.pallas_call(gather_grads_kernel, out_shape=(jax.ShapeDtypeStruct((2 *...  49.7 us

profile of v2, /device:TPU:8, one launch (start us, length us, event | category | flops | bytes accessed | tf_op | source)
XLA Modules:
  0.0 767.1 jit_solution(15824775009681062442)
XLA Ops:
  2.6 86.1 %spread.1 = (bf16[8,128,2048]{2,1,0:T(8,128)(2,1)}, f32[16,8,128]{2,1,0:T(8,128)}, bf16[8,2,128,768]{3,2,1,0:T(8,128)(2,1)}, bf16[2,2,64,2048]{3,2,1,0:T(8,128)(2,1)}) custom-call(bf16[128,2048]{1,0:T(8,128)(2,1)} %tokens.1, f32[8,128]{1,0:T(8,128)} %concatenate.30.note, bf16[128,1024]{1,0:T(8,128)(2,1)} %wq.1, bf16[128,512]{1,0:T(8,128)(2,1)} %wk.1, ...), custom_call_target="tpu_custom_call" | custom-call | tf_op jit(solution)/shard_map/spread/pallas_call | solution.py:1116
  89.8 3.3 multiply_reduce_fusion
  95.1 3.6 fusion.63
  100.1 2.0 copy.57
  102.1 2.0 copy.56
  104.2 2.0 copy.54
  106.2 2.0 copy.55
  108.3 4.7 fusion.47
  120.1 98.3 %attend_keys.1 = (bf16[8,2,2,128,512]{4,3,2,1,0:T(8,128)(2,1)}, f32[1024,256]{1,0:T(8,128)}, bf16[1024,256]{1,0:T(8,128)(2,1)}, f32[1024,1]{1,0:T(8,128)}, bf16[...) custom-call(bf16[1024,256]{1,0:T(8,128)(2,1)} %multiply_convert_fusion.5.query, ...), custom_call_target="tpu_custom_call" | custom-call | tf_op jit(solution)/shard_map/attend_keys/pallas_call | solution.py:1306
  218.4 4.3 convolution_convert_fusion
  222.7 58.5 %reduce_share.1 = (f32[128,2048]{1,0:T(8,128)}, bf16[8,2,128,1024]{3,2,1,0:T(8,128)(2,1)}, bf16[8,2,128,1024]{3,2,1,0:T(8,128)(2,1)}) custom-call(bf16[8,128,2048]{2,1,0:T(8,128)(2,1)} %bitcast.97, bf16[8,128,512]{2,1,0:T(8,128)(2,1)} %get-tuple-element.46.gate_in, bf16[8,128,512]{2,1,0:T(8,128)(2,1)} %get-tuple-element.47.up_in), custom_call_target="tpu_custom_call" | custom-call | tf_op jit(solution)/shard_map/reduce_share/pallas_call | solution.py:1158
  281.2 1.5 multiply_reduce_fusion.4
  283.7 46.6 %gather_share.1 = (bf16[8,128,2048]{2,1,0:T(8,128)(2,1)}, bf16[2,2,256,2048]{3,2,1,0:T(8,128)(2,1)}) custom-call(bf16[128,2048]{1,0:T(8,128)(2,1)} %multiply_convert_fusion.4.src, bf16[256,2048]{1,0:T(8,128)(2,1)} %wd.1), custom_call_target="tpu_custom_call" | custom-call | tf_op jit(solution)/shard_map/gather_share/pallas_call | solution.py:1186
  330.3 10.1 %fusion.64 = f32[1024,1024]{1,0:T(8,128)} fusion(bf16[1024,2048]{1,0:T(8,128)(2,1)} %bitcast.148, bf16[2048,1024]{1,0:T(8,128)(2,1)} %bitcast.146), kind=kOutput, calls=%fused_computation.117 | convolution fusion | flops 4294967296 | bytes 12582912 | tf_op jit(solution)/shard_map/dot_general | solution.py:39
  340.4 6.3 fusion.65
  346.7 10.0 %multiply_convert_fusion.1 = (bf16[1024,1024]{1,0:T(8,128)(2,1)}, bf16[1024,1024]{1,0:T(8,128)(2,1)S(1)}, bf16[1024,1024]{1,0:T(8,128)(2,1)}) fusion(f32[1024,1024]{1,0:T(8,128)} %fusion.64, f32[1024,1024]{1,0:T(8,128)} %fusion.65, bf16[1024,2048]{1,0:T(8,128)(2,1)S(1)} %bitcast.142, bf16[1024,2048]{1,0:T(8,128)(2,1)S(1)} %bitcast.139), kind=kOutput, calls=%fused_computation.7 | convolution fusion | flops 4311744512 | bytes 23068672 | tf_op jit(solution)/shard_map/dot_general | solution.py:43
  356.7 9.1 %fusion.66 = f32[1024,2048]{1,0:T(8,128)} fusion(bf16[1024,1024]{1,0:T(8,128)(2,1)S(1)} %get-tuple-element.78, bf16[2048,1024]{1,0:T(8,128)(2,1)} %bitcast.147), kind=kOutput, calls=%fused_computation.119 | convolution fusion | flops 4294967296 | bytes 14680064 | tf_op jit(solution)/shard_map/dot_general | solution.py:43
  365.8 8.6 %add_convert_fusion.1 = bf16[1024,2048]{1,0:T(8,128)(2,1)} fusion(f32[1024,2048]{1,0:T(8,128)} %fusion.66, bf16[1024,1024]{1,0:T(8,128)(2,1)S(1)} %copy-done.35, bf16[2048,1024]{1,0:T(8,128)(2,1)S(1)} %bitcast.145), kind=kOutput, calls=%fused_computation.4 | convolution fusion | flops 4299161600 | bytes 18874368 | tf_op jit(solution)/shard_map/dot_general | solution.py:43
  374.4 6.2 convolution_convert_fusion.3
  380.6 6.7 convolution_convert_fusion.2
  387.3 55.5 %reduce_grads.1 = (f32[128,2048]{1,0:T(8,128)}, bf16[8,128,512]{2,1,0:T(8,128)(2,1)}, bf16[8,128,512]{2,1,0:T(8,128)(2,1)}) custom-call(bf16[8,128,2048]{2,1,0:T(8,128)(2,1)} %bitcast.101, bf16[8,2,128,1024]{3,2,1,0:T(8,128)(2,1)} %bitcast.102, bf16[8,2,128,1024]{3,2,1,0:T(8,128)(2,1)} %bitcast.103), custom_call_target="tpu_custom_call" | custom-call | tf_op jit(solution)/shard_map/reduce_grads/pallas_call | solution.py:1529
  442.8 2.3 multiply_reduce_fusion.1
  445.2 2.3 fusion.59.src
  447.5 7.9 %convolution_convert_fusion.1 = bf16[1024,2048]{1,0:T(8,128)(2,1)} fusion(bf16[1024,1024]{1,0:T(8,128)(2,1)} %get-tuple-element.79, bf16[1024,2048]{1,0:T(8,128)(2,1)S(1)} %bitcast.143), kind=kOutput, calls=%fused_computation.12 | convolution fusion | flops 4297064448 | bytes 10485760 | tf_op jit(solution)/shard_map/dot_general | solution.py:49
  455.4 49.7 %gather_grads.1 = (bf16[8,128,2048]{2,1,0:T(8,128)(2,1)}, f32[256,2048]{1,0:T(8,128)}) custom-call(bf16[128,2048]{1,0:T(8,128)(2,1)} %fusion.59.src, bf16[2,2,256,2048]{3,2,1,0:T(8,128)(2,1)} %bitcast.105), custom_call_target="tpu_custom_call" | custom-call | tf_op jit(solution)/shard_map/gather_grads/pallas_call | solution.py:1563
  505.1 5.3 multiply_reduce_fusion.2
  512.0 4.1 copy.53
  516.8 3.3 reshape_reshape.12.key_column
  520.1 56.2 %attend_back.1 = (f32[8,128,256]{2,1,0:T(8,128)}, f32[4,256,256]{2,1,0:T(8,128)}, bf16[128,4096]{1,0:T(8,128)(2,1)}, bf16[128,4096]{1,0:T(8,128)(2,1)}) custom-call(bf16[1024,256]{1,0:T(8,128)(2,1)} %multiply_convert_fusion.5.query, bf16[1024,256]{1,0:T(8,128)(2,1)} %get-tuple-element.106.grad_out, bf16[8,2,2,128,512]{4,3,2,1,0:T(8,128)(2,1)} %get-tuple-element.56.keys_in, ...), custom_call_target="tpu_custom_call" | custom-call | tf_op jit(solution)/shard_map/attend_back/pallas_call | solution.py:1679
  576.4 2.3 multiply_bitcast_fusion
  578.7 1.6 copy.49
  580.2 2.4 fusion.37
  583.3 5.9 fusion.14
  589.2 2.6 fusion.40
  591.8 7.5 add_convert_fusion
  600.4 2.4 convolution_convert_fusion.6
  602.7 2.4 fusion.2
  605.1 2.3 convolution_convert_fusion.5
  607.4 69.7 %reduce_heads.1 = (f32[128,2048]{1,0:T(8,128)}, bf16[128,1024]{1,0:T(8,128)(2,1)}, bf16[128,512]{1,0:T(8,128)(2,1)}, bf16[128,512]{1,0:T(8,128)(2,1)}, bf16[64,2048]{1,0:T(8,128)(2,1)}) custom-call(bf16[8,128,2048]{2,1,0:T(8,128)(2,1)} %bitcast.98, bf16[8,2,128,256]{3,2,1,0:T(8,128)(2,1)} %bitcast.116, bf16[8,2,128,256]{3,2,1,0:T(8,128)(2,1)} %bitcast.117, ...), custom_call_target="tpu_custom_call" | custom-call | tf_op jit(solution)/shard_map/reduce_heads/pallas_call | solution.py:1881
  677.2 2.2 fusion.11
  679.4 9.3 %convolution_convert_fusion.4 = bf16[1024,2048]{1,0:T(8,128)(2,1)} fusion(bf16[1024,1024]{1,0:T(8,128)(2,1)} %get-tuple-element.79, bf16[1024,2048]{1,0:T(8,128)(2,1)} %bitcast.138), kind=kOutput, calls=%fused_computation.15 | convolution fusion | flops 4297064448 | bytes 10485760 | tf_op jit(solution)/shard_map/dot_general | solution.py:39
  688.7 52.0 %reduce_plane.1 = f32[128,2048]{1,0:T(8,128)} custom-call(bf16[8,128,2048]{2,1,0:T(8,128)(2,1)} %bitcast.104), custom_call_target="tpu_custom_call" | custom-call | tf_op jit(solution)/shard_map/reduce_plane/pallas_call | solution.py:725
  740.7 3.0 fusion.10
  744.6 10.0 %reduce_gains.1 = f32[8,128]{1,0:T(8,128)} custom-call(f32[16,8,128]{2,1,0:T(8,128)} %maximum_maximum_fusion.gains), custom_call_target="tpu_custom_call" | custom-call | tf_op jit(solution)/shard_map/reduce_gains/pallas_call | solution.py:1922
  755.9 1.9 convert_element_type.158
  757.8 1.6 convert_element_type.159
  761.0 2.8 convert_element_type.162
  763.8 1.5 convert_element_type.163
  (109 shorter events, 23.4 us)
Async XLA Ops:
  88.8 4.4 copy-start
  93.2 1.9 copy-start.10
  94.2 4.5 copy-start.6
  98.7 5.4 copy-start.20
  117.1 101.3 %copy-start.15 = (bf16[2,2,64,2048]{3,2,1,0:T(8,128)(2,1)S(1)}, bf16[2,2,64,2048]{3,2,1,0:T(8,128)(2,1)}, u32[]{:S(2)}) copy-start(bf16[2,2,64,2048]{3,2,1,0:T(8,128)(2,1)} %get-tuple-element.45) | copy-start | bytes 3145732
  118.4 104.3 %copy-start.21 = (f32[8,1,128]{2,0,1:T(8,128)}, f32[8,1,128]{2,0,1:T(8,128)S(1)}, u32[]{:S(2)}) copy-start(f32[8,1,128]{2,0,1:T(8,128)S(1)} %constant_dynamic-slice_fusion) | copy-start | bytes 12292
  222.7 58.5 %copy-start.4 = (bf16[128,2048]{1,0:T(8,128)(2,1)S(1)}, bf16[128,2048]{1,0:T(8,128)(2,1)}, u32[]{:S(2)}) copy-start(bf16[128,2048]{1,0:T(8,128)(2,1)} %tokens.1) | copy-start | bytes 1572868
  282.7 162.4 %copy-start.24 = (f32[128]{0:T(128)}, f32[128]{0:T(128)S(1)}, u32[]{:S(2)}) copy-start(f32[128]{0:T(128)S(1)} %add_rsqrt_fusion.2) | copy-start | bytes 1540
  330.3 10.1 %copy-start.32 = (bf16[8,2,128,1024]{3,2,1,0:T(8,128)(2,1)S(1)}, bf16[8,2,128,1024]{3,2,1,0:T(8,128)(2,1)}, u32[]{:S(2)}) copy-start(bf16[8,2,128,1024]{3,2,1,0:T(8,128)(2,1)} %get-tuple-element.51) | copy-start | bytes 12582916
  330.3 10.1 %copy-start.33 = (bf16[8,128,2048]{2,1,0:T(8,128)(2,1)S(1)}, bf16[8,128,2048]{2,1,0:T(8,128)(2,1)}, u32[]{:S(2)}) copy-start(bf16[8,128,2048]{2,1,0:T(8,128)(2,1)} %get-tuple-element.49) | copy-start | bytes 12582916
  340.4 6.3 copy-start.28
  340.4 6.3 copy-start.30
  356.7 9.1 %copy-start.35 = (bf16[1024,1024]{1,0:T(8,128)(2,1)S(1)}, bf16[1024,1024]{1,0:T(8,128)(2,1)}, u32[]{:S(2)}) copy-start(bf16[1024,1024]{1,0:T(8,128)(2,1)} %get-tuple-element.77) | copy-start | bytes 6291460
  365.8 8.6 %copy-start.34 = (bf16[8,128,2048]{2,1,0:T(8,128)(2,1)S(1)}, bf16[8,128,2048]{2,1,0:T(8,128)(2,1)}, u32[]{:S(2)}) copy-start(bf16[8,128,2048]{2,1,0:T(8,128)(2,1)} %get-tuple-element.49) | copy-start | bytes 12582916
  387.3 57.9 %copy-start.5 = (bf16[128,2048]{1,0:T(8,128)(2,1)S(1)}, bf16[128,2048]{1,0:T(8,128)(2,1)}, u32[]{:S(2)}) copy-start(bf16[128,2048]{1,0:T(8,128)(2,1)} %cot.1) | copy-start | bytes 1572868
  442.8 4.7 copy-start.31
  445.2 10.2 %copy-start.26 = (f32[128]{0:T(128)}, f32[128]{0:T(128)S(1)}, u32[]{:S(2)}) copy-start(f32[128]{0:T(128)S(1)} %broadcast_multiply_fusion.1) | copy-start | bytes 1540
  505.1 5.3 copy-start.2
  510.5 5.6 copy-start.16
  510.5 6.4 copy-start.18
  582.6 0.7 copy-start.13
  583.3 5.9 copy-start.8
  591.8 7.6 copy-start.1
  599.3 1.0 copy-start.14
  600.4 2.4 copy-start.7
  602.7 2.4 copy-start.11
  602.7 2.4 copy-start.29
  688.6 52.0 %copy-start.3 = (f32[128,2048]{1,0:T(8,128)S(1)}, f32[128,2048]{1,0:T(8,128)}, u32[]{:S(2)}) copy-start(f32[128,2048]{1,0:T(8,128)} %get-tuple-element.54) | copy-start | bytes 3145732
  688.6 52.0 %copy-start.25 = (f32[128]{0:T(128)S(1)}, f32[128]{0:T(128)}, u32[]{:S(2)}) copy-start(f32[128]{0:T(128)} %copy-done.24) | copy-start | bytes 1540
  688.7 52.0 %copy-start.27 = (f32[128]{0:T(128)S(1)}, f32[128]{0:T(128)}, u32[]{:S(2)}) copy-start(f32[128]{0:T(128)} %copy-done.26) | copy-start | bytes 1540
  740.7 3.2 copy-start.22
  740.7 3.2 copy-start.23
  740.7 18.7 %copy-start.19 = (bf16[128,512]{1,0:T(8,128)(2,1)S(1)}, bf16[128,512]{1,0:T(8,128)(2,1)}, u32[]{:S(2)}) copy-start(bf16[128,512]{1,0:T(8,128)(2,1)} %get-tuple-element.66) | copy-start | bytes 393220
  740.7 19.5 %copy-start.17 = (bf16[64,2048]{1,0:T(8,128)(2,1)S(1)}, bf16[64,2048]{1,0:T(8,128)(2,1)}, u32[]{:S(2)}) copy-start(bf16[64,2048]{1,0:T(8,128)(2,1)} %get-tuple-element.67) | copy-start | bytes 786436
  743.8 20.0 %copy-start.12 = (bf16[128,4096]{1,0:T(8,128)(2,1)S(1)}, bf16[128,4096]{1,0:T(8,128)(2,1)}, u32[]{:S(2)}) copy-start(bf16[128,4096]{1,0:T(8,128)(2,1)} %get-tuple-element.69) | copy-start | bytes 3145732
  755.9 9.4 %copy-start.9 = (f32[256,2048]{1,0:T(8,128)S(1)}, f32[256,2048]{1,0:T(8,128)}, u32[]{:S(2)}) copy-start(f32[256,2048]{1,0:T(8,128)} %get-tuple-element.132) | copy-start | bytes 6291460

commit v3 on v2

--- a/solution.py
+++ b/solution.py
@@ -539,6 +539,10 @@
         for line in range(LINE):
             for elem in (0, 1):
                 self.across(line, elem).wait_send()
+        self.finish_sends()
+        self.own_copy().wait()
+
+    def finish_sends(self):
         self.across_b().wait_send()
         for step in range(LINE - 1):
             for elem in range(4):
@@ -550,8 +554,6 @@
                 @pl.when(jnp.logical_and(self.z > 0, self.z + step <= LINE - 1))
                 def _():
                     self.down(step, elem).wait_send()
-
-        self.own_copy().wait()
 
 
 def gather_kernel(src, out, *sems):
@@ -846,31 +848,33 @@
         def _():
             self.out_push().start()
 
-    def relay(self):
+    def relay(self, step):
         @pl.when(self.owner)
         def _():
-            for step in range(LINE):
-                for kind in range(3):
-                    if step:
-                        self.pull(kind, self.near(step)).wait_recv()
-                    else:
-                        self.keep(kind).wait()
-                self.over(step).start()
+            for kind in range(3):
+                if step:
+                    self.pull(kind, self.near(step)).wait_recv()
+                else:
+                    self.keep(kind).wait()
+            self.over(step).start()
+
+    def relay_out(self):
+        @pl.when(self.owner)
+        def _():
             self.out_keep().wait()
             self.out_pull().wait_recv()
             self.out_over().start()
 
-    def relay_share(self):
-        for step in range(LINE):
-
-            @pl.when(jnp.logical_not(self.owner))
-            def _():
-                self.over(step).wait_recv()
-
-            for kind in range(3):
-                self.pull(kind, self.far(step)).wait_recv()
-            self.share((self.z + LINE - step) % LINE, self.c).start()
-
+    def relay_share(self, step):
+        @pl.when(jnp.logical_not(self.owner))
+        def _():
+            self.over(step).wait_recv()
+
+        for kind in range(3):
+            self.pull(kind, self.far(step)).wait_recv()
+        self.share((self.z + LINE - step) % LINE, self.c).start()
+
+    def relay_out_share(self):
         @pl.when(jnp.logical_not(self.owner))
         def _():
             self.out_over().wait_recv()
@@ -1084,129 +1088,244 @@
     return groups
 
 
-def spread_kernel(tokens, note, wq, wk, wv, wo, tok_out, note_out, qkv, out_w, *sems):
-    tok_sems, note_sems, attn_sems = split_refs(sems, (8, 3, 10))
-    greet_all(16, 2)
-    tok = Gather(tokens, tok_out, tok_sems)
-    notes = NoteSpread(note, note_out, note_sems)
-    attn = AttnSpread((wq, wk, wv, wo), (qkv, out_w), attn_sems)
-    attn.start()
-    tok.start()
-    notes.start()
-    tok.relay_b()
-    for elem in (2, 0, 1, 3):
-        tok.relay(0, elem)
-    attn.relay()
-    for elem in (2, 0, 1, 3):
-        tok.relay(1, elem)
-    attn.relay_share()
-    for elem in (2, 0, 1, 3):
-        tok.relay(2, elem)
-    notes.finish()
-    attn.finish()
-    tok.finish()
-
-
-def spread(tokens, note, wq, wk, wv, wo):
-    def shape(*dims):
-        return jax.ShapeDtypeStruct(dims, jnp.bfloat16)
-
-    rows, width = tokens.shape
-    depth = wq.shape[0]
-    return pl.pallas_call(
-        spread_kernel,
-        out_shape=(
-            shape(8, rows, width),
-            jax.ShapeDtypeStruct((16,) + note.shape, jnp.float32),
-            shape(8, 2, depth, 3 * HD),
-            shape(2, 2, wo.shape[0], width),
-        ),
-        in_specs=[INSIDE] * 6,
-        out_specs=(ANY,) * 4,
-        scratch_shapes=Gather.scratch() + NoteSpread.scratch() + AttnSpread.scratch(),
-        compiler_params=kernel_params(3),
-        name="spread",
-    )(tokens, note, wq, wk, wv, wo)
-
-
-def reduce_share_kernel(parts_in, gate_in, up_in, out, gate, up, parts, in_sem, *refs):
+def reduce_share_kernel(attended, out_w, gate_in, up_in, out, gate, up, parts, *refs):
     reduce_refs, share_sems = split_refs(refs, (9, 5))
-    load = pltpu.make_async_copy(parts_in, parts, in_sem)
-    load.start()
     z, y, c, h = place()
     greet(device(z, y, 1 - c, h))
     greet(device(z, y, c, 1 - h))
     greet_plane(2)
     reduce = Reduce(parts, reduce_refs)
     share = MlpShare((gate_in, up_in), (gate, up), share_sems)
+    rows, width = parts.shape[1:]
     share.start()
-    load.wait()
     for place_at in range(4):
+        line = reduce.order[place_at]
+        both = attended[pl.ds(pl.multiple_of(line * 2 * rows, 2 * rows), 2 * rows)]
+        parts[pl.ds(line * 2, 2)] = product(both, out_w[...]).astype(jnp.bfloat16).reshape(2, rows, width)
         reduce.start(place_at)
     for place_at in range(3):
         reduce.relay(place_at)
     reduce.total(out)
+    share.relay()
     reduce.finish()
-    share.relay()
     share.finish()
 
 
-def reduce_share(parts, gate, up):
-    shape = parts.shape
+def reduce_share(attended, out_w, gate, up):
     eight, depth, part = gate.shape
+    shape = (eight, attended.shape[0] // eight, out_w.shape[1])
     full = jax.ShapeDtypeStruct((eight, 2, depth, 2 * part), gate.dtype)
     return pl.pallas_call(
         reduce_share_kernel,
         out_shape=(jax.ShapeDtypeStruct(shape[1:], jnp.float32), full, full),
-        in_specs=[ANY, INSIDE, INSIDE],
+        in_specs=[INSIDE] * 4,
         out_specs=(INSIDE, ANY, ANY),
-        scratch_shapes=[pltpu.VMEM(shape, jnp.bfloat16), dma()] + Reduce.scratch(shape[2]) + MlpShare.scratch(),
+        scratch_shapes=[pltpu.VMEM(shape, jnp.bfloat16)] + Reduce.scratch(shape[2]) + MlpShare.scratch(),
         compiler_params=kernel_params(7),
         name="reduce_share",
-    )(parts, gate, up)
-
-
-def gather_share_kernel(src, wd, out, down, *sems):
-    gather_sems, down_sems = split_refs(sems, (8, 3))
+    )(attended, out_w, gate, up)
+
+
+def mlp_kernel(
+    src, wd, gate_in, up_in, cot_in,
+    mlp_out, normed_out, active, grad_gate, grad_up, grad_out,
+    normed, gate_w, up_w, down_w, gate_pre, up_pre, cot, parts, load_s, out_s, *refs,
+):
+    gather_sems, down_sems, reduce_refs = split_refs(refs, (8, 3, 9))
+    loads = [
+        local(gate_in, gate_w, load_s.at[0]),
+        local(up_in, up_w, load_s.at[1]),
+        local(cot_in, cot, load_s.at[2]),
+    ]
+    for load in loads:
+        load.start()
     z, y, c, h = place()
     greet(device(z, y, 1 - c, h))
     greet(device(z, y, c, 1 - h))
     greet_plane(2)
-    gather = Gather(src, out, gather_sems)
-    downs = DownSpread(wd, down, down_sems)
+    gather = Gather(src, normed, gather_sems)
+    downs = DownSpread(wd, down_w, down_sems)
+    reduce = Reduce(parts, reduce_refs)
     gather.start()
     downs.start()
-    gather.relays()
+    rows, width = normed.shape[1:]
+    hidden = gate_w.shape[1]
+    step = hidden // 4
+    pair = 2 * rows
+
+    def forward(chip, own=False):
+        shard = src if own else normed.at[chip]
+
+        @pl.loop(0, 4)
+        def _(tile):
+            columns = pl.ds(pl.multiple_of(tile * step, step), step)
+            gate_part = product(shard[...], gate_w[:, columns])
+            up_part = product(shard[...], up_w[:, columns])
+            gate_pre[chip, :, columns] = gate_part
+            up_pre[chip, :, columns] = up_part
+            active[chip, :, columns] = (gate_part * jax.nn.sigmoid(gate_part) * up_part).astype(jnp.bfloat16)
+
+    def forward_own(distance):
+        @pl.when(z - distance >= 0)
+        def _():
+            forward((z - distance) * 2 + y)
+
+        @pl.when(z + distance <= LINE - 1)
+        def _():
+            forward((z + distance) * 2 + y)
+
+    def forward_other(distance):
+        def one(line):
+            for elem in (0, 1):
+                gather.across_in(line, elem).wait_recv()
+            forward(line * 2 + 1 - y)
+
+        if distance == 0:
+            one(z)
+        else:
+
+            @pl.when(z - distance >= 0)
+            def _():
+                one(z - distance)
+
+            @pl.when(z + distance <= LINE - 1)
+            def _():
+                one(z + distance)
+
+    def relay(distance):
+        for elem in (2, 0, 1, 3):
+            gather.relay(distance - 1, elem)
+
+    gather.relay_b()
+    loads[0].wait()
+    loads[1].wait()
+    forward(z * 2 + y, own=True)
+    relay(1)
+    forward_other(0)
+    forward_own(1)
+    relay(2)
+    forward_other(1)
+    forward_own(2)
+    relay(3)
     downs.relay()
-    gather.finish()
+    forward_other(2)
+    forward_own(3)
+    forward_other(3)
+    gather.own_copy().wait()
+    store = local(normed, normed_out, out_s)
+    store.start()
     downs.finish()
 
-
-def gather_share(rows, wd):
+    def contribute(line):
+        both = pl.ds(line * 2, 2)
+
+        @pl.loop(0, 4)
+        def _(tile):
+            columns = pl.ds(pl.multiple_of(tile * (width // 4), width // 4), width // 4)
+            part = product(
+                active[both].reshape(pair, hidden), down_w[:, :, :, columns].reshape(hidden, width // 4)
+            )
+            parts[both, :, columns] = part.astype(jnp.bfloat16).reshape(2, rows, width // 4)
+
+    for place_at in range(4):
+        contribute(reduce.order[place_at])
+        reduce.start(place_at)
+    loads[2].wait()
+
+    def backward(line):
+        both = pl.ds(line * 2, 2)
+
+        @pl.loop(0, 4)
+        def _(tile):
+            columns = pl.ds(pl.multiple_of(tile * step, step), step)
+            grad_active = times_transposed(cot[both].reshape(pair, width), down_w[tile // 2, tile % 2])
+            gate_part = gate_pre[both, :, columns].reshape(pair, step)
+            up_part = up_pre[both, :, columns].reshape(pair, step)
+            sigmoid = jax.nn.sigmoid(gate_part)
+            silu = gate_part * sigmoid
+            gate_grad = grad_active * up_part * sigmoid * (1.0 + gate_part * (1.0 - sigmoid))
+            grad_gate[both, :, columns] = gate_grad.astype(jnp.bfloat16).reshape(2, rows, step)
+            grad_up[both, :, columns] = (grad_active * silu).astype(jnp.bfloat16).reshape(2, rows, step)
+
+        @pl.loop(0, 4)
+        def _(tile):
+            columns = pl.ds(pl.multiple_of(tile * (width // 4), width // 4), width // 4)
+            part = times_transposed(grad_gate[both].reshape(pair, hidden), gate_w[columns])
+            part += times_transposed(grad_up[both].reshape(pair, hidden), up_w[columns])
+            grad_out[both, :, columns] = part.astype(jnp.bfloat16).reshape(2, rows, width // 4)
+
+    for place_at in range(3):
+        backward(place_at)
+        reduce.relay(place_at)
+    backward(3)
+    reduce.total(mlp_out)
+    reduce.finish()
+    store.wait()
+    for line in range(LINE):
+        for elem in (0, 1):
+            gather.across(line, elem).wait_send()
+    gather.finish_sends()
+
+
+def run_mlp(src, wd, gate_w, up_w, cot):
+    rows, width = src.shape
+    hidden = gate_w.shape[1]
+
+    def room(*dims, dtype=jnp.bfloat16):
+        return pltpu.VMEM(dims, dtype)
+
+    def shape(*dims, dtype=jnp.bfloat16):
+        return jax.ShapeDtypeStruct(dims, dtype)
+
     return pl.pallas_call(
-        gather_share_kernel,
+        mlp_kernel,
         out_shape=(
-            jax.ShapeDtypeStruct((2 * LINE,) + rows.shape, rows.dtype),
-            jax.ShapeDtypeStruct((2, 2) + wd.shape, wd.dtype),
+            shape(rows, width, dtype=jnp.float32),
+            shape(8, rows, width),
+            shape(8, rows, hidden),
+            shape(8, rows, hidden),
+            shape(8, rows, hidden),
+            shape(8, rows, width),
         ),
-        in_specs=[INSIDE] * 2,
-        out_specs=(ANY,) * 2,
-        scratch_shapes=Gather.scratch() + DownSpread.scratch(),
+        in_specs=[INSIDE, INSIDE, ANY, ANY, ANY],
+        out_specs=(INSIDE, ANY, INSIDE, INSIDE, INSIDE, INSIDE),
+        scratch_shapes=[
+            room(8, rows, width), room(width, hidden), room(width, hidden), room(2, 2, *wd.shape),
+            room(8, rows, hidden, dtype=jnp.float32), room(8, rows, hidden, dtype=jnp.float32),
+            room(8, rows, width), room(8, rows, width), dma(3), dma(),
+        ] + Gather.scratch() + DownSpread.scratch() + Reduce.scratch(width),
         compiler_params=kernel_params(8),
-        name="gather_share",
-    )(rows, wd)
-
-
-def attend_kernel(
-    query, kv, query_ids, key_ids, cot, wg, wu,
-    kv_out, attended_out, attended_low_out, log_out, cot_out, gate, up,
-    keys, scores, total, own, x_s, x_r, c_s, c_r, out_sem, *sems,
+        name="run_mlp",
+    )(src, wd, gate_w, up_w, cot)
+
+
+def column_of(row):
+    size = row.shape[1]
+    same = lax.broadcasted_iota(jnp.int32, (size, size), 0) == lax.broadcasted_iota(jnp.int32, (size, size), 1)
+    return jnp.sum(jnp.where(same, row, 0.0), axis=1, keepdims=True)
+
+
+def row_of(column):
+    size = column.shape[0]
+    same = lax.broadcasted_iota(jnp.int32, (size, size), 0) == lax.broadcasted_iota(jnp.int32, (size, size), 1)
+    return jnp.sum(jnp.where(same, column, 0.0), axis=0, keepdims=True)
+
+
+def front_kernel(
+    tokens, cot, note, inv_freqs, wq, wk, wv, wo, wg, wu,
+    kv_out, normed_out, qkv_out, out_w, notes, cos_table, sine_table, query, attended_out, attended_low_out,
+    log_out, cot_out, gate, up,
+    gathered, normed, qkv_w, gain, query_ids, key_ids, kv, keys, scores, total,
+    own, x_s, x_r, c_s, c_r, store_s, *sems,
 ):
     z, y, c, h = place()
-    cot_sems, mlp_sems = split_refs(sems, (8, 3))
+    tok_sems, note_sems, attn_sems, cot_sems, mlp_sems = split_refs(sems, (8, 3, 10, 8, 3))
     greet_all(16, 2)
-    rows, width = key_ids.shape[2], query.shape[1]
-    pair = query.shape[0] // LINE
+    rows, width = tokens.shape[0], HD
+    pair = 2 * rows
+    tok = Gather(tokens, gathered, tok_sems)
+    notices = NoteSpread(note, notes, note_sems)
+    attn = AttnSpread((wq, wk, wv, wo), (qkv_w, out_w), attn_sems)
     cots = Gather(cot, cot_out, cot_sems)
     mlp = MlpSpread((wg, wu), (gate, up), mlp_sems)
 
@@ -1222,11 +1341,48 @@
         ref = keys.at[pl.ds(cut * 2, 2), core]
         return remote(ref, ref, c_s.at[cut], c_r.at[cut], device(z, y, 1 - c, h))
 
-    for cut in range(LINE):
+    def tables():
+        for blk in range(16):
+            gain[:, pl.ds(blk * rows, rows)] = notes[blk, 4:5, :]
+        for chip in range(8):
+            part = pl.ds(chip * rows, rows)
+            mine = notes[2 * chip + c]
+            angles = column_of(jnp.where(h == 0, mine[0:1], mine[1:2])) * inv_freqs[...]
+            cos_table[part] = jnp.cos(angles)
+            sine_table[part] = jnp.sin(angles)
+            query_ids[part] = column_of(jnp.where(h == 0, mine[2:3], mine[3:4]))
+            for piece in range(4):
+                key_ids[chip, :, pl.ds(piece * rows, rows)] = notes[2 * chip + piece // 2, 2 + piece % 2 : 3 + piece % 2, :]
+
+    def project(cut):
+        part = pl.ds(cut * pair, pair)
+        inputs = gathered[pl.ds(cut * 2, 2)].reshape(pair, tokens.shape[1]).astype(jnp.float32)
+        rows_normed = (inputs * rms_scale(inputs) * gain[...]).astype(jnp.bfloat16)
+        normed[part] = rows_normed
+        cos_rows, sine_rows = cos_table[part], sine_table[part]
+
+        def turn(lower, upper):
+            return (
+                (lower * cos_rows - upper * sine_rows).astype(jnp.bfloat16),
+                (upper * cos_rows + lower * sine_rows).astype(jnp.bfloat16),
+            )
+
+        def weight(columns):
+            return qkv_w[:, :, :, columns].reshape(tokens.shape[1], columns.size)
+
+        half = width // 2
+        projected = product(rows_normed, weight(pl.ds(0, width)))
+        lower, upper = turn(projected[:, :half], projected[:, half:])
+        query[part, :half] = (lower.astype(jnp.float32) * HD**-0.5).astype(jnp.bfloat16)
+        query[part, half:] = (upper.astype(jnp.float32) * HD**-0.5).astype(jnp.bfloat16)
+        projected = product(rows_normed, weight(pl.ds(width, 2 * width)))
+        lower, upper = turn(projected[:, :half], projected[:, half:width])
+        both = pl.ds(cut * 2, 2)
+        kv[both, :, :half] = lower.reshape(2, rows, half)
+        kv[both, :, half:width] = upper.reshape(2, rows, half)
+        kv[both, :, width:] = projected[:, width:].astype(jnp.bfloat16).reshape(2, rows, width)
         over(cut, h).start()
         keep(cut).start()
-    mlp.start()
-    cots.start()
 
     def pass_on(cut):
         keep(cut).wait()
@@ -1239,11 +1395,11 @@
         ids = query_ids[part]
 
         def maxima(block, best):
-            key = keys[block, :, :, :, :width].reshape(rows, width)
+            key = keys[block, :, :, :, :width].reshape(4 * rows, width)
             part_scores = times_transposed(query[part], key)
             part_scores = jnp.where(key_ids[block] <= ids, part_scores, -1e30)
             scores[block] = part_scores
-            for lane in range(rows // 128):
+            for lane in range(4 * rows // 128):
                 best = jnp.maximum(best, part_scores[:, lane * 128 : lane * 128 + 128])
             return best
 
@@ -1253,9 +1409,9 @@
 
         def mix(block, sums):
             weights = jnp.exp(scores[block] - row_max)
-            value = keys[block, :, :, :, width:].reshape(rows, width)
+            value = keys[block, :, :, :, width:].reshape(4 * rows, width)
             total[...] += product(weights.astype(jnp.bfloat16), value)
-            for lane in range(rows // 128):
+            for lane in range(4 * rows // 128):
                 sums = sums + weights[:, lane * 128 : lane * 128 + 128]
             return sums
 
@@ -1264,66 +1420,124 @@
         mixed = total[...] / row_sum
         attended_out[part] = mixed
         attended_low_out[part] = mixed.astype(jnp.bfloat16)
-        log_out[part] = row_max + jnp.log(row_sum)
-
+        log_out[place_at] = row_of(row_max + jnp.log(row_sum))
+
+    order = (2, 0, 1, 3)
+    attn.start()
+    tok.start()
+    notices.start()
+    tok.relay_b()
+    attn.relay(0)
+    for elem in order:
+        tok.relay(0, elem)
+    attn.relay(1)
+    attn.relay(2)
+    for elem in order:
+        tok.relay(1, elem)
+    attn.relay(3)
+    attn.relay_out()
+    notices.finish()
+    tables()
+    for elem in order:
+        tok.relay(2, elem)
+    cots.start()
+    mlp.start()
+    for step in range(LINE):
+        attn.relay_share(step)
+    attn.relay_out_share()
+    tok.finish()
+    attn.finish()
+    store_qkv = local(qkv_w, qkv_out, store_s.at[0])
+    store_qkv.start()
+    for cut in range(LINE):
+        project(cut)
+    store_normed = local(normed, normed_out, store_s.at[1])
+    store_normed.start()
+    cots.relay_b()
+    for elem in order:
+        cots.relay(0, elem)
     pass_on(0)
     pass_on(1)
     share(0, 1 - c).wait_recv()
     share(1, 1 - c).wait_recv()
     attend(0)
-    cots.relay_b()
-    for elem in (2, 0, 1, 3):
-        cots.relay(0, elem)
+    for elem in order:
+        cots.relay(1, elem)
     pass_on(2)
     share(2, 1 - c).wait_recv()
     attend(1)
     pass_on(3)
     share(3, 1 - c).wait_recv()
-    store = local(keys, kv_out, out_sem)
+    store = local(keys, kv_out, store_s.at[2])
     store.start()
     attend(2)
-    for elem in (2, 0, 1, 3):
-        cots.relay(1, elem)
+    for elem in order:
+        cots.relay(2, elem)
     attend(3)
-    for elem in (2, 0, 1, 3):
-        cots.relay(2, elem)
     cots.finish()
     mlp.finish()
     for cut in range(LINE):
         share(cut, c).wait_send()
         over(cut, h).wait_send()
     store.wait()
-
-
-def attend_keys(query, kv, query_ids, key_ids, cot, wg, wu):
-    eight, rows, width = kv.shape
+    store_normed.wait()
+    store_qkv.wait()
+
+
+def front(tokens, cot, note, inv_freqs, wq, wk, wv, wo, wg, wu):
+    rows, width = tokens.shape
     depth, part = wg.shape[0], wg.shape[1] // 8
-    tokens = query.shape[0]
+    token_rows = 8 * rows
+
+    def room(*dims, dtype=jnp.bfloat16):
+        return pltpu.VMEM(dims, dtype)
 
     def shape(*dims, dtype=jnp.bfloat16):
         return jax.ShapeDtypeStruct(dims, dtype)
 
+    f32 = jnp.float32
     return pl.pallas_call(
-        attend_kernel,
+        front_kernel,
         out_shape=(
-            shape(eight, 2, 2, rows, width),
-            shape(tokens, HD, dtype=jnp.float32),
-            shape(tokens, HD),
-            shape(tokens, 1, dtype=jnp.float32),
+            shape(8, 2, 2, rows, 2 * HD),
+            shape(token_rows, width),
+            shape(8, 2, depth, 3 * HD),
+            shape(2, 2, wo.shape[0], width),
+            shape(16, *note.shape, dtype=f32),
+            shape(token_rows, HD // 2, dtype=f32),
+            shape(token_rows, HD // 2, dtype=f32),
+            shape(token_rows, HD),
+            shape(token_rows, HD, dtype=f32),
+            shape(token_rows, HD),
+            shape(LINE, 1, token_rows // LINE, dtype=f32),
             shape(8, *cot.shape),
             shape(8, depth, part),
             shape(8, depth, part),
         ),
-        in_specs=[INSIDE] * 7,
-        out_specs=(ANY, INSIDE, INSIDE, INSIDE, ANY, ANY, ANY),
+        in_specs=[INSIDE] * 10,
+        out_specs=(ANY, ANY, ANY, ANY) + (INSIDE,) * 7 + (ANY, ANY, ANY),
         scratch_shapes=[
-            pltpu.VMEM((eight, 2, 2, rows, width), jnp.bfloat16),
-            pltpu.VMEM((eight, tokens // LINE, 4 * rows), jnp.float32),
-            pltpu.VMEM((tokens // LINE, HD), jnp.float32),
-        ] + [dma(4)] * 5 + [dma()] + Gather.scratch() + MlpSpread.scratch(),
-        compiler_params=kernel_params(4),
-        name="attend_keys",
-    )(query, kv, query_ids, key_ids, cot, wg, wu)
+            room(8, rows, width),
+            room(token_rows, width),
+            room(8, 2, depth, 3 * HD),
+            room(1, width, dtype=f32),
+            room(token_rows, 1, dtype=f32),
+            room(8, 1, 4 * rows, dtype=f32),
+            room(8, rows, 2 * HD),
+            room(8, 2, 2, rows, 2 * HD),
+            room(8, token_rows // LINE, 4 * rows, dtype=f32),
+            room(token_rows // LINE, HD, dtype=f32),
+        ]
+        + [dma(4)] * 5
+        + [dma(3)]
+        + Gather.scratch()
+        + NoteSpread.scratch()
+        + AttnSpread.scratch()
+        + Gather.scratch()
+        + MlpSpread.scratch(),
+        compiler_params=kernel_params(3),
+        name="front",
+    )(tokens, cot, note, inv_freqs, wq, wk, wv, wo, wg, wu)
 
 
 def add_into(target, *others):
@@ -1962,40 +2176,20 @@
             jnp.zeros((2, rows), f32),
         ]
     )
-    tokens_all, notes, qkv_w, out_w = spread(tokens, note, w_query, w_key, w_value, w_out)
-    tokens_all = tokens_all.reshape(token_rows, width)
+    inv_freqs = rope_base ** (-2.0 * jnp.arange(HD // 2, dtype=f32) / HD)
+    (
+        keys_values, normed, qkv_w, out_w, notes, cos_table, sine_table, scaled_query, attended, attended_low,
+        log_total, cot_all, gate_w, up_w,
+    ) = front(tokens, cotangent, note, inv_freqs[None], w_query, w_key, w_value, w_out, w_gate, w_up)
     qkv_w = qkv_w.reshape(width, 3 * HD)
     out_w = out_w.reshape(HD, width)
     gain_attn = notes[:, 4].reshape(1, width)
     gain_mlp = notes[:, 5].reshape(1, width)
     mine = lax.dynamic_index_in_dim(notes.reshape(8, 2, 8, rows), core, 1, False)
-    positions_mine = lax.dynamic_index_in_dim(mine[:, 0:2], half, 1, False).reshape(token_rows)
     ids_mine = lax.dynamic_index_in_dim(mine[:, 2:4], half, 1, False).reshape(token_rows)
     key_ids = notes[:, 2:4].reshape(32 * rows)
-
     score_scale = HD ** (-0.5)
-    inputs_all = tokens_all.astype(f32)
-    normed = (inputs_all * rms_scale(inputs_all) * gain_attn).astype(bf16)
-    cos_table, sine_table = rope_tables(positions_mine)
-    cos_table, sine_table = cos_table[:, 0], sine_table[:, 0]
-    projected = product(normed, qkv_w)
-    query = rotate(projected[:, :HD], cos_table, sine_table).astype(bf16)
-    key = rotate(projected[:, HD : 2 * HD], cos_table, sine_table).astype(bf16)
-    value = projected[:, 2 * HD :].astype(bf16)
-    scaled_query = (query.astype(f32) * score_scale).astype(bf16)
-    keys_values, attended, attended_low, log_total, cot_all, gate_w, up_w = attend_keys(
-        scaled_query,
-        jnp.concatenate([key, value], axis=1).reshape(8, rows, 2 * HD),
-        ids_mine[:, None],
-        key_ids.reshape(8, 1, 4 * rows),
-        cotangent,
-        w_gate,
-        w_up,
-    )
-    cot_all = cot_all.reshape(token_rows, width)
-    branch, gate_w, up_w = reduce_share(
-        product(attended_low, out_w).astype(bf16).reshape(8, rows, width), gate_w, up_w
-    )
+    branch, gate_w, up_w = reduce_share(attended_low, out_w, gate_w, up_w)
     hidden_part = gate_w.shape[3]
     gate_w = gate_w.reshape(width, hidden_part)
     up_w = up_w.reshape(width, hidden_part)
@@ -2004,24 +2198,18 @@
     inv_attn = rms_scale(inputs)
     hidden = inputs + branch
     inv_mlp = rms_scale(hidden)
-    normed_mlp, down_w = gather_share((hidden * inv_mlp * gain_mlp).astype(bf16), w_down)
+    mlp_own, normed_mlp, active, grad_gate, grad_up, grad_normed_part = run_mlp(
+        (hidden * inv_mlp * gain_mlp).astype(bf16), w_down, gate_w, up_w, cot_all
+    )
+    output = (hidden + mlp_own).astype(bf16)
     normed_mlp = normed_mlp.reshape(token_rows, width)
-    down_w = down_w.reshape(hidden_part, width)
-    gate_pre = product(normed_mlp, gate_w)
-    up_pre = product(normed_mlp, up_w)
-    sigmoid_gate = jax.nn.sigmoid(gate_pre)
-    active = (gate_pre * sigmoid_gate * up_pre).astype(bf16)
-    mlp_own = reduce_plane(product(active, down_w).astype(bf16).reshape(8, rows, width))
-    output = (hidden + mlp_own).astype(bf16)
-    grad_active = times_transposed(cot_all, down_w)
-    grad_gate = (
-        grad_active * up_pre * sigmoid_gate * (1.0 + gate_pre * (1.0 - sigmoid_gate))
-    ).astype(bf16)
-    grad_up = (grad_active * gate_pre * sigmoid_gate).astype(bf16)
-    grad_normed_part = times_transposed(grad_gate, gate_w) + times_transposed(grad_up, up_w)
+    active = active.reshape(token_rows, hidden_part)
+    grad_gate = grad_gate.reshape(token_rows, hidden_part)
+    grad_up = grad_up.reshape(token_rows, hidden_part)
+    cot_all = cot_all.reshape(token_rows, width)
     depth = w_query.shape[0]
     grad_normed_mlp, gate_quarter, up_quarter = reduce_grads(
-        grad_normed_part.astype(bf16).reshape(8, rows, width),
+        grad_normed_part,
         transposed_times(normed_mlp, grad_gate).astype(bf16).reshape(8, 2, depth, hidden_part),
         transposed_times(normed_mlp, grad_up).astype(bf16).reshape(8, 2, depth, hidden_part),
     )

time: 777 us -> 664 us (0.85)
  matrix products: 108 us -> 43.3 us
  other arithmetic: 44 us -> 25.2 us
  local copies, waits for them, and re-layouts: 31 us -> 15.9 us
  Pallas kernels: 583 us -> 568 us
    dot_general x6 -> x3, matrix products: 46.4 us -> 9.7 us  [times_transposed(): lax.dot_general(left, right, (((1,), (1,)), ((), ())), preferred_element_...]
    dot_general x5 -> x0, matrix products: 33.6 us -> none  [product(): return jnp.dot(left, right, preferred_element_type=jnp.float32)]
    pallas_call x4 -> x2, Pallas kernels: 283 us -> 258 us  [the longest x1 153 us: front(): pl.pallas_call(front_kernel, out_shape=(shape(8, 2, 2, rows, 2 * HD), sha...]
    unnamed x77 -> x47, local copies, waits for them, and re-layouts: 11.1 us -> 1.41 us
    pallas_call x1, Pallas kernels: 58.5 us -> 68.2 us  [reduce_share(): pl.pallas_call(reduce_share_kernel, out_shape=(jax.ShapeDtypeStruct(shape...]
where the time goes in v3:
time: 664 us; the launch traced here: 654 us
  Pallas kernels  568 us (86%)
  matrix products  43.3 us (7%)
  other arithmetic  25.2 us (4%)
  local copies, waits for them, and re-layouts  15.9 us (2%)
    pallas_call x1, Pallas kernels, front(): pl.pallas_call(front_kernel, out_shape=(shape(8, 2, 2, rows, 2 * HD), sha...  153 us
    pallas_call x1, Pallas kernels, run_mlp(): pl.pallas_call(mlp_kernel, out_shape=(shape(rows, width, dtype=jnp.float3...  105 us
    pallas_call x1, Pallas kernels, reduce_heads(): pl.pallas_call(reduce_heads_kernel, out_shape=(jax.ShapeDtypeStruct(shape...  69.9 us
    pallas_call x1, Pallas kernels, reduce_share(): pl.pallas_call(reduce_share_kernel, out_shape=(jax.ShapeDtypeStruct(shape...  68.2 us
    pallas_call x1, Pallas kernels, attend_back(): pl.pallas_call(attend_back_kernel, out_shape=(shape(eight, rows, HD, dtyp...  56.5 us
    pallas_call x1, Pallas kernels, reduce_grads(): pl.pallas_call(reduce_grads_kernel, out_shape=(jax.ShapeDtypeStruct(shape...  54.8 us
    pallas_call x1, Pallas kernels, gather_grads(): pl.pallas_call(gather_grads_kernel, out_shape=(jax.ShapeDtypeStruct((2 *...  49.5 us
    dot_general x6, matrix products, transposed_times(): lax.dot_general(left, right, (((0,), (0,)), ((), ())), preferred_element_...  33.6 us

profile of v3, /device:TPU:8, one launch (start us, length us, event | category | flops | bytes accessed | tf_op | source)
XLA Modules:
  0.0 653.7 jit_solution(15423794843028461188)
XLA Ops:
  0.6 0.0 copy-start.1
  0.7 0.8 convert_bitcast_fusion
  1.4 0.7 bitcast_convert_fusion.3
  2.1 0.6 concatenate.13.note
  2.7 0.5 multiply_power_fusion.inv_freqs
  3.2 152.8 %front.1 = (bf16[8,2,2,128,512]{4,3,2,1,0:T(8,128)(2,1)}, bf16[1024,2048]{1,0:T(8,128)(2,1)}, bf16[8,2,128,768]{3,2,1,0:T(8,128)(2,1)}, bf16[2,2,64,2048]{3,2,1,...) custom-call(bf16[128,2048]{1,0:T(8,128)(2,1)} %tokens.1, ...), custom_call_target="tpu_custom_call" | custom-call | tf_op jit(solution)/shard_map/front/pallas_call | solution.py:1499
  156.1 68.2 %reduce_share.1 = (f32[128,2048]{1,0:T(8,128)}, bf16[8,2,128,1024]{3,2,1,0:T(8,128)(2,1)}, bf16[8,2,128,1024]{3,2,1,0:T(8,128)(2,1)}) custom-call(bf16[1024,256]{1,0:T(8,128)(2,1)} %get-tuple-element.48.attended, bf16[256,2048]{1,0:T(8,128)(2,1)} %bitcast.75, bf16[8,128,512]{2,1,0:T(8,128)(2,1)} %get-tuple-element.50.gate_in, ...), custom_call_target="tpu_custom_call" | custom-call | tf_op jit(solution)/shard_map/reduce_share/pallas_call | solution.py:1118
  224.3 1.5 multiply_reduce_fusion.3
  225.8 0.9 multiply_convert_fusion.src
  226.8 105.3 %run_mlp.1 = (f32[128,2048]{1,0:T(8,128)}, bf16[8,128,2048]{2,1,0:T(8,128)(2,1)}, bf16[8,128,1024]{2,1,0:T(8,128)(2,1)}, bf16[8,128,1024]{2,1,0:T(8,128)(2,1)}, ...) custom-call(bf16[128,2048]{1,0:T(8,128)(2,1)} %multiply_convert_fusion.src, bf16[256,2048]{1,0:T(8,128)(2,1)} %wd.1, ...), custom_call_target="tpu_custom_call" | custom-call | tf_op jit(solution)/shard_map/run_mlp/pallas_call | solution.py:1280
  332.1 9.5 %bitcast_convert_fusion = bf16[1024,2048]{1,0:T(8,128)(2,1)} fusion(bf16[8,128,1024]{2,1,0:T(8,128)(2,1)} %get-tuple-element.64, bf16[8,128,2048]{2,1,0:T(8,128)(2,1)} %get-tuple-element.56.cot_in), kind=kOutput, calls=%fused_computation | convolution fusion | flops 4297064448 | bytes 10485760 | tf_op jit(solution)/shard_map/dot_general | solution.py:49
  341.6 6.3 bitcast_convert_fusion.1
  347.9 6.3 bitcast_convert_fusion.2
  354.1 54.8 %reduce_grads.1 = (f32[128,2048]{1,0:T(8,128)}, bf16[8,128,512]{2,1,0:T(8,128)(2,1)}, bf16[8,128,512]{2,1,0:T(8,128)(2,1)}) custom-call(bf16[8,128,2048]{2,1,0:T(8,128)(2,1)} %get-tuple-element.58.parts_in, bf16[8,2,128,1024]{3,2,1,0:T(8,128)(2,1)} %bitcast.69, bf16[8,2,128,1024]{3,2,1,0:T(8,128)(2,1)} %bitcast.68), custom_call_target="tpu_custom_call" | custom-call | tf_op jit(solution)/shard_map/reduce_grads/pallas_call | solution.py:1743
  408.9 1.6 multiply_reduce_fusion
  410.5 2.4 fusion.17.src
  412.9 49.5 %gather_grads.1 = (bf16[8,128,2048]{2,1,0:T(8,128)(2,1)}, f32[256,2048]{1,0:T(8,128)}) custom-call(bf16[128,2048]{1,0:T(8,128)(2,1)} %fusion.17.src, bf16[2,2,256,2048]{3,2,1,0:T(8,128)(2,1)} %bitcast.70), custom_call_target="tpu_custom_call" | custom-call | tf_op jit(solution)/shard_map/gather_grads/pallas_call | solution.py:1777
  462.5 5.2 multiply_reduce_fusion.1
  467.7 0.6 constant_dynamic-slice_fusion
  468.3 3.3 reshape_reshape.8.key_column
  471.6 3.1 slice.43
  474.7 3.9 copy.42
  478.6 56.5 %attend_back.1 = (f32[8,128,256]{2,1,0:T(8,128)}, f32[4,256,256]{2,1,0:T(8,128)}, bf16[128,4096]{1,0:T(8,128)(2,1)}, bf16[128,4096]{1,0:T(8,128)(2,1)}) custom-call(bf16[1024,256]{1,0:T(8,128)(2,1)} %get-tuple-element.63.query, bf16[1024,256]{1,0:T(8,128)(2,1)} %get-tuple-element.103.grad_out, bf16[8,2,2,128,512]{4,3,2,1,0:T(8,128)(2,1)} %get-tuple-element.66.keys_in, ...), custom_call_target="tpu_custom_call" | custom-call | tf_op jit(solution)/shard_map/attend_back/pallas_call | solution.py:1893
  535.1 1.4 multiply_subtract_fusion
  536.5 1.3 fusion.13
  537.9 0.0 copy-start.5
  537.9 4.7 convolution_convert_fusion.1
  542.6 1.1 multiply_bitcast_fusion
  543.7 1.6 copy.37
  545.2 1.4 subtract_convert_fusion
  546.6 4.7 convolution_convert_fusion.2
  551.3 1.3 fusion.11
  552.6 3.2 add_convert_fusion
  555.8 2.2 convolution_convert_fusion
  558.1 69.9 %reduce_heads.1 = (f32[128,2048]{1,0:T(8,128)}, bf16[128,1024]{1,0:T(8,128)(2,1)}, bf16[128,512]{1,0:T(8,128)(2,1)}, bf16[128,512]{1,0:T(8,128)(2,1)}, bf16[64,2048]{1,0:T(8,128)(2,1)}) custom-call(bf16[8,128,2048]{2,1,0:T(8,128)(2,1)} %bitcast.63, bf16[8,2,128,256]{3,2,1,0:T(8,128)(2,1)} %bitcast.78, bf16[8,2,128,256]{3,2,1,0:T(8,128)(2,1)} %bitcast.77, ...), custom_call_target="tpu_custom_call" | custom-call | tf_op jit(solution)/shard_map/reduce_heads/pallas_call | solution.py:2095
  628.0 1.7 fusion.8
  629.7 0.1 pad.2.clone
  629.8 0.7 maximum_maximum_fusion.gains
  630.5 11.2 %reduce_gains.1 = f32[8,128]{1,0:T(8,128)} custom-call(f32[16,8,128]{2,1,0:T(8,128)} %maximum_maximum_fusion.gains), custom_call_target="tpu_custom_call" | custom-call | tf_op jit(solution)/shard_map/reduce_gains/pallas_call | solution.py:2136
  641.7 1.3 slice_bitcast_fusion
  643.0 3.1 fusion.7
  646.0 0.8 convert_element_type.93
  646.9 0.8 convert_element_type.96
  647.7 0.7 convert_element_type.94
  648.4 0.7 convert_element_type.95
  649.2 1.5 convert_element_type.97
  650.7 1.5 convert_element_type.98
  652.2 1.3 copy.46
  (55 shorter events, 0.2 us)
Async XLA Ops:
  0.6 223.6 %copy-start.1 = (bf16[128,2048]{1,0:T(8,128)(2,1)S(1)}, bf16[128,2048]{1,0:T(8,128)(2,1)}, u32[]{:S(2)}) copy-start(bf16[128,2048]{1,0:T(8,128)(2,1)} %tokens.1) | copy-start | bytes 1572868
  156.1 69.7 %copy-start.18 = (f32[16,8,128]{2,1,0:T(8,128)S(1)}, f32[16,8,128]{2,1,0:T(8,128)}, u32[]{:S(2)}) copy-start(f32[16,8,128]{2,1,0:T(8,128)} %get-tuple-element.53) | copy-start | bytes 196612
  332.1 9.5 %copy-start.20 = (bf16[8,128,2048]{2,1,0:T(8,128)(2,1)S(1)}, bf16[8,128,2048]{2,1,0:T(8,128)(2,1)}, u32[]{:S(2)}) copy-start(bf16[8,128,2048]{2,1,0:T(8,128)(2,1)} %get-tuple-element.59) | copy-start | bytes 12582916
  332.1 9.5 %copy-start.22 = (bf16[8,128,1024]{2,1,0:T(8,128)(2,1)S(1)}, bf16[8,128,1024]{2,1,0:T(8,128)(2,1)}, u32[]{:S(2)}) copy-start(bf16[8,128,1024]{2,1,0:T(8,128)(2,1)} %get-tuple-element.61) | copy-start | bytes 6291460
  341.6 6.3 copy-start.21
  354.1 56.3 %copy-start.2 = (bf16[128,2048]{1,0:T(8,128)(2,1)S(1)}, bf16[128,2048]{1,0:T(8,128)(2,1)}, u32[]{:S(2)}) copy-start(bf16[128,2048]{1,0:T(8,128)(2,1)} %cot.1) | copy-start | bytes 1572868
  410.5 52.0 %copy-start.11 = (bf16[2,2,64,2048]{3,2,1,0:T(8,128)(2,1)S(1)}, bf16[2,2,64,2048]{3,2,1,0:T(8,128)(2,1)}, u32[]{:S(2)}) copy-start(bf16[2,2,64,2048]{3,2,1,0:T(8,128)(2,1)} %get-tuple-element.49) | copy-start | bytes 3145732
  478.6 56.5 %copy-start.3 = (f32[1024,128]{1,0:T(8,128)S(1)}, f32[1024,128]{1,0:T(8,128)}, u32[]{:S(2)}) copy-start(f32[1024,128]{1,0:T(8,128)} %get-tuple-element.72) | copy-start | bytes 1572868
  478.6 56.5 %copy-start.4 = (f32[1024,128]{1,0:T(8,128)S(1)}, f32[1024,128]{1,0:T(8,128)}, u32[]{:S(2)}) copy-start(f32[1024,128]{1,0:T(8,128)} %get-tuple-element.73) | copy-start | bytes 1572868
  537.9 4.7 copy-start.5
  537.9 4.7 copy-start.12
  546.6 4.7 copy-start.8
  551.3 1.3 copy-start.6
  552.6 3.3 copy-start.13
  552.6 3.3 copy-start.19
  558.1 84.9 %copy-start = (f32[128,2048]{1,0:T(8,128)S(1)}, f32[128,2048]{1,0:T(8,128)}, u32[]{:S(2)}) copy-start(f32[128,2048]{1,0:T(8,128)} %get-tuple-element.62) | copy-start | bytes 3145732
  628.0 18.0 %copy-start.15 = (bf16[128,1024]{1,0:T(8,128)(2,1)S(1)}, bf16[128,1024]{1,0:T(8,128)(2,1)}, u32[]{:S(2)}) copy-start(bf16[128,1024]{1,0:T(8,128)(2,1)} %get-tuple-element.78) | copy-start | bytes 786436
  628.0 18.9 %copy-start.14 = (bf16[64,2048]{1,0:T(8,128)(2,1)S(1)}, bf16[64,2048]{1,0:T(8,128)(2,1)}, u32[]{:S(2)}) copy-start(bf16[64,2048]{1,0:T(8,128)(2,1)} %get-tuple-element.81) | copy-start | bytes 786436
  629.7 18.0 %copy-start.17 = (bf16[128,512]{1,0:T(8,128)(2,1)S(1)}, bf16[128,512]{1,0:T(8,128)(2,1)}, u32[]{:S(2)}) copy-start(bf16[128,512]{1,0:T(8,128)(2,1)} %get-tuple-element.79) | copy-start | bytes 393220
  630.5 18.0 %copy-start.16 = (bf16[128,512]{1,0:T(8,128)(2,1)S(1)}, bf16[128,512]{1,0:T(8,128)(2,1)}, u32[]{:S(2)}) copy-start(bf16[128,512]{1,0:T(8,128)(2,1)} %get-tuple-element.80) | copy-start | bytes 393220
  642.9 6.2 copy-start.10
  646.0 4.7 copy-start.9
  646.0 6.2 copy-start.7

commit v4 on v3

--- a/solution.py
+++ b/solution.py
@@ -1088,70 +1088,42 @@
     return groups
 
 
-def reduce_share_kernel(attended, out_w, gate_in, up_in, out, gate, up, parts, *refs):
-    reduce_refs, share_sems = split_refs(refs, (9, 5))
-    z, y, c, h = place()
-    greet(device(z, y, 1 - c, h))
-    greet(device(z, y, c, 1 - h))
-    greet_plane(2)
-    reduce = Reduce(parts, reduce_refs)
-    share = MlpShare((gate_in, up_in), (gate, up), share_sems)
-    rows, width = parts.shape[1:]
-    share.start()
-    for place_at in range(4):
-        line = reduce.order[place_at]
-        both = attended[pl.ds(pl.multiple_of(line * 2 * rows, 2 * rows), 2 * rows)]
-        parts[pl.ds(line * 2, 2)] = product(both, out_w[...]).astype(jnp.bfloat16).reshape(2, rows, width)
-        reduce.start(place_at)
-    for place_at in range(3):
-        reduce.relay(place_at)
-    reduce.total(out)
-    share.relay()
-    reduce.finish()
-    share.finish()
-
-
-def reduce_share(attended, out_w, gate, up):
-    eight, depth, part = gate.shape
-    shape = (eight, attended.shape[0] // eight, out_w.shape[1])
-    full = jax.ShapeDtypeStruct((eight, 2, depth, 2 * part), gate.dtype)
-    return pl.pallas_call(
-        reduce_share_kernel,
-        out_shape=(jax.ShapeDtypeStruct(shape[1:], jnp.float32), full, full),
-        in_specs=[INSIDE] * 4,
-        out_specs=(INSIDE, ANY, ANY),
-        scratch_shapes=[pltpu.VMEM(shape, jnp.bfloat16)] + Reduce.scratch(shape[2]) + MlpShare.scratch(),
-        compiler_params=kernel_params(7),
-        name="reduce_share",
-    )(attended, out_w, gate, up)
-
-
-def mlp_kernel(
-    src, wd, gate_in, up_in, cot_in,
-    mlp_out, normed_out, active, grad_gate, grad_up, grad_out,
-    normed, gate_w, up_w, down_w, gate_pre, up_pre, cot, parts, load_s, out_s, *refs,
+def mid_kernel(
+    attended, out_w, gate_in, up_in, wd, tokens, gain, cot_in,
+    output, hidden_out, normed_out, active, grad_gate, grad_up, grad_out,
+    normed, src, total, gate_w, up_w, down_w, gate_pre, up_pre, cot, parts, load_s, out_s, *refs,
 ):
-    gather_sems, down_sems, reduce_refs = split_refs(refs, (8, 3, 9))
-    loads = [
-        local(gate_in, gate_w, load_s.at[0]),
-        local(up_in, up_w, load_s.at[1]),
-        local(cot_in, cot, load_s.at[2]),
-    ]
-    for load in loads:
-        load.start()
+    gather_sems, share_sems, down_sems, reduce_refs = split_refs(refs, (8, 5, 3, 9))
+    load = local(cot_in, cot, load_s)
+    load.start()
     z, y, c, h = place()
     greet(device(z, y, 1 - c, h))
     greet(device(z, y, c, 1 - h))
     greet_plane(2)
     gather = Gather(src, normed, gather_sems)
+    share = MlpShare((gate_in, up_in), (gate_w, up_w), share_sems)
     downs = DownSpread(wd, down_w, down_sems)
     reduce = Reduce(parts, reduce_refs)
-    gather.start()
-    downs.start()
     rows, width = normed.shape[1:]
-    hidden = gate_w.shape[1]
+    hidden = gate_w.shape[3]
     step = hidden // 4
     pair = 2 * rows
+    share.start()
+    for place_at in range(4):
+        line = reduce.order[place_at]
+        both = attended[pl.ds(pl.multiple_of(line * pair, pair), pair)]
+        parts[pl.ds(line * 2, 2)] = product(both, out_w[...]).astype(jnp.bfloat16).reshape(2, rows, width)
+        reduce.start(place_at)
+    for place_at in range(3):
+        reduce.relay(place_at)
+    reduce.total(total)
+    hidden_rows = tokens[...].astype(jnp.float32) + total[...]
+    hidden_out[...] = hidden_rows
+    src[...] = (hidden_rows * rms_scale(hidden_rows) * gain[...]).astype(jnp.bfloat16)
+    gather.start()
+    share.relay()
+    downs.start()
+    reduce.finish()
 
     def forward(chip, own=False):
         shard = src if own else normed.at[chip]
@@ -1159,8 +1131,8 @@
         @pl.loop(0, 4)
         def _(tile):
             columns = pl.ds(pl.multiple_of(tile * step, step), step)
-            gate_part = product(shard[...], gate_w[:, columns])
-            up_part = product(shard[...], up_w[:, columns])
+            gate_part = product(shard[...], gate_w[:, :, :, columns].reshape(width, step))
+            up_part = product(shard[...], up_w[:, :, :, columns].reshape(width, step))
             gate_pre[chip, :, columns] = gate_part
             up_pre[chip, :, columns] = up_part
             active[chip, :, columns] = (gate_part * jax.nn.sigmoid(gate_part) * up_part).astype(jnp.bfloat16)
@@ -1197,8 +1169,7 @@
             gather.relay(distance - 1, elem)
 
     gather.relay_b()
-    loads[0].wait()
-    loads[1].wait()
+    share.finish()
     forward(z * 2 + y, own=True)
     relay(1)
     forward_other(0)
@@ -1230,7 +1201,7 @@
     for place_at in range(4):
         contribute(reduce.order[place_at])
         reduce.start(place_at)
-    loads[2].wait()
+    load.wait()
 
     def backward(line):
         both = pl.ds(line * 2, 2)
@@ -1250,15 +1221,17 @@
         @pl.loop(0, 4)
         def _(tile):
             columns = pl.ds(pl.multiple_of(tile * (width // 4), width // 4), width // 4)
-            part = times_transposed(grad_gate[both].reshape(pair, hidden), gate_w[columns])
-            part += times_transposed(grad_up[both].reshape(pair, hidden), up_w[columns])
+            chips = pl.ds(tile * 2, 2)
+            part = times_transposed(grad_gate[both].reshape(pair, hidden), gate_w[chips].reshape(width // 4, hidden))
+            part += times_transposed(grad_up[both].reshape(pair, hidden), up_w[chips].reshape(width // 4, hidden))
             grad_out[both, :, columns] = part.astype(jnp.bfloat16).reshape(2, rows, width // 4)
 
     for place_at in range(3):
         backward(place_at)
         reduce.relay(place_at)
     backward(3)
-    reduce.total(mlp_out)
+    reduce.total(total)
+    output[...] = (hidden_out[...] + total[...]).astype(jnp.bfloat16)
     reduce.finish()
     store.wait()
     for line in range(LINE):
@@ -1267,9 +1240,10 @@
     gather.finish_sends()
 
 
-def run_mlp(src, wd, gate_w, up_w, cot):
-    rows, width = src.shape
-    hidden = gate_w.shape[1]
+def mid(attended, out_w, gate, up, wd, tokens, gain, cot):
+    eight, depth, part = gate.shape
+    rows, width = tokens.shape
+    hidden = 2 * part
 
     def room(*dims, dtype=jnp.bfloat16):
         return pltpu.VMEM(dims, dtype)
@@ -1277,26 +1251,29 @@
     def shape(*dims, dtype=jnp.bfloat16):
         return jax.ShapeDtypeStruct(dims, dtype)
 
+    f32 = jnp.float32
     return pl.pallas_call(
-        mlp_kernel,
+        mid_kernel,
         out_shape=(
-            shape(rows, width, dtype=jnp.float32),
+            shape(rows, width),
+            shape(rows, width, dtype=f32),
             shape(8, rows, width),
             shape(8, rows, hidden),
             shape(8, rows, hidden),
             shape(8, rows, hidden),
             shape(8, rows, width),
         ),
-        in_specs=[INSIDE, INSIDE, ANY, ANY, ANY],
-        out_specs=(INSIDE, ANY, INSIDE, INSIDE, INSIDE, INSIDE),
+        in_specs=[INSIDE] * 7 + [ANY],
+        out_specs=(INSIDE, INSIDE, ANY, INSIDE, INSIDE, INSIDE, INSIDE),
         scratch_shapes=[
-            room(8, rows, width), room(width, hidden), room(width, hidden), room(2, 2, *wd.shape),
-            room(8, rows, hidden, dtype=jnp.float32), room(8, rows, hidden, dtype=jnp.float32),
-            room(8, rows, width), room(8, rows, width), dma(3), dma(),
-        ] + Gather.scratch() + DownSpread.scratch() + Reduce.scratch(width),
+            room(8, rows, width), room(rows, width), room(rows, width, dtype=f32),
+            room(eight, 2, depth, hidden), room(eight, 2, depth, hidden), room(2, 2, *wd.shape),
+            room(8, rows, hidden, dtype=f32), room(8, rows, hidden, dtype=f32),
+            room(8, rows, width), room(8, rows, width), dma(), dma(),
+        ] + Gather.scratch() + MlpShare.scratch() + DownSpread.scratch() + Reduce.scratch(width),
         compiler_params=kernel_params(8),
-        name="run_mlp",
-    )(src, wd, gate_w, up_w, cot)
+        name="mid",
+    )(attended, out_w, gate, up, wd, tokens, gain, cot)
 
 
 def column_of(row):
@@ -1669,16 +1646,13 @@
             pltpu.VMEM((2, 2, rows, width), jnp.bfloat16),
             pltpu.VMEM((2, rows, width), jnp.bfloat16),
             pltpu.VMEM((rows, width), jnp.bfloat16),
-            dma(1), dma(2), dma(2),
+            dma(2), dma(2),
         ]
 
-    def __init__(self, source, out, refs):
-        self.source, self.out = source, out
-        self.store, self.sib, self.box, self.load_s, self.c_sr, self.x_sr = refs
+    def __init__(self, out, refs):
+        self.out = out
+        self.store, self.sib, self.box, self.c_sr, self.x_sr = refs
         self.z, self.y, self.c, self.h = place()
-
-    def load(self):
-        return local(self.source, self.store, self.load_s.at[0])
 
     def share(self):
         return remote(
@@ -1691,10 +1665,6 @@
             self.store.at[1 - self.h, self.c], self.box, self.x_sr.at[0], self.x_sr.at[1],
             device(self.z, self.y, self.c, 1 - self.h),
         )
-
-    def start(self):
-        self.load().wait()
-        self.share().start()
 
     def relay(self):
         self.share().wait_recv()
@@ -1709,101 +1679,228 @@
         self.over().wait_send()
 
 
-def reduce_grads_kernel(parts_in, gate_in, up_in, out, gate, up, parts, in_sem, *refs):
-    reduce_refs, grad_refs = split_refs(refs, (9, 11))
-    load = pltpu.make_async_copy(parts_in, parts, in_sem)
-    load.start()
+def turn_kernel(
+    parts_in, normed_in, gate_grad_in, up_grad_in, active_in, cot_in, hidden, gain, cot,
+    gathered, grad_hidden, gain_term, gate, up, down,
+    parts, normed, gate_grad, up_grad, active, cot_all, grad_normed, branch, load_s, *refs,
+):
+    reduce_refs, gather_sems, quarter_refs, down_refs = split_refs(refs, (9, 8, 11, 5))
+    loads = [
+        local(parts_in, parts, load_s.at[0]),
+        local(normed_in, normed, load_s.at[1]),
+        local(gate_grad_in, gate_grad, load_s.at[2]),
+        local(up_grad_in, up_grad, load_s.at[3]),
+        local(active_in, active, load_s.at[4]),
+        local(cot_in, cot_all, load_s.at[5]),
+    ]
+    for load in loads:
+        load.start()
     z, y, c, h = place()
-    grads = QuarterReduce((gate_in, up_in), (gate, up), grad_refs)
-    grads.start_loads()
+    grads = QuarterReduce((None, None), (gate, up), quarter_refs)
+    downs = DownReduce(down, down_refs)
     greet(device(z, y, 1 - c, h))
     greet(device(z, y, c, 1 - h))
     greet_plane(2)
     reduce = Reduce(parts, reduce_refs)
-    load.wait()
+    gather = Gather(branch, gathered, gather_sems)
+    loads[0].wait()
     for place_at in range(4):
         reduce.start(place_at)
-    grads.start(0)
-    grads.start(1)
+    for load in loads[1:]:
+        load.wait()
+    tokens, width = normed.shape
+    depth, wide = quarter_refs[0].shape[2:]
+
+    def weight_grad(kind, first, last):
+        source = (gate_grad, up_grad)[kind]
+        store = quarter_refs[kind]
+
+        @pl.loop(first, last)
+        def _(tile):
+            columns = pl.ds(pl.multiple_of(tile * 2 * depth, 2 * depth), 2 * depth)
+            part = transposed_times(normed[:, columns], source[...])
+            store[tile] = part.astype(jnp.bfloat16).reshape(2, depth, wide)
+
+    down_store = down_refs[0]
+    down_rows = down_store.shape[2]
+
+    def down_grad(tile):
+        columns = pl.ds(tile * down_rows, down_rows)
+
+        @pl.loop(0, 4)
+        def _(piece):
+            part_columns = pl.ds(pl.multiple_of(piece * (width // 4), width // 4), width // 4)
+            part = transposed_times(active[:, columns], cot_all[:, part_columns])
+            down_store[tile // 2, tile % 2, :, part_columns] = part.astype(jnp.bfloat16)
+
+    weight_grad(0, 0, 4)
+    grads.share(0, 0).start()
+    weight_grad(0, 4, 8)
+    grads.share(0, 1).start()
+    reduce.relay(0)
+    weight_grad(1, 0, 4)
     grads.relay(0)
-    reduce.relay(0)
+    grads.share(1, 0).start()
+    weight_grad(1, 4, 8)
+    grads.share(1, 1).start()
+    reduce.relay(1)
     grads.relay(1)
-    reduce.relay(1)
     reduce.relay(2)
-    reduce.total(out)
+    reduce.total(grad_normed)
+    inputs = hidden[...]
+    inv_scale = rms_scale(inputs)
+    unit_rows = inputs * inv_scale
+    grad_unit = grad_normed[...] * gain[...]
+    gain_term[...] = jnp.sum(grad_normed[...] * unit_rows, axis=0, keepdims=True)
+    mean = jnp.mean(grad_unit * unit_rows, axis=-1, keepdims=True)
+    grad_rows = cot[...].astype(jnp.float32) + inv_scale * (grad_unit - unit_rows * mean)
+    grad_hidden[...] = grad_rows
+    branch[...] = grad_rows.astype(jnp.bfloat16)
+    gather.start()
+    gather.relay_b()
+    for tile in range(4):
+        down_grad(tile)
+    downs.share().start()
+    for elem in (2, 0, 1, 3):
+        gather.relay(0, elem)
+    downs.relay()
     grads.finish(0)
+    for elem in (2, 0, 1, 3):
+        gather.relay(1, elem)
     grads.finish(1)
-    reduce.finish()
-
-
-def reduce_grads(parts, gate, up):
-    shape = parts.shape
-    depth, wide = gate.shape[2:]
-    quarter = jax.ShapeDtypeStruct((8, depth, wide // 2), gate.dtype)
-    return pl.pallas_call(
-        reduce_grads_kernel,
-        out_shape=(jax.ShapeDtypeStruct(shape[1:], jnp.float32), quarter, quarter),
-        in_specs=[ANY] * 3,
-        out_specs=(INSIDE,) * 3,
-        scratch_shapes=[pltpu.VMEM(shape, jnp.bfloat16), dma()]
-        + Reduce.scratch(shape[2])
-        + QuarterReduce.scratch(depth, wide),
-        compiler_params=kernel_params(9),
-        name="reduce_grads",
-    )(parts, gate, up)
-
-
-def gather_grads_kernel(src, down_in, out, down, *refs):
-    gather_sems, down_refs = split_refs(refs, (8, 6))
-    z, y, c, h = place()
-    downs = DownReduce(down_in, down, down_refs)
-    downs.load().start()
-    greet(device(z, y, 1 - c, h))
-    greet(device(z, y, c, 1 - h))
-    greet_plane(2)
-    gather = Gather(src, out, gather_sems)
-    gather.start()
-    downs.start()
-    gather.relay_b()
-    downs.relay()
-    for step in range(LINE - 1):
-        for elem in (2, 0, 1, 3):
-            gather.relay(step, elem)
+    for elem in (2, 0, 1, 3):
+        gather.relay(2, elem)
     downs.finish()
     gather.finish()
-
-
-def gather_grads(rows, down):
+    reduce.finish()
+
+
+def turn(parts, normed, gate_grad, up_grad, active, cot_all, hidden, gain, cot):
+    eight, rows, width = parts.shape
+    wide = gate_grad.shape[1]
+    depth = normed.shape[1] // 16
+    down_rows = wide // 4
+
+    def room(*dims, dtype=jnp.bfloat16):
+        return pltpu.VMEM(dims, dtype)
+
+    def shape(*dims, dtype=jnp.bfloat16):
+        return jax.ShapeDtypeStruct(dims, dtype)
+
+    f32 = jnp.float32
     return pl.pallas_call(
-        gather_grads_kernel,
+        turn_kernel,
         out_shape=(
-            jax.ShapeDtypeStruct((2 * LINE,) + rows.shape, rows.dtype),
-            jax.ShapeDtypeStruct(down.shape[2:], jnp.float32),
+            shape(eight, rows, width),
+            shape(rows, width, dtype=f32),
+            shape(1, width, dtype=f32),
+            shape(8, depth, wide // 2),
+            shape(8, depth, wide // 2),
+            shape(down_rows, width, dtype=f32),
         ),
-        in_specs=[INSIDE, ANY],
-        out_specs=(ANY, INSIDE),
-        scratch_shapes=Gather.scratch() + DownReduce.scratch(*down.shape[2:]),
-        compiler_params=kernel_params(10),
-        name="gather_grads",
-    )(rows, down)
+        in_specs=[ANY] * 6 + [INSIDE] * 3,
+        out_specs=(ANY,) + (INSIDE,) * 5,
+        scratch_shapes=[
+            room(*parts.shape), room(*normed.shape), room(*gate_grad.shape), room(*up_grad.shape),
+            room(*active.shape), room(*cot_all.shape), room(rows, width, dtype=f32), room(rows, width), dma(6),
+        ]
+        + Reduce.scratch(width)
+        + Gather.scratch()
+        + QuarterReduce.scratch(depth, wide)
+        + DownReduce.scratch(down_rows, width),
+        compiler_params=kernel_params(9),
+        name="turn",
+    )(parts, normed, gate_grad, up_grad, active, cot_all, hidden, gain, cot)
+
+
+class OutGrad:
+    @staticmethod
+    def scratch(rows, width):
+        def room(*dims):
+            return pltpu.VMEM(dims, jnp.bfloat16)
+
+        return [room(2, 2, rows, width), room(2, rows, width), room(2, rows, width), dma(2), dma(2), dma(2), dma(1)]
+
+    def __init__(self, out, refs):
+        self.out = out
+        self.store, self.sib, self.box, self.c_sr, self.x_sr, self.y_sr, self.own = refs
+        self.z, self.y, self.c, self.h = place()
+        self.me = device(self.z, self.y, self.c, self.h)
+        self.owner = self.h == self.y
+
+    def share(self):
+        return remote(
+            self.store.at[:, 1 - self.c], self.sib, self.c_sr.at[0], self.c_sr.at[1],
+            device(self.z, self.y, 1 - self.c, self.h),
+        )
+
+    def over(self):
+        return remote(
+            self.store.at[:, self.c], self.box, self.x_sr.at[0], self.x_sr.at[1],
+            device(self.z, self.y, self.c, 1 - self.h),
+        )
+
+    def move(self):
+        return remote(
+            self.store.at[1 - self.y, self.c], self.out, self.y_sr.at[0], self.y_sr.at[1],
+            device(self.z, 1 - self.y, self.c, self.h),
+        )
+
+    def keep(self):
+        return local(self.store.at[self.y, self.c], self.out, self.own.at[0])
+
+    def relay(self):
+        self.share().wait_recv()
+        for pair in range(2):
+            add_into(self.store.at[pair, self.c], self.sib.at[pair])
+
+        @pl.when(jnp.logical_not(self.owner))
+        def _():
+            self.over().start()
+
+    def send(self):
+        @pl.when(self.owner)
+        def _():
+            self.over().wait_recv()
+            for pair in range(2):
+                add_into(self.store.at[pair, self.c], self.box.at[pair])
+            self.move().start()
+            self.keep().start()
+
+    def finish(self):
+        self.share().wait_send()
+
+        @pl.when(jnp.logical_not(self.owner))
+        def _():
+            remote(self.out, self.out, self.y_sr.at[0], self.y_sr.at[1], self.me).wait_recv()
+            self.over().wait_send()
+
+        @pl.when(self.owner)
+        def _():
+            self.keep().wait()
+            self.move().wait_send()
 
 
 def attend_back_kernel(
-    query, grad_out, keys_in, keys_turned, log_row, delta_row, query_row, key_column, gate_in, up_in,
-    side_out, grad_query, gate, up,
-    keys, turned, parts, grad_key, grad_value, sib_in, x_in, z_in,
+    query, keys_in, branch_in, out_w, attended, attended_low, log_row, notes, cos_table, sine_table, gate_in, up_in,
+    side_out, grad_query, gate, up, out_grad,
+    keys, branch, grad_out, delta_row, query_row, key_column, grad_rot, parts, grad_key, grad_value, sib_in, x_in, z_in,
     load_s, c_s, c_r, x_s, x_r, z_s, z_r, *sems,
 ):
     z, y, c, h = place()
     mate = z + 1 - 2 * (z % 2)
-    loads = [local(keys_in, keys, load_s.at[0]), local(keys_turned, turned, load_s.at[1])]
+    loads = [local(keys_in, keys, load_s.at[0]), local(branch_in, branch, load_s.at[1])]
     for load in loads:
         load.start()
     greet_all(16, 2)
-    scatter = QuarterScatter((gate_in, up_in), (gate, up), sems)
+    scatter_sems, out_refs = split_refs(sems, (3, 7))
+    scatter = QuarterScatter((gate_in, up_in), (gate, up), scatter_sems)
+    outs = OutGrad(out_grad, out_refs)
     scatter.start()
-    rows, width = key_column.shape[1], query.shape[1]
-    pair = query.shape[0] // LINE
+    width = query.shape[1]
+    rows = branch.shape[1]
+    pair = 2 * rows
+    block_rows = 4 * rows
 
     def share(block):
         return remote(
@@ -1834,16 +1931,58 @@
         add_into(parts.at[block, c, h], sib_in.at[block, h], x_in.at[block])
         across(block).start()
 
+    def turn_back(values, part):
+        half = width // 2
+        lower, upper = values[:, :half], values[:, half:]
+        cos_rows, sine_rows = cos_table[part], sine_table[part]
+        return (
+            (lower * cos_rows + upper * sine_rows).astype(jnp.bfloat16),
+            (upper * cos_rows - lower * sine_rows).astype(jnp.bfloat16),
+        )
+
     def stage_four(block):
         across(block).wait_recv()
-        side_out[block] = parts[block, c, h, :, columns(z % 2)].astype(jnp.float32) + z_in[block].astype(jnp.float32)
-
+        total = parts[block, c, h, :, columns(z % 2)].astype(jnp.float32) + z_in[block].astype(jnp.float32)
+        part = pl.ds(block * rows, rows)
+
+        @pl.when(z % 2 == 0)
+        def _():
+            lower, upper = turn_back(total, part)
+            side_out[part, : width // 2] = lower
+            side_out[part, width // 2 :] = upper
+
+        @pl.when(z % 2 == 1)
+        def _():
+            side_out[part] = total.astype(jnp.bfloat16)
+
+    for chip in range(8):
+        mine = notes[2 * chip + c]
+        query_row[chip // 2, :, pl.ds((chip % 2) * rows, rows)] = jnp.where(h == 0, mine[2:3], mine[3:4])
+        for piece in range(4):
+            row = notes[2 * chip + piece // 2, 2 + piece % 2 : 3 + piece % 2, :]
+            key_column[chip, pl.ds(piece * rows, rows)] = column_of(row)
     for load in loads:
         load.wait()
-    grad_query[...] = jnp.zeros_like(grad_query)
+    grad_rot[...] = jnp.zeros_like(grad_rot)
+    for place_at in range(LINE):
+        part = pl.ds(place_at * pair, pair)
+        grad_rows = times_transposed(branch[pl.ds(place_at * 2, 2)].reshape(pair, branch.shape[2]), out_w[...])
+        grad_rows = grad_rows.astype(jnp.bfloat16)
+        grad_out[part] = grad_rows
+        delta = jnp.sum(grad_rows.astype(jnp.float32) * attended[part], axis=1, keepdims=True)
+        delta_row[place_at] = row_of(delta)
+    out_store = out_refs[0]
+
+    @pl.loop(0, 4)
+    def _(tile):
+        tile_columns = pl.ds(pl.multiple_of(tile * 512, 512), 512)
+        part = transposed_times(attended_low[...], branch[:, :, tile_columns].reshape(8 * rows, 512))
+        out_store[:, :, :, tile_columns] = part.astype(jnp.bfloat16).reshape(2, 2, out_store.shape[2], 512)
+
+    outs.share().start()
     for block in range(8):
-        key = keys[block, :, :, :, :width].reshape(rows, width)
-        value = keys[block, :, :, :, width:].reshape(rows, width)
+        key = keys[block, :, :, :, :width].reshape(block_rows, width)
+        value = keys[block, :, :, :, width:].reshape(block_rows, width)
         grad_key[...] = jnp.zeros_like(grad_key)
         grad_value[...] = jnp.zeros_like(grad_value)
 
@@ -1857,16 +1996,24 @@
             grad_scores = (weights * (grad_weights - delta_row[place_at])).astype(jnp.bfloat16)
             grad_key[...] += product(grad_scores, query[part])
             grad_value[...] += product(weights.astype(jnp.bfloat16), grad_out[part])
-            grad_query[place_at] += product(turned[block], grad_scores)
-
-        parts[block, :, :, :, :width] = grad_key[...].astype(jnp.bfloat16).reshape(2, 2, rows // 4, width)
-        parts[block, :, :, :, width:] = grad_value[...].astype(jnp.bfloat16).reshape(2, 2, rows // 4, width)
+            grad_rot[part] += transposed_times(grad_scores, key)
+
+        parts[block, :, :, :, :width] = grad_key[...].astype(jnp.bfloat16).reshape(2, 2, rows, width)
+        parts[block, :, :, :, width:] = grad_value[...].astype(jnp.bfloat16).reshape(2, 2, rows, width)
         share(block).start()
+        if block == 0:
+            outs.relay()
         if block >= 1:
             stage_two(block - 1)
         if block >= 4:
             stage_three(block - 4)
     stage_two(7)
+    outs.send()
+    for place_at in range(LINE):
+        part = pl.ds(place_at * pair, pair)
+        lower, upper = turn_back(grad_rot[part] * HD**-0.5, part)
+        grad_query[part, : width // 2] = lower
+        grad_query[part, width // 2 :] = upper
     for block in range(4, 8):
         stage_three(block)
         stage_four(block - 4)
@@ -1877,9 +2024,10 @@
         over(block).wait_send()
         across(block).wait_send()
     scatter.finish()
-
-
-def attend_back(query, grad_out, keys, keys_turned, log_row, delta_row, query_row, key_column, gate, up):
+    outs.finish()
+
+
+def attend_back(query, keys, branch, out_w, attended, attended_low, log_row, notes, cos_table, sine_table, gate, up, out_rows):
     eight, _, _, rows, width = keys.shape
     tokens = query.shape[0]
     depth, part = gate.shape[1:]
@@ -1890,52 +2038,53 @@
     def shape(*dims, dtype=jnp.bfloat16):
         return jax.ShapeDtypeStruct(dims, dtype)
 
+    f32 = jnp.float32
     return pl.pallas_call(
         attend_back_kernel,
         out_shape=(
-            shape(eight, rows, HD, dtype=jnp.float32),
-            shape(LINE, HD, tokens // LINE, dtype=jnp.float32),
+            shape(tokens, HD),
+            shape(tokens, HD),
             shape(depth, 8 * part),
             shape(depth, 8 * part),
+            shape(out_rows, out_w.shape[1]),
         ),
-        in_specs=[INSIDE, INSIDE, ANY, ANY, INSIDE, INSIDE, INSIDE, INSIDE, INSIDE, INSIDE],
-        out_specs=(INSIDE, INSIDE, ANY, ANY),
+        in_specs=[INSIDE, ANY, ANY] + [INSIDE] * 9,
+        out_specs=(INSIDE, INSIDE, ANY, ANY, ANY),
         scratch_shapes=[
-            room(*keys.shape), room(*keys_turned.shape), room(*keys.shape),
-            room(4 * rows, HD, dtype=jnp.float32), room(4 * rows, HD, dtype=jnp.float32),
+            room(*keys.shape), room(*branch.shape), room(tokens, HD),
+            room(LINE, 1, tokens // LINE, dtype=f32), room(LINE, 1, tokens // LINE, dtype=f32),
+            room(8, 4 * rows, 1, dtype=f32), room(tokens, HD, dtype=f32), room(*keys.shape),
+            room(4 * rows, HD, dtype=f32), room(4 * rows, HD, dtype=f32),
             room(eight, 2, rows, width), room(eight, rows, width), room(eight, rows, HD),
             dma(2),
-        ] + [dma(8)] * 6 + QuarterScatter.scratch(),
+        ] + [dma(8)] * 6 + QuarterScatter.scratch() + OutGrad.scratch(out_rows, out_w.shape[1]),
         compiler_params=kernel_params(11),
         name="attend_back",
-    )(query, grad_out, keys, keys_turned, log_row, delta_row, query_row, key_column, gate, up)
+    )(query, keys, branch, out_w, attended, attended_low, log_row, notes, cos_table, sine_table, gate, up)
 
 
 class HeadGrads:
     @staticmethod
-    def scratch(depth, out_rows, width):
+    def scratch(depth):
         def room(*dims):
             return pltpu.VMEM(dims, jnp.bfloat16)
 
         return [
-            room(8, 2, depth, HD), room(8, 2, depth, HD), room(2, 2, out_rows, width),
-            room(8, depth, HD), room(8, depth, HD), room(2, out_rows, width),
-            room(8, depth, HD), room(8, depth, HD), room(2, out_rows, width),
-            dma(3), dma(3), dma(3), dma(3), dma(3), dma(3, 8), dma(3, 4, 8), dma(2), dma(4),
+            room(8, 2, depth, HD), room(8, 2, depth, HD),
+            room(8, depth, HD), room(8, depth, HD),
+            room(8, depth, HD), room(8, depth, HD),
+            dma(2), dma(2), dma(2), dma(2), dma(3, 8), dma(3, 4, 8), dma(3),
         ]
 
-    def __init__(self, sources, outs, refs):
-        self.sources, self.outs = sources, outs
-        self.store, self.sib, self.box = refs[0:3], refs[3:6], refs[6:9]
-        (self.load_s, self.c_s, self.c_r, self.x_s, self.x_r, self.s, self.r, self.y_sr, self.own) = refs[9:]
+    def __init__(self, outs, refs):
+        self.outs = outs
+        self.store, self.sib, self.box = refs[0:2], refs[2:4], refs[4:6]
+        (self.c_s, self.c_r, self.x_s, self.x_r, self.s, self.r, self.own) = refs[6:]
         self.z, self.y, self.c, self.h = place()
         self.chip = self.z * 2 + self.y
         self.me = device(self.z, self.y, self.c, self.h)
         self.owner = self.h == self.y
 
-    def load(self, i):
-        return local(self.sources[i], self.store[i], self.load_s.at[i])
-
     def share(self, i):
         return remote(
             self.store[i].at[:, 1 - self.c], self.sib[i], self.c_s.at[i], self.c_r.at[i],
@@ -1966,61 +2115,38 @@
         ref = self.target(kind, line)
         return remote(ref, ref, self.s.at[kind, step], self.r.at[kind, line, step], self.me)
 
-    def out_move(self):
-        return remote(
-            self.store[2].at[1 - self.y, self.c], self.outs[3], self.y_sr.at[0], self.y_sr.at[1],
-            device(self.z, 1 - self.y, self.c, self.h),
-        )
-
-    def out_keep(self):
-        return local(self.store[2].at[self.y, self.c], self.outs[3], self.own.at[3])
-
-    def start_loads(self):
-        for i in range(3):
-            self.load(i).start()
-
-    def start(self):
-        for i in (2, 0, 1):
-            self.load(i).wait()
-            self.share(i).start()
-
-    def relay(self):
-        for i in (2, 0, 1):
-            self.share(i).wait_recv()
-
-            @pl.loop(0, self.sib[i].shape[0])
-            def _(at):
-                add_into(self.store[i].at[at, self.c], self.sib[i].at[at])
-
-            @pl.when(jnp.logical_not(self.owner))
-            def _():
-                self.over(i).start()
-
-    def scatter(self):
+    def relay(self, i):
+        self.share(i).wait_recv()
+
+        @pl.loop(0, 8)
+        def _(at):
+            add_into(self.store[i].at[at, self.c], self.sib[i].at[at])
+
+        @pl.when(jnp.logical_not(self.owner))
+        def _():
+            self.over(i).start()
+
+    def scatter(self, i):
         @pl.when(self.owner)
         def _():
-            for i in (2, 0, 1):
-                self.over(i).wait_recv()
-
-                @pl.loop(0, self.sib[i].shape[0])
-                def _(at):
-                    add_into(self.store[i].at[at, self.c], self.box[i].at[at])
-
-                if i == 2:
-                    self.out_move().start()
-                    self.out_keep().start()
-                elif i == 0:
-                    self.keep(0).start()
-                    for step in range(1, 8):
-                        self.push(0, step).start()
-                else:
-                    for kind in (1, 2):
-
-                        @pl.when(self.z % 2 == kind - 1)
-                        def _():
-                            self.keep(kind).start()
-                            for step in range(1, 8):
-                                self.push(kind, step).start()
+            self.over(i).wait_recv()
+
+            @pl.loop(0, 8)
+            def _(at):
+                add_into(self.store[i].at[at, self.c], self.box[i].at[at])
+
+            if i == 0:
+                self.keep(0).start()
+                for step in range(1, 8):
+                    self.push(0, step).start()
+            else:
+                for kind in (1, 2):
+
+                    @pl.when(self.z % 2 == kind - 1)
+                    def _():
+                        self.keep(kind).start()
+                        for step in range(1, 8):
+                            self.push(kind, step).start()
 
     def finish(self):
         for kind in range(3):
@@ -2039,14 +2165,11 @@
 
         @pl.when(jnp.logical_not(self.owner))
         def _():
-            remote(self.outs[3], self.outs[3], self.y_sr.at[0], self.y_sr.at[1], self.me).wait_recv()
-            for i in range(3):
+            for i in range(2):
                 self.over(i).wait_send()
 
         @pl.when(self.owner)
         def _():
-            self.out_keep().wait()
-            self.out_move().wait_send()
             for step in range(1, 8):
                 self.push(0, step).wait_send()
             for kind in (1, 2):
@@ -2056,92 +2179,144 @@
                     for step in range(1, 8):
                         self.push(kind, step).wait_send()
 
-        for i in range(3):
+        for i in range(2):
             self.share(i).wait_send()
 
 
-def reduce_heads_kernel(
-    parts_in, query_in, side_in, out_in, out, query, key, value, outw, parts, in_sem, *refs
+class GainSum:
+    @staticmethod
+    def scratch(rows):
+        return [
+            pltpu.VMEM((16, 8, rows), jnp.float32), pltpu.VMEM((32, 8, rows), jnp.float32), dma(32), dma(32),
+        ]
+
+    def __init__(self, out, refs):
+        self.out = out
+        self.terms, self.box, self.s, self.r = refs
+        self.blk, self.h = lax.axis_index("blk"), lax.axis_index("head")
+
+    def push(self, step):
+        other = (self.blk + step // 2) % 16
+        return remote(
+            self.terms.at[other], self.box.at[step], self.s.at[step], self.r.at[step], (other, (self.h + step % 2) % 2)
+        )
+
+    def start(self, attn_term, mlp_term):
+        rows = self.terms.shape[2]
+        self.terms[...] = jnp.zeros_like(self.terms)
+        for blk in range(16):
+            part = pl.ds(blk * rows, rows)
+            self.terms[blk, 0:1] = attn_term[:, part]
+            self.terms[blk, 1:2] = mlp_term[:, part]
+        for step in range(1, 32):
+            self.push(step).start()
+
+    def finish(self):
+        total = self.terms[self.blk]
+        for step in range(1, 32):
+            self.push(step).wait_recv()
+            total += self.box[step]
+        self.out[...] = total
+        for step in range(1, 32):
+            self.push(step).wait_send()
+
+
+def close_kernel(
+    normed_in, qkv_w, grad_query, grad_side, grad_hidden, tokens, gain, mlp_term,
+    tokens_grad, gains, query, key, value,
+    normed, weight, parts, grad_normed, attn_term, load_s, *refs,
 ):
-    reduce_refs, head_refs = split_refs(refs, (9, 18))
-    load = pltpu.make_async_copy(parts_in, parts, in_sem)
+    reduce_refs, head_refs, gain_refs = split_refs(refs, (9, 13, 4))
+    z, y, c, h = place()
+    load = local(normed_in, normed, load_s.at[0])
+    load_q = local(qkv_w.at[:, :, :, pl.ds(0, HD)], weight.at[0], load_s.at[1])
+    side_columns = pl.ds(pl.multiple_of((1 + z % 2) * HD, HD), HD)
+    load_side = local(qkv_w.at[:, :, :, side_columns], weight.at[1], load_s.at[2])
+    load_q.start()
+    load_side.start()
     load.start()
-    heads = HeadGrads((query_in, side_in, out_in), (query, key, value, outw), head_refs)
-    heads.start_loads()
     greet_all(16, 2)
     reduce = Reduce(parts, reduce_refs)
+    heads = HeadGrads((query, key, value), head_refs)
+    gain_sum = GainSum(gains, gain_refs)
+    rows, width = parts.shape[1:]
+    pair = 2 * rows
+    depth = head_refs[0].shape[2]
+    load_q.wait()
+    load_side.wait()
+    for place_at in range(4):
+        line = reduce.order[place_at]
+        both = pl.ds(pl.multiple_of(line * pair, pair), pair)
+
+        @pl.loop(0, 4)
+        def _(tile):
+            columns = pl.ds(pl.multiple_of(tile * (width // 4), width // 4), width // 4)
+            part = times_transposed(grad_query[both], weight[0, pl.ds(tile * 2, 2)].reshape(width // 4, HD))
+            part += times_transposed(grad_side[both], weight[1, pl.ds(tile * 2, 2)].reshape(width // 4, HD))
+            parts[pl.ds(line * 2, 2), :, columns] = part.astype(jnp.bfloat16).reshape(2, rows, width // 4)
+
+        reduce.start(place_at)
     load.wait()
-    for place_at in range(4):
-        reduce.start(place_at)
-    heads.start()
-    heads.relay()
+    for i, source in enumerate((grad_query, grad_side)):
+
+        @pl.loop(0, 4)
+        def _(tile):
+            columns = pl.ds(pl.multiple_of(tile * 4 * depth, 4 * depth), 4 * depth)
+            part = transposed_times(normed[:, columns], source[...])
+            head_refs[i][pl.ds(tile * 2, 2)] = part.astype(jnp.bfloat16).reshape(2, 2, depth, HD)
+
+        heads.share(i).start()
+    heads.relay(0)
+    heads.relay(1)
     reduce.relay(0)
     reduce.relay(1)
-    heads.scatter()
+    heads.scatter(0)
     reduce.relay(2)
-    reduce.total(out)
+    heads.scatter(1)
+    reduce.total(grad_normed)
+    inputs = tokens[...].astype(jnp.float32)
+    inv_scale = rms_scale(inputs)
+    unit_rows = inputs * inv_scale
+    attn_term[...] = jnp.sum(grad_normed[...] * unit_rows, axis=0, keepdims=True)
+    gain_sum.start(attn_term, mlp_term)
+    grad_unit = grad_normed[...] * gain[...]
+    mean = jnp.mean(grad_unit * unit_rows, axis=-1, keepdims=True)
+    tokens_grad[...] = (grad_hidden[...] + inv_scale * (grad_unit - unit_rows * mean)).astype(jnp.bfloat16)
     heads.finish()
     reduce.finish()
-
-
-def reduce_heads(parts, query, side, outw):
-    shape = parts.shape
-    depth = query.shape[2]
-    out_rows, width = outw.shape[2:]
-
-    def room(*dims):
-        return jax.ShapeDtypeStruct(dims, jnp.bfloat16)
-
+    gain_sum.finish()
+
+
+def close(normed, qkv_w, grad_query, grad_side, grad_hidden, tokens, gain, mlp_term):
+    rows, width = tokens.shape
+    depth = qkv_w.shape[2]
+
+    def room(*dims, dtype=jnp.bfloat16):
+        return pltpu.VMEM(dims, dtype)
+
+    def shape(*dims, dtype=jnp.bfloat16):
+        return jax.ShapeDtypeStruct(dims, dtype)
+
+    f32 = jnp.float32
     return pl.pallas_call(
-        reduce_heads_kernel,
+        close_kernel,
         out_shape=(
-            jax.ShapeDtypeStruct(shape[1:], jnp.float32),
-            room(depth, 4 * HD), room(depth, 2 * HD), room(depth, 2 * HD), room(out_rows, width),
+            shape(rows, width),
+            shape(8, rows, dtype=f32),
+            shape(depth, 4 * HD), shape(depth, 2 * HD), shape(depth, 2 * HD),
         ),
-        in_specs=[ANY] * 4,
-        out_specs=(INSIDE, ANY, ANY, ANY, ANY),
-        scratch_shapes=[pltpu.VMEM(shape, jnp.bfloat16), dma()]
-        + Reduce.scratch(shape[2])
-        + HeadGrads.scratch(depth, out_rows, width),
+        in_specs=[ANY, ANY] + [INSIDE] * 6,
+        out_specs=(INSIDE, INSIDE, ANY, ANY, ANY),
+        scratch_shapes=[
+            room(*normed.shape), room(2, 8, 2, depth, HD), room(8, rows, width),
+            room(rows, width, dtype=f32), room(1, width, dtype=f32), dma(3),
+        ]
+        + Reduce.scratch(width)
+        + HeadGrads.scratch(depth)
+        + GainSum.scratch(rows),
         compiler_params=kernel_params(6),
-        name="reduce_heads",
-    )(parts, query, side, outw)
-
-
-def gains_kernel(gains, out, box, own, send_sems, recv_sems):
-    blk, h = lax.axis_index("blk"), lax.axis_index("head")
-    greet_all(16, 2)
-
-    def push(step):
-        other = (blk + step // 2) % 16
-        return remote(
-            gains.at[other], box.at[step], send_sems.at[step], recv_sems.at[step], (other, (h + step % 2) % 2)
-        )
-
-    keep = local(gains.at[blk], box.at[0], own.at[0])
-    keep.start()
-    for step in range(1, 32):
-        push(step).start()
-    keep.wait()
-    total = box[0]
-    for step in range(1, 32):
-        push(step).wait_recv()
-        total += box[step]
-    out[...] = total
-    for step in range(1, 32):
-        push(step).wait_send()
-
-
-def reduce_gains(gains):
-    return pl.pallas_call(
-        gains_kernel,
-        out_shape=jax.ShapeDtypeStruct(gains.shape[1:], gains.dtype),
-        in_specs=[INSIDE],
-        out_specs=INSIDE,
-        scratch_shapes=[pltpu.VMEM((32,) + gains.shape[1:], gains.dtype), dma(1), dma(32), dma(32)],
-        compiler_params=kernel_params(12),
-        name="reduce_gains",
-    )(gains)
+        name="close",
+    )(normed, qkv_w, grad_query, grad_side, grad_hidden, tokens, gain, mlp_term)
 
 
 def fast_body(
@@ -2159,13 +2334,9 @@
     positions,
     cotangent,
 ):
-    z, y, core, half = place()
     rows, width = tokens.shape
     token_rows = 8 * rows
     f32, bf16 = jnp.float32, jnp.bfloat16
-
-    def own_half(values):
-        return lax.dynamic_index_in_dim(values, half, 0, False)
 
     note = jnp.concatenate(
         [
@@ -2181,89 +2352,43 @@
         keys_values, normed, qkv_w, out_w, notes, cos_table, sine_table, scaled_query, attended, attended_low,
         log_total, cot_all, gate_w, up_w,
     ) = front(tokens, cotangent, note, inv_freqs[None], w_query, w_key, w_value, w_out, w_gate, w_up)
-    qkv_w = qkv_w.reshape(width, 3 * HD)
     out_w = out_w.reshape(HD, width)
     gain_attn = notes[:, 4].reshape(1, width)
     gain_mlp = notes[:, 5].reshape(1, width)
-    mine = lax.dynamic_index_in_dim(notes.reshape(8, 2, 8, rows), core, 1, False)
-    ids_mine = lax.dynamic_index_in_dim(mine[:, 2:4], half, 1, False).reshape(token_rows)
-    key_ids = notes[:, 2:4].reshape(32 * rows)
-    score_scale = HD ** (-0.5)
-    branch, gate_w, up_w = reduce_share(attended_low, out_w, gate_w, up_w)
-    hidden_part = gate_w.shape[3]
-    gate_w = gate_w.reshape(width, hidden_part)
-    up_w = up_w.reshape(width, hidden_part)
-
-    inputs = tokens.astype(f32)
-    inv_attn = rms_scale(inputs)
-    hidden = inputs + branch
-    inv_mlp = rms_scale(hidden)
-    mlp_own, normed_mlp, active, grad_gate, grad_up, grad_normed_part = run_mlp(
-        (hidden * inv_mlp * gain_mlp).astype(bf16), w_down, gate_w, up_w, cot_all
-    )
-    output = (hidden + mlp_own).astype(bf16)
-    normed_mlp = normed_mlp.reshape(token_rows, width)
-    active = active.reshape(token_rows, hidden_part)
-    grad_gate = grad_gate.reshape(token_rows, hidden_part)
-    grad_up = grad_up.reshape(token_rows, hidden_part)
-    cot_all = cot_all.reshape(token_rows, width)
-    depth = w_query.shape[0]
-    grad_normed_mlp, gate_quarter, up_quarter = reduce_grads(
+    output, hidden, normed_mlp, active, grad_gate, grad_up, grad_normed_part = mid(
+        attended_low, out_w, gate_w, up_w, w_down, tokens, gain_mlp, cot_all
+    )
+    hidden_part = active.shape[2]
+    grad_branch, grad_hidden, mlp_term, gate_quarter, up_quarter, down_grad = turn(
         grad_normed_part,
-        transposed_times(normed_mlp, grad_gate).astype(bf16).reshape(8, 2, depth, hidden_part),
-        transposed_times(normed_mlp, grad_up).astype(bf16).reshape(8, 2, depth, hidden_part),
-    )
-    grad_down_w = transposed_times(active, cot_all).astype(bf16)
-    grad_hidden_norm, gain_mlp_term = norm_backward(grad_normed_mlp, hidden, inv_mlp, gain_mlp)
-    grad_hidden = cotangent.astype(f32) + grad_hidden_norm
-
-    grad_branch, down_grad = gather_grads(
-        grad_hidden.astype(bf16), grad_down_w.reshape(2, 2, w_down.shape[0], width)
-    )
-    grad_branch = grad_branch.reshape(token_rows, width)
-    grad_out_w = transposed_times(attended_low, grad_branch)
-    grad_attended = times_transposed(grad_branch, out_w).astype(bf16)
-    delta = jnp.sum(grad_attended.astype(f32) * attended, axis=-1)
-    keys_turned = jnp.swapaxes(keys_values[..., :HD].reshape(8, 4 * rows, HD), 1, 2)
-    side, grad_query_rot, gate_grad, up_grad = attend_back(
+        normed_mlp.reshape(token_rows, width),
+        grad_gate.reshape(token_rows, hidden_part),
+        grad_up.reshape(token_rows, hidden_part),
+        active.reshape(token_rows, hidden_part),
+        cot_all.reshape(token_rows, width),
+        hidden,
+        gain_mlp,
+        cotangent,
+    )
+
+    side_grad, grad_query, gate_grad, up_grad, out_grad = attend_back(
         scaled_query,
-        grad_attended,
         keys_values,
-        keys_turned,
-        log_total.reshape(LINE, 1, token_rows // LINE),
-        delta.reshape(LINE, 1, token_rows // LINE),
-        ids_mine.reshape(LINE, 1, token_rows // LINE),
-        key_ids.reshape(8, 4 * rows, 1),
+        grad_branch,
+        out_w,
+        attended,
+        attended_low,
+        log_total,
+        notes,
+        cos_table,
+        sine_table,
         gate_quarter,
         up_quarter,
-    )
-    side = side.reshape(token_rows, HD)
-    grad_query_rot = jnp.swapaxes(grad_query_rot, 1, 2).reshape(token_rows, HD) * score_scale
-    is_key = z % 2 == 0
-    side_grad = jnp.where(is_key, rotate(side, cos_table, -sine_table), side).astype(bf16)
-    grad_query = rotate(grad_query_rot, cos_table, -sine_table).astype(bf16)
-    side_w = jnp.where(is_key, qkv_w[:, HD : 2 * HD], qkv_w[:, 2 * HD :])
-    grad_normed_part = times_transposed(grad_query, qkv_w[:, :HD]) + times_transposed(
-        side_grad, side_w
-    )
-    grad_normed, query_grad, key_grad, value_grad, out_grad = reduce_heads(
-        grad_normed_part.astype(bf16).reshape(8, rows, width),
-        transposed_times(normed, grad_query).astype(bf16).reshape(8, 2, depth, HD),
-        transposed_times(normed, side_grad).astype(bf16).reshape(8, 2, depth, HD),
-        grad_out_w.astype(bf16).reshape(2, 2, w_out.shape[0], width),
-    )
-    grad_inputs_norm, gain_attn_term = norm_backward(grad_normed, inputs, inv_attn, gain_attn)
-    tokens_grad = (grad_hidden + grad_inputs_norm).astype(bf16)
-
-    gains = jnp.concatenate(
-        [
-            gain_attn_term.reshape(16, 1, rows),
-            gain_mlp_term.reshape(16, 1, rows),
-            jnp.zeros((16, 6, rows), f32),
-        ],
-        axis=1,
-    )
-    gain_grads = reduce_gains(gains)
+        w_out.shape[0],
+    )
+    tokens_grad, gain_grads, query_grad, key_grad, value_grad = close(
+        normed, qkv_w, grad_query, side_grad, grad_hidden, tokens, gain_attn, mlp_term
+    )
     return (
         output,
         tokens_grad,

time: 664 us -> 578 us (0.87)
  matrix products: 43.3 us -> 0 us
  Pallas kernels: 568 us -> 549 us
  other arithmetic: 25.2 us -> 10.8 us
  local copies, waits for them, and re-layouts: 15.9 us -> 6.35 us
    dot_general x9 -> x0, matrix products: 43.3 us -> none  [the longest x6 33.6 us: transposed_times(): lax.dot_general(left, right, (((0,), (0,)), ((), ())), preferred_element_...]
    pallas_call x7 -> x4, Pallas kernels: 415 us -> 396 us  [the longest x1 160 us: mid(): pl.pallas_call(mid_kernel, out_shape=(shape(rows, width), shape(rows, wid...]
    convert_element_type x4 -> x0, other arithmetic: 7.8 us -> none  [the longest x1 3.08 us: fast_body(): tokens_grad = (grad_hidden + grad_inputs_norm).astype(bf16)]
where the time goes in v4:
time: 578 us; the launch traced here: 567 us
  Pallas kernels  549 us (95%)
  other arithmetic  10.8 us (2%)
  local copies, waits for them, and re-layouts  6.35 us (1%)
    pallas_call x1, Pallas kernels, mid(): pl.pallas_call(mid_kernel, out_shape=(shape(rows, width), shape(rows, wid...  160 us
    pallas_call x1, Pallas kernels, front(): pl.pallas_call(front_kernel, out_shape=(shape(8, 2, 2, rows, 2 * HD), sha...  153 us
    pallas_call x1, Pallas kernels, turn(): pl.pallas_call(turn_kernel, out_shape=(shape(eight, rows, width), shape(r...  96.9 us
    pallas_call x1, Pallas kernels, close(): pl.pallas_call(close_kernel, out_shape=(shape(rows, width), shape(8, rows...  81 us
    pallas_call x1, Pallas kernels, attend_back(): pl.pallas_call(attend_back_kernel, out_shape=(shape(tokens, HD), shape(to...  58 us

profile of v4, /device:TPU:8, one launch (start us, length us, event | category | flops | bytes accessed | tf_op | source)
XLA Modules:
  0.0 567.3 jit_solution(5367822974305252369)
XLA Ops:
  0.6 0.5 multiply_power_fusion.inv_freqs
  1.2 0.7 bitcast_convert_fusion
  1.8 0.7 convert_bitcast_fusion
  2.5 0.6 concatenate.3.note
  3.2 152.8 %front.1 = (bf16[8,2,2,128,512]{4,3,2,1,0:T(8,128)(2,1)}, bf16[1024,2048]{1,0:T(8,128)(2,1)}, bf16[8,2,128,768]{3,2,1,0:T(8,128)(2,1)}, bf16[2,2,64,2048]{3,2,1,...) custom-call(bf16[128,2048]{1,0:T(8,128)(2,1)} %tokens.5, ...), custom_call_target="tpu_custom_call" | custom-call | tf_op jit(solution)/shard_map/front/pallas_call | solution.py:1476
  155.9 1.5 slice_bitcast_fusion
  157.5 160.3 %mid.1 = (bf16[128,2048]{1,0:T(8,128)(2,1)}, f32[128,2048]{1,0:T(8,128)}, bf16[8,128,2048]{2,1,0:T(8,128)(2,1)}, bf16[8,128,1024]{2,1,0:T(8,128)(2,1)}, bf16[8,1...) custom-call(bf16[1024,256]{1,0:T(8,128)(2,1)} %get-tuple-element.48.attended.attended_low, ...), custom_call_target="tpu_custom_call" | custom-call | tf_op jit(solution)/shard_map/mid/pallas_call | solution.py:1255
  317.7 96.9 %turn.1 = (bf16[8,128,2048]{2,1,0:T(8,128)(2,1)}, f32[128,2048]{1,0:T(8,128)}, f32[1,2048]{1,0:T(1,128)}, bf16[8,128,512]{2,1,0:T(8,128)(2,1)}, bf16[8,128,512]{2,1,0:T(8,128)(2,1)}, /*index=5*/f32[256,2048]{1,0:T(8,128)}) custom-call(bf16[8,128,2048]{2,1,0:T(8,128)(2,1)} %get-tuple-element.59.parts_in, bf16[1024,2048]{1,0:T(8,128)(2,1)} %bitcast.25, ...), custom_call_target="tpu_custom_call" | custom-call | tf_op jit(solution)/shard_map/turn/pallas_call | solution.py:1791
  414.7 58.0 %attend_back.1 = (bf16[1024,256]{1,0:T(8,128)(2,1)}, bf16[1024,256]{1,0:T(8,128)(2,1)}, bf16[128,4096]{1,0:T(8,128)(2,1)}, bf16[128,4096]{1,0:T(8,128)(2,1)}, bf16[64,2048]{1,0:T(8,128)(2,1)}) custom-call(bf16[1024,256]{1,0:T(8,128)(2,1)} %get-tuple-element.57.query, bf16[8,2,2,128,512]{4,3,2,1,0:T(8,128)(2,1)} %get-tuple-element.58.keys_in, ...), custom_call_target="tpu_custom_call" | custom-call | tf_op jit(solution)/shard_map/attend_back/pallas_call | solution.py:2042
  472.7 0.0 copy-start.5
  472.7 0.0 copy-start.2
  472.7 81.0 %close.1 = (bf16[128,2048]{1,0:T(8,128)(2,1)}, f32[8,128]{1,0:T(8,128)}, bf16[128,1024]{1,0:T(8,128)(2,1)}, bf16[128,512]{1,0:T(8,128)(2,1)}, bf16[128,512]{1,0:T(8,128)(2,1)}) custom-call(bf16[1024,2048]{1,0:T(8,128)(2,1)} %get-tuple-element.55.normed_in, bf16[8,2,128,768]{3,2,1,0:T(8,128)(2,1)} %get-tuple-element.56.qkv_w, ...), custom_call_target="tpu_custom_call" | custom-call | tf_op jit(solution)/shard_map/close/pallas_call | solution.py:2301
  553.7 0.0 copy-start.1
  553.7 1.3 slice_bitcast_fusion.2
  555.0 1.6 convert_element_type.29
  556.6 1.6 convert_element_type.30
  558.2 1.8 convert_element_type.28
  560.0 0.0 copy-done.5
  560.0 0.8 convert_element_type.31
  560.9 0.0 copy-done.2
  560.9 0.0 copy-start.3
  560.9 0.0 copy-start.4
  560.9 1.5 convert_element_type.32
  562.4 0.0 copy-done.1
  562.4 0.0 copy-start
  562.4 1.5 convert_element_type.33
  563.9 0.0 copy-done.3
  563.9 0.8 copy.27
  564.7 0.0 copy-done.4
  564.7 0.8 copy.28
  565.5 0.0 copy-done
  565.5 1.3 copy.29
  (1 shorter events, 0.0 us)
Async XLA Ops:
  472.7 87.4 %copy-start.5 = (bf16[64,2048]{1,0:T(8,128)(2,1)S(1)}, bf16[64,2048]{1,0:T(8,128)(2,1)}, u32[]{:S(2)}) copy-start(bf16[64,2048]{1,0:T(8,128)(2,1)} %get-tuple-element.81) | copy-start | bytes 786436
  472.7 88.2 %copy-start.2 = (bf16[128,4096]{1,0:T(8,128)(2,1)S(1)}, bf16[128,4096]{1,0:T(8,128)(2,1)}, u32[]{:S(2)}) copy-start(bf16[128,4096]{1,0:T(8,128)(2,1)} %get-tuple-element.82) | copy-start | bytes 3145732
  553.7 8.7 %copy-start.1 = (bf16[128,4096]{1,0:T(8,128)(2,1)S(1)}, bf16[128,4096]{1,0:T(8,128)(2,1)}, u32[]{:S(2)}) copy-start(bf16[128,4096]{1,0:T(8,128)(2,1)} %get-tuple-element.83) | copy-start | bytes 3145732
  560.9 3.1 copy-start.3
  560.9 3.9 copy-start.4
  562.4 3.1 copy-start

commit v5 on v4

--- a/solution.py
+++ b/solution.py
@@ -556,14 +556,6 @@
                     self.down(step, elem).wait_send()
 
 
-def gather_kernel(src, out, *sems):
-    greet_plane()
-    gather = Gather(src, out, sems)
-    gather.start()
-    gather.relays()
-    gather.finish()
-
-
 ANY = pl.BlockSpec(memory_space=pl.ANY)
 INSIDE = pl.BlockSpec(memory_space=pltpu.VMEM)
 
@@ -574,30 +566,33 @@
     )
 
 
-def gather_plane(rows):
-    return pl.pallas_call(
-        gather_kernel,
-        out_shape=jax.ShapeDtypeStruct((2 * LINE,) + rows.shape, rows.dtype),
-        in_specs=[INSIDE],
-        out_specs=ANY,
-        scratch_shapes=Gather.scratch(),
-        compiler_params=kernel_params(1),
-        name="gather_plane",
-    )(rows)
+def add_into(target, *others):
+    total = target[...].astype(jnp.float32)
+    for other in others:
+        total += other[...].astype(jnp.float32)
+    target[...] = total.astype(target.dtype)
 
 
 class Reduce:
-    CUTS = ((0, 64), (64, 64))
+    CUTS = ((0, 64), (64, 48))
+    LAST = (112, 16)
 
     @staticmethod
     def scratch(width):
-        inbox = pltpu.VMEM((LINE, 128, width), jnp.bfloat16)
-        return [inbox] * 3 + [pltpu.SemaphoreType.DMA((LINE, 2))] * 6
+        inbox = pltpu.VMEM((LINE, 112, width), jnp.bfloat16)
+        last = pltpu.VMEM((LINE, 2, 16, width), jnp.bfloat16)
+        sems = [pltpu.SemaphoreType.DMA((LINE, 2))] * 10 + [pltpu.SemaphoreType.DMA((2,))]
+        return [inbox] * 3 + [last] * 2 + [pltpu.VMEM((16, width), jnp.bfloat16)] + sems
+
+    COUNT = 17
 
     def __init__(self, parts, refs):
         self.parts = parts
-        self.y_in, self.up_in, self.dn_in = refs[:3]
-        self.y_s, self.y_r, self.up_s, self.up_r, self.dn_s, self.dn_r = refs[3:]
+        self.y_in, self.up_in, self.dn_in, self.up_last, self.dn_last, self.y_last = refs[:6]
+        (
+            self.y_s, self.y_r, self.up_s, self.up_r, self.dn_s, self.dn_r,
+            self.ul_s, self.ul_r, self.dl_s, self.dl_r, self.yl_sr,
+        ) = refs[6:]
         self.z, self.y, self.c, self.h = place()
         z = self.z
         self.order = (3 - 3 * (z // 2), (2 + 3 * z) % 5, 1 + z % 2, z)
@@ -623,36 +618,74 @@
             self.dn_s.at[line, cut], self.dn_r.at[line, cut], device(self.z - 1, self.y, self.c, self.h),
         )
 
+    def last(self, line, column):
+        return self.parts.at[line * 2 + column, pl.ds(*self.LAST)]
+
+    def last_up(self, line, column):
+        return remote(
+            self.last(line, column), self.up_last.at[line, column], self.ul_s.at[line, column],
+            self.ul_r.at[line, column], device(self.z + 1, self.y, self.c, self.h),
+        )
+
+    def last_down(self, line, column):
+        return remote(
+            self.last(line, column), self.dn_last.at[line, column], self.dl_s.at[line, column],
+            self.dl_r.at[line, column], device(self.z - 1, self.y, self.c, self.h),
+        )
+
+    def last_across(self):
+        return remote(
+            self.last(self.z, 1 - self.y), self.y_last, self.yl_sr.at[0], self.yl_sr.at[1],
+            device(self.z, 1 - self.y, self.c, self.h),
+        )
+
     def start(self, place_at):
+        line = self.order[place_at]
         for cut in range(2):
-            self.across(self.order[place_at], cut).start()
-
-    def own(self, line, cut):
-        return self.parts.at[line * 2 + self.y, self.rows(cut)]
+            self.across(line, cut).start()
+
+        @pl.when(jnp.logical_and(line > self.z, self.z == 0))
+        def _():
+            for column in range(2):
+                self.last_up(line, column).start()
+
+        @pl.when(jnp.logical_and(line < self.z, self.z == LINE - 1))
+        def _():
+            for column in range(2):
+                self.last_down(line, column).start()
+
+    def relay_last(self, line):
+        @pl.when(jnp.logical_and(line > self.z, self.z > 0))
+        def _():
+            for column in range(2):
+                self.last_up(line, column).wait_recv()
+                add_into(self.last(line, column), self.up_last.at[line, column])
+                self.last_up(line, column).start()
+
+        @pl.when(jnp.logical_and(line < self.z, self.z < LINE - 1))
+        def _():
+            for column in range(2):
+                self.last_down(line, column).wait_recv()
+                add_into(self.last(line, column), self.dn_last.at[line, column])
+                self.last_down(line, column).start()
 
     def relay(self, place_at):
         line = self.order[place_at]
         for cut in range(2):
             rows = self.rows(cut)
             self.across(line, cut).wait_recv()
-            target = self.parts.at[line * 2 + self.y]
+            target = self.parts.at[line * 2 + self.y, rows]
 
             @pl.when(line > self.z)
             def _():
                 @pl.when(self.z > 0)
                 def _():
                     self.up(line, cut).wait_recv()
-                    total = (
-                        target[rows].astype(jnp.float32)
-                        + self.y_in[line, rows].astype(jnp.float32)
-                        + self.up_in[line, rows].astype(jnp.float32)
-                    )
-                    target[rows] = total.astype(jnp.bfloat16)
+                    add_into(target, self.y_in.at[line, rows], self.up_in.at[line, rows])
 
                 @pl.when(self.z == 0)
                 def _():
-                    total = target[rows].astype(jnp.float32) + self.y_in[line, rows].astype(jnp.float32)
-                    target[rows] = total.astype(jnp.bfloat16)
+                    add_into(target, self.y_in.at[line, rows])
 
                 self.up(line, cut).start()
 
@@ -661,26 +694,39 @@
                 @pl.when(self.z < LINE - 1)
                 def _():
                     self.down(line, cut).wait_recv()
-                    total = (
-                        target[rows].astype(jnp.float32)
-                        + self.y_in[line, rows].astype(jnp.float32)
-                        + self.dn_in[line, rows].astype(jnp.float32)
-                    )
-                    target[rows] = total.astype(jnp.bfloat16)
+                    add_into(target, self.y_in.at[line, rows], self.dn_in.at[line, rows])
 
                 @pl.when(self.z == LINE - 1)
                 def _():
-                    total = target[rows].astype(jnp.float32) + self.y_in[line, rows].astype(jnp.float32)
-                    target[rows] = total.astype(jnp.bfloat16)
+                    add_into(target, self.y_in.at[line, rows])
 
                 self.down(line, cut).start()
+
+            if cut == 0:
+                self.relay_last(line)
 
     def total(self, out):
         line = self.z
+        last = pl.ds(*self.LAST)
+        own, other = line * 2 + self.y, line * 2 + 1 - self.y
+
+        @pl.when(self.z > 0)
+        def _():
+            for column in range(2):
+                self.last_up(line, column).wait_recv()
+                add_into(self.last(line, column), self.up_last.at[line, column])
+
+        @pl.when(self.z < LINE - 1)
+        def _():
+            for column in range(2):
+                self.last_down(line, column).wait_recv()
+                add_into(self.last(line, column), self.dn_last.at[line, column])
+
+        self.last_across().start()
         for cut in range(2):
             rows = self.rows(cut)
             self.across(line, cut).wait_recv()
-            out[rows] = self.parts[line * 2 + self.y, rows].astype(jnp.float32) + self.y_in[line, rows].astype(jnp.float32)
+            out[rows] = self.parts[own, rows].astype(jnp.float32) + self.y_in[line, rows].astype(jnp.float32)
         for cut in range(2):
             rows = self.rows(cut)
 
@@ -694,6 +740,9 @@
                 self.down(line, cut).wait_recv()
                 out[rows] += self.dn_in[line, rows].astype(jnp.float32)
 
+        self.last_across().wait_recv()
+        out[last] = self.parts[own, last].astype(jnp.float32) + self.y_last[...].astype(jnp.float32)
+
     def finish(self):
         for line in range(LINE):
             for cut in range(2):
@@ -702,37 +751,14 @@
                 @pl.when(self.z < line)
                 def _():
                     self.up(line, cut).wait_send()
+                    self.last_up(line, cut).wait_send()
 
                 @pl.when(self.z > line)
                 def _():
                     self.down(line, cut).wait_send()
-
-
-def reduce_kernel(parts_in, out, parts, in_sem, *refs):
-    load = pltpu.make_async_copy(parts_in, parts, in_sem)
-    load.start()
-    greet_plane()
-    reduce = Reduce(parts, refs)
-    load.wait()
-    for place_at in range(4):
-        reduce.start(place_at)
-    for place_at in range(3):
-        reduce.relay(place_at)
-    reduce.total(out)
-    reduce.finish()
-
-
-def reduce_plane(parts):
-    shape = parts.shape
-    return pl.pallas_call(
-        reduce_kernel,
-        out_shape=jax.ShapeDtypeStruct(shape[1:], jnp.float32),
-        in_specs=[ANY],
-        out_specs=INSIDE,
-        scratch_shapes=[pltpu.VMEM(shape, jnp.bfloat16), pltpu.SemaphoreType.DMA] + Reduce.scratch(shape[2]),
-        compiler_params=kernel_params(2),
-        name="reduce_plane",
-    )(parts)
+                    self.last_down(line, cut).wait_send()
+
+        self.last_across().wait_send()
 
 
 def dma(*shape):
@@ -745,14 +771,20 @@
 
 class AttnSpread:
     @staticmethod
-    def scratch():
-        return [dma(3, 4), dma(3, 4), dma(3, 8), dma(3), dma(4), dma(4), dma(4), dma(4), dma(4), dma(4)]
-
-    def __init__(self, weights, outs, sems):
+    def scratch(depth):
+        return [pltpu.VMEM((LINE, depth, 3 * HD), jnp.bfloat16)] + [
+            dma(3, 4), dma(3, 4), dma(3), dma(4), dma(4), dma(4), dma(4), dma(4), dma(4), dma(4), dma(4), dma(4), dma(4),
+        ]
+
+    COUNT = 14
+
+    def __init__(self, weights, outs, refs):
         self.weights, (self.qkv, self.out_w) = weights, outs
-        (self.s, self.f_s, self.r, self.own, self.x_s, self.x_r, self.c_s, self.c_r, self.o_s, self.o_r) = sems
+        (
+            self.stage, self.s, self.r, self.own, self.x_s, self.x_r, self.a_s, self.a_r, self.b_s, self.b_r,
+            self.c_s, self.c_r, self.o_s, self.o_r,
+        ) = refs
         self.z, self.y, self.c, self.h = place()
-        self.chip = self.z * 2 + self.y
         self.me = device(self.z, self.y, self.c, self.h)
         self.owner = self.h == self.y
 
@@ -760,39 +792,50 @@
         start = line * HD if kind == 0 else (line // 2) * HD
         return self.weights[kind].at[:, pl.ds(pl.multiple_of(start, HD), HD)]
 
-    def slot(self, kind, chip):
-        return self.qkv.at[chip, self.c, :, pl.ds(kind * HD, HD)]
-
-    def push(self, kind, step):
+    def slot(self, kind, line, owner):
+        columns = pl.ds(kind * HD, HD)
+        if owner:
+            return self.qkv.at[line * 2 + self.y, self.c, :, columns]
+        return self.stage.at[line, :, columns]
+
+    def push(self, kind, step, owner):
         line = (self.z + step) % LINE
         return remote(
-            self.source(kind, line), self.slot(kind, self.chip), self.s.at[kind, step], self.r.at[kind, self.chip],
-            device(line, self.h, self.c, self.h),
-        )
-
-    def push_far(self, kind, step):
-        line = (self.z + step) % LINE
-        return remote(
-            self.source(kind, line), self.slot(kind, self.chip), self.f_s.at[kind, step], self.r.at[kind, self.chip],
-            device(line, self.h, self.c, 1 - self.h),
-        )
-
-    def keep(self, kind):
-        return local(self.source(kind, self.z), self.slot(kind, self.chip), self.own.at[kind])
-
-    def pull(self, kind, chip):
-        ref = self.slot(kind, chip)
-        return remote(ref, ref, self.s.at[kind, 0], self.r.at[kind, chip], self.me)
-
-    def near(self, step):
-        return ((self.z + LINE - step) % LINE) * 2 + self.y
-
-    def far(self, step):
-        return ((self.z + LINE - step) % LINE) * 2 + 1 - self.y
-
-    def over(self, step):
-        ref = self.qkv.at[self.near(step), self.c]
-        return remote(ref, ref, self.x_s.at[step], self.x_r.at[step], device(self.z, self.y, self.c, 1 - self.h))
+            self.source(kind, line), self.slot(kind, self.z, owner), self.s.at[kind, step], self.r.at[kind, self.z],
+            device(line, self.y, self.c, self.h),
+        )
+
+    def pull(self, kind, line, owner):
+        ref = self.slot(kind, line, owner)
+        return remote(ref, ref, self.s.at[kind, 0], self.r.at[kind, line], self.me)
+
+    def keep(self, kind, owner):
+        return local(self.source(kind, self.z), self.slot(kind, self.z, owner), self.own.at[kind])
+
+    def over(self, line):
+        ref = self.qkv.at[line * 2 + self.y, self.c]
+        return remote(ref, ref, self.x_s.at[line], self.x_r.at[line], device(self.z, self.y, self.c, 1 - self.h))
+
+    def over_in(self, line):
+        ref = self.qkv.at[line * 2 + self.y, self.c]
+        return remote(ref, ref, self.x_s.at[line], self.x_r.at[line], self.me)
+
+    def across(self, line):
+        return remote(
+            self.stage.at[line], self.qkv.at[line * 2 + self.y, self.c], self.a_s.at[line], self.a_r.at[line],
+            device(self.z, 1 - self.y, self.c, self.h),
+        )
+
+    def across_far(self, line):
+        return remote(
+            self.stage.at[line], self.qkv.at[line * 2 + self.y, self.c], self.b_s.at[line], self.b_r.at[line],
+            device(self.z, 1 - self.y, self.c, 1 - self.h),
+        )
+
+    def far_in(self, line, owner):
+        ref = self.qkv.at[line * 2 + 1 - self.y, self.c]
+        s, r = (self.a_s, self.a_r) if owner else (self.b_s, self.b_r)
+        return remote(ref, ref, s.at[line], r.at[line], self.me)
 
     def share(self, line, core):
         ref = self.qkv.at[pl.ds(line * 2, 2), core]
@@ -819,44 +862,45 @@
         ref = self.out_w.at[:, core]
         return remote(ref, ref, self.o_s.at[3], self.o_r.at[3], device(self.z, self.y, 1 - self.c, self.h))
 
+    def each(self, act):
+        @pl.when(self.owner)
+        def _():
+            act(True)
+
+        @pl.when(jnp.logical_not(self.owner))
+        def _():
+            act(False)
+
     def start(self):
-        for kind in range(3):
-
-            @pl.when(self.owner)
-            def _():
-                self.keep(kind).start()
-
-            @pl.when(jnp.logical_not(self.owner))
-            def _():
-                self.push(kind, 0).start()
-                self.push_far(kind, 0).start()
-
-        for step in range(1, LINE):
+        def act(owner):
             for kind in range(3):
-                self.push(kind, step).start()
-
-            @pl.when(jnp.logical_not(self.owner))
-            def _():
+                self.keep(kind, owner).start()
+            for step in range(1, LINE):
                 for kind in range(3):
-                    self.push_far(kind, step).start()
-
-        @pl.when(self.owner)
-        def _():
-            self.out_keep().start()
-
-        @pl.when(jnp.logical_not(self.owner))
-        def _():
-            self.out_push().start()
+                    self.push(kind, step, owner).start()
+            if owner:
+                self.out_keep().start()
+            else:
+                self.out_push().start()
+
+        self.each(act)
 
     def relay(self, step):
-        @pl.when(self.owner)
-        def _():
+        line = (self.z + LINE - step) % LINE
+
+        def act(owner):
             for kind in range(3):
                 if step:
-                    self.pull(kind, self.near(step)).wait_recv()
+                    self.pull(kind, line, owner).wait_recv()
                 else:
-                    self.keep(kind).wait()
-            self.over(step).start()
+                    self.keep(kind, owner).wait()
+            if owner:
+                self.over(line).start()
+            else:
+                self.across(line).start()
+                self.across_far(line).start()
+
+        self.each(act)
 
     def relay_out(self):
         @pl.when(self.owner)
@@ -866,13 +910,15 @@
             self.out_over().start()
 
     def relay_share(self, step):
-        @pl.when(jnp.logical_not(self.owner))
-        def _():
-            self.over(step).wait_recv()
-
-        for kind in range(3):
-            self.pull(kind, self.far(step)).wait_recv()
-        self.share((self.z + LINE - step) % LINE, self.c).start()
+        line = (self.z + LINE - step) % LINE
+
+        def act(owner):
+            if not owner:
+                self.over_in(line).wait_recv()
+            self.far_in(line, owner).wait_recv()
+
+        self.each(act)
+        self.share(line, self.c).start()
 
     def relay_out_share(self):
         @pl.when(jnp.logical_not(self.owner))
@@ -887,23 +933,23 @@
             self.share(line, self.c).wait_send()
         self.out_share(1 - self.c).wait_recv()
         self.out_share(self.c).wait_send()
-        for kind in range(3):
-            for step in range(1, LINE):
-                self.push(kind, step).wait_send()
-
-        @pl.when(self.owner)
-        def _():
-            for step in range(LINE):
-                self.over(step).wait_send()
-            self.out_over().wait_send()
-
-        @pl.when(jnp.logical_not(self.owner))
-        def _():
+
+        def act(owner):
             for kind in range(3):
-                self.push(kind, 0).wait_send()
-                for step in range(LINE):
-                    self.push_far(kind, step).wait_send()
-            self.out_push().wait_send()
+                for step in range(1, LINE):
+                    self.push(kind, step, owner).wait_send()
+            for line in range(LINE):
+                if owner:
+                    self.over(line).wait_send()
+                else:
+                    self.across(line).wait_send()
+                    self.across_far(line).wait_send()
+            if owner:
+                self.out_over().wait_send()
+            else:
+                self.out_push().wait_send()
+
+        self.each(act)
 
 
 class MlpSpread:
@@ -1088,26 +1134,37 @@
     return groups
 
 
-def mid_kernel(
-    attended, out_w, gate_in, up_in, wd, tokens, gain, cot_in,
-    output, hidden_out, normed_out, active, grad_gate, grad_up, grad_out,
-    normed, src, total, gate_w, up_w, down_w, gate_pre, up_pre, cot, parts, load_s, out_s, *refs,
+def core_kernel(
+    attended, out_w, gate_in, up_in, wd, tokens, gain, cot, cot_in,
+    hidden_out, active, mlp_part, gathered, grad_hidden, gain_term, gate, up,
+    normed, src, total, gate_w, up_w, down_w, gate_factor, up_factor, cot_pairs, parts, stage, gate_grad, up_grad, branch,
+    cot_s, stage_s, *refs,
 ):
-    gather_sems, share_sems, down_sems, reduce_refs = split_refs(refs, (8, 5, 3, 9))
-    load = local(cot_in, cot, load_s)
-    load.start()
+    gather_sems, back_sems, share_sems, down_sems, reduce_refs, quarter_refs = split_refs(
+        refs, (8, 8, 5, 3, Reduce.COUNT, 8)
+    )
     z, y, c, h = place()
     greet(device(z, y, 1 - c, h))
     greet(device(z, y, c, 1 - h))
     greet_plane(2)
     gather = Gather(src, normed, gather_sems)
+    back = Gather(branch, gathered, back_sems)
     share = MlpShare((gate_in, up_in), (gate_w, up_w), share_sems)
     downs = DownSpread(wd, down_w, down_sems)
     reduce = Reduce(parts, reduce_refs)
+    grads = QuarterReduce((gate_w, up_w), (gate, up), quarter_refs)
     rows, width = normed.shape[1:]
     hidden = gate_w.shape[3]
     step = hidden // 4
     pair = 2 * rows
+    order = (2, 0, 1, 3)
+
+    def cot_load(place_at):
+        return local(cot_in.at[pl.ds(reduce.order[place_at] * 2, 2)], cot_pairs.at[place_at % 2], cot_s.at[place_at % 2])
+
+    cot_load(0).start()
+    cot_load(1).start()
+
     share.start()
     for place_at in range(4):
         line = reduce.order[place_at]
@@ -1133,9 +1190,12 @@
             columns = pl.ds(pl.multiple_of(tile * step, step), step)
             gate_part = product(shard[...], gate_w[:, :, :, columns].reshape(width, step))
             up_part = product(shard[...], up_w[:, :, :, columns].reshape(width, step))
-            gate_pre[chip, :, columns] = gate_part
-            up_pre[chip, :, columns] = up_part
-            active[chip, :, columns] = (gate_part * jax.nn.sigmoid(gate_part) * up_part).astype(jnp.bfloat16)
+            sigmoid = jax.nn.sigmoid(gate_part)
+            silu = gate_part * sigmoid
+            slope = sigmoid * (1.0 + gate_part * (1.0 - sigmoid))
+            gate_factor[chip, :, columns] = (up_part * slope).astype(jnp.bfloat16)
+            up_factor[chip, :, columns] = silu.astype(jnp.bfloat16)
+            active[chip, :, columns] = (silu * up_part).astype(jnp.bfloat16)
 
     def forward_own(distance):
         @pl.when(z - distance >= 0)
@@ -1165,7 +1225,7 @@
                 one(z + distance)
 
     def relay(distance):
-        for elem in (2, 0, 1, 3):
+        for elem in order:
             gather.relay(distance - 1, elem)
 
     gather.relay_b()
@@ -1183,64 +1243,113 @@
     forward_own(3)
     forward_other(3)
     gather.own_copy().wait()
-    store = local(normed, normed_out, out_s)
-    store.start()
     downs.finish()
 
+    def backward(place_at):
+        line = reduce.order[place_at]
+        both = pl.ds(line * 2, 2)
+        cot_load(place_at).wait()
+
+        @pl.loop(0, 4)
+        def _(tile):
+            columns = pl.ds(pl.multiple_of(tile * step, step), step)
+            grad_active = times_transposed(
+                cot_pairs[place_at % 2].reshape(pair, width), down_w[tile // 2, tile % 2]
+            ).reshape(2, rows, step)
+            gate_grad[both, :, columns] = (grad_active * gate_factor[both, :, columns].astype(jnp.float32)).astype(jnp.bfloat16)
+            up_grad[both, :, columns] = (grad_active * up_factor[both, :, columns].astype(jnp.float32)).astype(jnp.bfloat16)
+
+        if place_at < 2:
+            cot_load(place_at + 2).start()
+
+        @pl.loop(0, 4)
+        def _(tile):
+            columns = pl.ds(pl.multiple_of(tile * (width // 4), width // 4), width // 4)
+            chips = pl.ds(tile * 2, 2)
+            part = times_transposed(gate_grad[both].reshape(pair, hidden), gate_w[chips].reshape(width // 4, hidden))
+            part += times_transposed(up_grad[both].reshape(pair, hidden), up_w[chips].reshape(width // 4, hidden))
+            parts[both, :, columns] = part.astype(jnp.bfloat16).reshape(2, rows, width // 4)
+
+    def stage_store(line):
+        return local(stage, mlp_part.at[pl.ds(line * 2, 2)], stage_s)
+
     def contribute(line):
-        both = pl.ds(line * 2, 2)
+        if line:
+            stage_store(line - 1).wait()
 
         @pl.loop(0, 4)
         def _(tile):
             columns = pl.ds(pl.multiple_of(tile * (width // 4), width // 4), width // 4)
             part = product(
-                active[both].reshape(pair, hidden), down_w[:, :, :, columns].reshape(hidden, width // 4)
+                active[pl.ds(line * 2, 2)].reshape(pair, hidden), down_w[:, :, :, columns].reshape(hidden, width // 4)
             )
-            parts[both, :, columns] = part.astype(jnp.bfloat16).reshape(2, rows, width // 4)
-
-    for place_at in range(4):
-        contribute(reduce.order[place_at])
-        reduce.start(place_at)
-    load.wait()
-
-    def backward(line):
-        both = pl.ds(line * 2, 2)
-
-        @pl.loop(0, 4)
+            stage[:, :, columns] = part.astype(jnp.bfloat16).reshape(2, rows, width // 4)
+
+        stage_store(line).start()
+
+    def weight_grad(kind):
+        source = (gate_grad, up_grad)[kind]
+        store = (gate_w, up_w)[kind]
+
+        @pl.loop(0, 8)
         def _(tile):
-            columns = pl.ds(pl.multiple_of(tile * step, step), step)
-            grad_active = times_transposed(cot[both].reshape(pair, width), down_w[tile // 2, tile % 2])
-            gate_part = gate_pre[both, :, columns].reshape(pair, step)
-            up_part = up_pre[both, :, columns].reshape(pair, step)
-            sigmoid = jax.nn.sigmoid(gate_part)
-            silu = gate_part * sigmoid
-            gate_grad = grad_active * up_part * sigmoid * (1.0 + gate_part * (1.0 - sigmoid))
-            grad_gate[both, :, columns] = gate_grad.astype(jnp.bfloat16).reshape(2, rows, step)
-            grad_up[both, :, columns] = (grad_active * silu).astype(jnp.bfloat16).reshape(2, rows, step)
-
-        @pl.loop(0, 4)
-        def _(tile):
-            columns = pl.ds(pl.multiple_of(tile * (width // 4), width // 4), width // 4)
-            chips = pl.ds(tile * 2, 2)
-            part = times_transposed(grad_gate[both].reshape(pair, hidden), gate_w[chips].reshape(width // 4, hidden))
-            part += times_transposed(grad_up[both].reshape(pair, hidden), up_w[chips].reshape(width // 4, hidden))
-            grad_out[both, :, columns] = part.astype(jnp.bfloat16).reshape(2, rows, width // 4)
+            columns = pl.ds(pl.multiple_of(tile * pair, pair), pair)
+            part = transposed_times(
+                normed[:, :, columns].reshape(8 * rows, pair), source[...].reshape(8 * rows, hidden)
+            )
+            store[tile] = part.astype(jnp.bfloat16).reshape(2, rows, hidden)
 
     for place_at in range(3):
         backward(place_at)
-        reduce.relay(place_at)
+        reduce.start(place_at)
+    reduce.relay(0)
     backward(3)
+    reduce.start(3)
+    contribute(0)
+    contribute(1)
+    reduce.relay(1)
+    weight_grad(0)
+    for cut in range(2):
+        grads.share(0, cut).start()
+    contribute(2)
+    contribute(3)
+    reduce.relay(2)
+    grads.relay(0)
     reduce.total(total)
-    output[...] = (hidden_out[...] + total[...]).astype(jnp.bfloat16)
+
+    inputs = hidden_out[...]
+    inv_scale = rms_scale(inputs)
+    unit_rows = inputs * inv_scale
+    grad_unit = total[...] * gain[...]
+    mean = jnp.mean(grad_unit * unit_rows, axis=-1, keepdims=True)
+    grad_rows = cot[...].astype(jnp.float32) + inv_scale * (grad_unit - unit_rows * mean)
+    grad_hidden[...] = grad_rows
+    branch[...] = grad_rows.astype(jnp.bfloat16)
+    back.start()
+    gain_term[...] = jnp.sum(total[...] * unit_rows, axis=0, keepdims=True)
+    back.relay_b()
+    weight_grad(1)
+    for cut in range(2):
+        grads.share(1, cut).start()
+    for elem in order:
+        back.relay(0, elem)
+    grads.relay(1)
+    for elem in order:
+        back.relay(1, elem)
+    grads.finish(0)
+    for elem in order:
+        back.relay(2, elem)
+    grads.finish(1)
+    back.finish()
     reduce.finish()
-    store.wait()
+    stage_store(3).wait()
     for line in range(LINE):
         for elem in (0, 1):
             gather.across(line, elem).wait_send()
     gather.finish_sends()
 
 
-def mid(attended, out_w, gate, up, wd, tokens, gain, cot):
+def core(attended, out_w, gate, up, wd, tokens, gain, cot, cot_all):
     eight, depth, part = gate.shape
     rows, width = tokens.shape
     hidden = 2 * part
@@ -1253,27 +1362,36 @@
 
     f32 = jnp.float32
     return pl.pallas_call(
-        mid_kernel,
+        core_kernel,
         out_shape=(
-            shape(rows, width),
             shape(rows, width, dtype=f32),
-            shape(8, rows, width),
-            shape(8, rows, hidden),
-            shape(8, rows, hidden),
             shape(8, rows, hidden),
             shape(8, rows, width),
+            shape(8, rows, width),
+            shape(rows, width, dtype=f32),
+            shape(1, width, dtype=f32),
+            shape(8, depth, part),
+            shape(8, depth, part),
         ),
-        in_specs=[INSIDE] * 7 + [ANY],
-        out_specs=(INSIDE, INSIDE, ANY, INSIDE, INSIDE, INSIDE, INSIDE),
+        in_specs=[INSIDE, INSIDE, ANY, ANY, ANY, INSIDE, INSIDE, INSIDE, ANY],
+        out_specs=(INSIDE, INSIDE, ANY, ANY, INSIDE, INSIDE, INSIDE, INSIDE),
         scratch_shapes=[
             room(8, rows, width), room(rows, width), room(rows, width, dtype=f32),
             room(eight, 2, depth, hidden), room(eight, 2, depth, hidden), room(2, 2, *wd.shape),
-            room(8, rows, hidden, dtype=f32), room(8, rows, hidden, dtype=f32),
-            room(8, rows, width), room(8, rows, width), dma(), dma(),
-        ] + Gather.scratch() + MlpShare.scratch() + DownSpread.scratch() + Reduce.scratch(width),
+            room(8, rows, hidden), room(8, rows, hidden),
+            room(2, 2, rows, width), room(8, rows, width), room(2, rows, width),
+            room(8, rows, hidden), room(8, rows, hidden), room(rows, width),
+            dma(2), dma(),
+        ]
+        + Gather.scratch()
+        + Gather.scratch()
+        + MlpShare.scratch()
+        + DownSpread.scratch()
+        + Reduce.scratch(width)
+        + QuarterReduce.scratch(depth, hidden),
         compiler_params=kernel_params(8),
-        name="mid",
-    )(attended, out_w, gate, up, wd, tokens, gain, cot)
+        name="core",
+    )(attended, out_w, gate, up, wd, tokens, gain, cot, cot_all)
 
 
 def column_of(row):
@@ -1296,7 +1414,7 @@
     own, x_s, x_r, c_s, c_r, store_s, *sems,
 ):
     z, y, c, h = place()
-    tok_sems, note_sems, attn_sems, cot_sems, mlp_sems = split_refs(sems, (8, 3, 10, 8, 3))
+    tok_sems, note_sems, attn_sems, cot_sems, mlp_sems = split_refs(sems, (8, 3, AttnSpread.COUNT, 8, 3))
     greet_all(16, 2)
     rows, width = tokens.shape[0], HD
     pair = 2 * rows
@@ -1509,7 +1627,7 @@
         + [dma(3)]
         + Gather.scratch()
         + NoteSpread.scratch()
-        + AttnSpread.scratch()
+        + AttnSpread.scratch(depth)
         + Gather.scratch()
         + MlpSpread.scratch(),
         compiler_params=kernel_params(3),
@@ -1517,34 +1635,23 @@
     )(tokens, cot, note, inv_freqs, wq, wk, wv, wo, wg, wu)
 
 
-def add_into(target, *others):
-    total = target[...].astype(jnp.float32)
-    for other in others:
-        total += other[...].astype(jnp.float32)
-    target[...] = total.astype(target.dtype)
-
-
 class QuarterReduce:
     @staticmethod
     def scratch(depth, wide):
-        store = pltpu.VMEM((8, 2, depth, wide), jnp.bfloat16)
         sib = pltpu.VMEM((8, depth, wide), jnp.bfloat16)
         over = pltpu.VMEM((8, depth, wide // 2), jnp.bfloat16)
-        return [store, store, sib, sib, over, over] + [dma(2)] + [dma(2, 2)] * 4
-
-    def __init__(self, sources, outs, refs):
-        self.sources, self.outs = sources, outs
-        self.store, self.sib, self.box = refs[0:2], refs[2:4], refs[4:6]
-        self.load_s, self.c_s, self.c_r, self.x_s, self.x_r = refs[6:]
+        return [sib, sib, over, over] + [dma(2, 2)] * 4
+
+    def __init__(self, store, outs, refs):
+        self.store, self.outs = store, outs
+        self.sib, self.box = refs[0:2], refs[2:4]
+        self.c_s, self.c_r, self.x_s, self.x_r = refs[4:]
         self.z, self.y, self.c, self.h = place()
         self.part = self.box[0].shape[2]
 
     def columns(self, half):
         return pl.ds(pl.multiple_of(half * self.part, self.part), self.part)
 
-    def load(self, kind):
-        return local(self.sources[kind], self.store[kind], self.load_s.at[kind])
-
     def share(self, kind, cut):
         chips = pl.ds(cut * 4, 4)
         return remote(
@@ -1558,15 +1665,6 @@
             self.store[kind].at[chips, self.c, :, self.columns(1 - self.h)], self.box[kind].at[chips],
             self.x_s.at[kind, cut], self.x_r.at[kind, cut], device(self.z, self.y, self.c, 1 - self.h),
         )
-
-    def start_loads(self):
-        for kind in range(2):
-            self.load(kind).start()
-
-    def start(self, kind):
-        self.load(kind).wait()
-        for cut in range(2):
-            self.share(kind, cut).start()
 
     def relay(self, kind):
         columns = self.columns(1 - self.h)
@@ -1677,140 +1775,6 @@
         self.out[...] = total + self.box[...].astype(jnp.float32)
         self.share().wait_send()
         self.over().wait_send()
-
-
-def turn_kernel(
-    parts_in, normed_in, gate_grad_in, up_grad_in, active_in, cot_in, hidden, gain, cot,
-    gathered, grad_hidden, gain_term, gate, up, down,
-    parts, normed, gate_grad, up_grad, active, cot_all, grad_normed, branch, load_s, *refs,
-):
-    reduce_refs, gather_sems, quarter_refs, down_refs = split_refs(refs, (9, 8, 11, 5))
-    loads = [
-        local(parts_in, parts, load_s.at[0]),
-        local(normed_in, normed, load_s.at[1]),
-        local(gate_grad_in, gate_grad, load_s.at[2]),
-        local(up_grad_in, up_grad, load_s.at[3]),
-        local(active_in, active, load_s.at[4]),
-        local(cot_in, cot_all, load_s.at[5]),
-    ]
-    for load in loads:
-        load.start()
-    z, y, c, h = place()
-    grads = QuarterReduce((None, None), (gate, up), quarter_refs)
-    downs = DownReduce(down, down_refs)
-    greet(device(z, y, 1 - c, h))
-    greet(device(z, y, c, 1 - h))
-    greet_plane(2)
-    reduce = Reduce(parts, reduce_refs)
-    gather = Gather(branch, gathered, gather_sems)
-    loads[0].wait()
-    for place_at in range(4):
-        reduce.start(place_at)
-    for load in loads[1:]:
-        load.wait()
-    tokens, width = normed.shape
-    depth, wide = quarter_refs[0].shape[2:]
-
-    def weight_grad(kind, first, last):
-        source = (gate_grad, up_grad)[kind]
-        store = quarter_refs[kind]
-
-        @pl.loop(first, last)
-        def _(tile):
-            columns = pl.ds(pl.multiple_of(tile * 2 * depth, 2 * depth), 2 * depth)
-            part = transposed_times(normed[:, columns], source[...])
-            store[tile] = part.astype(jnp.bfloat16).reshape(2, depth, wide)
-
-    down_store = down_refs[0]
-    down_rows = down_store.shape[2]
-
-    def down_grad(tile):
-        columns = pl.ds(tile * down_rows, down_rows)
-
-        @pl.loop(0, 4)
-        def _(piece):
-            part_columns = pl.ds(pl.multiple_of(piece * (width // 4), width // 4), width // 4)
-            part = transposed_times(active[:, columns], cot_all[:, part_columns])
-            down_store[tile // 2, tile % 2, :, part_columns] = part.astype(jnp.bfloat16)
-
-    weight_grad(0, 0, 4)
-    grads.share(0, 0).start()
-    weight_grad(0, 4, 8)
-    grads.share(0, 1).start()
-    reduce.relay(0)
-    weight_grad(1, 0, 4)
-    grads.relay(0)
-    grads.share(1, 0).start()
-    weight_grad(1, 4, 8)
-    grads.share(1, 1).start()
-    reduce.relay(1)
-    grads.relay(1)
-    reduce.relay(2)
-    reduce.total(grad_normed)
-    inputs = hidden[...]
-    inv_scale = rms_scale(inputs)
-    unit_rows = inputs * inv_scale
-    grad_unit = grad_normed[...] * gain[...]
-    gain_term[...] = jnp.sum(grad_normed[...] * unit_rows, axis=0, keepdims=True)
-    mean = jnp.mean(grad_unit * unit_rows, axis=-1, keepdims=True)
-    grad_rows = cot[...].astype(jnp.float32) + inv_scale * (grad_unit - unit_rows * mean)
-    grad_hidden[...] = grad_rows
-    branch[...] = grad_rows.astype(jnp.bfloat16)
-    gather.start()
-    gather.relay_b()
-    for tile in range(4):
-        down_grad(tile)
-    downs.share().start()
-    for elem in (2, 0, 1, 3):
-        gather.relay(0, elem)
-    downs.relay()
-    grads.finish(0)
-    for elem in (2, 0, 1, 3):
-        gather.relay(1, elem)
-    grads.finish(1)
-    for elem in (2, 0, 1, 3):
-        gather.relay(2, elem)
-    downs.finish()
-    gather.finish()
-    reduce.finish()
-
-
-def turn(parts, normed, gate_grad, up_grad, active, cot_all, hidden, gain, cot):
-    eight, rows, width = parts.shape
-    wide = gate_grad.shape[1]
-    depth = normed.shape[1] // 16
-    down_rows = wide // 4
-
-    def room(*dims, dtype=jnp.bfloat16):
-        return pltpu.VMEM(dims, dtype)
-
-    def shape(*dims, dtype=jnp.bfloat16):
-        return jax.ShapeDtypeStruct(dims, dtype)
-
-    f32 = jnp.float32
-    return pl.pallas_call(
-        turn_kernel,
-        out_shape=(
-            shape(eight, rows, width),
-            shape(rows, width, dtype=f32),
-            shape(1, width, dtype=f32),
-            shape(8, depth, wide // 2),
-            shape(8, depth, wide // 2),
-            shape(down_rows, width, dtype=f32),
-        ),
-        in_specs=[ANY] * 6 + [INSIDE] * 3,
-        out_specs=(ANY,) + (INSIDE,) * 5,
-        scratch_shapes=[
-            room(*parts.shape), room(*normed.shape), room(*gate_grad.shape), room(*up_grad.shape),
-            room(*active.shape), room(*cot_all.shape), room(rows, width, dtype=f32), room(rows, width), dma(6),
-        ]
-        + Reduce.scratch(width)
-        + Gather.scratch()
-        + QuarterReduce.scratch(depth, wide)
-        + DownReduce.scratch(down_rows, width),
-        compiler_params=kernel_params(9),
-        name="turn",
-    )(parts, normed, gate_grad, up_grad, active, cot_all, hidden, gain, cot)
 
 
 class OutGrad:
@@ -2222,12 +2186,17 @@
 
 
 def close_kernel(
-    normed_in, qkv_w, grad_query, grad_side, grad_hidden, tokens, gain, mlp_term,
-    tokens_grad, gains, query, key, value,
-    normed, weight, parts, grad_normed, attn_term, load_s, *refs,
+    normed_in, qkv_w, mlp_part, active_in, cot_in, grad_query, grad_side, grad_hidden, hidden, tokens, gain, mlp_term,
+    output, tokens_grad, gains, down, query, key, value,
+    normed, weight, parts, mlp_parts, active, cot, total, attn_term, load_s, *refs,
 ):
-    reduce_refs, head_refs, gain_refs = split_refs(refs, (9, 13, 4))
+    reduce_refs, mlp_refs, head_refs, gain_refs, down_refs = split_refs(refs, (Reduce.COUNT, Reduce.COUNT, 13, 4, 5))
     z, y, c, h = place()
+    loads = [
+        local(active_in, active, load_s.at[3]),
+        local(cot_in, cot, load_s.at[4]),
+        local(mlp_part, mlp_parts, load_s.at[5]),
+    ]
     load = local(normed_in, normed, load_s.at[0])
     load_q = local(qkv_w.at[:, :, :, pl.ds(0, HD)], weight.at[0], load_s.at[1])
     side_columns = pl.ds(pl.multiple_of((1 + z % 2) * HD, HD), HD)
@@ -2235,8 +2204,12 @@
     load_q.start()
     load_side.start()
     load.start()
+    for later in loads:
+        later.start()
     greet_all(16, 2)
     reduce = Reduce(parts, reduce_refs)
+    mlp_reduce = Reduce(mlp_parts, mlp_refs)
+    downs = DownReduce(down, down_refs)
     heads = HeadGrads((query, key, value), head_refs)
     gain_sum = GainSum(gains, gain_refs)
     rows, width = parts.shape[1:]
@@ -2269,26 +2242,55 @@
     heads.relay(0)
     heads.relay(1)
     reduce.relay(0)
+    for later in loads:
+        later.wait()
+    down_rows = down.shape[0]
+
+    def down_grad(tile):
+        columns = pl.ds(tile * down_rows, down_rows)
+
+        @pl.loop(0, 4)
+        def _(piece):
+            wide = pl.ds(pl.multiple_of(piece * (width // 4), width // 4), width // 4)
+            part = transposed_times(
+                active[:, :, columns].reshape(8 * rows, down_rows), cot[:, :, wide].reshape(8 * rows, width // 4)
+            )
+            down_refs[0][tile // 2, tile % 2, :, wide] = part.astype(jnp.bfloat16)
+
+    for tile in range(4):
+        down_grad(tile)
+    downs.share().start()
     reduce.relay(1)
-    heads.scatter(0)
+    downs.relay()
     reduce.relay(2)
-    heads.scatter(1)
-    reduce.total(grad_normed)
+    reduce.total(total)
+    for place_at in range(4):
+        mlp_reduce.start(place_at)
     inputs = tokens[...].astype(jnp.float32)
     inv_scale = rms_scale(inputs)
     unit_rows = inputs * inv_scale
-    attn_term[...] = jnp.sum(grad_normed[...] * unit_rows, axis=0, keepdims=True)
+    attn_term[...] = jnp.sum(total[...] * unit_rows, axis=0, keepdims=True)
     gain_sum.start(attn_term, mlp_term)
-    grad_unit = grad_normed[...] * gain[...]
+    grad_unit = total[...] * gain[...]
     mean = jnp.mean(grad_unit * unit_rows, axis=-1, keepdims=True)
     tokens_grad[...] = (grad_hidden[...] + inv_scale * (grad_unit - unit_rows * mean)).astype(jnp.bfloat16)
+    reduce.finish()
+    heads.scatter(0)
+    heads.scatter(1)
+    mlp_reduce.relay(0)
+    downs.finish()
+    mlp_reduce.relay(1)
+    mlp_reduce.relay(2)
     heads.finish()
-    reduce.finish()
     gain_sum.finish()
-
-
-def close(normed, qkv_w, grad_query, grad_side, grad_hidden, tokens, gain, mlp_term):
+    mlp_reduce.total(total)
+    output[...] = (hidden[...] + total[...]).astype(jnp.bfloat16)
+    mlp_reduce.finish()
+
+
+def close(normed, qkv_w, mlp_part, active, cot, grad_query, grad_side, grad_hidden, hidden, tokens, gain, mlp_term):
     rows, width = tokens.shape
+    down_rows = active.shape[2] // 4
     depth = qkv_w.shape[2]
 
     def room(*dims, dtype=jnp.bfloat16):
@@ -2302,21 +2304,43 @@
         close_kernel,
         out_shape=(
             shape(rows, width),
+            shape(rows, width),
             shape(8, rows, dtype=f32),
+            shape(down_rows, width, dtype=f32),
             shape(depth, 4 * HD), shape(depth, 2 * HD), shape(depth, 2 * HD),
         ),
-        in_specs=[ANY, ANY] + [INSIDE] * 6,
-        out_specs=(INSIDE, INSIDE, ANY, ANY, ANY),
+        in_specs=[ANY] * 5 + [INSIDE] * 7,
+        out_specs=(INSIDE, INSIDE, INSIDE, INSIDE, ANY, ANY, ANY),
         scratch_shapes=[
-            room(*normed.shape), room(2, 8, 2, depth, HD), room(8, rows, width),
-            room(rows, width, dtype=f32), room(1, width, dtype=f32), dma(3),
+            room(*normed.shape), room(2, 8, 2, depth, HD), room(8, rows, width), room(8, rows, width),
+            room(*active.shape), room(*cot.shape),
+            room(rows, width, dtype=f32), room(1, width, dtype=f32), dma(6),
         ]
         + Reduce.scratch(width)
+        + Reduce.scratch(width)
         + HeadGrads.scratch(depth)
-        + GainSum.scratch(rows),
+        + GainSum.scratch(rows)
+        + DownReduce.scratch(down_rows, width),
         compiler_params=kernel_params(6),
         name="close",
-    )(normed, qkv_w, grad_query, grad_side, grad_hidden, tokens, gain, mlp_term)
+    )(normed, qkv_w, mlp_part, active, cot, grad_query, grad_side, grad_hidden, hidden, tokens, gain, mlp_term)
+
+
+def widen_kernel(*refs):
+    half = len(refs) // 2
+    for source, target in zip(refs[:half], refs[half:]):
+        target[...] = source[...].astype(target.dtype)
+
+
+def widen(arrays, dtypes):
+    return pl.pallas_call(
+        widen_kernel,
+        out_shape=tuple(jax.ShapeDtypeStruct(array.shape, dtype) for array, dtype in zip(arrays, dtypes)),
+        in_specs=[INSIDE] * len(arrays),
+        out_specs=(INSIDE,) * len(arrays),
+        compiler_params=pltpu.CompilerParams(vmem_limit_bytes=VMEM_BYTES),
+        name="widen",
+    )(*arrays)
 
 
 def fast_body(
@@ -2355,20 +2379,8 @@
     out_w = out_w.reshape(HD, width)
     gain_attn = notes[:, 4].reshape(1, width)
     gain_mlp = notes[:, 5].reshape(1, width)
-    output, hidden, normed_mlp, active, grad_gate, grad_up, grad_normed_part = mid(
-        attended_low, out_w, gate_w, up_w, w_down, tokens, gain_mlp, cot_all
-    )
-    hidden_part = active.shape[2]
-    grad_branch, grad_hidden, mlp_term, gate_quarter, up_quarter, down_grad = turn(
-        grad_normed_part,
-        normed_mlp.reshape(token_rows, width),
-        grad_gate.reshape(token_rows, hidden_part),
-        grad_up.reshape(token_rows, hidden_part),
-        active.reshape(token_rows, hidden_part),
-        cot_all.reshape(token_rows, width),
-        hidden,
-        gain_mlp,
-        cotangent,
+    hidden, active, mlp_part, grad_branch, grad_hidden, mlp_term, gate_quarter, up_quarter = core(
+        attended_low, out_w, gate_w, up_w, w_down, tokens, gain_mlp, cotangent, cot_all
     )
 
     side_grad, grad_query, gate_grad, up_grad, out_grad = attend_back(
@@ -2386,20 +2398,35 @@
         up_quarter,
         w_out.shape[0],
     )
-    tokens_grad, gain_grads, query_grad, key_grad, value_grad = close(
-        normed, qkv_w, grad_query, side_grad, grad_hidden, tokens, gain_attn, mlp_term
+    output, tokens_grad, gain_grads, down_grad, query_grad, key_grad, value_grad = close(
+        normed,
+        qkv_w,
+        mlp_part,
+        active,
+        cot_all,
+        grad_query,
+        side_grad,
+        grad_hidden,
+        hidden,
+        tokens,
+        gain_attn,
+        mlp_term,
+    )
+    arrays = (output, tokens_grad, query_grad, key_grad, value_grad, out_grad, gate_grad, up_grad, down_grad)
+    output, tokens_grad, query_grad, key_grad, value_grad, out_grad, gate_grad, up_grad, down_grad = widen(
+        arrays, (bf16, bf16) + (f32,) * 7
     )
     return (
         output,
         tokens_grad,
         gain_grads[0],
-        query_grad.astype(f32),
-        key_grad.astype(f32),
-        value_grad.astype(f32),
-        out_grad.astype(f32),
+        query_grad,
+        key_grad,
+        value_grad,
+        out_grad,
         gain_grads[1],
-        gate_grad.astype(f32),
-        up_grad.astype(f32),
+        gate_grad,
+        up_grad,
         down_grad,
     )
 

time: 578 us -> 547 us (0.946)
  Pallas kernels: 549 us -> 532 us
  other arithmetic: 10.8 us -> 1.9 us
    pallas_call x3, Pallas kernels: 338 us -> 323 us  [the longest x1 197 us: core(): pl.pallas_call(core_kernel, out_shape=(shape(rows, width, dtype=f32), sha...]
    convert_element_type x6 -> x0, other arithmetic: 8.94 us -> none  [the longest x1 1.79 us: fast_body(): query_grad.astype(f32)]
where the time goes in v5:
time: 547 us; the launch traced here: 538 us
  Pallas kernels  532 us (97%)
    pallas_call x1, Pallas kernels, core(): pl.pallas_call(core_kernel, out_shape=(shape(rows, width, dtype=f32), sha...  197 us
    pallas_call x1, Pallas kernels, front(): pl.pallas_call(front_kernel, out_shape=(shape(8, 2, 2, rows, 2 * HD), sha...  148 us
    pallas_call x1, Pallas kernels, close(): pl.pallas_call(close_kernel, out_shape=(shape(rows, width), shape(rows, w...  120 us
    pallas_call x1, Pallas kernels, attend_back(): pl.pallas_call(attend_back_kernel, out_shape=(shape(tokens, HD), shape(to...  60.8 us

profile of v5, /device:TPU:8, one launch (start us, length us, event | category | flops | bytes accessed | tf_op | source)
XLA Modules:
  0.0 538.2 jit_solution(1118027473122075418)
XLA Ops:
  0.6 0.5 multiply_power_fusion.inv_freqs
  1.2 0.7 bitcast_convert_fusion
  1.8 0.7 convert_bitcast_fusion
  2.5 0.6 concatenate.3.note
  3.2 148.4 %front.1 = (bf16[8,2,2,128,512]{4,3,2,1,0:T(8,128)(2,1)}, bf16[1024,2048]{1,0:T(8,128)(2,1)}, bf16[8,2,128,768]{3,2,1,0:T(8,128)(2,1)}, bf16[2,2,64,2048]{3,2,1,...) custom-call(bf16[128,2048]{1,0:T(8,128)(2,1)} %tokens.5, ...), custom_call_target="tpu_custom_call" | custom-call | tf_op jit(solution)/shard_map/front/pallas_call | solution.py:1594
  151.6 1.5 slice_bitcast_fusion
  153.1 196.7 %core.1 = (f32[128,2048]{1,0:T(8,128)}, bf16[8,128,1024]{2,1,0:T(8,128)(2,1)}, bf16[8,128,2048]{2,1,0:T(8,128)(2,1)}, bf16[8,128,2048]{2,1,0:T(8,128)(2,1)}, f32...) custom-call(bf16[1024,256]{1,0:T(8,128)(2,1)} %get-tuple-element.56.attended., ...), custom_call_target="tpu_custom_call" | custom-call | tf_op jit(solution)/shard_map/core/pallas_call | solution.py:1364
  349.8 60.8 %attend_back.1 = (bf16[1024,256]{1,0:T(8,128)(2,1)}, bf16[1024,256]{1,0:T(8,128)(2,1)}, bf16[128,4096]{1,0:T(8,128)(2,1)}, bf16[128,4096]{1,0:T(8,128)(2,1)}, bf16[64,2048]{1,0:T(8,128)(2,1)}) custom-call(bf16[1024,256]{1,0:T(8,128)(2,1)} %get-tuple-element.64.query, bf16[8,2,2,128,512]{4,3,2,1,0:T(8,128)(2,1)} %get-tuple-element.65.keys_in, ...), custom_call_target="tpu_custom_call" | custom-call | tf_op jit(solution)/shard_map/attend_back/pallas_call | solution.py:2006
  410.6 119.5 %close.1 = (bf16[128,2048]{1,0:T(8,128)(2,1)}, bf16[128,2048]{1,0:T(8,128)(2,1)}, f32[8,128]{1,0:T(8,128)}, f32[256,2048]{1,0:T(8,128)}, bf16[128,1024]{1,0:T(8,...) custom-call(bf16[1024,2048]{1,0:T(8,128)(2,1)} %get-tuple-element.54.normed_in, ...), custom_call_target="tpu_custom_call" | custom-call | tf_op jit(solution)/shard_map/close/pallas_call | solution.py:2303
  530.1 1.3 slice_bitcast_fusion.2
  531.4 6.4 %widen.1 = (bf16[128,2048]{1,0:T(8,128)(2,1)}, bf16[128,2048]{1,0:T(8,128)(2,1)}, f32[128,1024]{1,0:T(8,128)}, f32[128,512]{1,0:T(8,128)}, f32[128,512]{1,0:T(8,...) custom-call(bf16[128,2048]{1,0:T(8,128)(2,1)} %get-tuple-element.78.refs_0_, ...), custom_call_target="tpu_custom_call" | custom-call | tf_op jit(solution)/shard_map/widen/pallas_call | solution.py:2336
  (1 shorter events, 0.0 us)

commit v6 on v5

--- a/solution.py
+++ b/solution.py
@@ -1,6 +1,7 @@
 import jax
 import jax.numpy as jnp
 from jax import lax
+import numpy as np
 from jax.experimental import pallas as pl
 from jax.experimental.pallas import tpu as pltpu
 from jax.sharding import PartitionSpec as P
@@ -1299,22 +1300,40 @@
             )
             store[tile] = part.astype(jnp.bfloat16).reshape(2, rows, hidden)
 
+    at_end = jnp.logical_or(z == 0, z == LINE - 1)
+    inside = jnp.logical_not(at_end)
     for place_at in range(3):
         backward(place_at)
         reduce.start(place_at)
-    reduce.relay(0)
+
+    @pl.when(at_end)
+    def _():
+        reduce.relay(0)
+
     backward(3)
     reduce.start(3)
-    contribute(0)
-    contribute(1)
-    reduce.relay(1)
+
+    @pl.when(at_end)
+    def _():
+        reduce.relay(1)
+
+    @pl.when(inside)
+    def _():
+        reduce.relay(0)
+
     weight_grad(0)
     for cut in range(2):
         grads.share(0, cut).start()
-    contribute(2)
-    contribute(3)
+    contribute(0)
+
+    @pl.when(inside)
+    def _():
+        reduce.relay(1)
+
+    grads.relay(0)
     reduce.relay(2)
-    grads.relay(0)
+    for line in range(1, LINE):
+        contribute(line)
     reduce.total(total)
 
     inputs = hidden_out[...]
@@ -1408,9 +1427,9 @@
 
 def front_kernel(
     tokens, cot, note, inv_freqs, wq, wk, wv, wo, wg, wu,
-    kv_out, normed_out, qkv_out, out_w, notes, cos_table, sine_table, query, attended_out, attended_low_out,
+    kv_out, normed_out, qkv_out, out_w, notes, gain, mlp_gain, cos_table, sine_table, query, attended_out, attended_low_out,
     log_out, cot_out, gate, up,
-    gathered, normed, qkv_w, gain, query_ids, key_ids, kv, keys, scores, total,
+    gathered, normed, qkv_w, query_ids, key_ids, kv, keys, scores, total,
     own, x_s, x_r, c_s, c_r, store_s, *sems,
 ):
     z, y, c, h = place()
@@ -1439,6 +1458,7 @@
     def tables():
         for blk in range(16):
             gain[:, pl.ds(blk * rows, rows)] = notes[blk, 4:5, :]
+            mlp_gain[:, pl.ds(blk * rows, rows)] = notes[blk, 5:6, :]
         for chip in range(8):
             part = pl.ds(chip * rows, rows)
             mine = notes[2 * chip + c]
@@ -1599,6 +1619,8 @@
             shape(8, 2, depth, 3 * HD),
             shape(2, 2, wo.shape[0], width),
             shape(16, *note.shape, dtype=f32),
+            shape(1, width, dtype=f32),
+            shape(1, width, dtype=f32),
             shape(token_rows, HD // 2, dtype=f32),
             shape(token_rows, HD // 2, dtype=f32),
             shape(token_rows, HD),
@@ -1610,12 +1632,11 @@
             shape(8, depth, part),
         ),
         in_specs=[INSIDE] * 10,
-        out_specs=(ANY, ANY, ANY, ANY) + (INSIDE,) * 7 + (ANY, ANY, ANY),
+        out_specs=(ANY, ANY, ANY, ANY) + (INSIDE,) * 9 + (ANY, ANY, ANY),
         scratch_shapes=[
             room(8, rows, width),
             room(token_rows, width),
             room(8, 2, depth, 3 * HD),
-            room(1, width, dtype=f32),
             room(token_rows, 1, dtype=f32),
             room(8, 1, 4 * rows, dtype=f32),
             room(8, rows, 2 * HD),
@@ -1846,18 +1867,25 @@
 
 
 def attend_back_kernel(
-    query, keys_in, branch_in, out_w, attended, attended_low, log_row, notes, cos_table, sine_table, gate_in, up_in,
-    side_out, grad_query, gate, up, out_grad,
-    keys, branch, grad_out, delta_row, query_row, key_column, grad_rot, parts, grad_key, grad_value, sib_in, x_in, z_in,
+    query, keys_in, branch_in, mlp_part, hidden, out_w, attended, attended_low, log_row, notes, cos_table, sine_table,
+    gate_in, up_in,
+    side_out, grad_query, output, gate, up, out_grad,
+    mlp_parts, mlp_total, keys, branch, grad_out, delta_row, query_row, key_column, grad_rot, parts, grad_key, grad_value, sib_in, x_in, z_in,
     load_s, c_s, c_r, x_s, x_r, z_s, z_r, *sems,
 ):
     z, y, c, h = place()
     mate = z + 1 - 2 * (z % 2)
     loads = [local(keys_in, keys, load_s.at[0]), local(branch_in, branch, load_s.at[1])]
+    load_mlp = local(mlp_part, mlp_parts, load_s.at[2])
+    load_mlp.start()
     for load in loads:
         load.start()
     greet_all(16, 2)
-    scatter_sems, out_refs = split_refs(sems, (3, 7))
+    scatter_sems, out_refs, reduce_refs = split_refs(sems, (3, 7, Reduce.COUNT))
+    reduce = Reduce(mlp_parts, reduce_refs)
+    load_mlp.wait()
+    for place_at in range(4):
+        reduce.start(place_at)
     scatter = QuarterScatter((gate_in, up_in), (gate, up), scatter_sems)
     outs = OutGrad(out_grad, out_refs)
     scatter.start()
@@ -1973,6 +2001,11 @@
             stage_three(block - 4)
     stage_two(7)
     outs.send()
+
+    @pl.when(jnp.logical_or(z == 0, z == LINE - 1))
+    def _():
+        reduce.relay(0)
+
     for place_at in range(LINE):
         part = pl.ds(place_at * pair, pair)
         lower, upper = turn_back(grad_rot[part] * HD**-0.5, part)
@@ -1981,17 +2014,30 @@
     for block in range(4, 8):
         stage_three(block)
         stage_four(block - 4)
+
+    @pl.when(jnp.logical_and(z > 0, z < LINE - 1))
+    def _():
+        reduce.relay(0)
+
     for block in range(4, 8):
         stage_four(block)
+    reduce.relay(1)
+    reduce.relay(2)
     for block in range(8):
         share(block).wait_send()
         over(block).wait_send()
         across(block).wait_send()
+    outs.finish()
+    reduce.total(mlp_total)
+    output[...] = (hidden[...] + mlp_total[...]).astype(jnp.bfloat16)
     scatter.finish()
-    outs.finish()
-
-
-def attend_back(query, keys, branch, out_w, attended, attended_low, log_row, notes, cos_table, sine_table, gate, up, out_rows):
+    reduce.finish()
+
+
+def attend_back(
+    query, keys, branch, mlp_part, hidden, out_w, attended, attended_low, log_row, notes, cos_table, sine_table, gate, up,
+    out_rows,
+):
     eight, _, _, rows, width = keys.shape
     tokens = query.shape[0]
     depth, part = gate.shape[1:]
@@ -2008,23 +2054,30 @@
         out_shape=(
             shape(tokens, HD),
             shape(tokens, HD),
+            shape(*hidden.shape),
             shape(depth, 8 * part),
             shape(depth, 8 * part),
             shape(out_rows, out_w.shape[1]),
         ),
-        in_specs=[INSIDE, ANY, ANY] + [INSIDE] * 9,
-        out_specs=(INSIDE, INSIDE, ANY, ANY, ANY),
+        in_specs=[INSIDE, ANY, ANY, ANY] + [INSIDE] * 10,
+        out_specs=(INSIDE, INSIDE, INSIDE, ANY, ANY, ANY),
         scratch_shapes=[
-            room(*keys.shape), room(*branch.shape), room(tokens, HD),
+            room(*mlp_part.shape), room(*hidden.shape, dtype=f32), room(*keys.shape), room(*branch.shape), room(tokens, HD),
             room(LINE, 1, tokens // LINE, dtype=f32), room(LINE, 1, tokens // LINE, dtype=f32),
             room(8, 4 * rows, 1, dtype=f32), room(tokens, HD, dtype=f32), room(*keys.shape),
             room(4 * rows, HD, dtype=f32), room(4 * rows, HD, dtype=f32),
             room(eight, 2, rows, width), room(eight, rows, width), room(eight, rows, HD),
-            dma(2),
-        ] + [dma(8)] * 6 + QuarterScatter.scratch() + OutGrad.scratch(out_rows, out_w.shape[1]),
+            dma(3),
+        ]
+        + [dma(8)] * 6
+        + QuarterScatter.scratch()
+        + OutGrad.scratch(out_rows, out_w.shape[1])
+        + Reduce.scratch(hidden.shape[1]),
         compiler_params=kernel_params(11),
         name="attend_back",
-    )(query, keys, branch, out_w, attended, attended_low, log_row, notes, cos_table, sine_table, gate, up)
+    )(
+        query, keys, branch, mlp_part, hidden, out_w, attended, attended_low, log_row, notes, cos_table, sine_table, gate, up
+    )
 
 
 class HeadGrads:
@@ -2034,10 +2087,10 @@
             return pltpu.VMEM(dims, jnp.bfloat16)
 
         return [
-            room(8, 2, depth, HD), room(8, 2, depth, HD),
-            room(8, depth, HD), room(8, depth, HD),
-            room(8, depth, HD), room(8, depth, HD),
-            dma(2), dma(2), dma(2), dma(2), dma(3, 8), dma(3, 4, 8), dma(3),
+            room(LINE, 2, 2, depth, HD), room(LINE, 2, 2, depth, HD),
+            room(LINE, 2, depth, HD), room(LINE, 2, depth, HD),
+            room(LINE, depth, HD), room(LINE, depth, HD),
+            dma(2), dma(2), dma(2), dma(2), dma(3, 4), dma(3, 4), dma(3),
         ]
 
     def __init__(self, outs, refs):
@@ -2045,19 +2098,17 @@
         self.store, self.sib, self.box = refs[0:2], refs[2:4], refs[4:6]
         (self.c_s, self.c_r, self.x_s, self.x_r, self.s, self.r, self.own) = refs[6:]
         self.z, self.y, self.c, self.h = place()
-        self.chip = self.z * 2 + self.y
         self.me = device(self.z, self.y, self.c, self.h)
-        self.owner = self.h == self.y
 
     def share(self, i):
         return remote(
-            self.store[i].at[:, 1 - self.c], self.sib[i], self.c_s.at[i], self.c_r.at[i],
+            self.store[i].at[:, :, 1 - self.c], self.sib[i], self.c_s.at[i], self.c_r.at[i],
             device(self.z, self.y, 1 - self.c, self.h),
         )
 
     def over(self, i):
         return remote(
-            self.store[i].at[:, self.c], self.box[i], self.x_s.at[i], self.x_r.at[i],
+            self.store[i].at[:, 1 - self.h, self.c], self.box[i], self.x_s.at[i], self.x_r.at[i],
             device(self.z, self.y, self.c, 1 - self.h),
         )
 
@@ -2066,84 +2117,87 @@
         return self.outs[kind].at[:, pl.ds(pl.multiple_of(start, HD), HD)]
 
     def push(self, kind, step):
-        chip = (self.chip + step) % 8
-        return remote(
-            self.store[min(kind, 1)].at[chip, self.c], self.target(kind, self.z), self.s.at[kind, step],
-            self.r.at[kind, self.z, step], device(chip // 2, chip % 2, self.c, self.h),
+        line = (self.z + step) % LINE
+        return remote(
+            self.store[min(kind, 1)].at[line, self.h, self.c], self.target(kind, self.z), self.s.at[kind, step],
+            self.r.at[kind, self.z], device(line, self.h, self.c, self.y),
         )
 
     def keep(self, kind):
-        return local(self.store[min(kind, 1)].at[self.chip, self.c], self.target(kind, self.z), self.own.at[kind])
-
-    def pull(self, kind, line, step):
+        return local(self.store[min(kind, 1)].at[self.z, self.h, self.c], self.target(kind, self.z), self.own.at[kind])
+
+    def stays(self, step):
+        return self.h == self.y if step == 0 else self.h < 0
+
+    def pull(self, kind, line):
         ref = self.target(kind, line)
-        return remote(ref, ref, self.s.at[kind, step], self.r.at[kind, line, step], self.me)
+        return remote(ref, ref, self.s.at[kind, 0], self.r.at[kind, line], self.me)
 
     def relay(self, i):
         self.share(i).wait_recv()
 
-        @pl.loop(0, 8)
-        def _(at):
-            add_into(self.store[i].at[at, self.c], self.sib[i].at[at])
-
-        @pl.when(jnp.logical_not(self.owner))
-        def _():
-            self.over(i).start()
+        @pl.loop(0, LINE)
+        def _(line):
+            for pair in range(2):
+                add_into(self.store[i].at[line, pair, self.c], self.sib[i].at[line, pair])
+
+        self.over(i).start()
+
+    def each_kind(self, i, act):
+        if i == 0:
+            act(0)
+        else:
+            for kind in (1, 2):
+
+                @pl.when(self.z % 2 == kind - 1)
+                def _():
+                    act(kind)
 
     def scatter(self, i):
-        @pl.when(self.owner)
-        def _():
-            self.over(i).wait_recv()
-
-            @pl.loop(0, 8)
-            def _(at):
-                add_into(self.store[i].at[at, self.c], self.box[i].at[at])
-
-            if i == 0:
-                self.keep(0).start()
-                for step in range(1, 8):
-                    self.push(0, step).start()
-            else:
-                for kind in (1, 2):
-
-                    @pl.when(self.z % 2 == kind - 1)
-                    def _():
-                        self.keep(kind).start()
-                        for step in range(1, 8):
-                            self.push(kind, step).start()
+        self.over(i).wait_recv()
+
+        @pl.loop(0, LINE)
+        def _(line):
+            add_into(self.store[i].at[line, self.h, self.c], self.box[i].at[line])
+
+        def act(kind):
+            for step in range(4):
+
+                @pl.when(self.stays(step))
+                def _():
+                    self.keep(kind).start()
+
+                @pl.when(jnp.logical_not(self.stays(step)))
+                def _():
+                    self.push(kind, step).start()
+
+        self.each_kind(i, act)
 
     def finish(self):
         for kind in range(3):
             for line in range(LINE):
                 if kind and line % 2 != kind - 1:
                     continue
-                step = (self.chip + 8 - (line * 2 + self.h)) % 8
-
-                @pl.when(step != 0)
-                def _():
-                    self.pull(kind, line, step).wait_recv()
-
-                @pl.when(step == 0)
+                from_self = (self.z == line) & (self.y == self.h)
+
+                @pl.when(from_self)
                 def _():
                     self.keep(kind).wait()
 
-        @pl.when(jnp.logical_not(self.owner))
-        def _():
-            for i in range(2):
-                self.over(i).wait_send()
-
-        @pl.when(self.owner)
-        def _():
-            for step in range(1, 8):
-                self.push(0, step).wait_send()
-            for kind in (1, 2):
-
-                @pl.when(self.z % 2 == kind - 1)
+                @pl.when(jnp.logical_not(from_self))
                 def _():
-                    for step in range(1, 8):
-                        self.push(kind, step).wait_send()
+                    self.pull(kind, line).wait_recv()
+
+        def act(kind):
+            for step in range(4):
+
+                @pl.when(jnp.logical_not(self.stays(step)))
+                def _():
+                    self.push(kind, step).wait_send()
 
         for i in range(2):
+            self.each_kind(i, act)
+            self.over(i).wait_send()
             self.share(i).wait_send()
 
 
@@ -2186,16 +2240,15 @@
 
 
 def close_kernel(
-    normed_in, qkv_w, mlp_part, active_in, cot_in, grad_query, grad_side, grad_hidden, hidden, tokens, gain, mlp_term,
-    output, tokens_grad, gains, down, query, key, value,
-    normed, weight, parts, mlp_parts, active, cot, total, attn_term, load_s, *refs,
+    normed_in, qkv_w, active_in, cot_in, grad_query, grad_side, grad_hidden, tokens, gain, mlp_term,
+    tokens_grad, gains, down, query, key, value,
+    normed, weight, parts, active, cot, total, attn_term, load_s, *refs,
 ):
-    reduce_refs, mlp_refs, head_refs, gain_refs, down_refs = split_refs(refs, (Reduce.COUNT, Reduce.COUNT, 13, 4, 5))
+    reduce_refs, head_refs, gain_refs, down_refs = split_refs(refs, (Reduce.COUNT, 13, 4, 5))
     z, y, c, h = place()
     loads = [
         local(active_in, active, load_s.at[3]),
         local(cot_in, cot, load_s.at[4]),
-        local(mlp_part, mlp_parts, load_s.at[5]),
     ]
     load = local(normed_in, normed, load_s.at[0])
     load_q = local(qkv_w.at[:, :, :, pl.ds(0, HD)], weight.at[0], load_s.at[1])
@@ -2208,13 +2261,12 @@
         later.start()
     greet_all(16, 2)
     reduce = Reduce(parts, reduce_refs)
-    mlp_reduce = Reduce(mlp_parts, mlp_refs)
     downs = DownReduce(down, down_refs)
     heads = HeadGrads((query, key, value), head_refs)
     gain_sum = GainSum(gains, gain_refs)
     rows, width = parts.shape[1:]
     pair = 2 * rows
-    depth = head_refs[0].shape[2]
+    depth = head_refs[0].shape[3]
     load_q.wait()
     load_side.wait()
     for place_at in range(4):
@@ -2236,7 +2288,7 @@
         def _(tile):
             columns = pl.ds(pl.multiple_of(tile * 4 * depth, 4 * depth), 4 * depth)
             part = transposed_times(normed[:, columns], source[...])
-            head_refs[i][pl.ds(tile * 2, 2)] = part.astype(jnp.bfloat16).reshape(2, 2, depth, HD)
+            head_refs[i][tile] = part.astype(jnp.bfloat16).reshape(2, 2, depth, HD)
 
         heads.share(i).start()
     heads.relay(0)
@@ -2260,12 +2312,12 @@
     for tile in range(4):
         down_grad(tile)
     downs.share().start()
+    heads.scatter(0)
     reduce.relay(1)
+    heads.scatter(1)
     downs.relay()
     reduce.relay(2)
     reduce.total(total)
-    for place_at in range(4):
-        mlp_reduce.start(place_at)
     inputs = tokens[...].astype(jnp.float32)
     inv_scale = rms_scale(inputs)
     unit_rows = inputs * inv_scale
@@ -2274,21 +2326,13 @@
     grad_unit = total[...] * gain[...]
     mean = jnp.mean(grad_unit * unit_rows, axis=-1, keepdims=True)
     tokens_grad[...] = (grad_hidden[...] + inv_scale * (grad_unit - unit_rows * mean)).astype(jnp.bfloat16)
+    downs.finish()
+    heads.finish()
     reduce.finish()
-    heads.scatter(0)
-    heads.scatter(1)
-    mlp_reduce.relay(0)
-    downs.finish()
-    mlp_reduce.relay(1)
-    mlp_reduce.relay(2)
-    heads.finish()
     gain_sum.finish()
-    mlp_reduce.total(total)
-    output[...] = (hidden[...] + total[...]).astype(jnp.bfloat16)
-    mlp_reduce.finish()
-
-
-def close(normed, qkv_w, mlp_part, active, cot, grad_query, grad_side, grad_hidden, hidden, tokens, gain, mlp_term):
+
+
+def close(normed, qkv_w, active, cot, grad_query, grad_side, grad_hidden, tokens, gain, mlp_term):
     rows, width = tokens.shape
     down_rows = active.shape[2] // 4
     depth = qkv_w.shape[2]
@@ -2304,26 +2348,24 @@
         close_kernel,
         out_shape=(
             shape(rows, width),
-            shape(rows, width),
             shape(8, rows, dtype=f32),
             shape(down_rows, width, dtype=f32),
             shape(depth, 4 * HD), shape(depth, 2 * HD), shape(depth, 2 * HD),
         ),
-        in_specs=[ANY] * 5 + [INSIDE] * 7,
-        out_specs=(INSIDE, INSIDE, INSIDE, INSIDE, ANY, ANY, ANY),
+        in_specs=[ANY] * 4 + [INSIDE] * 6,
+        out_specs=(INSIDE, INSIDE, INSIDE, ANY, ANY, ANY),
         scratch_shapes=[
-            room(*normed.shape), room(2, 8, 2, depth, HD), room(8, rows, width), room(8, rows, width),
+            room(*normed.shape), room(2, 8, 2, depth, HD), room(8, rows, width),
             room(*active.shape), room(*cot.shape),
-            room(rows, width, dtype=f32), room(1, width, dtype=f32), dma(6),
+            room(rows, width, dtype=f32), room(1, width, dtype=f32), dma(5),
         ]
-        + Reduce.scratch(width)
         + Reduce.scratch(width)
         + HeadGrads.scratch(depth)
         + GainSum.scratch(rows)
         + DownReduce.scratch(down_rows, width),
         compiler_params=kernel_params(6),
         name="close",
-    )(normed, qkv_w, mlp_part, active, cot, grad_query, grad_side, grad_hidden, hidden, tokens, gain, mlp_term)
+    )(normed, qkv_w, active, cot, grad_query, grad_side, grad_hidden, tokens, gain, mlp_term)
 
 
 def widen_kernel(*refs):
@@ -2371,22 +2413,22 @@
             jnp.zeros((2, rows), f32),
         ]
     )
-    inv_freqs = rope_base ** (-2.0 * jnp.arange(HD // 2, dtype=f32) / HD)
+    inv_freqs = jnp.asarray((rope_base ** (-2.0 * np.arange(HD // 2) / HD)).astype(np.float32))
     (
-        keys_values, normed, qkv_w, out_w, notes, cos_table, sine_table, scaled_query, attended, attended_low,
+        keys_values, normed, qkv_w, out_w, notes, gain_attn, gain_mlp, cos_table, sine_table, scaled_query, attended, attended_low,
         log_total, cot_all, gate_w, up_w,
     ) = front(tokens, cotangent, note, inv_freqs[None], w_query, w_key, w_value, w_out, w_gate, w_up)
     out_w = out_w.reshape(HD, width)
-    gain_attn = notes[:, 4].reshape(1, width)
-    gain_mlp = notes[:, 5].reshape(1, width)
     hidden, active, mlp_part, grad_branch, grad_hidden, mlp_term, gate_quarter, up_quarter = core(
         attended_low, out_w, gate_w, up_w, w_down, tokens, gain_mlp, cotangent, cot_all
     )
 
-    side_grad, grad_query, gate_grad, up_grad, out_grad = attend_back(
+    side_grad, grad_query, output, gate_grad, up_grad, out_grad = attend_back(
         scaled_query,
         keys_values,
         grad_branch,
+        mlp_part,
+        hidden,
         out_w,
         attended,
         attended_low,
@@ -2398,16 +2440,14 @@
         up_quarter,
         w_out.shape[0],
     )
-    output, tokens_grad, gain_grads, down_grad, query_grad, key_grad, value_grad = close(
+    tokens_grad, gain_grads, down_grad, query_grad, key_grad, value_grad = close(
         normed,
         qkv_w,
-        mlp_part,
         active,
         cot_all,
         grad_query,
         side_grad,
         grad_hidden,
-        hidden,
         tokens,
         gain_attn,
         mlp_term,

time: 547 us -> 537 us (0.982)
  Pallas kernels: 532 us -> 524 us
    pallas_call x1, Pallas kernels: 120 us -> 75.5 us  [close(): pl.pallas_call(close_kernel, out_shape=(shape(rows, width), shape(8, rows...]
    pallas_call x1, Pallas kernels: 60.8 us -> 97.1 us  [attend_back(): pl.pallas_call(attend_back_kernel, out_shape=(shape(tokens, HD), shape(to...]
where the time goes in v6:
time: 537 us; the launch traced here: 528 us
  Pallas kernels  524 us (98%)
    pallas_call x1, Pallas kernels, core(): pl.pallas_call(core_kernel, out_shape=(shape(rows, width, dtype=f32), sha...  196 us
    pallas_call x1, Pallas kernels, front(): pl.pallas_call(front_kernel, out_shape=(shape(8, 2, 2, rows, 2 * HD), sha...  148 us
    pallas_call x1, Pallas kernels, attend_back(): pl.pallas_call(attend_back_kernel, out_shape=(shape(tokens, HD), shape(to...  97.1 us
    pallas_call x1, Pallas kernels, close(): pl.pallas_call(close_kernel, out_shape=(shape(rows, width), shape(8, rows...  75.5 us

profile of v6, /device:TPU:8, one launch (start us, length us, event | category | flops | bytes accessed | tf_op | source)
XLA Modules:
  0.0 528.1 jit_solution(15024400084022609120)
XLA Ops:
  0.6 0.7 bitcast_convert_fusion
  1.3 0.7 convert_bitcast_fusion
  2.0 0.6 concatenate.3.note
  2.6 148.4 %front.1 = (bf16[8,2,2,128,512]{4,3,2,1,0:T(8,128)(2,1)}, bf16[1024,2048]{1,0:T(8,128)(2,1)}, bf16[8,2,128,768]{3,2,1,0:T(8,128)(2,1)}, bf16[2,2,64,2048]{3,2,1,...) custom-call(bf16[128,2048]{1,0:T(8,128)(2,1)} %tokens.5, ...), custom_call_target="tpu_custom_call" | custom-call | tf_op jit(solution)/shard_map/front/pallas_call | solution.py:1614
  151.1 196.3 %core.1 = (f32[128,2048]{1,0:T(8,128)}, bf16[8,128,1024]{2,1,0:T(8,128)(2,1)}, bf16[8,128,2048]{2,1,0:T(8,128)(2,1)}, bf16[8,128,2048]{2,1,0:T(8,128)(2,1)}, f32...) custom-call(bf16[1024,256]{1,0:T(8,128)(2,1)} %get-tuple-element.58.attended., ...), custom_call_target="tpu_custom_call" | custom-call | tf_op jit(solution)/shard_map/core/pallas_call | solution.py:1383
  347.4 97.1 %attend_back.1 = (bf16[1024,256]{1,0:T(8,128)(2,1)}, bf16[1024,256]{1,0:T(8,128)(2,1)}, bf16[128,2048]{1,0:T(8,128)(2,1)}, bf16[128,4096]{1,0:T(8,128)(2,1)}, bf...) custom-call(bf16[1024,256]{1,0:T(8,128)(2,1)} %get-tuple-element.56.query, ...), custom_call_target="tpu_custom_call" | custom-call | tf_op jit(solution)/shard_map/attend_back/pallas_call | solution.py:2052
  444.5 75.5 %close.1 = (bf16[128,2048]{1,0:T(8,128)(2,1)}, f32[8,128]{1,0:T(8,128)}, f32[256,2048]{1,0:T(8,128)}, bf16[128,1024]{1,0:T(8,128)(2,1)}, bf16[128,512]{1,0:T(8,128)(2,1)}, /*index=5*/bf16[128,512]{1,0:T(8,128)(2,1)}) custom-call(bf16[1024,2048]{1,0:T(8,128)(2,1)} %get-tuple-element.75.normed_in, bf16[8,2,128,768]{3,2,1,0:T(8,128)(2,1)} %get-tuple-element.76.qkv_w, ...), custom_call_target="tpu_custom_call" | custom-call | tf_op jit(solution)/shard_map/close/pallas_call | solution.py:2347
  520.0 1.3 slice_bitcast_fusion
  521.3 6.4 %widen.1 = (bf16[128,2048]{1,0:T(8,128)(2,1)}, bf16[128,2048]{1,0:T(8,128)(2,1)}, f32[128,1024]{1,0:T(8,128)}, f32[128,512]{1,0:T(8,128)}, f32[128,512]{1,0:T(8,...) custom-call(bf16[128,2048]{1,0:T(8,128)(2,1)} %get-tuple-element.74.refs_0_, ...), custom_call_target="tpu_custom_call" | custom-call | tf_op jit(solution)/shard_map/widen/pallas_call | solution.py:2378
  (1 shorter events, 0.0 us)

commit v7 on v6

--- a/solution.py
+++ b/solution.py
@@ -1288,11 +1288,11 @@
 
         stage_store(line).start()
 
-    def weight_grad(kind):
+    def weight_grad(kind, first, last):
         source = (gate_grad, up_grad)[kind]
         store = (gate_w, up_w)[kind]
 
-        @pl.loop(0, 8)
+        @pl.loop(first, last)
         def _(tile):
             columns = pl.ds(pl.multiple_of(tile * pair, pair), pair)
             part = transposed_times(
@@ -1321,19 +1321,16 @@
     def _():
         reduce.relay(0)
 
-    weight_grad(0)
-    for cut in range(2):
-        grads.share(0, cut).start()
-    contribute(0)
+    weight_grad(0, 0, 4)
+    grads.share(0, 0).start()
 
     @pl.when(inside)
     def _():
         reduce.relay(1)
 
-    grads.relay(0)
     reduce.relay(2)
-    for line in range(1, LINE):
-        contribute(line)
+    weight_grad(0, 4, 8)
+    grads.share(0, 1).start()
     reduce.total(total)
 
     inputs = hidden_out[...]
@@ -1346,15 +1343,20 @@
     branch[...] = grad_rows.astype(jnp.bfloat16)
     back.start()
     gain_term[...] = jnp.sum(total[...] * unit_rows, axis=0, keepdims=True)
+    grads.relay(0)
     back.relay_b()
-    weight_grad(1)
     for cut in range(2):
+        weight_grad(1, cut * 4, cut * 4 + 4)
         grads.share(1, cut).start()
     for elem in order:
         back.relay(0, elem)
     grads.relay(1)
+    contribute(0)
+    contribute(1)
     for elem in order:
         back.relay(1, elem)
+    contribute(2)
+    contribute(3)
     grads.finish(0)
     for elem in order:
         back.relay(2, elem)
@@ -2269,6 +2271,8 @@
     depth = head_refs[0].shape[3]
     load_q.wait()
     load_side.wait()
+    load.wait()
+    attn_term[...] = jnp.zeros_like(attn_term)
     for place_at in range(4):
         line = reduce.order[place_at]
         both = pl.ds(pl.multiple_of(line * pair, pair), pair)
@@ -2279,9 +2283,12 @@
             part = times_transposed(grad_query[both], weight[0, pl.ds(tile * 2, 2)].reshape(width // 4, HD))
             part += times_transposed(grad_side[both], weight[1, pl.ds(tile * 2, 2)].reshape(width // 4, HD))
             parts[pl.ds(line * 2, 2), :, columns] = part.astype(jnp.bfloat16).reshape(2, rows, width // 4)
+            scaled = part * normed[both, columns].astype(jnp.float32)
+            attn_term[:, columns] += jnp.sum(scaled, axis=0, keepdims=True)
 
         reduce.start(place_at)
-    load.wait()
+    attn_term[...] = attn_term[...] / gain[...]
+    gain_sum.start(attn_term, mlp_term)
     for i, source in enumerate((grad_query, grad_side)):
 
         @pl.loop(0, 4)
@@ -2321,15 +2328,13 @@
     inputs = tokens[...].astype(jnp.float32)
     inv_scale = rms_scale(inputs)
     unit_rows = inputs * inv_scale
-    attn_term[...] = jnp.sum(total[...] * unit_rows, axis=0, keepdims=True)
-    gain_sum.start(attn_term, mlp_term)
     grad_unit = total[...] * gain[...]
     mean = jnp.mean(grad_unit * unit_rows, axis=-1, keepdims=True)
     tokens_grad[...] = (grad_hidden[...] + inv_scale * (grad_unit - unit_rows * mean)).astype(jnp.bfloat16)
+    gain_sum.finish()
     downs.finish()
     heads.finish()
     reduce.finish()
-    gain_sum.finish()
 
 
 def close(normed, qkv_w, active, cot, grad_query, grad_side, grad_hidden, tokens, gain, mlp_term):

time: 537 us -> 528 us (0.983)
  Pallas kernels: 524 us -> 516 us
    pallas_call x1, Pallas kernels: 196 us -> 190 us  [core(): pl.pallas_call(core_kernel, out_shape=(shape(rows, width, dtype=f32), sha...]
where the time goes in v7:
time: 528 us; the launch traced here: 520 us
  Pallas kernels  516 us (98%)
    pallas_call x1, Pallas kernels, core(): pl.pallas_call(core_kernel, out_shape=(shape(rows, width, dtype=f32), sha...  190 us
    pallas_call x1, Pallas kernels, front(): pl.pallas_call(front_kernel, out_shape=(shape(8, 2, 2, rows, 2 * HD), sha...  148 us
    pallas_call x1, Pallas kernels, attend_back(): pl.pallas_call(attend_back_kernel, out_shape=(shape(tokens, HD), shape(to...  96.5 us
    pallas_call x1, Pallas kernels, close(): pl.pallas_call(close_kernel, out_shape=(shape(rows, width), shape(8, rows...  74.7 us

profile of v7, /device:TPU:8, one launch (start us, length us, event | category | flops | bytes accessed | tf_op | source)
XLA Modules:
  0.0 520.0 jit_solution(17373099456591868978)
XLA Ops:
  0.6 0.7 bitcast_convert_fusion
  1.3 0.7 convert_bitcast_fusion
  2.0 0.6 concatenate.3.note
  2.6 148.4 %front.1 = (bf16[8,2,2,128,512]{4,3,2,1,0:T(8,128)(2,1)}, bf16[1024,2048]{1,0:T(8,128)(2,1)}, bf16[8,2,128,768]{3,2,1,0:T(8,128)(2,1)}, bf16[2,2,64,2048]{3,2,1,...) custom-call(bf16[128,2048]{1,0:T(8,128)(2,1)} %tokens.5, ...), custom_call_target="tpu_custom_call" | custom-call | tf_op jit(solution)/shard_map/front/pallas_call | solution.py:1616
  151.1 189.6 %core.1 = (f32[128,2048]{1,0:T(8,128)}, bf16[8,128,1024]{2,1,0:T(8,128)(2,1)}, bf16[8,128,2048]{2,1,0:T(8,128)(2,1)}, bf16[8,128,2048]{2,1,0:T(8,128)(2,1)}, f32...) custom-call(bf16[1024,256]{1,0:T(8,128)(2,1)} %get-tuple-element.58.attended., ...), custom_call_target="tpu_custom_call" | custom-call | tf_op jit(solution)/shard_map/core/pallas_call | solution.py:1385
  340.7 96.5 %attend_back.1 = (bf16[1024,256]{1,0:T(8,128)(2,1)}, bf16[1024,256]{1,0:T(8,128)(2,1)}, bf16[128,2048]{1,0:T(8,128)(2,1)}, bf16[128,4096]{1,0:T(8,128)(2,1)}, bf...) custom-call(bf16[1024,256]{1,0:T(8,128)(2,1)} %get-tuple-element.56.query, ...), custom_call_target="tpu_custom_call" | custom-call | tf_op jit(solution)/shard_map/attend_back/pallas_call | solution.py:2054
  437.2 74.7 %close.1 = (bf16[128,2048]{1,0:T(8,128)(2,1)}, f32[8,128]{1,0:T(8,128)}, f32[256,2048]{1,0:T(8,128)}, bf16[128,1024]{1,0:T(8,128)(2,1)}, bf16[128,512]{1,0:T(8,128)(2,1)}, /*index=5*/bf16[128,512]{1,0:T(8,128)(2,1)}) custom-call(bf16[1024,2048]{1,0:T(8,128)(2,1)} %get-tuple-element.75.normed_in, bf16[8,2,128,768]{3,2,1,0:T(8,128)(2,1)} %get-tuple-element.76.qkv_w, ...), custom_call_target="tpu_custom_call" | custom-call | tf_op jit(solution)/shard_map/close/pallas_call | solution.py:2352
  511.9 1.3 slice_bitcast_fusion
  513.2 6.4 %widen.1 = (bf16[128,2048]{1,0:T(8,128)(2,1)}, bf16[128,2048]{1,0:T(8,128)(2,1)}, f32[128,1024]{1,0:T(8,128)}, f32[128,512]{1,0:T(8,128)}, f32[128,512]{1,0:T(8,...) custom-call(bf16[128,2048]{1,0:T(8,128)(2,1)} %get-tuple-element.74.refs_0_, ...), custom_call_target="tpu_custom_call" | custom-call | tf_op jit(solution)/shard_map/widen/pallas_call | solution.py:2383
  (1 shorter events, 0.0 us)

commit v8 on v7

--- a/solution.py
+++ b/solution.py
@@ -1156,7 +1156,7 @@
     grads = QuarterReduce((gate_w, up_w), (gate, up), quarter_refs)
     rows, width = normed.shape[1:]
     hidden = gate_w.shape[3]
-    step = hidden // 4
+    step = hidden // 2
     pair = 2 * rows
     order = (2, 0, 1, 3)
 
@@ -1186,7 +1186,7 @@
     def forward(chip, own=False):
         shard = src if own else normed.at[chip]
 
-        @pl.loop(0, 4)
+        @pl.loop(0, 2)
         def _(tile):
             columns = pl.ds(pl.multiple_of(tile * step, step), step)
             gate_part = product(shard[...], gate_w[:, :, :, columns].reshape(width, step))
@@ -1251,11 +1251,11 @@
         both = pl.ds(line * 2, 2)
         cot_load(place_at).wait()
 
-        @pl.loop(0, 4)
+        @pl.loop(0, 2)
         def _(tile):
             columns = pl.ds(pl.multiple_of(tile * step, step), step)
             grad_active = times_transposed(
-                cot_pairs[place_at % 2].reshape(pair, width), down_w[tile // 2, tile % 2]
+                cot_pairs[place_at % 2].reshape(pair, width), down_w[tile].reshape(step, width)
             ).reshape(2, rows, step)
             gate_grad[both, :, columns] = (grad_active * gate_factor[both, :, columns].astype(jnp.float32)).astype(jnp.bfloat16)
             up_grad[both, :, columns] = (grad_active * up_factor[both, :, columns].astype(jnp.float32)).astype(jnp.bfloat16)

time: 528 us -> 525 us (level)
  no operation moved by 1% of the time
where the time goes in v8:
time: 525 us; the launch traced here: 517 us
  Pallas kernels  513 us (98%)
    pallas_call x1, Pallas kernels, core(): pl.pallas_call(core_kernel, out_shape=(shape(rows, width, dtype=f32), sha...  188 us
    pallas_call x1, Pallas kernels, front(): pl.pallas_call(front_kernel, out_shape=(shape(8, 2, 2, rows, 2 * HD), sha...  148 us
    pallas_call x1, Pallas kernels, attend_back(): pl.pallas_call(attend_back_kernel, out_shape=(shape(tokens, HD), shape(to...  96.2 us
    pallas_call x1, Pallas kernels, close(): pl.pallas_call(close_kernel, out_shape=(shape(rows, width), shape(8, rows...  74.1 us

profile of v8, /device:TPU:8, one launch (start us, length us, event | category | flops | bytes accessed | tf_op | source)
XLA Modules:
  0.0 517.1 jit_solution(7002340358118569077)
XLA Ops:
  0.6 0.7 bitcast_convert_fusion
  1.3 0.7 convert_bitcast_fusion
  2.0 0.6 concatenate.3.note
  2.6 148.4 %front.1 = (bf16[8,2,2,128,512]{4,3,2,1,0:T(8,128)(2,1)}, bf16[1024,2048]{1,0:T(8,128)(2,1)}, bf16[8,2,128,768]{3,2,1,0:T(8,128)(2,1)}, bf16[2,2,64,2048]{3,2,1,...) custom-call(bf16[128,2048]{1,0:T(8,128)(2,1)} %tokens.5, ...), custom_call_target="tpu_custom_call" | custom-call | tf_op jit(solution)/shard_map/front/pallas_call | solution.py:1616
  151.1 187.9 %core.1 = (f32[128,2048]{1,0:T(8,128)}, bf16[8,128,1024]{2,1,0:T(8,128)(2,1)}, bf16[8,128,2048]{2,1,0:T(8,128)(2,1)}, bf16[8,128,2048]{2,1,0:T(8,128)(2,1)}, f32...) custom-call(bf16[1024,256]{1,0:T(8,128)(2,1)} %get-tuple-element.58.attended., ...), custom_call_target="tpu_custom_call" | custom-call | tf_op jit(solution)/shard_map/core/pallas_call | solution.py:1385
  339.0 96.2 %attend_back.1 = (bf16[1024,256]{1,0:T(8,128)(2,1)}, bf16[1024,256]{1,0:T(8,128)(2,1)}, bf16[128,2048]{1,0:T(8,128)(2,1)}, bf16[128,4096]{1,0:T(8,128)(2,1)}, bf...) custom-call(bf16[1024,256]{1,0:T(8,128)(2,1)} %get-tuple-element.56.query, ...), custom_call_target="tpu_custom_call" | custom-call | tf_op jit(solution)/shard_map/attend_back/pallas_call | solution.py:2054
  435.2 74.1 %close.1 = (bf16[128,2048]{1,0:T(8,128)(2,1)}, f32[8,128]{1,0:T(8,128)}, f32[256,2048]{1,0:T(8,128)}, bf16[128,1024]{1,0:T(8,128)(2,1)}, bf16[128,512]{1,0:T(8,128)(2,1)}, /*index=5*/bf16[128,512]{1,0:T(8,128)(2,1)}) custom-call(bf16[1024,2048]{1,0:T(8,128)(2,1)} %get-tuple-element.75.normed_in, bf16[8,2,128,768]{3,2,1,0:T(8,128)(2,1)} %get-tuple-element.76.qkv_w, ...), custom_call_target="tpu_custom_call" | custom-call | tf_op jit(solution)/shard_map/close/pallas_call | solution.py:2352
  509.3 1.3 slice_bitcast_fusion
  510.6 6.4 %widen.1 = (bf16[128,2048]{1,0:T(8,128)(2,1)}, bf16[128,2048]{1,0:T(8,128)(2,1)}, f32[128,1024]{1,0:T(8,128)}, f32[128,512]{1,0:T(8,128)}, f32[128,512]{1,0:T(8,...) custom-call(bf16[128,2048]{1,0:T(8,128)(2,1)} %get-tuple-element.74.refs_0_, ...), custom_call_target="tpu_custom_call" | custom-call | tf_op jit(solution)/shard_map/widen/pallas_call | solution.py:2383
  (1 shorter events, 0.0 us)
